TPU v7x, 32 devices: a whole 2x2x4 slice. The times are simulated.
32 devices in a mesh: dp: 16 (over z, y, x), blk: 2 (over core).
Axes of the slice: x: 2, y: 2, z: 4, core: 2. Of those that a mesh axis runs over, the one named last changes fastest.
Arguments:
- tokens: bfloat16 [32, 1024, 1024], P('dp', 'blk'), may hold values from -6 to 6
- lengths: int32 [32], P('dp'), may hold values from 1 to 1024, as said below
- time_index: int32 [32], P('dp'), may hold values from 0 to 999
- qkv_weight: bfloat16 [1024, 3072], P('dp'), may hold values from -0.1875 to 0.1875
- out_weight: bfloat16 [1024, 1024], P('dp'), may hold values from -4 to 4
- up_weight: bfloat16 [1024, 4096], P('dp'), may hold values from -0.1875 to 0.1875
- down_weight: bfloat16 [4096, 1024], P('dp'), may hold values from -0.09375 to 0.09375
- time_weight: bfloat16 [128, 2048], P('dp'), may hold values from -0.25 to 0.25
- norm1_gain: bfloat16 [1024], P('dp'), may hold values from 0.5 to 1.5
- norm1_bias: bfloat16 [1024], P('dp'), may hold values from -4 to 4
- norm2_gain: bfloat16 [1024], P('dp'), may hold values from 0.5 to 1.5
- norm2_bias: bfloat16 [1024], P('dp'), may hold values from -4 to 4
- cotangent: bfloat16 [32, 1024, 1024], P('dp', 'blk'), may hold values from -6 to 6
Outputs:
- layer_out: bfloat16 [32, 1024, 1024], P('dp', 'blk')
- grad_tokens: bfloat16 [32, 1024, 1024], P('dp', 'blk')
- grad_qkv: float32 [1024, 3072], P('dp')
- grad_out_proj: float32 [1024, 1024], P('dp')
- grad_up: float32 [1024, 4096], P('dp')
- gradient_down_matrix: float32 [4096, 1024], P('dp')
- grad_time: float32 [128, 2048], P('dp')
- grad_gain1: float32 [1024], P('dp')
- grad_bias1: float32 [1024], P('dp')
- grad_gain2: float32 [1024], P('dp')
- grad_bias2: float32 [1024], P('dp')
Inputs may be any that keep to these rules, and one draw needn't show every extreme that they name: `lengths`: in each group of 2 consecutive sequences (one index of dp), at least one has length 1024.
All inputs are finite; a program needn't handle non-finite values.
Results may differ from a plain program's by a relative error of at most 0.022.
Values may be sent and summed in bfloat16 or wider, within the bound.
No kernel may reach another device: no remote copies, remote signals or barrier semaphores. Data moves between devices by JAX's collectives and lax.ppermute only.
A program may use at most 320 MiB of HBM per device.

v0:
```python
import math

import jax
import jax.numpy as jnp
from jax import lax
from jax.sharding import PartitionSpec as P

H = 16
HD = 64
TF = 128


highest = lax.Precision.HIGHEST
epsilon = 1e-05
masked = -1e30
start_max = -1e29


def passed_along(block, axis, distance):
    devices = range(lax.axis_size(axis))
    route = [((i - distance) % len(devices), i) for i in devices]
    return lax.ppermute(block, axis, route)


def layer_norm(inputs, norm_gain, norm_bias, time_scale):
    centre = inputs - jnp.mean(inputs, axis=-1, keepdims=True)
    spread = jnp.mean(centre * centre, axis=-1, keepdims=True)
    return centre * lax.rsqrt(spread + epsilon) * norm_gain * (1.0 + time_scale) + norm_bias


def time_features(time_steps, feature_count):
    half_width = feature_count // 2
    frequency = jnp.exp(
        jnp.arange(half_width, dtype=jnp.float32) * (-math.log(10000.0) / half_width)
    )
    angles = time_steps.astype(jnp.float32)[:, None] * frequency[None, :]
    return jnp.concatenate([jnp.sin(angles), jnp.cos(angles)], axis=-1)


def rotary_tables(positions, head_size):
    half_size = head_size // 2
    inverse = jnp.exp(
        jnp.arange(half_size, dtype=jnp.float32) * (-2.0 * math.log(10000.0) / head_size)
    )
    angles = positions.astype(jnp.float32)[:, None] * inverse[None, :]
    return (jnp.cos(angles), jnp.sin(angles))


def rotate(heads_in, cosine, sine_table):
    half_size = heads_in.shape[-1] // 2
    first_half = heads_in[..., :half_size]
    second = heads_in[..., half_size:]
    cos_rows = cosine[:, None, :]
    sin_rows = sine_table[:, None, :]
    return jnp.concatenate(
        [first_half * cos_rows - second * sin_rows, second * cos_rows + first_half * sin_rows],
        axis=-1,
    )


def unrotate(grads_in, cosine, sine_table):
    half_size = grads_in.shape[-1] // 2
    first_half = grads_in[..., :half_size]
    second = grads_in[..., half_size:]
    cos_rows = cosine[:, None, :]
    sin_rows = sine_table[:, None, :]
    return jnp.concatenate(
        [first_half * cos_rows + second * sin_rows, second * cos_rows - first_half * sin_rows],
        axis=-1,
    )


def smooth_gate(hidden_rows):
    return jax.nn.gelu(hidden_rows, approximate=True)


def block_scores(queries, key_block, key_start, seq_lengths):
    raw_scores = jnp.einsum(
        "sqhe,skhe->shqk", queries, key_block, preferred_element_type=jnp.float32
    ) * queries.shape[-1] ** (-0.5)
    key_places = key_start + jnp.arange(key_block.shape[1], dtype=jnp.int32)
    is_valid = key_places[None, :] < seq_lengths[:, None]
    return jnp.where(is_valid[:, None, None, :], raw_scores, masked)


def absorb(state, queries, key_block, value_block, key_start, seq_lengths):
    run_max, run_total, run_out = state
    scores = block_scores(queries, key_block, key_start, seq_lengths)
    new_max = jnp.maximum(run_max, jnp.max(scores, axis=-1))
    factor = jnp.exp(run_max - new_max)
    block_weights = jnp.exp(scores - new_max[..., None])
    run_total = run_total * factor + jnp.sum(block_weights, axis=-1)
    run_out = run_out * factor[..., None] + jnp.einsum(
        "shqk,skhe->shqe",
        block_weights.astype(jnp.bfloat16),
        value_block,
        preferred_element_type=jnp.float32,
    )
    return (new_max, run_total, run_out)


def back_block(
    queries, key_block, value_block, key_start, seq_lengths, log_total, delta, grad_heads
):
    scores = block_scores(queries, key_block, key_start, seq_lengths)
    probs_full = jnp.exp(scores - log_total[..., None])
    grad_values = jnp.einsum(
        "shqk,sqhe->skhe",
        probs_full.astype(jnp.bfloat16),
        grad_heads,
        preferred_element_type=jnp.float32,
    )
    grad_probs = jnp.einsum(
        "sqhe,skhe->shqk", grad_heads, value_block, preferred_element_type=jnp.float32
    )
    grad_scores = (probs_full * (grad_probs - delta[..., None])).astype(jnp.bfloat16)
    inv_root = queries.shape[-1] ** (-0.5)
    grad_queries = (
        jnp.einsum("shqk,skhe->sqhe", grad_scores, key_block, preferred_element_type=jnp.float32)
        * inv_root
    )
    grad_keys = (
        jnp.einsum("shqk,sqhe->skhe", grad_scores, queries, preferred_element_type=jnp.float32)
        * inv_root
    )
    return (grad_queries, grad_keys, grad_values)


def shards(
    tokens,
    lengths,
    time_index,
    qkv_weight,
    out_weight,
    up_weight,
    down_weight,
    time_weight,
    norm1_gain,
    norm1_bias,
    norm2_gain,
    norm2_bias,
    cotangent,
):
    seq_count, block_len, model_width = tokens.shape
    cycle_size = lax.axis_size("blk")
    my_index = lax.axis_index("blk")
    local_start = my_index * block_len
    gathered = (
        lax.all_gather(qkv_weight, "dp", axis=0, tiled=True),
        lax.all_gather(out_weight, "dp", axis=0, tiled=True),
        lax.all_gather(up_weight, "dp", axis=0, tiled=True),
        lax.all_gather(down_weight, "dp", axis=0, tiled=True),
        lax.all_gather(time_weight, "dp", axis=0, tiled=True),
        lax.all_gather(norm1_gain, "dp", axis=0, tiled=True),
        lax.all_gather(norm1_bias, "dp", axis=0, tiled=True),
        lax.all_gather(norm2_gain, "dp", axis=0, tiled=True),
        lax.all_gather(norm2_bias, "dp", axis=0, tiled=True),
    )
    (
        query_key_value_matrix,
        output_matrix,
        up_matrix,
        down_matrix,
        w_time,
        gain_one,
        bias_one,
        gain_two,
        bias_two,
    ) = gathered
    gain_one = gain_one.astype(jnp.float32)
    bias_one = bias_one.astype(jnp.float32)
    gain_two = gain_two.astype(jnp.float32)
    bias_two = bias_two.astype(jnp.float32)
    features = time_features(time_index, TF)
    scales = jnp.dot(features, w_time.astype(jnp.float32), precision=highest)
    scale_one = scales[:, None, :model_width]
    scale_two = scales[:, None, model_width:]
    inputs = tokens.astype(jnp.float32)
    normed, norm_one_back = jax.vjp(layer_norm, inputs, gain_one, bias_one, scale_one)
    normalized_lowprec = normed.astype(jnp.bfloat16)
    packed_rows = jnp.einsum(
        "ajg,gb->ajb",
        normalized_lowprec,
        query_key_value_matrix,
        preferred_element_type=jnp.float32,
    )
    cosine, sine_table = rotary_tables(local_start + jnp.arange(block_len, dtype=jnp.int32), HD)
    heads_shape = (seq_count, block_len, H, HD)
    queries = rotate(
        packed_rows[..., :model_width].reshape(heads_shape), cosine, sine_table
    ).astype(jnp.bfloat16)
    key_rows = rotate(
        packed_rows[..., model_width : 2 * model_width].reshape(heads_shape), cosine, sine_table
    ).astype(jnp.bfloat16)
    value_rows = packed_rows[..., 2 * model_width :].reshape(heads_shape).astype(jnp.bfloat16)
    state = (
        jnp.full((seq_count, H, block_len), start_max, jnp.float32),
        jnp.zeros((seq_count, H, block_len), jnp.float32),
        jnp.zeros((seq_count, H, block_len, HD), jnp.float32),
    )
    state = absorb(state, queries, key_rows, value_rows, local_start, lengths)
    moving_keys, moving_values = (key_rows, value_rows)
    for turn_index in range(1, cycle_size):
        moving_keys, moving_values = passed_along((moving_keys, moving_values), "blk", 1)
        owner = (my_index - turn_index) % cycle_size
        state = absorb(state, queries, moving_keys, moving_values, owner * block_len, lengths)
    run_max, run_total, run_out = state
    log_total = run_max + jnp.log(run_total)
    heads_out = jnp.transpose(run_out / run_total[..., None], (0, 2, 1, 3))
    mixed_lowprec = heads_out.reshape(seq_count, block_len, model_width).astype(jnp.bfloat16)
    middle_rows = inputs + jnp.einsum(
        "ajg,gb->ajb", mixed_lowprec, output_matrix, preferred_element_type=jnp.float32
    )
    normed_two, norm_two_back = jax.vjp(layer_norm, middle_rows, gain_two, bias_two, scale_two)
    normalized_second_lowprec = normed_two.astype(jnp.bfloat16)
    hidden_rows = jnp.einsum(
        "vxp,pa->vxa", normalized_second_lowprec, up_matrix, preferred_element_type=jnp.float32
    )
    active, gate_back = jax.vjp(smooth_gate, hidden_rows)
    activation_lowprec = active.astype(jnp.bfloat16)
    layer_out = (
        middle_rows
        + jnp.einsum(
            "unr,rv->unv", activation_lowprec, down_matrix, preferred_element_type=jnp.float32
        )
    ).astype(jnp.bfloat16)
    query_key_value_matrix, output_matrix, up_matrix, down_matrix = (
        lax.all_gather(qkv_weight, "dp", axis=0, tiled=True),
        lax.all_gather(out_weight, "dp", axis=0, tiled=True),
        lax.all_gather(up_weight, "dp", axis=0, tiled=True),
        lax.all_gather(down_weight, "dp", axis=0, tiled=True),
    )
    gradient_down_matrix = jnp.einsum(
        "qxn,qxr->nr", activation_lowprec, cotangent, preferred_element_type=jnp.float32
    )
    gradient_activation = jnp.einsum(
        "prx,ux->pru", cotangent, down_matrix, preferred_element_type=jnp.float32
    )
    gradient_hidden_rows = gate_back(gradient_activation)[0].astype(jnp.bfloat16)
    grad_up = jnp.einsum(
        "qzw,qzu->wu",
        normalized_second_lowprec,
        gradient_hidden_rows,
        preferred_element_type=jnp.float32,
    )
    grad_normed_two = jnp.einsum(
        "wny,ky->wnk", gradient_hidden_rows, up_matrix, preferred_element_type=jnp.float32
    )
    grad_mid_part, grad_gain_two, grad_bias_two, grad_scale_two = norm_two_back(grad_normed_two)
    grad_middle = cotangent.astype(jnp.float32) + grad_mid_part
    gradient_middle_lowprec = grad_middle.astype(jnp.bfloat16)
    grad_outw = jnp.einsum(
        "yph,ypi->hi", mixed_lowprec, gradient_middle_lowprec, preferred_element_type=jnp.float32
    )
    grad_mixed = jnp.einsum(
        "wuo,xo->wux", gradient_middle_lowprec, output_matrix, preferred_element_type=jnp.float32
    )
    grad_heads = grad_mixed.reshape(heads_shape).astype(jnp.bfloat16)
    delta = jnp.transpose(jnp.sum(grad_heads.astype(jnp.float32) * heads_out, axis=-1), (0, 2, 1))
    grad_queries = jnp.zeros(heads_shape, jnp.float32)
    grad_keys = jnp.zeros(heads_shape, jnp.float32)
    grad_values = jnp.zeros(heads_shape, jnp.float32)
    moving_keys, moving_values = (key_rows, value_rows)
    for turn_index in range(cycle_size):
        owner = (my_index - turn_index) % cycle_size
        part_query, part_key, part_value = back_block(
            queries,
            moving_keys,
            moving_values,
            owner * block_len,
            lengths,
            log_total,
            delta,
            grad_heads,
        )
        grad_queries = grad_queries + part_query
        grad_keys = grad_keys + part_key
        grad_values = grad_values + part_value
        if turn_index + 1 < cycle_size:
            moving_keys, moving_values = passed_along((moving_keys, moving_values), "blk", 1)
        grad_keys, grad_values = (
            passed_along(grad_keys.astype(jnp.bfloat16), "blk", 1).astype(grad_keys.dtype),
            passed_along(grad_values.astype(jnp.bfloat16), "blk", 1).astype(grad_values.dtype),
        )
    flat_shape = (seq_count, block_len, model_width)
    grad_query_raw = (
        unrotate(grad_queries, cosine, sine_table).reshape(flat_shape).astype(jnp.bfloat16)
    )
    grad_key_raw = unrotate(grad_keys, cosine, sine_table).reshape(flat_shape).astype(jnp.bfloat16)
    grad_value_raw = grad_values.reshape(flat_shape).astype(jnp.bfloat16)
    gradient_packed_rows = jnp.concatenate([grad_query_raw, grad_key_raw, grad_value_raw], axis=-1)
    grad_qkv = jnp.einsum(
        "yph,ypi->hi", normalized_lowprec, gradient_packed_rows, preferred_element_type=jnp.float32
    )
    gradient_normalized = jnp.einsum(
        "wuo,xo->wux",
        gradient_packed_rows,
        query_key_value_matrix,
        preferred_element_type=jnp.float32,
    )
    grad_in_part, grad_gain_one, grad_bias_one, grad_scale_one = norm_one_back(gradient_normalized)
    grad_tokens = (grad_middle + grad_in_part).astype(jnp.bfloat16)
    grad_scales = jnp.concatenate([grad_scale_one[:, 0, :], grad_scale_two[:, 0, :]], axis=-1)
    grad_time = jnp.dot(features.T, grad_scales, precision=highest)
    grad_list = (
        grad_qkv,
        grad_outw,
        grad_up,
        gradient_down_matrix,
        grad_time,
        grad_gain_one,
        grad_bias_one,
        grad_gain_two,
        grad_bias_two,
    )
    reduced = (
        lax.psum_scatter(
            grad_list[0].astype(jnp.bfloat16), "dp", scatter_dimension=0, tiled=True
        ).astype(jnp.float32),
        lax.psum_scatter(
            grad_list[1].astype(jnp.bfloat16), "dp", scatter_dimension=0, tiled=True
        ).astype(jnp.float32),
        lax.psum_scatter(
            grad_list[2].astype(jnp.bfloat16), "dp", scatter_dimension=0, tiled=True
        ).astype(jnp.float32),
        lax.psum_scatter(
            grad_list[3].astype(jnp.bfloat16), "dp", scatter_dimension=0, tiled=True
        ).astype(jnp.float32),
        lax.psum_scatter(
            grad_list[4].astype(jnp.bfloat16), "dp", scatter_dimension=0, tiled=True
        ).astype(jnp.float32),
        lax.psum_scatter(
            grad_list[5].astype(jnp.bfloat16), "dp", scatter_dimension=0, tiled=True
        ).astype(jnp.float32),
        lax.psum_scatter(
            grad_list[6].astype(jnp.bfloat16), "dp", scatter_dimension=0, tiled=True
        ).astype(jnp.float32),
        lax.psum_scatter(
            grad_list[7].astype(jnp.bfloat16), "dp", scatter_dimension=0, tiled=True
        ).astype(jnp.float32),
        lax.psum_scatter(
            grad_list[8].astype(jnp.bfloat16), "dp", scatter_dimension=0, tiled=True
        ).astype(jnp.float32),
    )
    summed = (
        lax.psum(reduced[0].astype(jnp.bfloat16), "blk").astype(jnp.float32),
        lax.psum(reduced[1].astype(jnp.bfloat16), "blk").astype(jnp.float32),
        lax.psum(reduced[2].astype(jnp.bfloat16), "blk").astype(jnp.float32),
        lax.psum(reduced[3].astype(jnp.bfloat16), "blk").astype(jnp.float32),
        lax.psum(reduced[4].astype(jnp.bfloat16), "blk").astype(jnp.float32),
        lax.psum(reduced[5].astype(jnp.bfloat16), "blk").astype(jnp.float32),
        lax.psum(reduced[6].astype(jnp.bfloat16), "blk").astype(jnp.float32),
        lax.psum(reduced[7].astype(jnp.bfloat16), "blk").astype(jnp.float32),
        lax.psum(reduced[8].astype(jnp.bfloat16), "blk").astype(jnp.float32),
    )
    return (
        layer_out,
        grad_tokens,
        summed[0],
        summed[1],
        summed[2],
        summed[3],
        summed[4],
        summed[5],
        summed[6],
        summed[7],
        summed[8],
    )


def solution(mesh):
    return jax.shard_map(
        shards,
        mesh=mesh,
        in_specs=(
            P("dp", "blk", None),
            P("dp"),
            P("dp"),
            P("dp", None),
            P("dp", None),
            P("dp", None),
            P("dp", None),
            P("dp", None),
            P("dp"),
            P("dp"),
            P("dp"),
            P("dp"),
            P("dp", "blk", None),
        ),
        out_specs=(
            P("dp", "blk", None),
            P("dp", "blk", None),
            P("dp", None),
            P("dp", None),
            P("dp", None),
            P("dp", None),
            P("dp", None),
            P("dp"),
            P("dp"),
            P("dp"),
            P("dp"),
        ),
        check_vma=False,
    )
```

profile of v0, /device:TPU:1, one launch (start us, length us, event | category | flops | bytes accessed | tf_op | source)
XLA Modules:
  0.0 1234.8 jit_solution(7261933057094617670)
XLA Ops:
  16.1 36.8 %all-reduce.9 = (bf16[1024]{0:T(1024)(128)(2,1)S(1)}, bf16[1024]{0:T(1024)(128)(2,1)S(1)}, bf16[1024]{0:T(1024)(128)(2,1)S(1)}, bf16[1024]{0:T(1024)(128)(2,1)S(1)}) all-reduce(bf16[1024]{0:T(1024)(128)(2,1)S(1)} %dynamic-update-slice.1, bf16[1024]{0:T(1024)(128)(2,1)S(1)} %dynamic-update-slice, ...), channel_id=1, replica_groups=mesh['dp'=16,'blk'=2] {'dp'}, use_global_device_ids=true, to_apply=%add.1 | all-reduce | flops 4096 | bytes 16384
  53.0 1.9 convert_reduce_fusion
  55.7 36.4 %all_gather.32 = bf16[128,2048]{1,0:T(8,128)(2,1)S(1)} all-gather(bf16[8,2048]{1,0:T(8,128)(2,1)S(1)} %copy-done.40), channel_id=1, replica_groups=mesh['dp'=16,'blk'=2] {'dp'}, dimensions={0}, use_global_device_ids=true | all-gather | bytes 557056 | tf_op jit(solution)/shard_map/all_gather | solution.py:153
  93.6 20.5 %all-gather.5.cloned.1.call-done = bf16[1024,3072]{1,0:T(8,128)(2,1)} async-done(((bf16[64,3072]{1,0:T(8,128)(2,1)}), bf16[1024,3072]{1,0:T(8,128)(2,1)}) %all-gather.5.cloned.1.call-update) | async-done | bytes 6291472 | tf_op jit(solution)/shard_map/all_gather | solution.py:149
  114.0 9.1 fusion.35
  123.2 4.6 fusion.100
  127.8 2.4 copy-done.15
  130.2 5.4 copy.70
  135.6 5.4 copy.71
  141.0 6.0 subtract_convert_fusion.3
  150.7 3.8 slice.85
  154.5 4.0 copy.72
  158.5 16.5 %select_reduce_fusion = (f32[2,16,512]{2,1,0:T(8,128)S(1)}, f32[2,16,512,512]{2,3,1,0:T(8,128)}) fusion(pred[2,512]{1,0:T(4,128)(4,1)S(1)} %get-tuple-element.67, bf16[2,512,16,32]{1,3,2,0:T(8,128)(2,1)} %copy-done.12, bf16[2,512,16,32]{1,3,2,0:T(8,128)(2,1)} %copy-done.14, bf16[2,512,16,32]{1,3,2,0:T(8,128)(2,1)} %get-tuple-element.45, ...), kind=kOutput, calls=%fused_computation.7 | convolution fusion | flops 1107279872 | bytes 37815296 | tf_op jit(solution)/shard_map/sqhe,skhe->shqk/dot_general | solution.py:78
  175.1 16.9 %fusion.102 = (f32[2,16,512]{2,1,0:T(8,128)S(1)}, f32[2,16,512,512]{2,3,1,0:T(8,128)}) fusion(bf16[2,512,16,64]{1,3,2,0:T(8,128)(2,1)} %collective-permute-done, bf16[2,512,16,32]{1,3,2,0:T(8,128)(2,1)S(1)} %copy-done.6, bf16[2,512,16,32]{1,3,2,0:T(8,128)(2,1)S(1)} %get-tuple-element.44, pred[2,512]{1,0:T(4,128)(4,1)S(1)} %get-tuple-element.66), kind=kOutput, calls=%fused_computation.164 | convolution fusion | flops 1103085568 | bytes 37815296 | tf_op jit(solution)/shard_map/sqhe,skhe->shqk/dot_general | solution.py:78
  192.0 13.5 %fusion = f32[2,16,512]{2,1,0:T(8,128)S(1)} fusion(f32[2,16,512,512]{2,3,1,0:T(8,128)} %get-tuple-element.69, f32[2,16,512]{2,1,0:T(8,128)S(1)} %get-tuple-element.56), kind=kLoop, calls=%fused_computation.8 | loop fusion | flops 16760832 | bytes 33685504 | tf_op jit(solution)/shard_map/reduce_sum | solution.py:92
  205.5 7.2 copy-done.3
  212.7 7.6 fusion.3
  220.3 16.8 %fusion.21 = f32[2,16,512,64]{2,3,1,0:T(8,128)} fusion(bf16[2,512,16,64]{1,3,2,0:T(8,128)(2,1)} %bitcast.143, f32[2,16,512,512]{2,3,1,0:T(8,128)} %get-tuple-element.71, f32[2,16,512]{2,1,0:T(8,128)S(1)} %get-tuple-element.55, pred[2,512]{1,0:T(4,128)(4,1)S(1)} %get-tuple-element.67), kind=kOutput, calls=%fused_computation.31 | convolution fusion | flops 1107296256 | bytes 39912448 | tf_op jit(solution)/shard_map/shqk,skhe->shqe/dot_general | solution.py:93
  237.1 19.7 %fusion.97 = (bf16[2,512,16,64]{1,3,2,0:T(8,128)(2,1)}, f32[2,16,512,64]{2,3,1,0:T(8,128)}) fusion(f32[2,512,16]{1,2,0:T(8,128)S(1)} %get-tuple-element.51, f32[2,512,16]{1,2,0:T(8,128)S(1)} %get-tuple-element.50, f32[2,16,512,64]{2,3,1,0:T(8,128)} %fusion.21, f32[2,512,16]{1,2,0:T(8,128)S(1)} %get-tuple-element.54, ...), kind=kOutput, calls=%fused_computation.159 | convolution fusion | flops 1095761920 | bytes 46399488 | tf_op jit(solution)/shard_map/shqk,skhe->shqe/dot_general | solution.py:93
  256.8 4.9 fusion.103
  261.7 1.9 copy-done.10
  264.3 26.4 %all-gather.9.cloned.1.call-done = bf16[1024,4096]{1,0:T(8,128)(2,1)} async-done(((bf16[64,4096]{1,0:T(8,128)(2,1)}), bf16[1024,4096]{1,0:T(8,128)(2,1)}) %all-gather.9.cloned.1.call-update) | async-done | bytes 8388624 | tf_op jit(solution)/shard_map/all_gather | solution.py:151
  290.8 16.8 %fusion.31 = f32[2,512,4096]{2,1,0:T(8,128)} fusion(bf16[1024,4096]{1,0:T(8,128)(2,1)} %all-gather.9.cloned.1.call-done, f32[2,512,1024]{2,1,0:T(8,128)} %copy-done.10, f32[1024]{0:T(1024)S(1)} %convert_element_type.213, f32[2,1024]{1,0:T(2,128)S(1)} %get-tuple-element.57, f32[1024]{0:T(1024)S(1)} %convert_element_type.212, f32[2,512]{1,0:T(2,128)S(1)} %fusion.85, ...), kind=kOutput, calls=%fused_computation.41 | convolution fusion | flops 8596226048 | bytes 29384704 | tf_op jit(solution)/shard_map/vxp,pa->vxa/dot_general | solution.py:216
  307.6 96.9 %all-gather.11.cloned.1.call-done = bf16[4096,1024]{1,0:T(8,128)(2,1)} async-done(((bf16[256,1024]{1,0:T(8,128)(2,1)}), bf16[4096,1024]{1,0:T(8,128)(2,1)}) %all-gather.11.cloned.1.call-update) | async-done | bytes 8388624 | tf_op jit(solution)/shard_map/all_gather | solution.py:152
  404.5 22.8 %fusion.12 = bf16[2,512,4096]{2,1,0:T(8,128)(2,1)} fusion(f32[2,512,4096]{2,1,0:T(8,128)} %fusion.31, bf16[2,512,1024]{2,1,0:T(8,128)(2,1)S(1)} %copy-done.16, bf16[4096,1024]{1,0:T(8,128)(2,1)} %all-gather.11.cloned.1.call-done), kind=kOutput, calls=%fused_computation.22 | convolution fusion | flops 8673820672 | bytes 35651584 | tf_op jit(solution)/shard_map/prx,ux->pru/dot_general | solution.py:236
  427.2 16.7 %multiply_reduce_fusion = (bf16[1024]{0:T(1024)(128)(2,1)}, f32[2,512]{1,0:T(2,128)S(1)}, f32[2,1024]{1,0:T(2,128)}, bf16[1024]{0:T(1024)(128)(2,1)}, f32[2,512,1024]{2,1,0:T(8,128)S(1)}) fusion(f32[2,512,1024]{2,1,0:T(8,128)} %copy-done.10, f32[2,1024]{1,0:T(2,128)S(1)} %get-tuple-element.57, f32[2,512]{1,0:T(2,128)S(1)} %fusion.85, ...), kind=kOutput, calls=%fused_computation.77 | convolution fusion | flops 8602512384 | bytes 25202688 | tf_op jit(solution)/shard_map/wny,ky->wnk/dot_general | solution.py:246
  449.1 3.7 fusion.66
  452.8 2.9 copy.76
  455.7 5.4 multiply_reduce_fusion.2
  461.1 15.6 %convert_bitcast_fusion = bf16[2,512,16,64]{1,3,2,0:T(8,128)(2,1)} fusion(bf16[2,512,16,64]{1,3,2,0:T(8,128)(2,1)S(1)} %bitcast.132, f32[2,16,512,512]{2,3,1,0:T(8,128)} %get-tuple-element.71, f32[2,16,512]{2,1,0:T(8,128)S(1)} %log_add_fusion, pred[2,512]{1,0:T(4,128)(4,1)S(1)} %copy-done.54), kind=kOutput, calls=%fused_computation.98 | convolution fusion | flops 1108344832 | bytes 37815296 | tf_op jit(solution)/shard_map/shqk,sqhe->skhe/dot_general | solution.py:107
  476.7 22.4 %multiply_convert_fusion.1 = bf16[2,16,512,512]{2,3,1,0:T(8,128)(2,1)} fusion(f32[2,16,512,512]{2,3,1,0:T(8,128)} %get-tuple-element.71, bf16[2,512,16,64]{1,3,2,0:T(8,128)(2,1)S(1)} %bitcast.133, bf16[2,512,16,64]{1,3,2,0:T(8,128)(2,1)} %bitcast.144, f32[2,16,512]{2,1,0:T(8,128)S(1)} %bitcast.145, f32[2,16,512]{2,1,0:T(8,128)S(1)} %log_add_fusion, ...), kind=kOutput, calls=%fused_computation.2 | convolution fusion | flops 1124073472 | bytes 54658048 | tf_op jit(solution)/shard_map/sqhe,skhe->shqk/dot_general | solution.py:113
  499.1 10.4 fusion.73
  511.0 3.6 bitcast_convert_fusion.3
  514.8 20.4 %multiply_convert_fusion = bf16[2,16,512,512]{2,3,1,0:T(8,128)(2,1)} fusion(f32[2,16,512,512]{2,3,1,0:T(8,128)} %get-tuple-element.69, bf16[2,512,16,64]{1,3,2,0:T(8,128)(2,1)S(1)} %bitcast.134, bf16[2,512,16,64]{1,3,2,0:T(8,128)(2,1)} %collective-permute-done.1, f32[2,16,512]{2,1,0:T(8,128)S(1)} %bitcast.146, f32[2,16,512]{2,1,0:T(8,128)S(1)} %log_add_fusion), kind=kOutput, calls=%fused_computation | convolution fusion | flops 1107296256 | bytes 54657024 | tf_op jit(solution)/shard_map/sqhe,skhe->shqk/dot_general | solution.py:113
  535.2 11.1 fusion.52
  546.8 15.7 %fusion.51 = bf16[2,512,16,64]{1,3,2,0:T(8,128)(2,1)} fusion(bf16[2,512,16,64]{1,3,2,0:T(8,128)(2,1)} %collective-permute-done.4, bf16[2,512,16,64]{1,3,2,0:T(8,128)(2,1)S(1)} %bitcast.135, f32[2,16,512,512]{2,3,1,0:T(8,128)} %get-tuple-element.69, f32[2,16,512]{2,1,0:T(8,128)S(1)} %log_add_fusion), kind=kOutput, calls=%fused_computation.70 | convolution fusion | flops 1093664768 | bytes 39911424 | tf_op jit(solution)/shard_map/shqk,sqhe->skhe/dot_general | solution.py:107
  562.6 9.2 fusion.98
  571.8 9.3 multiply_bitcast_fusion
  581.1 2.2 convert_element_type.230
  583.4 2.4 add_convert_fusion.4
  585.9 2.4 copy.85
  588.4 2.7 pad_maximum_fusion.6
  591.2 4.1 copy.86
  595.3 4.1 copy.87
  599.4 12.5 %bitcast_convert_fusion.2 = bf16[1024,3072]{1,0:T(8,128)(2,1)} fusion(bf16[2,512,1024]{2,1,0:T(8,128)(2,1)} %copy.87, bf16[2,512,1024]{2,1,0:T(8,128)(2,1)} %copy.86, bf16[2,512,1024]{2,1,0:T(8,128)(2,1)} %copy.85, bf16[2,512,1024]{2,1,0:T(8,128)(2,1)S(1)} %copy-done.2, f32[1024]{0:T(1024)S(1)} %copy-done.51, f32[2,1024]{1,0:T(2,128)S(1)} %copy-done.25, ...), kind=kOutput, calls=%fused_computation.34 | convolution fusion | flops 6471811072 | bytes 14704640 | tf_op jit(solution)/shard_map/yph,ypi->hi/dot_general | solution.py:292
  612.7 15.7 %bitcast_convert_fusion.1 = bf16[1024,4096]{1,0:T(8,128)(2,1)} fusion(bf16[2,512,4096]{2,1,0:T(8,128)(2,1)} %fusion.12, f32[2,512,1024]{2,1,0:T(8,128)} %copy-done.10, f32[1024]{0:T(1024)S(1)} %copy-done.53, f32[2,1024]{1,0:T(2,128)S(1)} %copy-done.39, f32[1024]{0:T(1024)S(1)} %copy-done.42, f32[2,512]{1,0:T(2,128)S(1)} %copy-done.44, ...), kind=kOutput, calls=%fused_computation.26 | convolution fusion | flops 8600420352 | bytes 20996096 | tf_op jit(solution)/shard_map/qzw,qzu->wu/dot_general | solution.py:240
  628.4 18.5 %bitcast_convert_fusion = bf16[4096,1024]{1,0:T(8,128)(2,1)} fusion(bf16[2,512,1024]{2,1,0:T(8,128)(2,1)} %param.25, f32[2,512,4096]{2,1,0:T(8,128)} %fusion.31), kind=kOutput, calls=%fused_computation.25 | convolution fusion | flops 8631877632 | bytes 27262976 | tf_op jit(solution)/shard_map/qxn,qxr->nr/dot_general | solution.py:233
  647.0 11.2 fusion.50
  658.2 1.9 copy-done.9
  660.1 2.6 fusion.48
  662.7 1.9 convolution_convert_fusion
  665.4 89.7 %reduce-scatter.6.cloned.1.call-done = bf16[64,3072]{1,0:T(8,128)(2,1)} async-done(((bf16[1024,3072]{1,0:T(8,128)(2,1)}), bf16[64,3072]{1,0:T(8,128)(2,1)}) %reduce-scatter.6.cloned.1.call-update) | async-done | bytes 393232 | tf_op jit(solution)/shard_map/reduce_scatter | solution.py:317
  755.0 180.4 %reduce-scatter.10.cloned.1.call-done = bf16[64,4096]{1,0:T(8,128)(2,1)} async-done(((bf16[1024,4096]{1,0:T(8,128)(2,1)}), bf16[64,4096]{1,0:T(8,128)(2,1)}) %reduce-scatter.10.cloned.1.call-update) | async-done | bytes 524304 | tf_op jit(solution)/shard_map/reduce_scatter | solution.py:323
  935.4 182.6 %reduce-scatter.12.cloned.1.call-done = bf16[256,1024]{1,0:T(8,128)(2,1)} async-done(((bf16[4096,1024]{1,0:T(8,128)(2,1)}), bf16[256,1024]{1,0:T(8,128)(2,1)}) %reduce-scatter.12.cloned.1.call-update) | async-done | bytes 524304 | tf_op jit(solution)/shard_map/reduce_scatter | solution.py:326
  1118.0 18.0 %add_convert_fusion.1 = bf16[2,512,1024]{2,1,0:T(8,128)(2,1)} fusion(f32[2,512,1024]{2,1,0:T(8,128)} %copy-done.10, bf16[4096,1024]{1,0:T(8,128)(2,1)} %all-gather.11.cloned.1.call-done, f32[2,512,4096]{2,1,0:T(8,128)} %fusion.31), kind=kOutput, calls=%fused_computation.85 | convolution fusion | flops 8629780480 | bytes 31457280 | tf_op jit(solution)/shard_map/unr,rv->unv/dot_general | solution.py:223
  1136.0 36.3 %all-reduce.8 = (bf16[1024]{0:T(1024)(128)(2,1)S(1)}, bf16[1024]{0:T(1024)(128)(2,1)S(1)}, bf16[1024]{0:T(1024)(128)(2,1)S(1)}, bf16[1024]{0:T(1024)(128)(2,1)S(1)}) all-reduce(bf16[1024]{0:T(1024)(128)(2,1)S(1)} %get-tuple-element.14, bf16[1024]{0:T(1024)(128)(2,1)S(1)} %get-tuple-element.18, ...), channel_id=7, replica_groups=mesh['dp'=16,'blk'=2] {'dp'}, use_global_device_ids=true, to_apply=%region_26.27.clone | all-reduce | flops 4096 | bytes 16384
  1172.6 6.1 add_convert_fusion
  1178.7 10.3 reduce-scatter.14.cloned.1.call-done
  1189.0 15.6 %all-reduce.10 = (bf16[8,2048]{1,0:T(8,128)(2,1)S(1)}, bf16[64]{0:T(256)(128)(2,1)S(1)}, bf16[64]{0:T(256)(128)(2,1)S(1)}, bf16[64]{0:T(256)(128)(2,1)S(1)}, bf16[64]{0:T(256)(128)(2,1)S(1)}) all-reduce(bf16[8,2048]{1,0:T(8,128)(2,1)} %reduce-scatter.14.cloned.1.call-done, ...), channel_id=1, replica_groups=mesh['dp'=16,'blk'=2] {'blk'}, use_global_device_ids=true, to_apply=%region_24.25 | all-reduce | flops 16640 | bytes 66560 | tf_op jit(solution)/shard_map/psum | solution.py:350
  1207.4 12.6 %all-reduce.14.cloned.1.call-done = (bf16[64,3072]{1,0:T(8,128)(2,1)}, bf16[64,1024]{1,0:T(8,128)(2,1)}, bf16[64,4096]{1,0:T(8,128)(2,1)}, bf16[256,1024]{1,0:T(8,128)(2,1)}) async-done(((bf16[64,3072]{1,0:T(8,128)(2,1)}, bf16[64,1024]{1,0:T(8,128)(2,1)}, bf16[64,4096]{1,0:T(8,128)(2,1)}, bf16[256,1024]{1,0:T(8,128)(2,1)}), (bf16[64,3072]{1,0:T(8,128)(2,1)}, bf16[64,1024]{1,0:T(8,128)(2,1)}, ...) | async-done | bytes 1572880 | tf_op jit(solution)/shard_map/psum | solution.py:346
  1219.9 1.6 convert_element_type.243
  1221.5 1.9 convert_element_type.241
  1223.5 2.1 convert_element_type.245
  1225.5 2.1 convert_element_type.247
  (197 shorter events, 26.1 us)
Async XLA Ops:
  7.2 47.8 %copy-start.1 = (bf16[2,512,1024]{2,1,0:T(8,128)(2,1)S(1)}, bf16[2,512,1024]{2,1,0:T(8,128)(2,1)}, u32[]{:S(2)}) copy-start(bf16[2,512,1024]{2,1,0:T(8,128)(2,1)} %param.13) | copy-start | bytes 6291460
  7.2 48.5 %copy-start.40 = (bf16[8,2048]{1,0:T(8,128)(2,1)S(1)}, bf16[8,2048]{1,0:T(8,128)(2,1)}, u32[]{:S(2)}) copy-start(bf16[8,2048]{1,0:T(8,128)(2,1)} %param.20) | copy-start | bytes 98308
  7.2 106.8 %all-gather.5.cloned.1.call-start = ((), (), s32[]{:S(2)}) async-start(), calls=%async_computation.5 | async-start | bytes 6684672 | tf_op jit(solution)/shard_map/all_gather | solution.py:149
  7.9 248.9 %all-gather.7.cloned.1.call-start = ((), (), s32[]{:S(2)}) async-start(), calls=%async_computation.6 | async-start | bytes 2228224 | tf_op jit(solution)/shard_map/all_gather | solution.py:150
  8.7 282.1 %all-gather.9.cloned.1.call-start = ((), (), s32[]{:S(2)}) async-start(), calls=%async_computation.7 | async-start | bytes 8912896 | tf_op jit(solution)/shard_map/all_gather | solution.py:151
  9.4 395.0 %all-gather.11.cloned.1.call-start = ((), (), s32[]{:S(2)}) async-start(), calls=%async_computation.8 | async-start | bytes 8912896 | tf_op jit(solution)/shard_map/all_gather | solution.py:152
  10.0 655.4 %reduce-scatter.8.cloned.1.call-start = ((), (), s32[]{:S(2)}) async-start(), calls=%async_computation.10 | async-start | bytes 2228224 | tf_op jit(solution)/shard_map/reduce_scatter | solution.py:320
  52.9 70.2 %copy-start.50 = (f32[1024]{0:T(1024)}, f32[1024]{0:T(1024)S(1)}, u32[]{:S(2)}) copy-start(f32[1024]{0:T(1024)S(1)} %convert_element_type.204) | copy-start | bytes 12292
  53.0 70.2 %copy-start.30 = (f32[1024]{0:T(1024)}, f32[1024]{0:T(1024)S(1)}, u32[]{:S(2)}) copy-start(f32[1024]{0:T(1024)S(1)} %convert_element_type.202) | copy-start | bytes 12292
  54.9 68.2 %copy-start.26 = (f32[2,512]{1,0:T(2,128)}, f32[2,512]{1,0:T(2,128)S(1)}, u32[]{:S(2)}) copy-start(f32[2,512]{1,0:T(2,128)S(1)} %broadcast_multiply_fusion.1) | copy-start | bytes 12292
  55.6 36.6 %copy-start.36 = (f32[2,512]{1,0:T(2,128)}, f32[2,512]{1,0:T(2,128)S(1)}, u32[]{:S(2)}) copy-start(f32[2,512]{1,0:T(2,128)S(1)} %fusion.49) | copy-start | bytes 12292
  55.7 67.5 %copy-start.32 = (f32[2,512]{1,0:T(2,128)}, f32[2,512]{1,0:T(2,128)S(1)}, u32[]{:S(2)}) copy-start(f32[2,512]{1,0:T(2,128)S(1)} %fusion.84) | copy-start | bytes 12292
  93.2 29.9 %copy-start.24 = (f32[2,1024]{1,0:T(2,128)}, f32[2,1024]{1,0:T(2,128)S(1)}, u32[]{:S(2)}) copy-start(f32[2,1024]{1,0:T(2,128)S(1)} %get-tuple-element.58) | copy-start | bytes 24580
  93.2 350.8 %copy-start.38 = (f32[2,1024]{1,0:T(2,128)}, f32[2,1024]{1,0:T(2,128)S(1)}, u32[]{:S(2)}) copy-start(f32[2,1024]{1,0:T(2,128)S(1)} %get-tuple-element.57) | copy-start | bytes 24580
  93.5 47.5 %copy-start.20 = (f32[512,32]{0,1:T(8,128)}, f32[512,32]{0,1:T(8,128)S(1)}, u32[]{:S(2)}) copy-start(f32[512,32]{0,1:T(8,128)S(1)} %get-tuple-element.59) | copy-start | bytes 196612
  93.5 47.5 %copy-start.22 = (f32[512,32]{0,1:T(8,128)}, f32[512,32]{0,1:T(8,128)S(1)}, u32[]{:S(2)}) copy-start(f32[512,32]{0,1:T(8,128)S(1)} %get-tuple-element.60) | copy-start | bytes 196612
  123.2 7.0 copy-start.15
  147.0 2.4 copy-start.14
  147.0 28.1 %copy-start.4 = (bf16[2,512,16,32]{1,3,2,0:T(8,128)(2,1)}, bf16[2,512,16,32]{1,3,2,0:T(8,128)(2,1)S(1)}, u32[]{:S(2)}) copy-start(bf16[2,512,16,32]{1,3,2,0:T(8,128)(2,1)S(1)} %get-tuple-element.44) | copy-start | bytes 3145732
  147.0 3.1 copy-start.57
  149.4 25.6 %collective-permute-start = (bf16[2,512,16,64]{1,3,2,0:T(8,128)(2,1)}, bf16[2,512,16,64]{1,3,2,0:T(8,128)(2,1)}, u32[]{:S(2)}, u32[]{:S(2)}) collective-permute-start(bf16[2,512,16,64]{1,3,2,0:T(8,128)(2,1)} %pad_maximum_fusion.4), channel_id=1, source_target_pairs={{1,0},{0,1},{3,2},{2,3},{5,4},{4,5},{7,6},{6,7},{9,8},{8,9},{11,10... | collective-permute-start | bytes 6291464 | tf_op jit(solution)/shard_map/ppermute | solution.py:22
  150.0 293.9 %copy-start.41 = (f32[1024]{0:T(1024)}, f32[1024]{0:T(1024)S(1)}, u32[]{:S(2)}) copy-start(f32[1024]{0:T(1024)S(1)} %convert_element_type.212) | copy-start | bytes 12292
  150.0 140.7 %copy-start.52 = (f32[1024]{0:T(1024)}, f32[1024]{0:T(1024)S(1)}, u32[]{:S(2)}) copy-start(f32[1024]{0:T(1024)S(1)} %convert_element_type.213) | copy-start | bytes 12292
  158.5 78.7 %collective-permute-start.1 = (bf16[2,512,16,64]{1,3,2,0:T(8,128)(2,1)}, bf16[2,512,16,64]{1,3,2,0:T(8,128)(2,1)}, u32[]{:S(2)}, u32[]{:S(2)}) collective-permute-start(bf16[2,512,16,64]{1,3,2,0:T(8,128)(2,1)} %bitcast.142), channel_id=1, source_target_pairs={{1,0},{0,1},{3,2},{2,3},{5,4},{4,5},{7,6},{6,7},{9,8},{8,9},{11,10... | collective-permute-start | bytes 6291464 | tf_op jit(solution)/shard_map/ppermute | solution.py:22
  158.5 16.6 %copy-start.6 = (bf16[2,512,16,32]{1,3,2,0:T(8,128)(2,1)S(1)}, bf16[2,512,16,32]{1,3,2,0:T(8,128)(2,1)}, u32[]{:S(2)}) copy-start(bf16[2,512,16,32]{1,3,2,0:T(8,128)(2,1)} %get-tuple-element.45) | copy-start | bytes 3145732
  192.0 20.7 %copy-start.3 = (f32[2,16,512,512]{2,3,1,0:T(8,128)S(1)}, f32[2,16,512,512]{2,3,1,0:T(8,128)}, u32[]{:S(2)}) copy-start(f32[2,16,512,512]{2,3,1,0:T(8,128)} %get-tuple-element.71) | copy-start | bytes 100663296
  261.7 182.3 %copy-start.28 = (f32[2,512]{1,0:T(2,128)}, f32[2,512]{1,0:T(2,128)S(1)}, u32[]{:S(2)}) copy-start(f32[2,512]{1,0:T(2,128)S(1)} %broadcast_multiply_fusion) | copy-start | bytes 12292
  264.3 179.7 %copy-start.43 = (f32[2,512]{1,0:T(2,128)}, f32[2,512]{1,0:T(2,128)S(1)}, u32[]{:S(2)}) copy-start(f32[2,512]{1,0:T(2,128)S(1)} %fusion.85) | copy-start | bytes 12292
  290.8 113.7 %copy-start.16 = (bf16[2,512,1024]{2,1,0:T(8,128)(2,1)S(1)}, bf16[2,512,1024]{2,1,0:T(8,128)(2,1)}, u32[]{:S(2)}) copy-start(bf16[2,512,1024]{2,1,0:T(8,128)(2,1)} %param.25) | copy-start | bytes 6291460
  427.2 16.8 %copy-start.11 = (f32[2,512,1024]{2,1,0:T(8,128)S(1)}, f32[2,512,1024]{2,1,0:T(8,128)}, u32[]{:S(2)}) copy-start(f32[2,512,1024]{2,1,0:T(8,128)} %copy-done.10) | copy-start | bytes 12582916
  445.6 2.1 copy-start
  445.6 2.1 copy-start.34
  445.6 3.5 copy-start.58
  455.7 5.4 copy-start.54
  476.7 22.4 %copy-start.5 = (bf16[2,512,16,32]{1,3,2,0:T(8,128)(2,1)S(1)}, bf16[2,512,16,32]{1,3,2,0:T(8,128)(2,1)}, u32[]{:S(2)}) copy-start(bf16[2,512,16,32]{1,3,2,0:T(8,128)(2,1)} %copy-done.4) | copy-start | bytes 3145732
  476.7 22.4 %copy-start.7 = (bf16[2,512,16,32]{1,3,2,0:T(8,128)(2,1)S(1)}, bf16[2,512,16,32]{1,3,2,0:T(8,128)(2,1)}, u32[]{:S(2)}) copy-start(bf16[2,512,16,32]{1,3,2,0:T(8,128)(2,1)} %get-tuple-element.45) | copy-start | bytes 3145732
  499.1 11.9 copy-start.17
  499.1 11.9 copy-start.19
  509.5 25.6 %collective-permute-start.2 = (bf16[2,512,16,64]{1,3,2,0:T(8,128)(2,1)}, bf16[2,512,16,64]{1,3,2,0:T(8,128)(2,1)}, u32[]{:S(2)}, u32[]{:S(2)}) collective-permute-start(bf16[2,512,16,64]{1,3,2,0:T(8,128)(2,1)} %fusion.73), channel_id=1, source_target_pairs={{1,0},{0,1},{3,2},{2,3},{5,4},{4,5},{7,6},{6,7},{9,8},{8,9},{11,10... | collective-permute-start | bytes 6291464 | tf_op jit(solution)/shard_map/ppermute | solution.py:22
  514.6 240.4 %reduce-scatter.6.cloned.1.call-start = ((), (), s32[]{:S(2)}) async-start(), calls=%async_computation.9 | async-start | bytes 6684672 | tf_op jit(solution)/shard_map/reduce_scatter | solution.py:317
  514.7 20.5 %copy-start.8 = (bf16[2,512,16,32]{1,3,2,0:T(8,128)(2,1)S(1)}, bf16[2,512,16,32]{1,3,2,0:T(8,128)(2,1)}, u32[]{:S(2)}) copy-start(bf16[2,512,16,32]{1,3,2,0:T(8,128)(2,1)} %get-tuple-element.45) | copy-start | bytes 3145732
  514.7 32.1 %collective-permute-start.4 = (bf16[2,512,16,64]{1,3,2,0:T(8,128)(2,1)}, bf16[2,512,16,64]{1,3,2,0:T(8,128)(2,1)}, u32[]{:S(2)}, u32[]{:S(2)}) collective-permute-start(bf16[2,512,16,64]{1,3,2,0:T(8,128)(2,1)} %convert_bitcast_fusion), channel_id=1, source_target_pairs={{1,0},{0,1},{3,2},{2,3},{5,4},{4,5},{7,6},{6,7},{9,8},{8,9},{11,10... | collective-permute-start | bytes 6291464 | tf_op jit(solution)/shard_map/ppermute | solution.py:22
  546.3 16.3 %copy-start.13 = (bf16[2,512,16,32]{1,3,2,0:T(8,128)(2,1)S(1)}, bf16[2,512,16,32]{1,3,2,0:T(8,128)(2,1)}, u32[]{:S(2)}) copy-start(bf16[2,512,16,32]{1,3,2,0:T(8,128)(2,1)} %copy-done.12) | copy-start | bytes 3145732
  546.3 34.9 %collective-permute-start.3 = (bf16[2,512,16,64]{1,3,2,0:T(8,128)(2,1)}, bf16[2,512,16,64]{1,3,2,0:T(8,128)(2,1)}, u32[]{:S(2)}, u32[]{:S(2)}) collective-permute-start(bf16[2,512,16,64]{1,3,2,0:T(8,128)(2,1)} %fusion.52), channel_id=1, source_target_pairs={{1,0},{0,1},{3,2},{2,3},{5,4},{4,5},{7,6},{6,7},{9,8},{8,9},{11,10... | collective-permute-start | bytes 6291464 | tf_op jit(solution)/shard_map/ppermute | solution.py:22
  562.5 32.8 %collective-permute-start.5 = (bf16[2,512,16,64]{1,3,2,0:T(8,128)(2,1)}, bf16[2,512,16,64]{1,3,2,0:T(8,128)(2,1)}, u32[]{:S(2)}, u32[]{:S(2)}) collective-permute-start(bf16[2,512,16,64]{1,3,2,0:T(8,128)(2,1)} %fusion.51), channel_id=1, source_target_pairs={{1,0},{0,1},{3,2},{2,3},{5,4},{4,5},{7,6},{6,7},{9,8},{8,9},{11,10... | collective-permute-start | bytes 6291464 | tf_op jit(solution)/shard_map/ppermute | solution.py:22
  581.1 2.3 copy-start.21
  581.1 2.3 copy-start.23
  591.1 8.2 copy-start.2
  591.1 8.2 copy-start.25
  591.1 8.2 copy-start.27
  591.1 8.2 copy-start.31
  591.1 8.2 copy-start.33
  591.1 8.2 copy-start.51
  612.0 323.4 %reduce-scatter.10.cloned.1.call-start = ((), (), s32[]{:S(2)}) async-start(), calls=%async_computation.11 | async-start | bytes 8912896 | tf_op jit(solution)/shard_map/reduce_scatter | solution.py:323
  628.4 489.6 %reduce-scatter.12.cloned.1.call-start = ((), (), s32[]{:S(2)}) async-start(), calls=%async_computation.12 | async-start | bytes 8912896 | tf_op jit(solution)/shard_map/reduce_scatter | solution.py:326
  646.9 11.3 copy-start.37
  646.9 542.1 %reduce-scatter.14.cloned.1.call-start = ((), (), s32[]{:S(2)}) async-start(), calls=%async_computation.13 | async-start | bytes 557056 | tf_op jit(solution)/shard_map/reduce_scatter | solution.py:329
  658.1 4.6 copy-start.46
  658.1 4.6 copy-start.48
  658.1 4.6 copy-start.49
  664.7 555.3 %all-reduce.14.cloned.1.call-start = ((), (), s32[]{:S(2)}) async-start(), calls=%async_computation.14 | async-start | bytes 3145728 | tf_op jit(solution)/shard_map/psum | solution.py:346
  1118.0 18.0 %copy-start.55 = (bf16[1024]{0:T(1024)(128)(2,1)S(1)}, bf16[1024]{0:T(1024)(128)(2,1)}, u32[]{:S(2)}) copy-start(bf16[1024]{0:T(1024)(128)(2,1)} %get-tuple-element.11) | copy-start | bytes 6148
  1118.0 18.0 %copy-start.56 = (bf16[1024]{0:T(1024)(128)(2,1)S(1)}, bf16[1024]{0:T(1024)(128)(2,1)}, u32[]{:S(2)}) copy-start(bf16[1024]{0:T(1024)(128)(2,1)} %get-tuple-element.17) | copy-start | bytes 6148
  1118.0 54.6 %copy-start.35 = (f32[2,512]{1,0:T(2,128)S(1)}, f32[2,512]{1,0:T(2,128)}, u32[]{:S(2)}) copy-start(f32[2,512]{1,0:T(2,128)} %copy-done.34) | copy-start | bytes 12292
  (11 other events, 11.4 us)
Sparse Core Ops, SparseCore 0:
  10.8 103.1 all-gather.4
  116.8 59.9 all-gather.6
  179.6 111.1 all-gather.8
  293.4 111.0 all-gather.10
  514.8 67.2 reduce-scatter.7
  612.1 142.8 reduce-scatter.5
  757.3 178.0 reduce-scatter.9
  937.7 180.2 reduce-scatter.11
  1120.8 68.1 reduce-scatter.13
  1191.6 28.2 all-reduce.13
where the time goes:
time: 1240 us; the launch traced here: 1230 us
  waiting for transfers between devices  622 us (50%)
  matrix products  340 us (27%)
  blocking collectives  125 us (10%)
  other arithmetic  67.9 us (5%)
  local copies, waits for them, and re-layouts  60.3 us (5%)
  between operations  16.6 us (1%)
    reduce_scatter x1, waiting for transfers between devices, shards(): lax.psum_scatter(grad_list[3].astype(jnp.bfloat16), 'dp', scatter_dimensi...  183 us
    reduce_scatter x1, waiting for transfers between devices, shards(): lax.psum_scatter(grad_list[2].astype(jnp.bfloat16), 'dp', scatter_dimensi...  180 us
    all_gather x1, waiting for transfers between devices, shards(): lax.all_gather(down_weight, 'dp', axis=0, tiled=True)  96.9 us
    reduce_scatter x1, waiting for transfers between devices, shards(): lax.psum_scatter(grad_list[0].astype(jnp.bfloat16), 'dp', scatter_dimensi...  89.7 us
    unnamed x2, blocking collectives  73.1 us
    dot_general x2, matrix products, back_block(): jnp.einsum('sqhe,skhe->shqk', grad_heads, value_block, preferred_element_...  42.8 us
    dot_general x2, matrix products, absorb(): jnp.einsum('shqk,skhe->shqe', block_weights.astype(jnp.bfloat16), value_b...  36.5 us
    all_gather x1, blocking collectives, shards(): lax.all_gather(time_weight, 'dp', axis=0, tiled=True)  36.4 us
  transfers between devices with their start and end apart: 16, of which 8 were waited for; matrix products, arithmetic and copies ran while one was open for 27% of the time, Pallas kernels for 0%

commit v1 on v0

v1 whole, which is shorter than its diff:
```python
import functools
import math

import jax
import jax.numpy as jnp
from jax import lax
from jax.experimental import pallas as pl
from jax.experimental.pallas import tpu as pltpu
from jax.sharding import PartitionSpec as P

H = 16
HD = 64
TF = 128
EPS = 1e-05
MASKED = -1e30
F32 = jnp.float32
BF16 = jnp.bfloat16
AXES = ("dp", "blk")
LANES = 128
ROWS = 256
VMEM_LIMIT = 58 << 20
ANY = pl.BlockSpec(memory_space=pl.ANY)


class Grid:
    def __init__(self, groups, blocks):
        self.groups, self.blocks = groups, blocks
        self.n0, self.n = {16: (4, 2), 32: (2, 4)}.get(groups, (groups, 1))
        self.chunks = self.n * self.n

    def coords(self, d):
        return d // self.chunks, d // self.n % self.n, d % self.n

    def join(self, z, a, b):
        return (z * self.n + a) * self.n + b

    def shift(self, v, phase, k):
        pairs = []
        for d in range(self.groups):
            for b in range(self.blocks):
                at = list(self.coords(d))
                axis = 0 if phase == 0 else (3 - phase if b % 2 == 0 else phase)
                size = self.n if axis else self.n0
                at[axis] = (at[axis] - k) % size
                pairs.append((d * self.blocks + b, self.join(*at) * self.blocks + b))
        return lax.ppermute(v, AXES, pairs)

    def swap(self, v):
        pairs = []
        for d in range(self.groups):
            for b in range(self.blocks):
                pairs.append((d * self.blocks + b, d * self.blocks + (b ^ 1)))
        return lax.ppermute(v, AXES, pairs)

    def places(self, core):
        _, a, b = self.coords(lax.axis_index("dp"))
        first = jnp.where(core == 0, b, a)
        second = jnp.where(core == 0, a, b)
        out = []
        for k2 in range(self.n):
            for k1 in range(self.n):
                p1, p2 = (first + k1) % self.n, (second + k2) % self.n
                out += [jnp.where(core == 0, p2, p1), jnp.where(core == 0, p1, p2)]
        return out


def rolled(parts, index):
    n = len(parts)
    if n == 1:
        return parts[0][None]
    both = jnp.stack(list(parts) + list(parts[:-1]))
    return lax.dynamic_slice_in_dim(both, (n - index) % n, n, 0)


def dot(a, b, ca=1, cb=0):
    return lax.dot_general(a, b, (((ca,), (cb,)), ((), ())), preferred_element_type=F32)


def spec(shape, index):
    return pl.BlockSpec(shape, index)


def whole(shape):
    return pl.BlockSpec(shape, lambda *_: (0,) * len(shape))


SCALARS = pl.BlockSpec(memory_space=pltpu.SMEM)


def call(kernel, name, grid, ins, outs, shapes, scratch, flops, moved, prefetch=0):
    return pl.pallas_call(
        kernel,
        grid_spec=pltpu.PrefetchScalarGridSpec(
            num_scalar_prefetch=prefetch, grid=grid, in_specs=ins, out_specs=outs, scratch_shapes=scratch
        ),
        out_shape=[jax.ShapeDtypeStruct(s, t) for s, t in shapes],
        compiler_params=pltpu.CompilerParams(vmem_limit_bytes=VMEM_LIMIT),
        cost_estimate=pl.CostEstimate(flops=flops, bytes_accessed=moved, transcendentals=0),
        name=name,
    )


def fetch(place, pieces, matrix, sem, half, start, size, z=None):
    count, width = len(pieces) // 2, pieces[0].shape[-1]
    zs = slice(None) if z is None else z

    def go(base):
        for i in range(base, base + count):
            pltpu.make_async_copy(
                pieces[i].at[zs, :, pl.ds(start, size)],
                matrix.at[zs, place[3 * i], place[3 * i + 1], :, pl.ds(half * width + start, size)],
                sem,
            ).start()

    pl.when(place[2] == half)(lambda: go(0))
    pl.when(place[2] != half)(lambda: go(count))


def arrived(matrix, sem, start, size, z=None):
    zs = slice(None) if z is None else z
    block = matrix.at[zs, :, :, :, pl.ds(start, size)]
    pltpu.make_async_copy(block, block, sem).wait()


def matrix_shape(grid, piece):
    n0, rows, width = piece.shape
    return (n0, grid.n, grid.n, rows, 2 * width)


def columns(matrix, start, size):
    block = matrix[:, :, :, :, pl.ds(start, size)]
    return block.reshape(-1, size)


def normalized(x):
    centre = x - jnp.mean(x, axis=-1, keepdims=True)
    inverse = lax.rsqrt(jnp.mean(centre * centre, axis=-1, keepdims=True) + EPS)
    return centre * inverse, inverse


def turned(x, cosine, sine):
    lane = lax.broadcasted_iota(jnp.int32, (1, LANES), 1)
    swapped = jnp.where(lane % HD < HD // 2, pltpu.roll(x, LANES - HD // 2, 1), pltpu.roll(x, HD // 2, 1))
    return x * cosine + swapped * sine


def start_blocks(place, pieces, matrix, sems, block):
    width = pieces[0].shape[-1]
    for half in range(2):
        for j in range(width // block):
            fetch(place, pieces, matrix, sems.at[half * (width // block) + j], half, j * block, block)


def qkv_kernel(count, block, place, x, gain, bias, cosine, sine, *refs):
    pieces = refs[:count]
    normed, packed, matrix, sems = refs[count:]
    j = pl.program_id(0)
    per = normed.shape[1] // block

    @pl.when(j == 0)
    def _():
        start_blocks(place, pieces, matrix, sems, block)
        rows = x.shape[0]
        for r in range(0, rows, ROWS):
            hat, _ = normalized(x[r : r + ROWS, :].astype(F32))
            normed[r : r + ROWS, :] = (hat * gain[...] + bias[...]).astype(BF16)

    start = pl.multiple_of(j * block, block)
    arrived(matrix, sems.at[j], start, block)
    weight = columns(matrix, start, block)
    for r in range(0, x.shape[0], ROWS):
        rows = slice(r, r + ROWS)
        result = dot(normed[rows, :], weight)

        @pl.when(j < 2 * per)
        def _():
            scale = jnp.where(j < per, HD ** (-0.5), 1.0).astype(F32)
            for c in range(0, block, LANES):
                part = turned(result[:, c : c + LANES], cosine[rows, :], sine[rows, :])
                packed[0, rows, c : c + LANES] = (part * scale).astype(BF16)

        @pl.when(j >= 2 * per)
        def _():
            packed[0, rows, :] = result.astype(BF16)


def qkv_product(grid, places, x, gain, bias, cosine, sine, pieces, block=512):
    rows, width = x.shape
    per = width // block
    size = rows * width
    return call(
        functools.partial(qkv_kernel, len(pieces), block), "qkv", (3 * per,),
        [SCALARS, whole(x.shape), whole((1, width)), whole((1, width)), whole((rows, LANES)), whole((rows, LANES))]
        + [ANY] * len(pieces),
        [whole(x.shape), spec((1, rows, block), lambda j: (j // per, 0, j % per))],
        [(x.shape, BF16), ((3,) + x.shape, BF16)],
        [pltpu.VMEM(matrix_shape(grid, pieces[0]), BF16), pltpu.SemaphoreType.DMA((3 * per,))],
        6 * size * width, 6 * width * width + 10 * size,
    )(places, x, gain, bias, cosine, sine, *pieces)


def attend_kernel(step, q, k, v, mask, mixed, lse):
    p = pl.program_id(0)
    lane = lax.broadcasted_iota(jnp.int32, (1, LANES), 1)
    zero = jnp.zeros((), BF16)
    mine = [lane < HD, lane >= HD]
    keys = [jnp.where(m, k[0], zero) for m in mine]
    values = [jnp.where(m, v[0], zero) for m in mine]
    away = mask[...]

    @pl.when(p == 0)
    def _():
        lse[...] = jnp.zeros_like(lse)

    def body(i, _):
        rows = pl.ds(pl.multiple_of(i * step, step), step)
        queries, kept = q[0, rows, :], lse[rows, :]
        out = None
        for h in range(2):
            scores = dot(queries, keys[h], 1, 1) + away
            top = jnp.max(scores, axis=-1, keepdims=True)
            weights = jnp.exp(scores - top)
            total = jnp.sum(weights, axis=-1, keepdims=True)
            part = dot(weights.astype(BF16), values[h]) * (1.0 / total)
            out = part if out is None else out + part
            kept = jnp.where(lane == 2 * p + h, top + jnp.log(total), kept)
        lse[rows, :] = kept
        mixed[rows, :] = out.astype(BF16)
        return 0

    lax.fori_loop(0, q.shape[1] // step, body, 0)


def attend(q, k, v, mask):
    rows, width, places = q.shape[1], q.shape[2], k.shape[1]
    pair = lambda v, lead: spec((1, v.shape[1], LANES), lambda p: (lead, 0, p))
    last = 1 if k is q else 0
    return call(
        functools.partial(attend_kernel, min(rows, 512)), "attend", (width // LANES,),
        [pair(q, 0), pair(k, last), pair(v, 2 * last), whole((1, places))],
        [spec((rows, LANES), lambda p: (0, p)), whole((rows, LANES))],
        [((rows, width), BF16), ((rows, LANES), F32)], [],
        16 * rows * places * width, 8 * rows * width,
    )(q, k, v, mask)


def thirds(x):
    a = x.astype(BF16)
    rest = x - a.astype(F32)
    b = rest.astype(BF16)
    return a, b, (rest - b.astype(F32)).astype(BF16)


def attend_back_kernel(step, merged, q, k, v, mixed, grad, lse, mask, cosine, sine, *refs):
    if merged:
        out, key_sum, value_sum = refs
        put = lambda lead, rows, x: out.__setitem__((lead, rows, slice(None)), x)
        key_cos, key_sin = cosine, sine
    else:
        key_cos, key_sin, out_q, out_k, out_v, key_sum, value_sum = refs
        put = lambda lead, rows, x: (out_q, out_k, out_v)[lead].__setitem__((rows, slice(None)), x)
    p = pl.program_id(0)
    lane = lax.broadcasted_iota(jnp.int32, (1, LANES), 1)
    zero, one = jnp.zeros((), BF16), jnp.ones((), BF16)
    mine = [lane < HD, lane >= HD]
    spare = [HD, 0]
    keys, keys_more, values_more = [], [], []
    for h in range(2):
        ones = (lane >= spare[h]) & (lane < spare[h] + 3)
        own = jnp.where(mine[h], k[0], zero)
        keys.append(own)
        keys_more.append(jnp.where(ones, one, jnp.where(lane == spare[h] + 3, mask[...], own)))
        values_more.append(jnp.where(ones, one, jnp.where(mine[h], v[0], zero)))
    key_sum[...] = jnp.zeros_like(key_sum)
    value_sum[...] = jnp.zeros_like(value_sum)

    def body(i, _):
        rows = pl.ds(pl.multiple_of(i * step, step), step)
        queries, grads = q[0, rows, :], grad[rows, :]
        kept = lse[rows, :]
        product = grads.astype(F32) * mixed[rows, :].astype(F32)
        total = None
        for h in range(2):
            delta = jnp.sum(jnp.where(mine[h], product, 0.0), axis=-1, keepdims=True)
            log_sum = jnp.sum(jnp.where(lane == 2 * p + h, kept, 0.0), axis=-1, keepdims=True)
            own_q = jnp.where(mine[h], queries, zero)
            own_g = jnp.where(mine[h], grads, zero)
            more_q = jnp.where(lane == spare[h] + 3, one, own_q)
            more_g = own_g
            for t, (a, b) in enumerate(zip(thirds(-log_sum), thirds(-delta))):
                more_q = jnp.where(lane == spare[h] + t, a, more_q)
                more_g = jnp.where(lane == spare[h] + t, b, more_g)
            probs = jnp.exp(dot(keys_more[h], more_q, 1, 1))
            grad_scores = (probs * dot(values_more[h], more_g, 1, 1)).astype(BF16)
            value_sum[...] += dot(probs.astype(BF16), own_g)
            key_sum[...] += dot(grad_scores, own_q)
            part = dot(keys[h], grad_scores, 0, 0)
            total = part if total is None else total + part
        grad_q = turned(total.T, cosine[rows, :], -sine[rows, :]) * HD ** (-0.5)
        put(0, rows, grad_q.astype(BF16))
        return 0

    lax.fori_loop(0, q.shape[1] // step, body, 0)
    every = slice(None)
    put(1, every, turned(key_sum[...], key_cos[...], -key_sin[...]).astype(BF16))
    put(2, every, value_sum[...].astype(BF16))


def attend_back(q, k, v, mixed, grad, lse, mask, tables, key_tables):
    rows, width, places = q.shape[1], q.shape[2], k.shape[1]
    merged = k is q
    pair = lambda v, lead: spec((1, v.shape[1], LANES), lambda p: (lead, 0, p))
    flat = lambda n: spec((n, LANES), lambda p: (0, p))
    last = 1 if merged else 0
    more = [] if merged else list(key_tables)
    if merged:
        outs, shapes = [spec((3, rows, LANES), lambda p: (0, 0, p))], [((3, rows, width), BF16)]
    else:
        outs, shapes = [flat(rows), flat(places), flat(places)], [((n, width), BF16) for n in (rows, places, places)]
    return call(
        functools.partial(attend_back_kernel, min(rows, 512), merged), "attend_back", (width // LANES,),
        [pair(q, 0), pair(k, last), pair(v, 2 * last), flat(rows), flat(rows), whole((rows, LANES)), whole((places, 1))]
        + [whole((rows, LANES))] * 2 + [whole((places, LANES))] * len(more),
        outs, shapes, [pltpu.VMEM((places, LANES), F32)] * 2,
        40 * rows * places * width, 16 * rows * width,
    )(q, k, v, mixed, grad, lse, mask, *tables, *more)


def out_kernel(count, block, place, mixed, x, gain, bias, *refs):
    pieces = refs[:count]
    middle, normed, matrix, total, sems = refs[count:]
    j, steps = pl.program_id(0), pl.num_programs(0)

    @pl.when(j == 0)
    def _():
        start_blocks(place, pieces, matrix, sems, block)

    start = pl.multiple_of(j * block, block)
    arrived(matrix, sems.at[j], start, block)
    total[:, pl.ds(start, block)] = dot(mixed[...], columns(matrix, start, block))

    @pl.when(j == steps - 1)
    def _():
        for r in range(0, x.shape[0], ROWS):
            rows = slice(r, r + ROWS)
            row = x[rows, :].astype(F32) + total[rows, :]
            middle[rows, :] = row.astype(BF16)
            hat, _ = normalized(row)
            normed[rows, :] = (hat * gain[...] + bias[...]).astype(BF16)


def out_product(grid, places, mixed, x, gain, bias, pieces, block=512):
    rows, width = x.shape
    block = min(block, pieces[0].shape[-1])
    size = rows * width
    return call(
        functools.partial(out_kernel, len(pieces), block), "out", (width // block,),
        [SCALARS, whole(x.shape), whole(x.shape), whole((1, width)), whole((1, width))] + [ANY] * len(pieces),
        [whole(x.shape), whole(x.shape)], [(x.shape, BF16)] * 2,
        [pltpu.VMEM(matrix_shape(grid, pieces[0]), BF16), pltpu.VMEM(x.shape, F32),
         pltpu.SemaphoreType.DMA((width // block,))],
        2 * size * width, 2 * width * width + 8 * size,
    )(places, mixed, x, gain, bias, *pieces)


def up_kernel(count, block, place, normed, *refs):
    pieces = refs[:count]
    active, slope, matrix, sems = refs[count:]
    j = pl.program_id(0)

    @pl.when(j == 0)
    def _():
        start_blocks(place, pieces, matrix, sems, block)

    start = pl.multiple_of(j * block, block)
    arrived(matrix, sems.at[j], start, block)
    weight = columns(matrix, start, block)
    root = math.sqrt(2.0 / math.pi)
    for r in range(0, normed.shape[0], ROWS):
        rows = slice(r, r + ROWS)
        h = dot(normed[rows, :], weight)
        square = h * h
        t = jnp.tanh(h * (root + (root * 0.044715) * square))
        half = 0.5 + 0.5 * t
        active[rows, :] = (h * half).astype(BF16)
        slope[rows, :] = (
            half + (h * half) * (1.0 - t) * (root + (3.0 * 0.044715 * root) * square)
        ).astype(BF16)


def up_product(grid, places, normed, pieces, block=512):
    rows, width = normed.shape
    full = 2 * pieces[0].shape[-1]
    out = spec((rows, block), lambda j: (0, j))
    return call(
        functools.partial(up_kernel, len(pieces), block), "up", (full // block,),
        [SCALARS, whole(normed.shape)] + [ANY] * len(pieces),
        [out, out], [((rows, full), BF16)] * 2,
        [pltpu.VMEM(matrix_shape(grid, pieces[0]), BF16), pltpu.SemaphoreType.DMA((full // block,))],
        2 * rows * width * full, 2 * width * full + 4 * rows * full,
    )(places, normed, *pieces)


def start_levels(place, pieces, matrix, sems):
    width = pieces[0].shape[-1]
    for z in range(pieces[0].shape[0]):
        for half in range(2):
            fetch(place, pieces, matrix, sems.at[z], half, 0, width, z)


def down_kernel(count, place, active, middle, *refs):
    pieces = refs[:count]
    out, matrix, total, sems = refs[count:]
    z, steps = pl.program_id(0), pl.num_programs(0)

    @pl.when(z == 0)
    def _():
        start_levels(place, pieces, matrix, sems)
        total[...] = middle[...].astype(F32)

    width = matrix.shape[-1]
    arrived(matrix, sems.at[z], 0, width, z)
    total[...] += dot(active[...], matrix[z].reshape(-1, width))

    @pl.when(z == steps - 1)
    def _():
        out[...] = total[...].astype(BF16)


def down_product(grid, places, active, middle, pieces):
    rows, full = active.shape
    width = middle.shape[1]
    part = full // grid.n0
    return call(
        functools.partial(down_kernel, len(pieces)), "down", (grid.n0,),
        [SCALARS, spec((rows, part), lambda z: (0, z)), whole(middle.shape)] + [ANY] * len(pieces),
        [whole(middle.shape)], [(middle.shape, BF16)],
        [pltpu.VMEM(matrix_shape(grid, pieces[0]), BF16), pltpu.VMEM(middle.shape, F32),
         pltpu.SemaphoreType.DMA((grid.n0,))],
        2 * rows * width * full, 2 * width * full + 2 * rows * full,
    )(places, active, middle, *pieces)[0]


def hidden_back_kernel(count, place, grad, slope, *refs):
    pieces = refs[:count]
    out, matrix, sems = refs[count:]
    z = pl.program_id(0)

    @pl.when(z == 0)
    def _():
        start_levels(place, pieces, matrix, sems)

    width = matrix.shape[-1]
    arrived(matrix, sems.at[z], 0, width, z)
    weight = matrix[z].reshape(-1, width)
    for r in range(0, grad.shape[0], ROWS):
        rows = slice(r, r + ROWS)
        out[rows, :] = (dot(grad[rows, :], weight, 1, 1) * slope[rows, :].astype(F32)).astype(BF16)


def hidden_back(grid, places, grad, slope, pieces):
    rows, full = slope.shape
    width = grad.shape[1]
    part = spec((rows, full // grid.n0), lambda z: (0, z))
    return call(
        functools.partial(hidden_back_kernel, len(pieces)), "hidden_back", (grid.n0,),
        [SCALARS, whole(grad.shape), part] + [ANY] * len(pieces),
        [part], [(slope.shape, BF16)],
        [pltpu.VMEM(matrix_shape(grid, pieces[0]), BF16), pltpu.SemaphoreType.DMA((grid.n0,))],
        2 * rows * width * full, 2 * width * full + 4 * rows * full,
    )(places, grad, slope, *pieces)[0]


def norm_back_kernel(count, block, lead, place, grad, x, gain, base, *refs):
    pieces = refs[:count]
    out, hat_sum, grad_sum, matrix, total, sems = refs[count:]
    j, steps = pl.program_id(0), pl.num_programs(0)

    @pl.when(j == 0)
    def _():
        start_blocks(place, pieces, matrix, sems, block)
        total[...] = jnp.zeros_like(total)

    start = pl.multiple_of(j * block, block)
    arrived(matrix, sems.at[j], start, block)
    total[...] += dot(grad[0] if lead else grad[...], columns(matrix, start, block), 1, 1)

    @pl.when(j == steps - 1)
    def _():
        sums = [jnp.zeros((1, x.shape[1]), F32)] * 2
        for r in range(0, x.shape[0], ROWS):
            rows = slice(r, r + ROWS)
            hat, inverse = normalized(x[rows, :].astype(F32))
            back = total[rows, :]
            sums[0] = sums[0] + jnp.sum(back * hat, axis=0, keepdims=True)
            sums[1] = sums[1] + jnp.sum(back, axis=0, keepdims=True)
            inner = back * gain[...]
            mean = jnp.mean(inner, axis=-1, keepdims=True)
            lean = jnp.mean(inner * hat, axis=-1, keepdims=True)
            out[rows, :] = (base[rows, :].astype(F32) + inverse * (inner - mean - hat * lean)).astype(BF16)
        hat_sum[...], grad_sum[...] = sums


def norm_back(grid, places, grad, x, gain, base, pieces, block=512):
    rows, width = x.shape
    full = 2 * pieces[0].shape[-1]
    lead = grad.ndim == 3
    per = width // block
    if lead:
        part = spec((1, rows, block), lambda j: (j // per, 0, j % per))
    else:
        part = spec((rows, block), lambda j: (0, j))
    return call(
        functools.partial(norm_back_kernel, len(pieces), block, lead), "norm_back", (full // block,),
        [SCALARS, part, whole(x.shape), whole((1, width)), whole(x.shape)] + [ANY] * len(pieces),
        [whole(x.shape), whole((1, width)), whole((1, width))], [(x.shape, BF16), ((1, width), F32), ((1, width), F32)],
        [pltpu.VMEM(matrix_shape(grid, pieces[0]), BF16), pltpu.VMEM(x.shape, F32),
         pltpu.SemaphoreType.DMA((full // block,))],
        2 * rows * width * full, 2 * width * full + 2 * rows * full + 6 * rows * width,
    )(places, grad, x, gain, base, *pieces)


def heads_back_kernel(count, block, place, grad, *refs):
    pieces = refs[:count]
    out, matrix, total, sems = refs[count:]
    j, steps = pl.program_id(0), pl.num_programs(0)

    @pl.when(j == 0)
    def _():
        start_blocks(place, pieces, matrix, sems, block)
        total[...] = jnp.zeros_like(total)

    start = pl.multiple_of(j * block, block)
    arrived(matrix, sems.at[j], start, block)
    total[...] += dot(grad[...], columns(matrix, start, block), 1, 1)

    @pl.when(j == steps - 1)
    def _():
        out[...] = total[...].astype(BF16)


def heads_back(grid, places, grad, pieces, block=512):
    rows, width = grad.shape
    block = min(block, pieces[0].shape[-1])
    return call(
        functools.partial(heads_back_kernel, len(pieces), block), "heads_back", (width // block,),
        [SCALARS, spec((rows, block), lambda j: (0, j))] + [ANY] * len(pieces),
        [whole(grad.shape)], [(grad.shape, BF16)],
        [pltpu.VMEM(matrix_shape(grid, pieces[0]), BF16), pltpu.VMEM(grad.shape, F32),
         pltpu.SemaphoreType.DMA((width // block,))],
        2 * rows * width * width, 2 * width * width + 4 * rows * width,
    )(places, grad, *pieces)[0]


def row_chunks_kernel(chunks, per, place, a, b, sent, kept, turned_a, result):
    j = pl.program_id(0)

    @pl.when(j == 0)
    def _():
        turned_a[...] = a[...].T

    grad = dot(turned_a[...], b[0] if len(b.shape) == 3 else b[...])
    result[...] = grad.reshape(result.shape)

    def put(out, base):
        for i in range(chunks):
            at = 3 * (base + i)
            out[i] = result[:, place[at], place[at + 1]].astype(BF16)

    pl.when(j < per)(lambda: put(sent, chunks))
    pl.when(j >= per)(lambda: put(kept, 0))


def row_chunks(grid, places, a, b, block=512):
    rows, width = a.shape
    lead = b.ndim == 3
    full = b.shape[-1] * (3 if lead else 1)
    per = full // 2 // block
    chunks, part = grid.chunks, width // grid.groups
    many = b.shape[-1] // block

    def at(j, place):
        half = jnp.where(j < per, 1 - place[2], place[2])
        return half * per + j % per

    if lead:
        b_spec = spec((1, rows, block), lambda j, place: (at(j, place) // many, 0, at(j, place) % many))
    else:
        b_spec = spec((rows, block), lambda j, place: (0, at(j, place)))
    shape = (chunks, grid.n0, part, full // 2)
    out = (chunks, grid.n0, part, block)
    return call(
        functools.partial(row_chunks_kernel, chunks, per), "row_chunks", (2 * per,),
        [whole(a.shape), b_spec],
        [spec(out, lambda j, place: (0, 0, 0, jnp.minimum(j, per - 1))),
         spec(out, lambda j, place: (0, 0, 0, jnp.maximum(j - per, 0)))],
        [(shape, BF16), (shape, BF16)],
        [pltpu.VMEM((width, rows), BF16), pltpu.VMEM((grid.n0, grid.n, grid.n, part, block), F32)],
        2 * rows * width * full, 2 * width * full + 2 * rows * (full + width), prefetch=1,
    )(places, a, b)


def wide_chunks_kernel(chunks, place, *refs):
    n0 = len(refs) - 3
    parts, b, sent, kept = refs[:n0], refs[n0], refs[n0 + 1], refs[n0 + 2]

    def put(out):
        for z in range(n0):
            out[0, z] = dot(parts[z][...], b[...], 0, 0).astype(BF16)

    pl.when(pl.program_id(0) < chunks)(lambda: put(sent))
    pl.when(pl.program_id(0) >= chunks)(lambda: put(kept))


def wide_chunks(grid, places, a, b):
    rows, full = a.shape
    width = b.shape[1]
    chunks, part, n = grid.chunks, full // grid.groups, grid.n

    def index(j, place):
        i = jnp.where(j < chunks, chunks + j, j - chunks)
        return place[3 * i], place[3 * i + 1], place[3 * i + 2]

    def a_spec(z):
        def at(j, place):
            first, second, _ = index(j, place)
            return 0, (z * n + first) * n + second

        return spec((rows, part), at)

    shape = (chunks, grid.n0, part, width // 2)
    out = (1, grid.n0, part, width // 2)
    return call(
        functools.partial(wide_chunks_kernel, chunks), "wide_chunks", (2 * chunks,),
        [a_spec(z) for z in range(grid.n0)] + [spec((rows, width // 2), lambda j, place: (0, index(j, place)[2]))],
        [spec(out, lambda j, place: (jnp.minimum(j, chunks - 1), 0, 0, 0)),
         spec(out, lambda j, place: (jnp.maximum(j - chunks, 0), 0, 0, 0))],
        [(shape, BF16), (shape, BF16)], [],
        2 * rows * width * full, 2 * width * full + 2 * rows * (full + width), prefetch=1,
    )(places, *([a] * grid.n0), b)


def gather(grid, shard, core):
    z, _, _ = grid.coords(lax.axis_index("dp"))
    width = shard.shape[1] // 2
    mine = lax.dynamic_slice_in_dim(shard, core * width, width, 1)
    column = rolled([mine] + [grid.shift(mine, 0, k) for k in range(1, grid.n0)], z)
    level = [column] + [grid.shift(column, 1, k) for k in range(1, grid.n)]
    pieces = list(level)
    for k in range(1, grid.n):
        pieces += [grid.shift(v, 2, k) for v in level]
    return pieces + [grid.swap(v) for v in pieces]


def scatter(grid, sent, kept, core):
    z, _, _ = grid.coords(lax.axis_index("dp"))
    n = grid.n
    shape = (n, n) + kept.shape[1:]
    kept, came = kept.reshape(shape), grid.swap(sent).reshape(shape)

    def plus(*vs):
        return functools.reduce(lambda a, b: a + b, [v.astype(F32) for v in vs])

    seconds = [grid.shift(plus(kept[k], came[k]).astype(BF16), 2, -k) for k in range(1, n)]
    firsts = [
        grid.shift(plus(kept[0, k], came[0, k], *[v[k] for v in seconds]).astype(BF16), 1, -k) for k in range(1, n)
    ]
    column = plus(kept[0, 0], came[0, 0], *[v[0] for v in seconds], *firsts).astype(BF16)
    own = lax.dynamic_index_in_dim(column, z, 0, keepdims=False).astype(F32)
    for k in range(1, grid.n0):
        there = lax.dynamic_index_in_dim(column, (z + k) % grid.n0, 0, keepdims=False)
        own = own + grid.shift(there, 0, -k).astype(F32)
    own = over_ranks(grid, own).astype(BF16)
    other = grid.swap(own)
    return jnp.where(
        core == 0, jnp.concatenate([own, other], axis=1), jnp.concatenate([other, own], axis=1)
    ).astype(F32)


def rank_groups(grid):
    return [[b for b in range(grid.blocks) if b % 2 == c] for c in range(2)]


def over_ranks(grid, v):
    if grid.blocks == 2:
        return v
    return lax.psum(v.astype(BF16), "blk", axis_index_groups=rank_groups(grid)).astype(F32)


def gather_small(grid, v):
    z, a, b = grid.coords(lax.axis_index("dp"))

    def along(v, axis, size, index):
        parts = [v]
        for k in range(1, size):
            pairs = []
            for d in range(grid.groups):
                at = list(grid.coords(d))
                at[axis] = (at[axis] - k) % size
                for c in range(grid.blocks):
                    pairs.append((d * grid.blocks + c, grid.join(*at) * grid.blocks + c))
            parts.append(lax.ppermute(v, AXES, pairs))
        return rolled(parts, index)

    v = along(v, 2, grid.n, b)
    v = along(v, 1, grid.n, a)
    v = along(v, 0, grid.n0, z)
    return v.reshape((grid.groups,) + v.shape[3:])


def time_features(time_steps):
    half = TF // 2
    frequency = jnp.exp(jnp.arange(half, dtype=F32) * (-math.log(10000.0) / half))
    angles = time_steps.astype(F32)[:, None] * frequency[None, :]
    return jnp.concatenate([jnp.sin(angles), jnp.cos(angles)], axis=-1)


def rotary_tables(positions):
    half = HD // 2
    inverse = jnp.exp(jnp.arange(half, dtype=F32) * (-2.0 * math.log(10000.0) / HD))
    angles = positions.astype(F32)[:, None] * inverse[None, :]
    cosine, sine = jnp.cos(angles), jnp.sin(angles)
    return jnp.tile(cosine, (1, 4)), jnp.tile(jnp.concatenate([-sine, sine], axis=1), (1, 2))


def shards(
    tokens, lengths, time_index, qkv_weight, out_weight, up_weight, down_weight, time_weight,
    norm1_gain, norm1_bias, norm2_gain, norm2_bias, cotangent,
):
    grid = Grid(lax.axis_size("dp"), lax.axis_size("blk"))
    ranks = grid.blocks // 2
    _, block_len, width = tokens.shape
    block = lax.axis_index("blk")
    core, rank = block % 2, block // 2
    rows = 2 * block_len

    def own_sequence(v):
        mine = lax.dynamic_index_in_dim(v, core, 0, keepdims=False)
        theirs = lax.dynamic_index_in_dim(v, 1 - core, 0, keepdims=False)
        return jnp.concatenate([mine, grid.swap(theirs)], axis=0)

    def to_blocks(v):
        mine, theirs = v[:block_len], grid.swap(v[block_len:])
        return jnp.where(core == 0, jnp.stack([mine, theirs]), jnp.stack([theirs, mine]))

    def with_half(list_, half):
        return [v for i in range(grid.chunks) for v in (list_[2 * i], list_[2 * i + 1], half)]

    at = jnp.stack(with_half(grid.places(core), core) + with_half(grid.places(1 - core), 1 - core)).astype(jnp.int32)

    norms = jnp.stack([norm1_gain, norm1_bias, norm2_gain, norm2_bias])
    t_rows, t_cols = time_weight.shape
    flat = jnp.concatenate([time_weight.reshape(-1), norms.reshape(-1)])
    small = jnp.pad(flat, (0, -flat.shape[0] % 1024)).reshape(-1, LANES)
    small = gather_small(grid, small).reshape(grid.groups, -1)
    time_matrix = small[:, : t_rows * t_cols].reshape(-1, t_cols).astype(F32)
    per = width // grid.groups
    norms = small[:, t_rows * t_cols : t_rows * t_cols + 4 * per].reshape(grid.groups, 4, per)
    norms = norms.transpose(1, 0, 2).reshape(4, width).astype(F32)
    gain1, bias1, gain2, bias2 = norms[0], norms[1], norms[2], norms[3]

    qkv_pieces = gather(grid, qkv_weight, core)
    x = own_sequence(tokens)
    my_time = lax.dynamic_slice_in_dim(time_index, core, 1, 0)
    length = lax.dynamic_index_in_dim(lengths, core, 0, keepdims=False)
    scales = jnp.dot(time_features(my_time), time_matrix, precision=lax.Precision.HIGHEST)[0]
    scale1, scale2 = 1.0 + scales[:width], 1.0 + scales[width:]
    eff1, eff2 = (gain1 * scale1)[None], (gain2 * scale2)[None]
    out_pieces = gather(grid, out_weight, core)
    up_pieces = gather(grid, up_weight, core)
    down_pieces = gather(grid, down_weight, core)
    cot = own_sequence(cotangent)

    in_block = jnp.arange(block_len, dtype=jnp.int32)
    my_places = jnp.concatenate([core * block_len + in_block, (1 - core) * block_len + in_block])
    key_places = jnp.concatenate([r * rows + my_places for r in range(ranks)])
    tables = rotary_tables(rank * rows + my_places)
    key_tables = rotary_tables(key_places) if ranks > 1 else None
    mask = jnp.where(key_places < length, 0.0, MASKED).astype(F32)

    normed1, packed = qkv_product(grid, at, x, eff1, bias1[None], *tables, qkv_pieces)
    queries = keys = values = packed
    if ranks > 1:
        keys, values = lax.all_gather(
            (packed[1], packed[2]), "blk", axis=0, tiled=True, axis_index_groups=rank_groups(grid)
        )
        keys, values = keys[None], values[None]
    mixed, lse = attend(queries, keys, values, mask[None])
    middle, normed2 = out_product(grid, at, mixed, x, eff2, bias2[None], out_pieces)
    active, slope = up_product(grid, at, normed2, up_pieces)
    grad_down = scatter(grid, *wide_chunks(grid, at, active, cot), core)
    grad_hidden = hidden_back(grid, at, cot, slope, down_pieces)
    grad_up = scatter(grid, *row_chunks(grid, at, normed2, grad_hidden), core)
    layer_out = to_blocks(down_product(grid, at, active, middle, down_pieces))
    grad_middle, sum2, bias2_sum = norm_back(grid, at, grad_hidden, middle, eff2, cot, up_pieces)
    grad_out = scatter(grid, *row_chunks(grid, at, mixed, grad_middle), core)
    grad_heads = heads_back(grid, at, grad_middle, out_pieces)
    back = attend_back(
        queries, keys, values, mixed, grad_heads, lse, mask[:, None].astype(BF16), tables, key_tables
    )
    if ranks > 1:
        grad_keys, grad_values = lax.psum_scatter(
            (back[1], back[2]), "blk", scatter_dimension=0, tiled=True, axis_index_groups=rank_groups(grid)
        )
        grad_packed = jnp.stack([back[0], grad_keys, grad_values])
    else:
        grad_packed = back[0]
    grad_qkv = scatter(grid, *row_chunks(grid, at, normed1, grad_packed), core)
    grad_x, sum1, bias1_sum = norm_back(grid, at, grad_packed, x, eff1, grad_middle, qkv_pieces)
    grad_tokens = to_blocks(grad_x)
    sum1, sum2, bias1_sum, bias2_sum = sum1[0], sum2[0], bias1_sum[0], bias2_sum[0]

    mine = jnp.concatenate(
        [
            sum1 * gain1, sum2 * gain2, sum1 * scale1, bias1_sum, sum2 * scale2, bias2_sum,
            jnp.full((LANES,), my_time[0], F32),
        ]
    ).reshape(-1, LANES)
    every = gather_small(grid, mine)
    parts = [every]
    for k in range(1, grid.blocks):
        pairs = [
            (d * grid.blocks + b, d * grid.blocks + (b - k) % grid.blocks)
            for d in range(grid.groups) for b in range(grid.blocks)
        ]
        parts.append(lax.ppermute(every, AXES, pairs))
    every = jnp.stack(parts).reshape(grid.blocks * grid.groups, -1)
    group = lax.axis_index("dp")
    all_features = time_features(every[:, 6 * width])
    my_features = lax.dynamic_slice_in_dim(all_features, group * t_rows, t_rows, 1)
    grad_time = lax.dot_general(
        my_features, every[:, : 2 * width], (((0,), (0,)), ((), ())), precision=lax.Precision.HIGHEST
    )
    sums = jnp.sum(every[:, 2 * width : 6 * width].reshape(-1, 4, width), axis=0)
    sums = lax.dynamic_slice_in_dim(sums, group * per, per, 1)
    return (
        layer_out, grad_tokens, grad_qkv, grad_out, grad_up, grad_down, grad_time,
        sums[0], sums[1], sums[2], sums[3],
    )


def solution(mesh):
    rows = P("dp", "blk", None)
    matrix = P("dp", None)
    vector = P("dp")
    return jax.shard_map(
        shards,
        mesh=mesh,
        in_specs=(rows, vector, vector) + (matrix,) * 5 + (vector,) * 4 + (rows,),
        out_specs=(rows, rows) + (matrix,) * 5 + (vector,) * 4,
        check_vma=False,
    )
```

time: 1240 us -> 678 us (0.55)
  waiting for transfers between devices: 622 us -> 200 us
  matrix products: 340 us -> 1.37 us
  Pallas kernels: 0 us -> 275 us
  blocking collectives: 125 us -> 0 us
  starting transfers between devices: 3.15 us -> 96.2 us
  other arithmetic: 67.9 us -> 43.8 us
  between operations: 16.6 us -> 2.52 us
    reduce_scatter x5 -> x0, waiting for transfers between devices: 463 us -> none  [the longest x1 183 us: shards(): lax.psum_scatter(grad_list[3].astype(jnp.bfloat16), 'dp', scatter_dimensi...]
    dot_general x26 -> x2, matrix products: 340 us -> 1.37 us  [the longest x1 1 us: shards(): lax.dot_general(my_features, every[:, :2 * width], (((0,), (0,)), ((), ()...]
    pallas_call x0 -> x14, Pallas kernels: none -> 275 us  [the longest x1 57.4 us: attend_back(): call(functools.partial(attend_back_kernel, min(rows, 512), merged), 'atte...]
    ppermute x6 -> x83, waiting for transfers between devices: 0.02 us -> 200 us  [the longest x44 167 us: shift(): return lax.ppermute(v, AXES, pairs)]
    all_gather x4 -> x0, waiting for transfers between devices: 144 us -> none  [the longest x1 96.9 us: shards(): lax.all_gather(down_weight, 'dp', axis=0, tiled=True)]
    ppermute x6 -> x83, starting transfers between devices: 2.75 us -> 96.2 us  [the longest x44 51.1 us: shift(): return lax.ppermute(v, AXES, pairs)]
    unnamed x2 -> x0, blocking collectives: 73.1 us -> none
    all_gather x1 -> x0, blocking collectives: 36.4 us -> none  [shards(): lax.all_gather(time_weight, 'dp', axis=0, tiled=True)]
  transfers between devices with their start and end apart: 16 -> 83, of which waited for: 8 -> 26; matrix products, arithmetic and copies ran while one was open for 27% -> 13% of each run, Pallas kernels for 0% -> 20%
where the time goes in v1:
time: 678 us; the launch traced here: 667 us
  Pallas kernels  275 us (41%)
  waiting for transfers between devices  200 us (29%)
  starting transfers between devices  96.2 us (14%)
  local copies, waits for them, and re-layouts  48.6 us (7%)
  other arithmetic  43.8 us (6%)
    ppermute x44, waiting for transfers between devices, shift(): return lax.ppermute(v, AXES, pairs)  167 us
    pallas_call x1, Pallas kernels, attend_back(): call(functools.partial(attend_back_kernel, min(rows, 512), merged), 'atte...  57.4 us
    ppermute x44, starting transfers between devices, shift(): return lax.ppermute(v, AXES, pairs)  51.1 us
    pallas_call x3, Pallas kernels, row_chunks(): call(functools.partial(row_chunks_kernel, chunks, per), 'row_chunks', (2...  37.7 us
    pallas_call x1, Pallas kernels, attend(): call(functools.partial(attend_kernel, min(rows, 512)), 'attend', (width /...  36.9 us
    pallas_call x2, Pallas kernels, norm_back(): call(functools.partial(norm_back_kernel, len(pieces), block, lead), 'norm...  35.8 us
    ppermute x10, waiting for transfers between devices, along(): parts.append(lax.ppermute(v, AXES, pairs))  32.5 us
    ppermute x28, starting transfers between devices, swap(): return lax.ppermute(v, AXES, pairs)  28.8 us
  transfers between devices with their start and end apart: 83, of which 26 were waited for; matrix products, arithmetic and copies ran while one was open for 13% of the time, Pallas kernels for 20%

profile of v1, /device:TPU:1, one launch (start us, length us, event | category | flops | bytes accessed | tf_op | source)
XLA Modules:
  0.0 667.1 jit_solution(10661731224159386320)
XLA Ops:
  2.4 4.2 collective-permute-start.6
  11.9 2.8 collective-permute-start.16
  20.2 2.8 dynamic-slice_bitcast_fusion.3
  35.9 2.9 collective-permute-start.26
  48.0 3.2 collective-permute-start.36
  60.7 7.6 %collective-permute-done.3 = bf16[2,2,136,128]{3,2,1,0:T(8,128)(2,1)S(1)} collective-permute-done((bf16[2,2,136,128]{3,2,1,0:T(8,128)(2,1)S(1)}, bf16[2,2,136,128]{3,2,1,0:T(8,128)(2,1)S(1)}, u32[]{:S(2)}, u32[]{:S(2)}) %collective-permute-start.3) | collective-permute-done | bytes 139296 | tf_op jit(solution)/shard_map/ppermute | solution.py:702
  68.2 4.4 collective-permute-start.4
  72.7 2.9 collective-permute-done.4
  75.6 4.3 collective-permute-start.5
  79.9 6.2 collective-permute-done.5
  88.4 2.7 collective-permute-start.22
  91.1 2.2 collective-permute-done.19.refs_1_
  93.5 11.8 %collective-permute-done.37 = bf16[256,512]{1,0:T(8,128)(2,1)S(1)} collective-permute-done((bf16[256,512]{1,0:T(8,128)(2,1)S(1)}, bf16[256,512]{1,0:T(8,128)(2,1)S(1)}, u32[]{:S(2)}, u32[]{:S(2)}) %collective-permute-start.37) | collective-permute-done | bytes 262176 | tf_op jit(solution)/shard_map/ppermute | solution.py:46
  109.9 14.8 %collective-permute-done.9.refs_1_ = bf16[4,64,1536]{2,1,0:T(8,128)(2,1)} collective-permute-done((bf16[4,64,1536]{2,1,0:T(8,128)(2,1)S(1)}, bf16[4,64,1536]{2,1,0:T(8,128)(2,1)}, u32[]{:S(2)}, u32[]{:S(2)}) %collective-permute-start.9) | collective-permute-done | bytes 786464 | tf_op jit(solution)/shard_map/ppermute | solution.py:46
  130.0 17.4 %collective-permute-done.29.refs_1_ = bf16[4,64,2048]{2,1,0:T(8,128)(2,1)S(1)} collective-permute-done((bf16[4,64,2048]{2,1,0:T(8,128)(2,1)}, bf16[4,64,2048]{2,1,0:T(8,128)(2,1)S(1)}, u32[]{:S(2)}, u32[]{:S(2)}) %collective-permute-start.29) | collective-permute-done | bytes 1048608 | tf_op jit(solution)/shard_map/ppermute | solution.py:46
  147.4 5.0 collective-permute-start.13
  153.0 13.7 %collective-permute-done.11.refs_3_ = bf16[4,64,1536]{2,1,0:T(8,128)(2,1)} collective-permute-done((bf16[4,64,1536]{2,1,0:T(8,128)(2,1)}, bf16[4,64,1536]{2,1,0:T(8,128)(2,1)}, u32[]{:S(2)}, u32[]{:S(2)}) %collective-permute-start.11) | collective-permute-done | bytes 786464 | tf_op jit(solution)/shard_map/ppermute | solution.py:46
  166.8 3.2 collective-permute-start.15
  177.8 2.8 pad_maximum_fusion.x
  182.2 22.7 %qkv.1 = (bf16[1024,1024]{1,0:T(8,128)(2,1)}, bf16[3,1024,1024]{2,1,0:T(8,128)(2,1)}) custom-call(s32[24]{0:T(128)} %stack.270.place, bf16[1024,1024]{1,0:T(8,128)(2,1)} %pad_maximum_fusion.x, f32[1,1024]{1,0:T(1,128)} %mul.130.gain, f32[1,1024]{1,0:T(1,128)} %slice.178.bias, f32[1024,128]{1,0:T(8,128)} %copy.56.cosine, f32[1024,128]{1,0:T(8,128)} %copy.57.sine, ...), custom_call_target="tpu_custom_call" | custom-call | flops 6442450944 | bytes 16777216 | tf_op jit(solution)/shard_map/qkv/pallas_call | solution.py:191
  206.1 5.0 collective-permute-done.41.refs_3_
  211.9 36.9 %attend.1 = (bf16[1024,1024]{1,0:T(8,128)(2,1)}, f32[1024,128]{1,0:T(8,128)}) custom-call(bf16[3,1024,1024]{2,1,0:T(8,128)(2,1)} %get-tuple-element.33.q.k.v, bf16[3,1024,1024]{2,1,0:T(8,128)(2,1)} %get-tuple-element.33.q.k.v, bf16[3,1024,1024]{2,1,0:T(8,128)(2,1)} %get-tuple-element.33.q.k.v, f32[1,1024]{1,0:T(1,128)} %compare_select_fusion.1.mask), custom_call_target="tpu_custom_call" | custom-call | flops 17179869184 | bytes 8388608 | tf_op jit(solution)/shard_map/attend/pallas_call | solution.py:238
  248.8 9.6 %out.1 = (bf16[1024,1024]{1,0:T(8,128)(2,1)}, bf16[1024,1024]{1,0:T(8,128)(2,1)}) custom-call(s32[24]{0:T(128)} %stack.270.place, bf16[1024,1024]{1,0:T(8,128)(2,1)} %get-tuple-element.34.mixed.a, bf16[1024,1024]{1,0:T(8,128)(2,1)} %pad_maximum_fusion.x, f32[1,1024]{1,0:T(1,128)} %bitcast.307, f32[1,1024]{1,0:T(1,128)} %slice.182.bias, ...), custom_call_target="tpu_custom_call" | custom-call | flops 2147483648 | bytes 10485760 | tf_op jit(solution)/shard_map/out/pallas_call | solution.py:356
  258.4 21.1 %up.1 = (bf16[1024,4096]{1,0:T(8,128)(2,1)}, bf16[1024,4096]{1,0:T(8,128)(2,1)}) custom-call(s32[24]{0:T(128)} %stack.270.place, bf16[1024,1024]{1,0:T(8,128)(2,1)} %get-tuple-element.35.normed.a, bf16[4,64,2048]{2,1,0:T(8,128)(2,1)} %constant_dynamic-slice_fusion.4.refs_0_, bf16[4,64,2048]{2,1,0:T(8,128)(2,1)} %copy-done.22, ...), custom_call_target="tpu_custom_call" | custom-call | flops 8589934592 | bytes 25165824 | tf_op jit(solution)/shard_map/up/pallas_call | solution.py:395
  280.9 15.1 %hidden_back.1.grad.b = bf16[1024,4096]{1,0:T(8,128)(2,1)} custom-call(s32[24]{0:T(128)} %stack.270.place, bf16[1024,1024]{1,0:T(8,128)(2,1)} %pad_maximum_fusion.1.grad.base.refs_4_, bf16[1024,4096]{1,0:T(8,128)(2,1)} %get-tuple-element.38.slope, bf16[4,256,512]{2,1,0:T(8,128)(2,1)} %constant_dynamic-slice_fusion.2.refs_0_, ...), custom_call_target="tpu_custom_call" | custom-call | flops 8589934592 | bytes 25165824 | tf_op jit(solution)/shard_map/hidden_back/pallas_call | solution.py:465
  296.0 16.4 %row_chunks.5 = (bf16[4,4,64,2048]{3,2,1,0:T(8,128)(2,1)}, bf16[4,4,64,2048]{3,2,1,0:T(8,128)(2,1)}) custom-call(s32[24]{0:T(128)} %stack.270.place, bf16[1024,1024]{1,0:T(8,128)(2,1)} %get-tuple-element.35.normed.a, bf16[1024,4096]{1,0:T(8,128)(2,1)} %hidden_back.1.grad.b), custom_call_target="tpu_custom_call" | custom-call | flops 8589934592 | bytes 18874368 | tf_op jit(solution)/shard_map/row_chunks/pallas_call | solution.py:592
  312.4 19.2 %norm_back.2 = (bf16[1024,1024]{1,0:T(8,128)(2,1)}, f32[1,1024]{1,0:T(1,128)}, f32[1,1024]{1,0:T(1,128)}) custom-call(s32[24]{0:T(128)} %stack.270.place, bf16[1024,4096]{1,0:T(8,128)(2,1)} %hidden_back.1.grad.b, bf16[1024,1024]{1,0:T(8,128)(2,1)} %get-tuple-element.37.middle.x, f32[1,1024]{1,0:T(1,128)} %bitcast.308, ...), custom_call_target="tpu_custom_call" | custom-call | flops 8589934592 | bytes 23068672 | tf_op jit(solution)/shard_map/norm_back/pallas_call | solution.py:513
  331.6 7.4 %row_chunks.4 = (bf16[4,4,64,512]{3,2,1,0:T(8,128)(2,1)}, bf16[4,4,64,512]{3,2,1,0:T(8,128)(2,1)}) custom-call(s32[24]{0:T(128)} %stack.270.place, bf16[1024,1024]{1,0:T(8,128)(2,1)} %get-tuple-element.34.mixed.a, bf16[1024,1024]{1,0:T(8,128)(2,1)} %get-tuple-element.39.grad.base.b), custom_call_target="tpu_custom_call" | custom-call | flops 2147483648 | bytes 6291456 | tf_op jit(solution)/shard_map/row_chunks/pallas_call | solution.py:592
  339.0 6.7 %heads_back.1.grad = bf16[1024,1024]{1,0:T(8,128)(2,1)} custom-call(s32[24]{0:T(128)} %stack.270.place, bf16[1024,1024]{1,0:T(8,128)(2,1)} %get-tuple-element.39.grad.base.b, bf16[4,64,512]{2,1,0:T(8,128)(2,1)} %copy-done.16, bf16[4,64,512]{2,1,0:T(8,128)(2,1)} %copy-done.30, bf16[4,64,512]{2,1,0:T(8,128)(2,1)} %copy-done.31, ...), custom_call_target="tpu_custom_call" | custom-call | flops 2147483648 | bytes 6291456 | tf_op jit(solution)/shard_map/heads_back/pallas_call | solution.py:545
  345.7 57.4 %attend_back.1.grad.b = bf16[3,1024,1024]{2,1,0:T(8,128)(2,1)} custom-call(bf16[3,1024,1024]{2,1,0:T(8,128)(2,1)} %get-tuple-element.33.q.k.v, bf16[3,1024,1024]{2,1,0:T(8,128)(2,1)} %get-tuple-element.33.q.k.v, bf16[3,1024,1024]{2,1,0:T(8,128)(2,1)} %get-tuple-element.33.q.k.v, bf16[1024,1024]{1,0:T(8,128)(2,1)} %get-tuple-element.34.mixed.a, ...), custom_call_target="tpu_custom_call" | custom-call | flops 42949672960 | bytes 16777216 | tf_op jit(solution)/shard_map/attend_back/pallas_call | solution.py:320
  403.2 16.6 %norm_back.3 = (bf16[1024,1024]{1,0:T(8,128)(2,1)}, f32[1,1024]{1,0:T(1,128)}, f32[1,1024]{1,0:T(1,128)}) custom-call(s32[24]{0:T(128)} %stack.270.place, bf16[3,1024,1024]{2,1,0:T(8,128)(2,1)} %attend_back.1.grad.b, bf16[1024,1024]{1,0:T(8,128)(2,1)} %pad_maximum_fusion.x, f32[1,1024]{1,0:T(1,128)} %mul.130.gain, ...), custom_call_target="tpu_custom_call" | custom-call | flops 6442450944 | bytes 18874368 | tf_op jit(solution)/shard_map/norm_back/pallas_call | solution.py:513
  422.0 16.9 %wide_chunks.1 = (bf16[4,4,256,512]{3,2,1,0:T(8,128)(2,1)}, bf16[4,4,256,512]{3,2,1,0:T(8,128)(2,1)}) custom-call(s32[24]{0:T(128)} %stack.270.place, bf16[1024,4096]{1,0:T(8,128)(2,1)} %get-tuple-element.36.active.refs_0_.refs_1_.refs_2_.refs_3_, bf16[1024,4096]{1,0:T(8,128)(2,1)} %get-tuple-element.36.active.refs_0_.refs_1_.refs_2_.refs_3_, ...), custom_call_target="tpu_custom_call" | custom-call | flops 8589934592 | bytes 18874368 | tf_op jit(solution)/shard_map/wide_chunks/pallas_call | solution.py:633
  439.7 13.9 %row_chunks.3 = (bf16[4,4,64,1536]{3,2,1,0:T(8,128)(2,1)}, bf16[4,4,64,1536]{3,2,1,0:T(8,128)(2,1)}) custom-call(s32[24]{0:T(128)} %stack.270.place, bf16[1024,1024]{1,0:T(8,128)(2,1)} %get-tuple-element.42.a, bf16[3,1024,1024]{2,1,0:T(8,128)(2,1)} %attend_back.1.grad.b), custom_call_target="tpu_custom_call" | custom-call | flops 6442450944 | bytes 14680064 | tf_op jit(solution)/shard_map/row_chunks/pallas_call | solution.py:592
  453.8 15.0 %down.1 = bf16[1024,1024]{1,0:T(8,128)(2,1)} custom-call(s32[24]{0:T(128)} %stack.270.place, bf16[1024,4096]{1,0:T(8,128)(2,1)} %get-tuple-element.36.active.refs_0_.refs_1_.refs_2_.refs_3_, bf16[1024,1024]{1,0:T(8,128)(2,1)} %get-tuple-element.37.middle.x, bf16[4,256,512]{2,1,0:T(8,128)(2,1)} %constant_dynamic-slice_fusion.2.refs_0_, ...), custom_call_target="tpu_custom_call" | custom-call | flops 8589934592 | bytes 16777216 | tf_op jit(solution)/shard_map/down/pallas_call | solution.py:434
  469.0 3.0 collective-permute-done.78
  473.2 2.5 collective-permute-done.79
  476.0 4.9 collective-permute-done.80
  480.9 5.4 collective-permute-done.81
  486.7 4.5 collective-permute-start.82
  492.2 1.8 collective-permute-start.57
  495.9 4.9 collective-permute-done.57
  500.8 1.8 fusion.17
  504.3 4.1 collective-permute-done.58
  511.1 2.4 add_convert_fusion.2
  513.5 1.8 collective-permute-start.50
  515.4 2.4 add_convert_fusion
  518.4 2.4 add_convert_fusion.1
  521.9 5.4 collective-permute-done.59
  527.7 3.5 collective-permute-done.60
  531.4 3.3 maximum_select_fusion.1
  534.7 3.2 collective-permute-start.62
  542.4 21.9 %collective-permute-done.71 = bf16[2,4,256,512]{3,2,1,0:T(8,128)(2,1)S(1)} collective-permute-done((bf16[2,4,256,512]{3,2,1,0:T(8,128)(2,1)S(1)}, bf16[2,4,256,512]{3,2,1,0:T(8,128)(2,1)S(1)}, u32[]{:S(2)}, u32[]{:S(2)}) %collective-permute-start.71) | collective-permute-done | bytes 2097184 | tf_op jit(solution)/shard_map/ppermute | solution.py:46
  566.7 31.3 %collective-permute-done.64 = bf16[2,4,64,2048]{3,2,1,0:T(8,128)(2,1)S(1)} collective-permute-done((bf16[2,4,64,2048]{3,2,1,0:T(8,128)(2,1)S(1)}, bf16[2,4,64,2048]{3,2,1,0:T(8,128)(2,1)S(1)}, u32[]{:S(2)}, u32[]{:S(2)}) %collective-permute-start.64) | collective-permute-done | bytes 2097184 | tf_op jit(solution)/shard_map/ppermute | solution.py:46
  598.0 1.8 fusion.3
  603.4 2.2 collective-permute-start.54
  605.6 1.8 fusion.2
  607.9 6.0 collective-permute-done.65
  613.8 1.9 fusion.5
  618.3 13.4 %collective-permute-start.67 = (bf16[64,2048]{1,0:T(8,128)(2,1)S(1)}, bf16[64,2048]{1,0:T(8,128)(2,1)S(1)}, u32[]{:S(2)}, u32[]{:S(2)}) collective-permute-start(bf16[64,2048]{1,0:T(8,128)(2,1)S(1)} %get-tuple-element.84), channel_id=1, source_target_pairs={{0,16},{1,17},{2,18},{3,19},{4,20},{5,21},{6,22},{7,23},{8,24},{9,... | collective-permute-start | bytes 786440 | tf_op jit(solution)/shard_map/ppermute | solution.py:46
  631.8 3.6 collective-permute-start.68
  635.5 14.5 %collective-permute-done.74 = bf16[256,512]{1,0:T(8,128)(2,1)S(1)} collective-permute-done((bf16[256,512]{1,0:T(8,128)(2,1)S(1)}, bf16[256,512]{1,0:T(8,128)(2,1)S(1)}, u32[]{:S(2)}, u32[]{:S(2)}) %collective-permute-start.74) | collective-permute-done | bytes 262176 | tf_op jit(solution)/shard_map/ppermute | solution.py:46
  649.9 2.4 collective-permute-start.55
  652.5 8.6 %collective-permute-done.67 = bf16[64,2048]{1,0:T(8,128)(2,1)S(1)} collective-permute-done((bf16[64,2048]{1,0:T(8,128)(2,1)S(1)}, bf16[64,2048]{1,0:T(8,128)(2,1)S(1)}, u32[]{:S(2)}, u32[]{:S(2)}) %collective-permute-start.67) | collective-permute-done | bytes 262176 | tf_op jit(solution)/shard_map/ppermute | solution.py:46
  661.3 2.4 collective-permute-start.69
  (327 shorter events, 100.8 us)
Async XLA Ops:
  2.4 43.9 %collective-permute-start.6 = (bf16[64,1536]{1,0:T(8,128)(2,1)}, bf16[64,1536]{1,0:T(8,128)(2,1)}, u32[]{:S(2)}, u32[]{:S(2)}) collective-permute-start(bf16[64,1536]{1,0:T(8,128)(2,1)} %get-tuple-element.68), channel_id=1, source_target_pairs={{0,24},{1,25},{2,26},{3,27},{4,28},{5,29},{6,30},{7,31},{8,0},{9,1... | collective-permute-start | bytes 589832 | tf_op jit(solution)/shard_map/ppermute | solution.py:46
  6.5 41.4 %collective-permute-start.7 = (bf16[64,1536]{1,0:T(8,128)(2,1)}, bf16[64,1536]{1,0:T(8,128)(2,1)}, u32[]{:S(2)}, u32[]{:S(2)}) collective-permute-start(bf16[64,1536]{1,0:T(8,128)(2,1)} %get-tuple-element.68), channel_id=1, source_target_pairs={{0,16},{1,17},{2,18},{3,19},{4,20},{5,21},{6,22},{7,23},{8,24},{9,... | collective-permute-start | bytes 589832 | tf_op jit(solution)/shard_map/ppermute | solution.py:46
  6.5 46.3 %collective-permute-start.8 = (bf16[64,1536]{1,0:T(8,128)(2,1)}, bf16[64,1536]{1,0:T(8,128)(2,1)}, u32[]{:S(2)}, u32[]{:S(2)}) collective-permute-start(bf16[64,1536]{1,0:T(8,128)(2,1)} %get-tuple-element.68), channel_id=1, source_target_pairs={{0,8},{1,9},{2,10},{3,11},{4,12},{5,13},{6,14},{7,15},{8,16},{9,17... | collective-permute-start | bytes 589832 | tf_op jit(solution)/shard_map/ppermute | solution.py:46
  9.2 22.4 %collective-permute-start.1 = (bf16[136,128]{1,0:T(8,128)(2,1)}, bf16[136,128]{1,0:T(8,128)(2,1)}, u32[]{:S(2)}, u32[]{:S(2)}) collective-permute-start(bf16[136,128]{1,0:T(8,128)(2,1)} %get-tuple-element.91), channel_id=1, source_target_pairs={{0,2},{1,3},{2,0},{3,1},{4,6},{5,7},{6,4},{7,5},{8,10},{9,11},{10,... | collective-permute-start | bytes 104456 | tf_op jit(solution)/shard_map/ppermute | solution.py:702
  11.9 22.1 %collective-permute-start.16 = (bf16[64,512]{1,0:T(8,128)(2,1)}, bf16[64,512]{1,0:T(8,128)(2,1)}, u32[]{:S(2)}, u32[]{:S(2)}) collective-permute-start(bf16[64,512]{1,0:T(8,128)(2,1)} %get-tuple-element.66), channel_id=1, source_target_pairs={{0,24},{1,25},{2,26},{3,27},{4,28},{5,29},{6,30},{7,31},{8,0},{9,1... | collective-permute-start | bytes 196616 | tf_op jit(solution)/shard_map/ppermute | solution.py:46
  35.9 50.4 %collective-permute-start.26 = (bf16[64,2048]{1,0:T(8,128)(2,1)S(1)}, bf16[64,2048]{1,0:T(8,128)(2,1)S(1)}, u32[]{:S(2)}, u32[]{:S(2)}) collective-permute-start(bf16[64,2048]{1,0:T(8,128)(2,1)S(1)} %get-tuple-element.64), channel_id=1, source_target_pairs={{0,24},{1,25},{2,26},{3,27},{4,28},{5,29},{6,30},{7,31},{8,0},{9,1... | collective-permute-start | bytes 786440 | tf_op jit(solution)/shard_map/ppermute | solution.py:46
  45.8 41.9 %collective-permute-start.27 = (bf16[64,2048]{1,0:T(8,128)(2,1)S(1)}, bf16[64,2048]{1,0:T(8,128)(2,1)S(1)}, u32[]{:S(2)}, u32[]{:S(2)}) collective-permute-start(bf16[64,2048]{1,0:T(8,128)(2,1)S(1)} %get-tuple-element.64), channel_id=1, source_target_pairs={{0,16},{1,17},{2,18},{3,19},{4,20},{5,21},{6,22},{7,23},{8,24},{9,... | collective-permute-start | bytes 786440 | tf_op jit(solution)/shard_map/ppermute | solution.py:46
  46.3 41.8 %collective-permute-start.28 = (bf16[64,2048]{1,0:T(8,128)(2,1)S(1)}, bf16[64,2048]{1,0:T(8,128)(2,1)S(1)}, u32[]{:S(2)}, u32[]{:S(2)}) collective-permute-start(bf16[64,2048]{1,0:T(8,128)(2,1)S(1)} %get-tuple-element.64), channel_id=1, source_target_pairs={{0,8},{1,9},{2,10},{3,11},{4,12},{5,13},{6,14},{7,15},{8,16},{9,17... | collective-permute-start | bytes 786440 | tf_op jit(solution)/shard_map/ppermute | solution.py:46
  48.0 40.4 %collective-permute-start.36 = (bf16[256,512]{1,0:T(8,128)(2,1)S(1)}, bf16[256,512]{1,0:T(8,128)(2,1)S(1)}, u32[]{:S(2)}, u32[]{:S(2)}) collective-permute-start(bf16[256,512]{1,0:T(8,128)(2,1)S(1)} %get-tuple-element.62), channel_id=1, source_target_pairs={{0,24},{1,25},{2,26},{3,27},{4,28},{5,29},{6,30},{7,31},{8,0},{9,1... | collective-permute-start | bytes 786440 | tf_op jit(solution)/shard_map/ppermute | solution.py:46
  52.8 15.4 %collective-permute-start.3 = (bf16[2,2,136,128]{3,2,1,0:T(8,128)(2,1)S(1)}, bf16[2,2,136,128]{3,2,1,0:T(8,128)(2,1)S(1)}, u32[]{:S(2)}, u32[]{:S(2)}) collective-permute-start(bf16[2,2,136,128]{3,2,1,0:T(8,128)(2,1)S(1)} %get-tuple-element.70), channel_id=1, source_target_pairs={{0,24},{1,25},{2,26},{3,27},{4,28},{5,29},{6,30},{7,31},{8,0},{9,1... | collective-permute-start | bytes 417800 | tf_op jit(solution)/shard_map/ppermute | solution.py:702
  75.6 10.5 %collective-permute-start.5 = (bf16[2,2,136,128]{3,2,1,0:T(8,128)(2,1)S(1)}, bf16[2,2,136,128]{3,2,1,0:T(8,128)(2,1)S(1)}, u32[]{:S(2)}, u32[]{:S(2)}) collective-permute-start(bf16[2,2,136,128]{3,2,1,0:T(8,128)(2,1)S(1)} %get-tuple-element.70), channel_id=1, source_target_pairs={{0,8},{1,9},{2,10},{3,11},{4,12},{5,13},{6,14},{7,15},{8,16},{9,17... | collective-permute-start | bytes 417800 | tf_op jit(solution)/shard_map/ppermute | solution.py:702
  86.1 19.1 %collective-permute-start.37 = (bf16[256,512]{1,0:T(8,128)(2,1)S(1)}, bf16[256,512]{1,0:T(8,128)(2,1)S(1)}, u32[]{:S(2)}, u32[]{:S(2)}) collective-permute-start(bf16[256,512]{1,0:T(8,128)(2,1)S(1)} %get-tuple-element.62), channel_id=1, source_target_pairs={{0,16},{1,17},{2,18},{3,19},{4,20},{5,21},{6,22},{7,23},{8,24},{9,... | collective-permute-start | bytes 786440 | tf_op jit(solution)/shard_map/ppermute | solution.py:46
  86.2 19.6 %collective-permute-start.38 = (bf16[256,512]{1,0:T(8,128)(2,1)S(1)}, bf16[256,512]{1,0:T(8,128)(2,1)S(1)}, u32[]{:S(2)}, u32[]{:S(2)}) collective-permute-start(bf16[256,512]{1,0:T(8,128)(2,1)S(1)} %get-tuple-element.62), channel_id=1, source_target_pairs={{0,8},{1,9},{2,10},{3,11},{4,12},{5,13},{6,14},{7,15},{8,16},{9,17... | collective-permute-start | bytes 786440 | tf_op jit(solution)/shard_map/ppermute | solution.py:46
  88.1 18.0 %collective-permute-start.20 = (bf16[4,64,512]{2,1,0:T(8,128)(2,1)S(1)}, bf16[4,64,512]{2,1,0:T(8,128)(2,1)S(1)}, u32[]{:S(2)}, u32[]{:S(2)}) collective-permute-start(bf16[4,64,512]{2,1,0:T(8,128)(2,1)S(1)} %constant_dynamic-slice_fusion.6.refs_0_), channel_id=1, source_target_pairs={{0,4},{1,3},{2,6},{3,1},{4,0},{5,7},{6,2},{7,5},{8,12},{9,11},{10,... | collective-permute-start | bytes 786440 | tf_op jit(solution)/shard_map/ppermute | solution.py:46
  88.4 17.9 %collective-permute-start.22 = (bf16[4,64,512]{2,1,0:T(8,128)(2,1)S(1)}, bf16[4,64,512]{2,1,0:T(8,128)(2,1)S(1)}, u32[]{:S(2)}, u32[]{:S(2)}) collective-permute-start(bf16[4,64,512]{2,1,0:T(8,128)(2,1)S(1)} %constant_dynamic-slice_fusion.6.refs_0_), channel_id=1, source_target_pairs={{0,1},{1,0},{2,3},{3,2},{4,5},{5,4},{6,7},{7,6},{8,9},{9,8},{10,11... | collective-permute-start | bytes 786440 | tf_op jit(solution)/shard_map/ppermute | solution.py:53
  93.3 13.5 %collective-permute-start.21 = (bf16[4,64,512]{2,1,0:T(8,128)(2,1)S(1)}, bf16[4,64,512]{2,1,0:T(8,128)(2,1)S(1)}, u32[]{:S(2)}, u32[]{:S(2)}) collective-permute-start(bf16[4,64,512]{2,1,0:T(8,128)(2,1)S(1)} %collective-permute-done.19.refs_1_), channel_id=1, source_target_pairs={{0,4},{1,3},{2,6},{3,1},{4,0},{5,7},{6,2},{7,5},{8,12},{9,11},{10,... | collective-permute-start | bytes 786440 | tf_op jit(solution)/shard_map/ppermute | solution.py:46
  105.8 18.8 %collective-permute-start.9 = (bf16[4,64,1536]{2,1,0:T(8,128)(2,1)S(1)}, bf16[4,64,1536]{2,1,0:T(8,128)(2,1)}, u32[]{:S(2)}, u32[]{:S(2)}) collective-permute-start(bf16[4,64,1536]{2,1,0:T(8,128)(2,1)S(1)} %constant_dynamic-slice_fusion.8.refs_0_), channel_id=1, source_target_pairs={{0,2},{1,5},{2,0},{3,7},{4,6},{5,1},{6,4},{7,3},{8,10},{9,13},{10,... | collective-permute-start | bytes 2359304 | tf_op jit(solution)/shard_map/ppermute | solution.py:46
  106.1 19.4 %collective-permute-start.10 = (bf16[4,64,1536]{2,1,0:T(8,128)(2,1)S(1)}, bf16[4,64,1536]{2,1,0:T(8,128)(2,1)}, u32[]{:S(2)}, u32[]{:S(2)}) collective-permute-start(bf16[4,64,1536]{2,1,0:T(8,128)(2,1)S(1)} %constant_dynamic-slice_fusion.8.refs_0_), channel_id=1, source_target_pairs={{0,4},{1,3},{2,6},{3,1},{4,0},{5,7},{6,2},{7,5},{8,12},{9,11},{10,... | collective-permute-start | bytes 2359304 | tf_op jit(solution)/shard_map/ppermute | solution.py:46
  107.0 18.7 %collective-permute-start.12 = (bf16[4,64,1536]{2,1,0:T(8,128)(2,1)S(1)}, bf16[4,64,1536]{2,1,0:T(8,128)(2,1)S(1)}, u32[]{:S(2)}, u32[]{:S(2)}) collective-permute-start(bf16[4,64,1536]{2,1,0:T(8,128)(2,1)S(1)} %constant_dynamic-slice_fusion.8.refs_0_), channel_id=1, source_target_pairs={{0,1},{1,0},{2,3},{3,2},{4,5},{5,4},{6,7},{7,6},{8,9},{9,8},{10,11... | collective-permute-start | bytes 2359304 | tf_op jit(solution)/shard_map/ppermute | solution.py:53
  108.0 20.2 %collective-permute-start = (bf16[512,1024]{1,0:T(8,128)(2,1)S(1)}, bf16[512,1024]{1,0:T(8,128)(2,1)S(1)}, u32[]{:S(2)}, u32[]{:S(2)}) collective-permute-start(bf16[512,1024]{1,0:T(8,128)(2,1)S(1)} %copy-done.7), channel_id=1, source_target_pairs={{0,1},{1,0},{2,3},{3,2},{4,5},{5,4},{6,7},{7,6},{8,9},{9,8},{10,11... | collective-permute-start | bytes 3145736 | tf_op jit(solution)/shard_map/ppermute | solution.py:53
  108.5 21.5 %collective-permute-start.47 = (bf16[512,1024]{1,0:T(8,128)(2,1)S(1)}, bf16[512,1024]{1,0:T(8,128)(2,1)S(1)}, u32[]{:S(2)}, u32[]{:S(2)}) collective-permute-start(bf16[512,1024]{1,0:T(8,128)(2,1)S(1)} %copy-done.6), channel_id=1, source_target_pairs={{0,1},{1,0},{2,3},{3,2},{4,5},{5,4},{6,7},{7,6},{8,9},{9,8},{10,11... | collective-permute-start | bytes 3145736 | tf_op jit(solution)/shard_map/ppermute | solution.py:53
  124.6 22.8 %collective-permute-start.29 = (bf16[4,64,2048]{2,1,0:T(8,128)(2,1)}, bf16[4,64,2048]{2,1,0:T(8,128)(2,1)S(1)}, u32[]{:S(2)}, u32[]{:S(2)}) collective-permute-start(bf16[4,64,2048]{2,1,0:T(8,128)(2,1)} %constant_dynamic-slice_fusion.4.refs_0_), channel_id=1, source_target_pairs={{0,2},{1,5},{2,0},{3,7},{4,6},{5,1},{6,4},{7,3},{8,10},{9,13},{10,... | collective-permute-start | bytes 3145736 | tf_op jit(solution)/shard_map/ppermute | solution.py:46
  125.5 26.9 %collective-permute-start.30 = (bf16[4,64,2048]{2,1,0:T(8,128)(2,1)}, bf16[4,64,2048]{2,1,0:T(8,128)(2,1)S(1)}, u32[]{:S(2)}, u32[]{:S(2)}) collective-permute-start(bf16[4,64,2048]{2,1,0:T(8,128)(2,1)} %constant_dynamic-slice_fusion.4.refs_0_), channel_id=1, source_target_pairs={{0,4},{1,3},{2,6},{3,1},{4,0},{5,7},{6,2},{7,5},{8,12},{9,11},{10,... | collective-permute-start | bytes 3145736 | tf_op jit(solution)/shard_map/ppermute | solution.py:46
  125.8 41.0 %collective-permute-start.11 = (bf16[4,64,1536]{2,1,0:T(8,128)(2,1)}, bf16[4,64,1536]{2,1,0:T(8,128)(2,1)}, u32[]{:S(2)}, u32[]{:S(2)}) collective-permute-start(bf16[4,64,1536]{2,1,0:T(8,128)(2,1)} %collective-permute-done.9.refs_1_), channel_id=1, source_target_pairs={{0,4},{1,3},{2,6},{3,1},{4,0},{5,7},{6,2},{7,5},{8,12},{9,11},{10,... | collective-permute-start | bytes 2359304 | tf_op jit(solution)/shard_map/ppermute | solution.py:46
  128.2 46.2 %collective-permute-start.32 = (bf16[4,64,2048]{2,1,0:T(8,128)(2,1)}, bf16[4,64,2048]{2,1,0:T(8,128)(2,1)}, u32[]{:S(2)}, u32[]{:S(2)}) collective-permute-start(bf16[4,64,2048]{2,1,0:T(8,128)(2,1)} %constant_dynamic-slice_fusion.4.refs_0_), channel_id=1, source_target_pairs={{0,1},{1,0},{2,3},{3,2},{4,5},{5,4},{6,7},{7,6},{8,9},{9,8},{10,11... | collective-permute-start | bytes 3145736 | tf_op jit(solution)/shard_map/ppermute | solution.py:53
  129.9 44.5 %collective-permute-start.39 = (bf16[4,256,512]{2,1,0:T(8,128)(2,1)}, bf16[4,256,512]{2,1,0:T(8,128)(2,1)}, u32[]{:S(2)}, u32[]{:S(2)}) collective-permute-start(bf16[4,256,512]{2,1,0:T(8,128)(2,1)} %constant_dynamic-slice_fusion.2.refs_0_), channel_id=1, source_target_pairs={{0,2},{1,5},{2,0},{3,7},{4,6},{5,1},{6,4},{7,3},{8,10},{9,13},{10,... | collective-permute-start | bytes 3145736 | tf_op jit(solution)/shard_map/ppermute | solution.py:46
  147.4 28.5 %collective-permute-start.13 = (bf16[4,64,1536]{2,1,0:T(8,128)(2,1)}, bf16[4,64,1536]{2,1,0:T(8,128)(2,1)}, u32[]{:S(2)}, u32[]{:S(2)}) collective-permute-start(bf16[4,64,1536]{2,1,0:T(8,128)(2,1)} %collective-permute-done.9.refs_1_), channel_id=1, source_target_pairs={{0,1},{1,0},{2,3},{3,2},{4,5},{5,4},{6,7},{7,6},{8,9},{9,8},{10,11... | collective-permute-start | bytes 2359304 | tf_op jit(solution)/shard_map/ppermute | solution.py:53
  152.4 24.1 %collective-permute-start.14 = (bf16[4,64,1536]{2,1,0:T(8,128)(2,1)}, bf16[4,64,1536]{2,1,0:T(8,128)(2,1)}, u32[]{:S(2)}, u32[]{:S(2)}) collective-permute-start(bf16[4,64,1536]{2,1,0:T(8,128)(2,1)} %collective-permute-done.10.refs_2_), channel_id=1, source_target_pairs={{0,1},{1,0},{2,3},{3,2},{4,5},{5,4},{6,7},{7,6},{8,9},{9,8},{10,11... | collective-permute-start | bytes 2359304 | tf_op jit(solution)/shard_map/ppermute | solution.py:53
  166.8 9.8 %collective-permute-start.15 = (bf16[4,64,1536]{2,1,0:T(8,128)(2,1)}, bf16[4,64,1536]{2,1,0:T(8,128)(2,1)}, u32[]{:S(2)}, u32[]{:S(2)}) collective-permute-start(bf16[4,64,1536]{2,1,0:T(8,128)(2,1)} %collective-permute-done.11.refs_3_), channel_id=1, source_target_pairs={{0,1},{1,0},{2,3},{3,2},{4,5},{5,4},{6,7},{7,6},{8,9},{9,8},{10,11... | collective-permute-start | bytes 2359304 | tf_op jit(solution)/shard_map/ppermute | solution.py:53
  174.4 30.5 %collective-permute-start.40 = (bf16[4,256,512]{2,1,0:T(8,128)(2,1)}, bf16[4,256,512]{2,1,0:T(8,128)(2,1)S(1)}, u32[]{:S(2)}, u32[]{:S(2)}) collective-permute-start(bf16[4,256,512]{2,1,0:T(8,128)(2,1)} %constant_dynamic-slice_fusion.2.refs_0_), channel_id=1, source_target_pairs={{0,4},{1,3},{2,6},{3,1},{4,0},{5,7},{6,2},{7,5},{8,12},{9,11},{10,... | collective-permute-start | bytes 3145736 | tf_op jit(solution)/shard_map/ppermute | solution.py:46
  174.5 31.0 %collective-permute-start.31 = (bf16[4,64,2048]{2,1,0:T(8,128)(2,1)}, bf16[4,64,2048]{2,1,0:T(8,128)(2,1)}, u32[]{:S(2)}, u32[]{:S(2)}) collective-permute-start(bf16[4,64,2048]{2,1,0:T(8,128)(2,1)} %copy-done.22), channel_id=1, source_target_pairs={{0,4},{1,3},{2,6},{3,1},{4,0},{5,7},{6,2},{7,5},{8,12},{9,11},{10,... | collective-permute-start | bytes 3145736 | tf_op jit(solution)/shard_map/ppermute | solution.py:46
  175.9 29.6 %collective-permute-start.33 = (bf16[4,64,2048]{2,1,0:T(8,128)(2,1)}, bf16[4,64,2048]{2,1,0:T(8,128)(2,1)}, u32[]{:S(2)}, u32[]{:S(2)}) collective-permute-start(bf16[4,64,2048]{2,1,0:T(8,128)(2,1)} %copy-done.22), channel_id=1, source_target_pairs={{0,1},{1,0},{2,3},{3,2},{4,5},{5,4},{6,7},{7,6},{8,9},{9,8},{10,11... | collective-permute-start | bytes 3145736 | tf_op jit(solution)/shard_map/ppermute | solution.py:53
  176.5 29.5 %collective-permute-start.34 = (bf16[4,64,2048]{2,1,0:T(8,128)(2,1)}, bf16[4,64,2048]{2,1,0:T(8,128)(2,1)}, u32[]{:S(2)}, u32[]{:S(2)}) collective-permute-start(bf16[4,64,2048]{2,1,0:T(8,128)(2,1)} %copy-done.24), channel_id=1, source_target_pairs={{0,1},{1,0},{2,3},{3,2},{4,5},{5,4},{6,7},{7,6},{8,9},{9,8},{10,11... | collective-permute-start | bytes 3145736 | tf_op jit(solution)/shard_map/ppermute | solution.py:53
  176.6 34.5 %collective-permute-start.41 = (bf16[4,256,512]{2,1,0:T(8,128)(2,1)}, bf16[4,256,512]{2,1,0:T(8,128)(2,1)S(1)}, u32[]{:S(2)}, u32[]{:S(2)}) collective-permute-start(bf16[4,256,512]{2,1,0:T(8,128)(2,1)} %collective-permute-done.39.refs_1_), channel_id=1, source_target_pairs={{0,4},{1,3},{2,6},{3,1},{4,0},{5,7},{6,2},{7,5},{8,12},{9,11},{10,... | collective-permute-start | bytes 3145736 | tf_op jit(solution)/shard_map/ppermute | solution.py:46
  204.9 74.6 %collective-permute-start.42 = (bf16[4,256,512]{2,1,0:T(8,128)(2,1)}, bf16[4,256,512]{2,1,0:T(8,128)(2,1)S(1)}, u32[]{:S(2)}, u32[]{:S(2)}) collective-permute-start(bf16[4,256,512]{2,1,0:T(8,128)(2,1)} %constant_dynamic-slice_fusion.2.refs_0_), channel_id=1, source_target_pairs={{0,1},{1,0},{2,3},{3,2},{4,5},{5,4},{6,7},{7,6},{8,9},{9,8},{10,11... | collective-permute-start | bytes 3145736 | tf_op jit(solution)/shard_map/ppermute | solution.py:53
  205.5 74.1 %collective-permute-start.43 = (bf16[4,256,512]{2,1,0:T(8,128)(2,1)}, bf16[4,256,512]{2,1,0:T(8,128)(2,1)S(1)}, u32[]{:S(2)}, u32[]{:S(2)}) collective-permute-start(bf16[4,256,512]{2,1,0:T(8,128)(2,1)} %collective-permute-done.39.refs_1_), channel_id=1, source_target_pairs={{0,1},{1,0},{2,3},{3,2},{4,5},{5,4},{6,7},{7,6},{8,9},{9,8},{10,11... | collective-permute-start | bytes 3145736 | tf_op jit(solution)/shard_map/ppermute | solution.py:53
  205.6 74.0 %collective-permute-start.44 = (bf16[4,256,512]{2,1,0:T(8,128)(2,1)S(1)}, bf16[4,256,512]{2,1,0:T(8,128)(2,1)}, u32[]{:S(2)}, u32[]{:S(2)}) collective-permute-start(bf16[4,256,512]{2,1,0:T(8,128)(2,1)S(1)} %collective-permute-done.40.refs_2_), channel_id=1, source_target_pairs={{0,1},{1,0},{2,3},{3,2},{4,5},{5,4},{6,7},{7,6},{8,9},{9,8},{10,11... | collective-permute-start | bytes 3145736 | tf_op jit(solution)/shard_map/ppermute | solution.py:53
  206.0 52.4 %collective-permute-start.35 = (bf16[4,64,2048]{2,1,0:T(8,128)(2,1)}, bf16[4,64,2048]{2,1,0:T(8,128)(2,1)}, u32[]{:S(2)}, u32[]{:S(2)}) collective-permute-start(bf16[4,64,2048]{2,1,0:T(8,128)(2,1)} %collective-permute-done.31.refs_3_), channel_id=1, source_target_pairs={{0,1},{1,0},{2,3},{3,2},{4,5},{5,4},{6,7},{7,6},{8,9},{9,8},{10,11... | collective-permute-start | bytes 3145736 | tf_op jit(solution)/shard_map/ppermute | solution.py:53
  211.1 68.5 %collective-permute-start.45 = (bf16[4,256,512]{2,1,0:T(8,128)(2,1)S(1)}, bf16[4,256,512]{2,1,0:T(8,128)(2,1)}, u32[]{:S(2)}, u32[]{:S(2)}) collective-permute-start(bf16[4,256,512]{2,1,0:T(8,128)(2,1)S(1)} %collective-permute-done.41.refs_3_), channel_id=1, source_target_pairs={{0,1},{1,0},{2,3},{3,2},{4,5},{5,4},{6,7},{7,6},{8,9},{9,8},{10,11... | collective-permute-start | bytes 3145736 | tf_op jit(solution)/shard_map/ppermute | solution.py:53
  421.9 46.9 %collective-permute-start.77 = (f32[49,128]{1,0:T(8,128)S(1)}, f32[49,128]{1,0:T(8,128)S(1)}, u32[]{:S(2)}, u32[]{:S(2)}) collective-permute-start(f32[49,128]{1,0:T(8,128)S(1)} %bitcast.284), channel_id=1, source_target_pairs={{0,2},{1,3},{2,0},{3,1},{4,6},{5,7},{6,4},{7,5},{8,10},{9,11},{10,... | collective-permute-start | bytes 75272 | tf_op jit(solution)/shard_map/ppermute | solution.py:702
  438.9 76.5 %collective-permute-start.70 = (bf16[4,4,256,512]{3,2,1,0:T(8,128)(2,1)}, bf16[4,4,256,512]{3,2,1,0:T(8,128)(2,1)}, u32[]{:S(2)}, u32[]{:S(2)}) collective-permute-start(bf16[4,4,256,512]{3,2,1,0:T(8,128)(2,1)} %get-tuple-element.50), channel_id=1, source_target_pairs={{0,1},{1,0},{2,3},{3,2},{4,5},{5,4},{6,7},{7,6},{8,9},{9,8},{10,11... | collective-permute-start | bytes 12582920 | tf_op jit(solution)/shard_map/ppermute | solution.py:53
  439.2 79.2 %collective-permute-start.63 = (bf16[4,4,64,2048]{3,2,1,0:T(8,128)(2,1)}, bf16[4,4,64,2048]{3,2,1,0:T(8,128)(2,1)}, u32[]{:S(2)}, u32[]{:S(2)}) collective-permute-start(bf16[4,4,64,2048]{3,2,1,0:T(8,128)(2,1)} %get-tuple-element.48), channel_id=1, source_target_pairs={{0,1},{1,0},{2,3},{3,2},{4,5},{5,4},{6,7},{7,6},{8,9},{9,8},{10,11... | collective-permute-start | bytes 12582920 | tf_op jit(solution)/shard_map/ppermute | solution.py:53
  439.4 51.8 %collective-permute-start.56 = (bf16[4,4,64,512]{3,2,1,0:T(8,128)(2,1)S(1)}, bf16[4,4,64,512]{3,2,1,0:T(8,128)(2,1)S(1)}, u32[]{:S(2)}, u32[]{:S(2)}) collective-permute-start(bf16[4,4,64,512]{3,2,1,0:T(8,128)(2,1)S(1)} %copy-done.26), channel_id=1, source_target_pairs={{0,1},{1,0},{2,3},{3,2},{4,5},{5,4},{6,7},{7,6},{8,9},{9,8},{10,11... | collective-permute-start | bytes 3145736 | tf_op jit(solution)/shard_map/ppermute | solution.py:53
  453.5 57.5 %collective-permute-start.49 = (bf16[4,4,64,1536]{3,2,1,0:T(8,128)(2,1)}, bf16[4,4,64,1536]{3,2,1,0:T(8,128)(2,1)}, u32[]{:S(2)}, u32[]{:S(2)}) collective-permute-start(bf16[4,4,64,1536]{3,2,1,0:T(8,128)(2,1)} %get-tuple-element.44), channel_id=1, source_target_pairs={{0,1},{1,0},{2,3},{3,2},{4,5},{5,4},{6,7},{7,6},{8,9},{9,8},{10,11... | collective-permute-start | bytes 9437192 | tf_op jit(solution)/shard_map/ppermute | solution.py:53
  492.2 8.6 %collective-permute-start.57 = (bf16[2,4,64,512]{3,2,1,0:T(8,128)(2,1)S(1)}, bf16[2,4,64,512]{3,2,1,0:T(8,128)(2,1)S(1)}, u32[]{:S(2)}, u32[]{:S(2)}) collective-permute-start(bf16[2,4,64,512]{3,2,1,0:T(8,128)(2,1)S(1)} %add_convert_fusion.3), channel_id=1, source_target_pairs={{0,4},{1,3},{2,6},{3,1},{4,0},{5,7},{6,2},{7,5},{8,12},{9,11},{10,... | collective-permute-start | bytes 1572872 | tf_op jit(solution)/shard_map/ppermute | solution.py:46
  495.1 26.6 %collective-permute-start.48 = (bf16[512,1024]{1,0:T(8,128)(2,1)}, bf16[512,1024]{1,0:T(8,128)(2,1)}, u32[]{:S(2)}, u32[]{:S(2)}) collective-permute-start(bf16[512,1024]{1,0:T(8,128)(2,1)} %get-tuple-element.72), channel_id=1, source_target_pairs={{0,1},{1,0},{2,3},{3,2},{4,5},{5,4},{6,7},{7,6},{8,9},{9,8},{10,11... | collective-permute-start | bytes 3145736 | tf_op jit(solution)/shard_map/ppermute | solution.py:53
  508.4 29.6 %collective-permute-start.46 = (bf16[512,1024]{1,0:T(8,128)(2,1)}, bf16[512,1024]{1,0:T(8,128)(2,1)S(1)}, u32[]{:S(2)}, u32[]{:S(2)}) collective-permute-start(bf16[512,1024]{1,0:T(8,128)(2,1)} %get-tuple-element.76), channel_id=1, source_target_pairs={{0,1},{1,0},{2,3},{3,2},{4,5},{5,4},{6,7},{7,6},{8,9},{9,8},{10,11... | collective-permute-start | bytes 3145736 | tf_op jit(solution)/shard_map/ppermute | solution.py:53
  513.5 26.8 %collective-permute-start.50 = (bf16[2,4,64,1536]{3,2,1,0:T(8,128)(2,1)S(1)}, bf16[2,4,64,1536]{3,2,1,0:T(8,128)(2,1)S(1)}, u32[]{:S(2)}, u32[]{:S(2)}) collective-permute-start(bf16[2,4,64,1536]{3,2,1,0:T(8,128)(2,1)S(1)} %add_convert_fusion.2), channel_id=1, source_target_pairs={{0,4},{1,3},{2,6},{3,1},{4,0},{5,7},{6,2},{7,5},{8,12},{9,11},{10,... | collective-permute-start | bytes 4718600 | tf_op jit(solution)/shard_map/ppermute | solution.py:46
  517.7 46.6 %collective-permute-start.71 = (bf16[2,4,256,512]{3,2,1,0:T(8,128)(2,1)S(1)}, bf16[2,4,256,512]{3,2,1,0:T(8,128)(2,1)S(1)}, u32[]{:S(2)}, u32[]{:S(2)}) collective-permute-start(bf16[2,4,256,512]{3,2,1,0:T(8,128)(2,1)S(1)} %add_convert_fusion), channel_id=1, source_target_pairs={{0,4},{1,3},{2,6},{3,1},{4,0},{5,7},{6,2},{7,5},{8,12},{9,11},{10,... | collective-permute-start | bytes 6291464 | tf_op jit(solution)/shard_map/ppermute | solution.py:46
  520.8 77.3 %collective-permute-start.64 = (bf16[2,4,64,2048]{3,2,1,0:T(8,128)(2,1)S(1)}, bf16[2,4,64,2048]{3,2,1,0:T(8,128)(2,1)S(1)}, u32[]{:S(2)}, u32[]{:S(2)}) collective-permute-start(bf16[2,4,64,2048]{3,2,1,0:T(8,128)(2,1)S(1)} %add_convert_fusion.1), channel_id=1, source_target_pairs={{0,4},{1,3},{2,6},{3,1},{4,0},{5,7},{6,2},{7,5},{8,12},{9,11},{10,... | collective-permute-start | bytes 6291464 | tf_op jit(solution)/shard_map/ppermute | solution.py:46
  542.1 58.5 %collective-permute-start.51 = (bf16[4,64,1536]{2,1,0:T(8,128)(2,1)S(1)}, bf16[4,64,1536]{2,1,0:T(8,128)(2,1)S(1)}, u32[]{:S(2)}, u32[]{:S(2)}) collective-permute-start(bf16[4,64,1536]{2,1,0:T(8,128)(2,1)S(1)} %fusion.6), channel_id=1, source_target_pairs={{0,2},{1,5},{2,0},{3,7},{4,6},{5,1},{6,4},{7,3},{8,10},{9,13},{10,... | collective-permute-start | bytes 2359304 | tf_op jit(solution)/shard_map/ppermute | solution.py:46
  566.0 39.6 %collective-permute-start.72 = (bf16[4,256,512]{2,1,0:T(8,128)(2,1)S(1)}, bf16[4,256,512]{2,1,0:T(8,128)(2,1)S(1)}, u32[]{:S(2)}, u32[]{:S(2)}) collective-permute-start(bf16[4,256,512]{2,1,0:T(8,128)(2,1)S(1)} %fusion), channel_id=1, source_target_pairs={{0,2},{1,5},{2,0},{3,7},{4,6},{5,1},{6,4},{7,3},{8,10},{9,13},{10,... | collective-permute-start | bytes 3145736 | tf_op jit(solution)/shard_map/ppermute | solution.py:46
  599.8 14.0 %collective-permute-start.65 = (bf16[4,64,2048]{2,1,0:T(8,128)(2,1)S(1)}, bf16[4,64,2048]{2,1,0:T(8,128)(2,1)S(1)}, u32[]{:S(2)}, u32[]{:S(2)}) collective-permute-start(bf16[4,64,2048]{2,1,0:T(8,128)(2,1)S(1)} %fusion.3), channel_id=1, source_target_pairs={{0,2},{1,5},{2,0},{3,7},{4,6},{5,1},{6,4},{7,3},{8,10},{9,13},{10,... | collective-permute-start | bytes 3145736 | tf_op jit(solution)/shard_map/ppermute | solution.py:46
  602.2 13.7 %collective-permute-start.52 = (bf16[64,1536]{1,0:T(8,128)(2,1)S(1)}, bf16[64,1536]{1,0:T(8,128)(2,1)S(1)}, u32[]{:S(2)}, u32[]{:S(2)}) collective-permute-start(bf16[64,1536]{1,0:T(8,128)(2,1)S(1)} %get-tuple-element.85), channel_id=1, source_target_pairs={{0,8},{1,9},{2,10},{3,11},{4,12},{5,13},{6,14},{7,15},{8,16},{9,17... | collective-permute-start | bytes 589832 | tf_op jit(solution)/shard_map/ppermute | solution.py:46
  602.2 15.9 %collective-permute-start.53 = (bf16[64,1536]{1,0:T(8,128)(2,1)S(1)}, bf16[64,1536]{1,0:T(8,128)(2,1)S(1)}, u32[]{:S(2)}, u32[]{:S(2)}) collective-permute-start(bf16[64,1536]{1,0:T(8,128)(2,1)S(1)} %get-tuple-element.87), channel_id=1, source_target_pairs={{0,16},{1,17},{2,18},{3,19},{4,20},{5,21},{6,22},{7,23},{8,24},{9,... | collective-permute-start | bytes 589832 | tf_op jit(solution)/shard_map/ppermute | solution.py:46
  603.4 14.9 %collective-permute-start.54 = (bf16[64,1536]{1,0:T(8,128)(2,1)S(1)}, bf16[64,1536]{1,0:T(8,128)(2,1)S(1)}, u32[]{:S(2)}, u32[]{:S(2)}) collective-permute-start(bf16[64,1536]{1,0:T(8,128)(2,1)S(1)} %get-tuple-element.86), channel_id=1, source_target_pairs={{0,24},{1,25},{2,26},{3,27},{4,28},{5,29},{6,30},{7,31},{8,0},{9,1... | collective-permute-start | bytes 589832 | tf_op jit(solution)/shard_map/ppermute | solution.py:46
  607.5 24.3 %collective-permute-start.73 = (bf16[256,512]{1,0:T(8,128)(2,1)S(1)}, bf16[256,512]{1,0:T(8,128)(2,1)S(1)}, u32[]{:S(2)}, u32[]{:S(2)}) collective-permute-start(bf16[256,512]{1,0:T(8,128)(2,1)S(1)} %get-tuple-element.79), channel_id=1, source_target_pairs={{0,8},{1,9},{2,10},{3,11},{4,12},{5,13},{6,14},{7,15},{8,16},{9,17... | collective-permute-start | bytes 786440 | tf_op jit(solution)/shard_map/ppermute | solution.py:46
  613.8 36.1 %collective-permute-start.74 = (bf16[256,512]{1,0:T(8,128)(2,1)S(1)}, bf16[256,512]{1,0:T(8,128)(2,1)S(1)}, u32[]{:S(2)}, u32[]{:S(2)}) collective-permute-start(bf16[256,512]{1,0:T(8,128)(2,1)S(1)} %get-tuple-element.81), channel_id=1, source_target_pairs={{0,16},{1,17},{2,18},{3,19},{4,20},{5,21},{6,22},{7,23},{8,24},{9,... | collective-permute-start | bytes 786440 | tf_op jit(solution)/shard_map/ppermute | solution.py:46
  615.8 36.4 %collective-permute-start.75 = (bf16[256,512]{1,0:T(8,128)(2,1)S(1)}, bf16[256,512]{1,0:T(8,128)(2,1)S(1)}, u32[]{:S(2)}, u32[]{:S(2)}) collective-permute-start(bf16[256,512]{1,0:T(8,128)(2,1)S(1)} %get-tuple-element.80), channel_id=1, source_target_pairs={{0,24},{1,25},{2,26},{3,27},{4,28},{5,29},{6,30},{7,31},{8,0},{9,1... | collective-permute-start | bytes 786440 | tf_op jit(solution)/shard_map/ppermute | solution.py:46
  618.1 34.4 %collective-permute-start.66 = (bf16[64,2048]{1,0:T(8,128)(2,1)S(1)}, bf16[64,2048]{1,0:T(8,128)(2,1)S(1)}, u32[]{:S(2)}, u32[]{:S(2)}) collective-permute-start(bf16[64,2048]{1,0:T(8,128)(2,1)S(1)} %get-tuple-element.82), channel_id=1, source_target_pairs={{0,8},{1,9},{2,10},{3,11},{4,12},{5,13},{6,14},{7,15},{8,16},{9,17... | collective-permute-start | bytes 786440 | tf_op jit(solution)/shard_map/ppermute | solution.py:46
  618.3 42.8 %collective-permute-start.67 = (bf16[64,2048]{1,0:T(8,128)(2,1)S(1)}, bf16[64,2048]{1,0:T(8,128)(2,1)S(1)}, u32[]{:S(2)}, u32[]{:S(2)}) collective-permute-start(bf16[64,2048]{1,0:T(8,128)(2,1)S(1)} %get-tuple-element.84), channel_id=1, source_target_pairs={{0,16},{1,17},{2,18},{3,19},{4,20},{5,21},{6,22},{7,23},{8,24},{9,... | collective-permute-start | bytes 786440 | tf_op jit(solution)/shard_map/ppermute | solution.py:46
  631.8 29.4 %collective-permute-start.68 = (bf16[64,2048]{1,0:T(8,128)(2,1)S(1)}, bf16[64,2048]{1,0:T(8,128)(2,1)S(1)}, u32[]{:S(2)}, u32[]{:S(2)}) collective-permute-start(bf16[64,2048]{1,0:T(8,128)(2,1)S(1)} %get-tuple-element.83), channel_id=1, source_target_pairs={{0,24},{1,25},{2,26},{3,27},{4,28},{5,29},{6,30},{7,31},{8,0},{9,1... | collective-permute-start | bytes 786440 | tf_op jit(solution)/shard_map/ppermute | solution.py:46
  649.9 13.8 %collective-permute-start.55 = (bf16[64,1536]{1,0:T(8,128)(2,1)S(1)}, bf16[64,1536]{1,0:T(8,128)(2,1)S(1)}, u32[]{:S(2)}, u32[]{:S(2)}) collective-permute-start(bf16[64,1536]{1,0:T(8,128)(2,1)S(1)} %fusion.23), channel_id=1, source_target_pairs={{0,1},{1,0},{2,3},{3,2},{4,5},{5,4},{6,7},{7,6},{8,9},{9,8},{10,11... | collective-permute-start | bytes 589832 | tf_op jit(solution)/shard_map/ppermute | solution.py:53
  652.4 12.3 %collective-permute-start.76 = (bf16[256,512]{1,0:T(8,128)(2,1)S(1)}, bf16[256,512]{1,0:T(8,128)(2,1)S(1)}, u32[]{:S(2)}, u32[]{:S(2)}) collective-permute-start(bf16[256,512]{1,0:T(8,128)(2,1)S(1)} %fusion.13), channel_id=1, source_target_pairs={{0,1},{1,0},{2,3},{3,2},{4,5},{5,4},{6,7},{7,6},{8,9},{9,8},{10,11... | collective-permute-start | bytes 786440 | tf_op jit(solution)/shard_map/ppermute | solution.py:53
  (56 other events, 792.8 us)

commit v2 on v1

v2 whole, which is shorter than its diff:
```python
import functools
import math

import jax
import jax.numpy as jnp
import numpy as np
from jax import lax
from jax.experimental import pallas as pl
from jax.experimental.pallas import tpu as pltpu
from jax.sharding import PartitionSpec as P

H = 16
HD = 64
TF = 128
EPS = 1e-05
MASKED = -1e30
F32 = jnp.float32
BF16 = jnp.bfloat16
AXES = ("dp", "blk")
LANES = 128
ROWS = 256
VMEM_LIMIT = 58 << 20
ANY = pl.BlockSpec(memory_space=pl.ANY)


class Grid:
    def __init__(self, groups, blocks):
        self.groups, self.blocks = groups, blocks
        self.n0, self.n = {8: (2, 2), 16: (4, 2), 32: (2, 4), 64: (4, 4)}[groups]
        self.chunks = self.n * self.n

    def coords(self, d):
        return d // self.chunks, d // self.n % self.n, d % self.n

    def join(self, z, a, b):
        return (z * self.n + a) * self.n + b

    def shift(self, v, phase, k):
        pairs = []
        for d in range(self.groups):
            for b in range(self.blocks):
                at = list(self.coords(d))
                axis = 0 if phase == 0 else (3 - phase if b % 2 == 0 else phase)
                at[axis] = (at[axis] - k) % self.n if axis else at[axis] ^ k
                pairs.append((d * self.blocks + b, self.join(*at) * self.blocks + b))
        return lax.ppermute(v, AXES, pairs)

    def swap(self, v):
        pairs = []
        for d in range(self.groups):
            for b in range(self.blocks):
                pairs.append((d * self.blocks + b, d * self.blocks + (b ^ 1)))
        return lax.ppermute(v, AXES, pairs)

    def places(self):
        table = []
        for d in range(self.groups):
            _, a, b = self.coords(d)
            for core in [c % 2 for c in range(self.blocks)]:
                row = []
                for c in (core, 1 - core):
                    for k2 in range(self.n):
                        for k1 in range(self.n):
                            k = (k2, k1) if c == 0 else (k1, k2)
                            row += [(a + k[0]) % self.n, (b + k[1]) % self.n, c]
                table.append(row)
        return np.array(table, np.int32)

def tie(x, *after):
    return lax.optimization_barrier((x, after))[0] if after else x


def dot(a, b, ca=1, cb=0):
    return lax.dot_general(a, b, (((ca,), (cb,)), ((), ())), preferred_element_type=F32)


def spec(shape, index):
    return pl.BlockSpec(shape, index)


def whole(shape):
    return pl.BlockSpec(shape, lambda *_: (0,) * len(shape))


SCALARS = pl.BlockSpec(memory_space=pltpu.SMEM)


def call(kernel, name, grid, ins, outs, shapes, scratch, flops, moved, prefetch=0):
    return pl.pallas_call(
        kernel,
        grid_spec=pltpu.PrefetchScalarGridSpec(
            num_scalar_prefetch=prefetch, grid=grid, in_specs=ins, out_specs=outs, scratch_shapes=scratch
        ),
        out_shape=[jax.ShapeDtypeStruct(s, t) for s, t in shapes],
        compiler_params=pltpu.CompilerParams(vmem_limit_bytes=VMEM_LIMIT),
        cost_estimate=pl.CostEstimate(flops=flops, bytes_accessed=moved, transcendentals=0),
        name=name,
    )


def fetch(place, pieces, span, matrix, sem, half, start, size, z=None):
    count, (lead, width) = len(pieces) // 2, span
    zs = slice(None) if z is None else z

    def go(base):
        for i in range(base, base + count):
            pltpu.make_async_copy(
                pieces[i].at[zs, :, pl.ds(lead + start, size)],
                matrix.at[zs, place[3 * i], place[3 * i + 1], :, pl.ds(half * width + start, size)],
                sem,
            ).start()

    pl.when(place[2] == half)(lambda: go(0))
    pl.when(place[2] != half)(lambda: go(count))


def arrived(matrix, sem, start, size, z=None):
    zs = slice(None) if z is None else z
    block = matrix.at[zs, :, :, :, pl.ds(start, size)]
    pltpu.make_async_copy(block, block, sem).wait()


def matrix_shape(grid, weight):
    (piece, *_), (_, width) = weight
    return (piece.shape[0], grid.n, grid.n, piece.shape[1], 2 * width)


def columns(matrix, start, size):
    block = matrix[:, :, :, :, pl.ds(start, size)]
    return block.reshape(-1, size)


def normalized(x):
    centre = x - jnp.mean(x, axis=-1, keepdims=True)
    inverse = lax.rsqrt(jnp.mean(centre * centre, axis=-1, keepdims=True) + EPS)
    return centre * inverse, inverse


def turned(x, cosine, sine):
    lane = lax.broadcasted_iota(jnp.int32, (1, LANES), 1)
    swapped = jnp.where(lane % HD < HD // 2, pltpu.roll(x, LANES - HD // 2, 1), pltpu.roll(x, HD // 2, 1))
    return x * cosine + swapped * sine


def start_blocks(place, pieces, span, matrix, sems, block, first=0):
    per = span[1] // block
    for half in range(2):
        for j in range(per):
            fetch(place, pieces, span, matrix, sems.at[first + half * per + j], half, j * block, block)


def rolled_kernel(place, *refs):
    k, out = 0, refs[-1]
    for part in refs[:-1]:
        for i in range(part.shape[0]):
            out[place[0] ^ k] = part[i]
            k += 1


def rolled(parts, index):
    shape = (sum(p.shape[0] for p in parts),) + parts[0].shape[1:]
    if shape[0] == 1:
        return parts[0]
    return call(
        rolled_kernel, "rolled", (1,), [SCALARS] + [whole(p.shape) for p in parts], [whole(shape)],
        [(shape, parts[0].dtype)], [], 0, 4 * math.prod(shape),
    )(index.astype(jnp.int32)[None], *parts)[0]


def qkv_kernel(count, span, first, place, *refs):
    if first:
        x, gain, bias, cosine, sine = refs[:5]
        pieces = refs[5 : 5 + count]
        normed, normed_t, packed, matrix, sems = refs[5 + count :]
    else:
        normed, cosine, sine = refs[:3]
        pieces = refs[3 : 3 + count]
        packed, matrix, sems = refs[3 + count :]
    half = pl.program_id(0)
    width = packed.shape[1]
    part = width // 3
    rows = normed.shape[0]

    @pl.when(half == 0)
    def _():
        start_blocks(place, pieces, span, matrix, sems, width)
        if first:
            for r in range(0, rows, ROWS):
                hat, _ = normalized(x[r : r + ROWS, :].astype(F32))
                row = (hat * gain[...] + bias[...]).astype(BF16)
                normed[r : r + ROWS, :] = row
                normed_t[:, r : r + ROWS] = row.T

    start = pl.multiple_of(half * width, width)
    arrived(matrix, sems.at[half], start, width)
    weight = columns(matrix, start, width)
    for r in range(0, rows, ROWS):
        at = slice(r, r + ROWS)
        for t in range(3):
            result = dot(normed[at, :], weight[:, t * part : (t + 1) * part])
            for c in range(0, part, LANES):
                piece = result[:, c : c + LANES]
                if t < 2:
                    piece = turned(piece, cosine[at, :], sine[at, :])
                if t == 0:
                    piece = piece * HD ** (-0.5)
                packed[at, t * part + c : t * part + c + LANES] = piece.astype(BF16)


def qkv_product(grid, places, source, cosine, sine, weight):
    first = len(source) == 3
    rows, width = source[0].shape
    pieces, span = weight
    part = span[1]
    outs, shapes = [spec((rows, part), lambda j: (0, j))], [((rows, 2 * part), BF16)]
    if first:
        outs = [whole((rows, width)), whole((width, rows))] + outs
        shapes = [((rows, width), BF16), ((width, rows), BF16)] + shapes
    return call(
        functools.partial(qkv_kernel, len(pieces), span, first), "qkv", (2,),
        [SCALARS] + [whole(v.shape) for v in source] + [whole((rows, LANES))] * 2 + [ANY] * len(pieces),
        outs, shapes,
        [pltpu.VMEM(matrix_shape(grid, weight), BF16), pltpu.SemaphoreType.DMA((2,))],
        4 * rows * width * part, 4 * width * part + 6 * rows * width + 4 * rows * part,
    )(places, *source, cosine, sine, *pieces)


def attend_kernel(step, q, kv, mask, mixed, lse):
    lane = lax.broadcasted_iota(jnp.int32, (1, LANES), 1)
    zero = jnp.zeros((), BF16)
    mine = [lane < HD, lane >= HD]
    part = q.shape[1] // 3
    away = mask[...]

    lse[...] = jnp.zeros_like(lse)
    for c in range(0, part, LANES):
        keys = [jnp.where(m, kv[:, part + c : part + c + LANES], zero) for m in mine]
        values = [jnp.where(m, kv[:, 2 * part + c : 2 * part + c + LANES], zero) for m in mine]

        def body(i, _):
            rows = pl.ds(pl.multiple_of(i * step, step), step)
            queries, kept = q[rows, c : c + LANES], lse[rows, :]
            out = None
            for h in range(2):
                scores = dot(queries, keys[h], 1, 1) + away
                top = jnp.max(scores, axis=-1, keepdims=True)
                weights = jnp.exp(scores - top)
                total = jnp.sum(weights, axis=-1, keepdims=True)
                product = dot(weights.astype(BF16), values[h]) * (1.0 / total)
                out = product if out is None else out + product
                kept = jnp.where(lane == c // HD + h, top + jnp.log(total), kept)
            lse[rows, :] = kept
            mixed[rows, c : c + LANES] = out.astype(BF16)
            return 0

        lax.fori_loop(0, q.shape[0] // step, body, 0)


def attend(half, q, kv, mask):
    rows, width, places = q.shape[0], q.shape[1] // 6, kv.shape[0]
    part = lambda v: spec((v.shape[0], 3 * width), lambda p: (0, half))
    return call(
        functools.partial(attend_kernel, min(rows, 512)), "attend", (1,),
        [part(q), part(kv), whole((1, places))],
        [whole((rows, width)), whole((rows, LANES))],
        [((rows, width), BF16), ((rows, LANES), F32)], [],
        16 * rows * places * width, 8 * rows * width,
    )(q, kv, mask)


def thirds(x):
    a = x.astype(BF16)
    rest = x - a.astype(F32)
    b = rest.astype(BF16)
    return a, b, (rest - b.astype(F32)).astype(BF16)


def attend_back_kernel(step, q, kv, mixed, grad, lse, mask, cosine, sine, *refs):
    merged = len(refs) == 3
    if merged:
        out, key_sum, value_sum = refs
        key_cos, key_sin = cosine, sine
        out_q = out_kv = out
    else:
        key_cos, key_sin, out_q, out_kv, key_sum, value_sum = refs
    part = q.shape[1] // 3
    before = part if merged else 0
    lane = lax.broadcasted_iota(jnp.int32, (1, LANES), 1)
    zero, one = jnp.zeros((), BF16), jnp.ones((), BF16)
    mine = [lane < HD, lane >= HD]
    spare = [HD, 0]
    for c in range(0, part, LANES):
        k, v = kv[:, part + c : part + c + LANES], kv[:, 2 * part + c : 2 * part + c + LANES]
        keys, keys_more, values_more = [], [], []
        for h in range(2):
            ones = (lane >= spare[h]) & (lane < spare[h] + 3)
            own = jnp.where(mine[h], k, zero)
            keys.append(own)
            keys_more.append(jnp.where(ones, one, jnp.where(lane == spare[h] + 3, mask[...], own)))
            values_more.append(jnp.where(ones, one, jnp.where(mine[h], v, zero)))
        key_sum[...] = jnp.zeros_like(key_sum)
        value_sum[...] = jnp.zeros_like(value_sum)

        def body(i, _):
            rows = pl.ds(pl.multiple_of(i * step, step), step)
            queries, grads = q[rows, c : c + LANES], grad[rows, c : c + LANES]
            kept = lse[rows, :]
            product = grads.astype(F32) * mixed[rows, c : c + LANES].astype(F32)
            total = None
            for h in range(2):
                delta = jnp.sum(jnp.where(mine[h], product, 0.0), axis=-1, keepdims=True)
                head = c // HD + h
                log_sum = jnp.sum(jnp.where(lane == head, kept, 0.0), axis=-1, keepdims=True)
                own_q = jnp.where(mine[h], queries, zero)
                own_g = jnp.where(mine[h], grads, zero)
                more_q = jnp.where(lane == spare[h] + 3, one, own_q)
                more_g = own_g
                for t, (a, b) in enumerate(zip(thirds(-log_sum), thirds(-delta))):
                    more_q = jnp.where(lane == spare[h] + t, a, more_q)
                    more_g = jnp.where(lane == spare[h] + t, b, more_g)
                probs = jnp.exp(dot(keys_more[h], more_q, 1, 1))
                grad_scores = (probs * dot(values_more[h], more_g, 1, 1)).astype(BF16)
                value_sum[...] += dot(probs.astype(BF16), own_g)
                key_sum[...] += dot(grad_scores, own_q)
                product_q = dot(keys[h], grad_scores, 0, 0)
                total = product_q if total is None else total + product_q
            grad_q = turned(total.T, cosine[rows, :], -sine[rows, :]) * HD ** (-0.5)
            out_q[rows, c : c + LANES] = grad_q.astype(BF16)
            return 0

        lax.fori_loop(0, q.shape[0] // step, body, 0)
        out_kv[:, before + c : before + c + LANES] = turned(key_sum[...], key_cos[...], -key_sin[...]).astype(BF16)
        out_kv[:, before + part + c : before + part + c + LANES] = value_sum[...].astype(BF16)


def attend_back(group, half, q, kv, mixed, grad, lse, mask, tables, key_tables):
    rows, width, places = q.shape[0], q.shape[1] // 6, kv.shape[0]
    merged = kv is q
    more = [] if merged else list(key_tables)
    column = lambda n, w, at: spec((n, w), lambda p: (0, at))
    if merged:
        shapes = [((rows, 3 * width), BF16)]
    else:
        shapes = [((rows, width), BF16), ((places, 2 * width), BF16)]
    return call(
        functools.partial(attend_back_kernel, min(rows, 512)), "attend_back", (1,),
        [column(rows, 3 * width, half), column(places, 3 * width, half), whole((rows, width)),
         column(rows, width, 2 * group + half), whole((rows, LANES)), whole((places, 1))]
        + [whole((rows, LANES))] * 2 + [whole((places, LANES))] * len(more),
        [whole(s) for s, _ in shapes], shapes, [pltpu.VMEM((places, LANES), F32)] * 2,
        40 * rows * places * width, 16 * rows * width,
    )(q, kv, mixed, grad, lse, mask, *tables, *more)


def out_kernel(count, span, block, place, x, gain, bias, *refs):
    pieces, mixed = refs[:count], refs[count:-7]
    middle, normed, normed_t, matrix, taken, total, sems = refs[-7:]
    j, steps = pl.program_id(0), pl.num_programs(0)

    @pl.when(j == 0)
    def _():
        start_blocks(place, pieces, span, matrix, sems, block)
        part = mixed[0].shape[1]
        for i, v in enumerate(mixed):
            taken[:, i * part : (i + 1) * part] = v[...]

    start = pl.multiple_of(j * block, block)
    arrived(matrix, sems.at[j], start, block)
    total[:, pl.ds(start, block)] = dot(taken[...], columns(matrix, start, block))

    @pl.when(j == steps - 1)
    def _():
        for r in range(0, x.shape[0], ROWS):
            rows = slice(r, r + ROWS)
            row = x[rows, :].astype(F32) + total[rows, :]
            middle[rows, :] = row.astype(BF16)
            hat, _ = normalized(row)
            row = (hat * gain[...] + bias[...]).astype(BF16)
            normed[rows, :] = row
            normed_t[:, rows] = row.T


def out_product(grid, places, mixed, x, gain, bias, weight, block=512):
    rows, width = x.shape
    pieces, span = weight
    block = min(block, span[1])
    size = rows * width
    return call(
        functools.partial(out_kernel, len(pieces), span, block), "out", (width // block,),
        [SCALARS, whole(x.shape), whole((1, width)), whole((1, width))] + [ANY] * len(pieces)
        + [whole(v.shape) for v in mixed],
        [whole(x.shape), whole(x.shape), whole((width, rows))], [(x.shape, BF16)] * 2 + [((width, rows), BF16)],
        [pltpu.VMEM(matrix_shape(grid, weight), BF16), pltpu.VMEM(x.shape, BF16), pltpu.VMEM(x.shape, F32),
         pltpu.SemaphoreType.DMA((width // block,))],
        2 * size * width, 2 * width * width + 8 * size,
    )(places, x, gain, bias, *pieces, *mixed)


def up_kernel(count, span, block, place, normed, *refs):
    pieces = refs[:count]
    active, slope, matrix, sems = refs[count:]
    j = pl.program_id(0)

    @pl.when(j == 0)
    def _():
        start_blocks(place, pieces, span, matrix, sems, block)

    start = pl.multiple_of(j * block, block)
    arrived(matrix, sems.at[j], start, block)
    weight = columns(matrix, start, block)
    root = math.sqrt(2.0 / math.pi)
    for r in range(0, normed.shape[0], ROWS):
        rows = slice(r, r + ROWS)
        h = dot(normed[rows, :], weight)
        square = h * h
        t = jnp.tanh(h * (root + (root * 0.044715) * square))
        half = 0.5 + 0.5 * t
        active[rows, :] = (h * half).astype(BF16)
        slope[rows, :] = (
            half + (h * half) * (1.0 - t) * (root + (3.0 * 0.044715 * root) * square)
        ).astype(BF16)


def up_product(grid, places, normed, weight, block=512):
    rows, width = normed.shape
    pieces, span = weight
    full = 2 * span[1]
    out = spec((rows, block), lambda j: (0, j))
    return call(
        functools.partial(up_kernel, len(pieces), span, block), "up", (full // block,),
        [SCALARS, whole(normed.shape)] + [ANY] * len(pieces),
        [out, out], [((rows, full), BF16)] * 2,
        [pltpu.VMEM(matrix_shape(grid, weight), BF16), pltpu.SemaphoreType.DMA((full // block,))],
        2 * rows * width * full, 2 * width * full + 4 * rows * full,
    )(places, normed, *pieces)


def start_levels(place, pieces, span, matrix, sems):
    for z in range(pieces[0].shape[0]):
        for half in range(2):
            fetch(place, pieces, span, matrix, sems.at[z], half, 0, span[1], z)


def down_kernel(count, span, place, active, middle, *refs):
    pieces = refs[:count]
    out, matrix, total, sems = refs[count:]
    z, steps = pl.program_id(0), pl.num_programs(0)

    @pl.when(z == 0)
    def _():
        start_levels(place, pieces, span, matrix, sems)
        total[...] = middle[...].astype(F32)

    width = matrix.shape[-1]
    arrived(matrix, sems.at[z], 0, width, z)
    total[...] += dot(active[...], matrix[z].reshape(-1, width))

    @pl.when(z == steps - 1)
    def _():
        out[...] = total[...].astype(BF16)


def down_product(grid, places, side, active, middle, weight):
    rows, full = active.shape
    pieces, span = weight
    half = (rows // 2, middle.shape[1])
    part = full // grid.n0
    return call(
        functools.partial(down_kernel, len(pieces), span), "down", (grid.n0,),
        [SCALARS, spec((rows // 2, part), lambda z: (side, z)), spec(half, lambda z: (side, 0))] + [ANY] * len(pieces),
        [whole(half)], [(half, BF16)],
        [pltpu.VMEM(matrix_shape(grid, weight), BF16), pltpu.VMEM(half, F32), pltpu.SemaphoreType.DMA((grid.n0,))],
        half[0] * half[1] * full * 2, 2 * half[1] * full + 2 * half[0] * full,
    )(places, active, middle, *pieces)[0]


def hidden_back_kernel(count, span, place, grad, slope, *refs):
    pieces = refs[:count]
    out, matrix, sems = refs[count:]
    z = pl.program_id(0)

    @pl.when(z == 0)
    def _():
        start_levels(place, pieces, span, matrix, sems)

    width = matrix.shape[-1]
    arrived(matrix, sems.at[z], 0, width, z)
    weight = matrix[z].reshape(-1, width)
    for r in range(0, grad.shape[0], ROWS):
        rows = slice(r, r + ROWS)
        out[rows, :] = (dot(grad[rows, :], weight, 1, 1) * slope[rows, :].astype(F32)).astype(BF16)


def hidden_back(grid, places, grad, slope, weight):
    rows, full = slope.shape
    pieces, span = weight
    width = grad.shape[1]
    part = spec((rows, full // grid.n0), lambda z: (0, z))
    return call(
        functools.partial(hidden_back_kernel, len(pieces), span), "hidden_back", (grid.n0,),
        [SCALARS, whole(grad.shape), part] + [ANY] * len(pieces),
        [part], [(slope.shape, BF16)],
        [pltpu.VMEM(matrix_shape(grid, weight), BF16), pltpu.SemaphoreType.DMA((grid.n0,))],
        2 * rows * width * full, 2 * width * full + 4 * rows * full,
    )(places, grad, slope, *pieces)[0]


def norm_back_kernel(spans, starts, count, count_outs, place, x, gain, base, *refs):
    pieces, grads, outs = refs[: count * len(spans)], refs[count * len(spans) : -6 - count_outs], refs[-6 - count_outs :]
    *outs, sums, matrix, taken, total, sems, grad_sems = outs
    block = taken.shape[-1]
    full = matrix.shape[-1] // len(spans)

    def grad_copy(i):
        which, start = starts[i]
        return pltpu.make_async_copy(grads[which].at[:, pl.ds(start, block)], taken.at[i], grad_sems.at[i])

    for i in range(len(starts)):
        grad_copy(i).start()
        if i * block % full == 0:
            which = i * block // full
            part = matrix.at[:, :, :, :, pl.ds(which * full, full)]
            start_blocks(place, pieces[count * which : count * (which + 1)], spans[which], part, sems, block, i)
    for i in range(len(starts)):
        grad_copy(i).wait()
        arrived(matrix, sems.at[i], i * block, block)
        product = dot(taken[i], columns(matrix, i * block, block), 1, 1)
        total[...] = product if i == 0 else total[...] + product
    added = [jnp.zeros((1, x.shape[1]), F32)] * 2
    each = x.shape[0] // count_outs
    for r in range(0, x.shape[0], min(ROWS, each)):
        rows = slice(r, r + min(ROWS, each))
        hat, inverse = normalized(x[rows, :].astype(F32))
        back = total[rows, :]
        added[0] = added[0] + jnp.sum(back * hat, axis=0, keepdims=True)
        added[1] = added[1] + jnp.sum(back, axis=0, keepdims=True)
        inner = back * gain[...]
        mean = jnp.mean(inner, axis=-1, keepdims=True)
        lean = jnp.mean(inner * hat, axis=-1, keepdims=True)
        result = (base[rows, :].astype(F32) + inverse * (inner - mean - hat * lean)).astype(BF16)
        outs[r // each][r % each : r % each + result.shape[0], :] = result
    sums[...] = jnp.concatenate(added, axis=0)


def norm_back(grid, places, grads, x, gain, base, weights, block, outs=1):
    rows, width = x.shape
    starts = [(i, s) for i, g in enumerate(grads) for s in range(0, g.shape[1], block)]
    *outer, cols = matrix_shape(grid, weights[0])
    full = cols * len(weights)
    count = len(weights[0][0])
    return call(
        functools.partial(norm_back_kernel, [w[1] for w in weights], starts, count, outs), "norm_back", (1,),
        [SCALARS, whole(x.shape), whole((1, width)), whole(x.shape)] + [ANY] * (len(weights) * count + len(grads)),
        [whole((rows // outs, width))] * outs + [whole((2, width))],
        [((rows // outs, width), BF16)] * outs + [((2, width), F32)],
        [pltpu.VMEM((*outer, full), BF16), pltpu.VMEM((len(starts), rows, block), BF16),
         pltpu.VMEM(x.shape, F32), pltpu.SemaphoreType.DMA((len(starts),)), pltpu.SemaphoreType.DMA((len(starts),))],
        2 * rows * width * full, 2 * width * full + 2 * rows * full + 6 * rows * width,
    )(places, x, gain, base, *[v for w in weights for v in w[0]], *grads)


def heads_back_kernel(count, span, block, place, grad, *refs):
    pieces = refs[:count]
    out, matrix, total, sems = refs[count:]
    j, steps = pl.program_id(0), pl.num_programs(0)

    @pl.when(j == 0)
    def _():
        start_blocks(place, pieces, span, matrix, sems, block)
        total[...] = jnp.zeros_like(total)

    start = pl.multiple_of(j * block, block)
    arrived(matrix, sems.at[j], start, block)
    total[...] += dot(grad[...], columns(matrix, start, block), 1, 1)

    @pl.when(j == steps - 1)
    def _():
        out[...] = total[...].astype(BF16)


def heads_back(grid, places, grad, weight, block=512):
    rows, width = grad.shape
    pieces, span = weight
    block = min(block, span[1])
    return call(
        functools.partial(heads_back_kernel, len(pieces), span, block), "heads_back", (width // block,),
        [SCALARS, spec((rows, block), lambda j: (0, j))] + [ANY] * len(pieces),
        [whole(grad.shape)], [(grad.shape, BF16)],
        [pltpu.VMEM(matrix_shape(grid, weight), BF16), pltpu.VMEM(grad.shape, F32),
         pltpu.SemaphoreType.DMA((width // block,))],
        2 * rows * width * width, 2 * width * width + 4 * rows * width,
    )(places, grad, *pieces)[0]


def spread(place, result, outs, came, kept, lead=0):
    size = result.shape[-1]
    to = slice(lead, lead + size)
    chunks = len(outs) if kept else outs[0].shape[0]
    for i in range(chunks):
        at = 3 * (i if kept else chunks + i)
        part = result[:, place[at], place[at + 1]]
        if came is not None:
            part = part + came[i, :, :, to].astype(F32)
        if kept:
            outs[i][:, :, to] = part.astype(BF16)
        else:
            outs[0][i, :, :, to] = part.astype(BF16)


def chunk_outputs(grid, kept, part, full, block, index):
    if kept:
        out, shape = spec((grid.n0, part, block), lambda *a: (0, 0, index(*a))), (grid.n0, part, full)
        return [out] * grid.chunks, [(shape, BF16)] * grid.chunks
    shape = (grid.chunks, grid.n0, part, full)
    return [spec(shape[:-1] + (block,), lambda *a: (0, 0, 0, index(*a)))], [(shape, BF16)]


def row_chunks_kernel(kept, fused, place, a, b, *refs):
    came, outs, result = (refs[0], refs[1:-1], refs[-1]) if fused else (None, refs[:-1], refs[-1])
    result[...] = dot(a[...], b[...]).reshape(result.shape)
    spread(place, result, outs, came, kept)


def row_chunks(grid, places, kept, a, b, came=None, block=512):
    width, rows = a.shape
    full = b.shape[1] // 2
    per = full // block
    part = width // grid.groups
    outs, shapes = chunk_outputs(grid, kept, part, full, block, lambda j, place: j)
    more, extra = [], []
    if came is not None:
        more, extra = [spec(came.shape[:-1] + (block,), lambda j, place: (0, 0, 0, j))], [came]
    return call(
        functools.partial(row_chunks_kernel, kept, came is not None), "row_chunks", (per,),
        [whole(a.shape), spec((rows, block), lambda j, place: (0, (place[2] if kept else 1 - place[2]) * per + j))]
        + more,
        outs, shapes, [pltpu.VMEM((grid.n0, grid.n, grid.n, part, block), F32)],
        2 * rows * width * full, 2 * width * full + 2 * rows * (full + width), prefetch=1,
    )(places, a, b, *extra)


def heads_chunks_kernel(kept, more, fused, place, a, *refs):
    halves, refs = refs[:2], list(refs[2:])
    came = refs.pop(0) if fused else None
    if more:
        mixed, grad, refs, (result, last, turned_mixed) = refs[:more], refs[more], refs[more + 1 : -3], refs[-3:]
        part = mixed[0].shape[1]
        for i, v in enumerate(mixed):
            turned_mixed[i * part : (i + 1) * part, :] = v[...].T
    else:
        *refs, result = refs
    mine = place[2] if kept else 1 - place[2]

    def products(h):
        result[...] = dot(a[...], halves[h][...]).reshape(result.shape)
        if more:
            width = last.shape[-1]
            last[...] = dot(turned_mixed[...], grad[:, h * width : (h + 1) * width]).reshape(last.shape)

    for h in range(2):
        pl.when(mine == h)(functools.partial(products, h))
    spread(place, result, refs, came, kept)
    if more:
        spread(place, last, refs, came, kept, result.shape[-1])


def heads_chunks(grid, places, kept, a, halves, mixed=(), grad=None, came=None):
    width, rows = a.shape
    block, more = halves[0].shape[1], len(mixed)
    part = width // grid.groups
    full = block + (width // 2 if more else 0)
    outs, shapes = chunk_outputs(grid, kept, part, full, full, lambda j, place: 0)
    level = (grid.n0, grid.n, grid.n, part)
    scratch = [pltpu.VMEM(level + (block,), F32)]
    extra = [] if came is None else [came]
    if more:
        extra += [*mixed, grad]
        scratch += [pltpu.VMEM(level + (width // 2,), F32), pltpu.VMEM((width, rows), BF16)]
    return call(
        functools.partial(heads_chunks_kernel, kept, more, came is not None), "heads_chunks", (1,),
        [whole(v.shape) for v in (a, *halves, *extra)], outs, shapes, scratch,
        2 * rows * width * full, 2 * width * full + 2 * rows * (full + width), prefetch=1,
    )(places, a, *halves, *extra)


def wide_chunks_kernel(n0, kept, fused, place, *refs):
    parts, b = refs[:n0], refs[n0]
    came, outs = (refs[n0 + 1], refs[n0 + 2 :]) if fused else (None, refs[n0 + 1 :])
    j = pl.program_id(0)

    def put(out):
        for z, part in enumerate(parts):
            result = dot(part[...], b[...], 0, 0)
            if fused:
                result = result + came[0, z].astype(F32)
            out[z] = result.astype(BF16)

    if kept:
        for i, out in enumerate(outs):
            pl.when(j == i)(functools.partial(put, out))
    else:
        put(outs[0].at[0])


def wide_chunks(grid, places, kept, a, b, came=None):
    rows, full = a.shape
    width = b.shape[1]
    chunks, part, n = grid.chunks, full // grid.groups, grid.n
    base = 0 if kept else chunks

    def a_spec(z):
        return spec((rows, part), lambda j, at: (0, (z * n + at[3 * (base + j)]) * n + at[3 * (base + j) + 1]))

    shape = (grid.n0, part, width // 2)
    by_chunk = spec((1,) + shape, lambda j, at: (j, 0, 0, 0))
    extra = [] if came is None else [came]
    if kept:
        outs, shapes = [whole(shape)] * chunks, [(shape, BF16)] * chunks
    else:
        outs, shapes = [by_chunk], [((chunks,) + shape, BF16)]
    return call(
        functools.partial(wide_chunks_kernel, grid.n0, kept, came is not None), "wide_chunks", (chunks,),
        [a_spec(z) for z in range(grid.n0)]
        + [spec((rows, width // 2), lambda j, at: (0, at[3 * base + 2]))] + [by_chunk] * len(extra),
        outs, shapes, [],
        rows * width * full, width * full + 2 * rows * (full + width), prefetch=1,
    )(places, *([a] * grid.n0), b, *extra)


class Line:
    def __init__(self):
        self.now = ()

    def at(self, *values):
        values = tie(values, *self.now)
        return values[0] if len(values) == 1 else values

    def mark(self, *values):
        self.now = values


class Pull:
    def __init__(self, grid, line, mine):
        self.grid, self.line, self.mine = grid, line, mine[None]
        self.parts = [self.mine]
        self.place = grid.coords(lax.axis_index("dp"))[0]

    def outer(self):
        self.mine = self.line.at(self.mine)
        self.parts = [self.mine] + [self.grid.shift(self.mine, 0, k) for k in range(1, self.grid.n0)]
        return self.parts[1:]

    def outer_step(self):
        held = self.parts[0] if len(self.parts) == 1 else jnp.concatenate(self.line.at(self.parts))
        if held.shape[0] == self.grid.n0:
            return ()
        held = self.line.at(held)
        self.parts = [held, self.grid.shift(held, 0, held.shape[0])]
        return self.parts[1:]

    def inner(self):
        column = self.line.at(rolled(self.line.at(self.parts), self.place))
        self.level = [column] + [self.grid.shift(column, 1, k) for k in range(1, self.grid.n)]
        self.pieces, self.swapped = list(self.level), {}
        return self.level[1:]

    def last(self):
        level = self.line.at(self.level)
        for k in range(1, self.grid.n):
            self.pieces += [self.grid.shift(v, 2, k) for v in level]
        return self.pieces[self.grid.n :]

    def swap(self, *which):
        n, out = self.grid.n, []
        for kind in which:
            for i in range(n * n):
                if (i % n > 0) + 2 * (i // n > 0) == kind:
                    self.swapped[i] = self.grid.swap(self.line.at(self.pieces[i]))
                    out.append(self.swapped[i])
        return out

    def weight(self, lead=0, width=None):
        pieces = self.pieces + [self.swapped[i] for i in range(len(self.pieces))]
        return pieces, (lead, self.mine.shape[-1] if width is None else width)


def plus(*vs):
    return functools.reduce(lambda a, b: a + b, [v.astype(F32) for v in vs])


class Push:
    def __init__(self, grid, line, sent):
        self.grid, self.line = grid, line
        self.came, self.second_in, self.first_in = grid.swap(sent), {}, []

    def keep(self, chunks, fused):
        self.terms = [[v] if fused else [v, self.came[i]] for i, v in enumerate(chunks)]
        return chunks

    def second(self, others):
        n, out = self.grid.n, []
        for k2 in range(1, n):
            for k1 in range(1, n) if others else (0,):
                terms = self.line.at(self.terms[k2 * n + k1])
                value = terms[0] if len(terms) == 1 else plus(*terms).astype(BF16)
                self.second_in[k2, k1] = self.grid.shift(value, 2, -k2)
                out.append(self.second_in[k2, k1])
        return out

    def first(self):
        n = range(1, self.grid.n)
        for k in n:
            terms = self.line.at(self.terms[k] + [self.second_in[k2, k] for k2 in n])
            self.first_in.append(self.grid.shift(plus(*terms).astype(BF16), 1, -k))
        return self.first_in

    def outer(self):
        seconds = [self.second_in[k, 0] for k in range(1, self.grid.n)]
        total = plus(*self.line.at(self.terms[0] + seconds + self.first_in)).astype(BF16)
        z = self.grid.coords(lax.axis_index("dp"))[0]
        size = self.grid.n0 // 2
        total = total.reshape((2, size) + total.shape[1:])
        pick = lambda v, i: lax.dynamic_index_in_dim(v, i, 0, keepdims=False)
        here, there = pick(total, z // size), pick(total, 1 - z // size)
        self.on, self.mine = 1 - z % size, z % size
        if size == 1:
            self.own, self.far = [here[0]], [self.grid.shift(there[0], 0, 1)]
            return self.far
        self.own = [pick(here, self.mine)]
        self.onward, self.rest = pick(here, self.on), pick(there, self.mine)
        self.far_on = self.grid.shift(pick(there, self.on), 0, size)
        self.far = []
        return [self.far_on, self.rest]

    def outer_rest(self):
        if self.grid.n0 == 2:
            return ()
        rest, onward = self.line.at(self.rest, [self.onward, self.far_on])
        self.far = [self.grid.shift(rest, 0, 2), self.grid.shift(plus(*onward).astype(BF16), 0, 1)]
        return self.far

    def own_half(self):
        self.own = over_ranks(self.grid, plus(*self.line.at(self.own + self.far))).astype(BF16)
        self.other = self.grid.swap(self.own)
        return self.other

    def result(self, core, lead=0, width=None):
        own, other = [v.astype(F32)[:, lead : None if width is None else lead + width] for v in (self.own, self.other)]
        return jnp.where(core == 0, jnp.concatenate([own, other], axis=1), jnp.concatenate([other, own], axis=1))


def rank_groups(grid):
    return [[b for b in range(grid.blocks) if b % 2 == c] for c in range(2)]


def over_ranks(grid, v):
    if grid.blocks == 2:
        return v
    return lax.psum(v.astype(BF16), "blk", axis_index_groups=rank_groups(grid)).astype(F32)


def doubled(grid, v, bit):
    pairs = [
        (d * grid.blocks + c, (d ^ bit) * grid.blocks + c) for d in range(grid.groups) for c in range(grid.blocks)
    ]
    return lax.ppermute(v, AXES, pairs)


def time_features(time_steps, index):
    half = TF // 2
    frequency = jnp.exp((index % half).astype(F32) * (-math.log(10000.0) / half))
    angles = time_steps.astype(F32)[:, None] * frequency[None, :]
    return jnp.where(index[None, :] < half, jnp.sin(angles), jnp.cos(angles))


def rotary_tables(length):
    half = HD // 2
    inverse = np.exp(np.arange(half) * (-2.0 * math.log(10000.0) / HD)).astype(np.float32)
    angles = np.arange(length, dtype=np.float32)[:, None] * inverse[None, :]
    cosine, sine = np.cos(angles.astype(np.float64)), np.sin(angles.astype(np.float64))
    return np.tile(cosine, (1, 4)).astype(np.float32), np.tile(np.concatenate([-sine, sine], 1), (1, 2)).astype(np.float32)


def sums_kernel(first, second, gain1, gain2, scale1, scale2, time, out):
    out[0:1, :] = first[0:1, :] * scale1[...]
    out[1:2, :] = first[1:2, :]
    out[2:3, :] = second[0:1, :] * scale2[...]
    out[3:4, :] = second[1:2, :]
    out[4:5, :] = first[0:1, :] * gain1[...]
    out[5:6, :] = second[0:1, :] * gain2[...]
    out[6:7, :] = jnp.broadcast_to(time[...], (1, out.shape[1]))
    out[7:8, :] = jnp.zeros((1, out.shape[1]), F32)


def shards(
    tokens, lengths, time_index, qkv_weight, out_weight, up_weight, down_weight, time_weight,
    norm1_gain, norm1_bias, norm2_gain, norm2_bias, cotangent,
):
    grid = Grid(lax.axis_size("dp"), lax.axis_size("blk"))
    ranks = grid.blocks // 2
    _, block_len, width = tokens.shape
    block = lax.axis_index("blk")
    core, rank = block % 2, block // 2
    rows = 2 * block_len
    at = lax.dynamic_index_in_dim(
        jnp.asarray(grid.places()), lax.axis_index("dp") * grid.blocks + block, 0, keepdims=False
    )

    def swapped(v):
        return grid.swap(lax.dynamic_index_in_dim(v, 1 - core, 0, keepdims=False))

    def joined(v, theirs):
        return jnp.concatenate([lax.dynamic_index_in_dim(v, core, 0, keepdims=False), theirs], axis=0)

    def columns_of(v, start, size):
        return lax.dynamic_slice_in_dim(v, start, size, 1)

    line = Line()
    mine = []
    for g in range(2):
        parts = [columns_of(qkv_weight, (4 * t + 2 * g + core) * (width // 4), width // 4) for t in range(3)]
        mine.append(jnp.concatenate(parts, axis=1))
    heads_a = Pull(grid, line, mine[0])
    group_width = mine[0].shape[1]

    t_rows, t_cols = time_weight.shape
    group, per = lax.axis_index("dp"), width // grid.groups
    norms = jnp.stack([norm1_gain, norm1_bias, norm2_gain, norm2_bias]).reshape(-1, LANES)
    small = jnp.concatenate([time_weight, jnp.pad(norms, ((0, t_rows - norms.shape[0]), (0, 0)))], axis=1)[None]
    inner_bits = [1 << i for i in range((grid.chunks - 1).bit_length())]
    bits = [grid.chunks << i for i in range((grid.n0 - 1).bit_length())] + inner_bits
    reach = np.zeros((grid.groups,), np.int32)
    for i, bit in enumerate(bits):
        reach[1 << i : 2 << i] = reach[: 1 << i] ^ bit

    def small_step(v, bit):
        far = doubled(grid, v, bit)
        return jnp.concatenate([v, far]), far

    moved = heads_a.outer()
    small, far = small_step(small, bits[0])
    theirs = swapped(tokens)
    line.mark(moved, far, theirs)

    moved = heads_a.inner()
    out_weight, up_weight, down_weight = line.at(out_weight, up_weight, down_weight)
    for weight in (out_weight, up_weight, down_weight):
        half = weight.shape[1] // 2
        mine.append(columns_of(weight, core * half, half))
    heads_b = Pull(grid, line, jnp.concatenate(mine[1:3], axis=1))
    up_w, down_w = Pull(grid, line, mine[3]), Pull(grid, line, mine[4])
    more = heads_b.outer_step()
    small, far = small_step(line.at(small), bits[1])
    x = joined(*line.at(tokens, theirs))
    line.mark(moved, more, far, x)

    moved = heads_a.last()
    swaps = heads_a.swap(0, 1)
    later = heads_b.outer_step()
    small, far = small_step(line.at(small), bits[2])
    in_block = jnp.arange(block_len, dtype=jnp.int32)
    my_places = jnp.concatenate([core * block_len + in_block, (1 - core) * block_len + in_block])
    key_places = jnp.concatenate([r * rows + my_places for r in range(ranks)])
    full_tables = line.at([jnp.asarray(t) for t in rotary_tables(rows * ranks)])

    def table_of(t, r):
        return [lax.dynamic_slice_in_dim(t, r * rows + c * block_len, block_len, 0) for c in (core, 1 - core)]

    tables = [jnp.concatenate(table_of(t, rank)) for t in full_tables]
    key_tables = ()
    if ranks > 1:
        key_tables = [jnp.concatenate([v for r in range(ranks) for v in table_of(t, r)]) for t in full_tables]
    length = lax.dynamic_index_in_dim(line.at(lengths), core, 0, keepdims=False)
    mask = jnp.where(key_places < length, 0.0, MASKED).astype(F32)
    mask_column = mask[:, None].astype(BF16)
    line.mark(moved, swaps, far, tables, mask_column)

    swaps = heads_a.swap(2, 3)
    up_more = up_w.outer_step()
    for bit in bits[3:]:
        small, far = small_step(line.at(small), bit)
    my_time = lax.dynamic_slice_in_dim(time_index, core, 1, 0)
    index = jnp.arange(TF, dtype=jnp.int32)
    reach = jnp.asarray(reach)
    features = line.at(time_features(my_time, (group ^ reach[index // t_rows]) * t_rows + index % t_rows))
    line.mark(swaps, far, features, later)
    small = line.at(small)
    time_matrix = small[:, :, :t_cols].reshape(TF, t_cols).astype(F32)
    norms = small[:, : 4 * per // LANES, t_cols:].reshape(grid.groups, 4 * per).astype(F32)
    order = (group ^ reach)[:, None] == jnp.arange(grid.groups, dtype=jnp.int32)
    norms = lax.dot_general(
        order.astype(F32), norms, (((0,), (0,)), ((), ())), precision=lax.Precision.HIGHEST
    ).reshape(grid.groups, 4, per)
    norms = norms.transpose(1, 0, 2).reshape(4, 1, width)
    gain1, bias1, gain2, bias2 = norms[0], norms[1], norms[2], norms[3]
    scales = 1.0 + jnp.dot(features, time_matrix, precision=lax.Precision.HIGHEST)
    scale1, scale2 = scales[:, :width], scales[:, width:]
    eff1, eff2 = gain1 * scale1, gain2 * scale2
    moved = heads_b.inner()
    line.mark(eff1, eff2, bias1, bias2, up_more)

    def gathered(v):
        if ranks == 1:
            return v
        return lax.all_gather(v, "blk", axis=0, tiled=True, axis_index_groups=rank_groups(grid))

    later = up_w.outer_step()
    theirs = swapped(line.at(cotangent))
    normed1, normed1_t, packed_a = qkv_product(grid, at, line.at((x, eff1, bias1)), *tables, heads_a.weight())
    wide_a = gathered(packed_a)
    line.mark(packed_a, moved, theirs)

    moved = heads_b.last()
    swaps = heads_b.swap(0, 1)
    att = {}
    packed_a, mask = line.at(packed_a, mask)
    if ranks == 1:
        wide_a = packed_a
    att[0, 0] = attend(0, packed_a, wide_a, mask[None])
    line.mark(att[0, 0], moved, swaps)

    swaps = heads_b.swap(2, 3)
    more = down_w.outer_step()
    cot = joined(*line.at(cotangent, theirs))
    att[0, 1] = attend(1, packed_a, wide_a, line.at(mask)[None])
    line.mark(att[0, 1], swaps, cot, later, more)

    moved = up_w.inner()
    later = down_w.outer_step()
    (packed_b,) = qkv_product(grid, at, (line.at(normed1),), *tables, heads_b.weight(0, group_width))
    wide_b = gathered(packed_b)
    line.mark(packed_b, moved)

    moved = up_w.last()
    packed_b, mask = line.at(packed_b, mask)
    if ranks == 1:
        wide_b = packed_b
    att[1, 0] = attend(0, packed_b, wide_b, mask[None])
    line.mark(att[1, 0])

    swaps = up_w.swap(0, 1)
    att[1, 1] = attend(1, packed_b, wide_b, line.at(mask)[None])
    mixed = [att[i][0] for i in ((0, 0), (0, 1), (1, 0), (1, 1))]
    line.mark(att[1, 1], moved, swaps, later)

    swaps = up_w.swap(2, 3)
    moved = down_w.inner()
    out_weight = heads_b.weight(group_width, width // 2)
    middle, normed2, normed2_t = out_product(grid, at, line.at(mixed), x, eff2, bias2, out_weight)
    line.mark(normed2, swaps, moved)

    moved = down_w.last()
    swaps = down_w.swap(0, 1)
    active, slope = up_product(grid, at, line.at(normed2), up_w.weight())
    line.mark(active, moved, swaps)

    swaps = down_w.swap(2, 3)
    (sent,) = wide_chunks(grid, at, False, *line.at(active, cot))
    line.mark(sent, swaps)

    push_down = Push(grid, line, line.at(sent))
    grad_hidden = hidden_back(grid, at, *line.at(cot, slope), down_w.weight())
    line.mark(grad_hidden, push_down.came)

    kept = push_down.keep(wide_chunks(grid, at, True, *line.at(active, cot, push_down.came)), True)
    line.mark(kept)

    down = push_down.second(True)
    (sent,) = row_chunks(grid, at, False, *line.at(normed2_t, grad_hidden))
    line.mark(sent)

    push_up = Push(grid, line, line.at(sent))
    down += push_down.second(False)
    grad_middle, sums2 = norm_back(grid, at, line.at((grad_hidden,)), middle, eff2, cot, (up_w.weight(),), 512)
    line.mark(grad_middle, down, push_up.came)

    down = push_down.first()
    kept = push_up.keep(row_chunks(grid, at, True, *line.at(normed2_t, grad_hidden, push_up.came)), True)
    line.mark(kept)

    grad_heads = heads_back(grid, at, line.at(grad_middle), out_weight)
    line.mark(grad_heads, down)

    def back(group, half, grad_heads):
        packed, wide = ((packed_a, wide_a), (packed_b, wide_b))[group]
        mixed, lse = att[group, half]
        parts = attend_back(group, half, packed, wide, mixed, grad_heads, lse, mask_column, tables, key_tables)
        if ranks == 1:
            return parts[0]
        rest = lax.psum_scatter(
            parts[1], "blk", scatter_dimension=0, tiled=True, axis_index_groups=rank_groups(grid)
        )
        return jnp.concatenate([parts[0], rest], axis=1)

    down = push_down.outer()
    up = push_up.second(True)
    back_a0 = back(0, 0, line.at(grad_heads))
    line.mark(back_a0, down, up)

    down = push_down.outer_rest()
    up = push_up.first()
    back_a1 = back(0, 1, line.at(grad_heads))
    line.mark(back_a1, up)

    up = push_up.second(False)
    (sent,) = heads_chunks(grid, at, False, *line.at(normed1_t, (back_a0, back_a1), mixed, grad_middle))
    line.mark(sent, down, up)

    push_a = Push(grid, line, line.at(sent))
    up = push_up.outer()
    down = push_down.own_half()
    back_b0 = back(1, 0, line.at(grad_heads))
    line.mark(back_b0, up, push_a.came, down)

    up = push_up.outer_rest()
    kept = heads_chunks(grid, at, True, *line.at(normed1_t, (back_a0, back_a1), mixed, grad_middle, push_a.came))
    push_a.keep(kept, True)
    line.mark(kept)

    heads = push_a.second(True) + push_a.second(False)
    grad_down = push_down.result(core)
    back_b1 = back(1, 1, line.at(grad_heads))
    line.mark(back_b1, heads, up)

    heads = push_a.first()
    up = push_up.own_half()
    (sent,) = heads_chunks(grid, at, False, *line.at(normed1_t, (back_b0, back_b1)))
    line.mark(sent, up)

    push_b = Push(grid, line, line.at(sent))
    kept = push_b.keep(heads_chunks(grid, at, True, *line.at(normed1_t, (back_b0, back_b1))), False)
    line.mark(kept, push_b.came, heads)

    last = push_b.second(True) + push_b.second(False)
    heads = push_a.outer()
    grads = line.at((back_a0, back_a1, back_b0, back_b1))
    grad_x, grad_x_theirs, sums1 = norm_back(
        grid, at, grads, x, eff1, grad_middle, (heads_a.weight(), heads_b.weight(0, group_width)), group_width, 2
    )
    line.mark(sums1, last, heads)

    def sums_step(v, far):
        return jnp.concatenate([v[:4] + far[:4], v[4:], far[4:]])

    vector, two = whole((1, width)), whole((2, width))
    every = call(
        sums_kernel, "sums", (1,), [two, two] + [vector] * 4 + [whole((1, 1))], [whole((8, width))], [((8, width), F32)],
        [], 0, 64 * width,
    )(line.at(sums1), sums2, gain1, gain2, scale1, scale2, my_time.astype(F32)[None])[0]
    bits = [grid.chunks << i for i in reversed(range((grid.n0 - 1).bit_length()))] + inner_bits
    far = doubled(grid, every, bits[0])
    last = push_b.first()
    heads = push_a.outer_rest()
    grad_x_theirs = grid.swap(line.at(grad_x_theirs))
    out_theirs = down_product(grid, at, 1, *line.at(active, middle), down_w.weight())
    line.mark(out_theirs, last, heads, far, grad_x_theirs)

    every = sums_step(*line.at(every, far))
    far = doubled(grid, every, bits[1])
    last = push_b.outer()
    heads = push_a.own_half()
    out_theirs = grid.swap(line.at(out_theirs))
    grad_up = push_up.result(core)
    out_mine = down_product(grid, at, 0, *line.at(active, middle), down_w.weight())
    line.mark(out_mine, last, heads, far, out_theirs)

    def to_blocks(mine, theirs):
        return jnp.where(core == 0, jnp.stack([mine, theirs]), jnp.stack([theirs, mine]))

    every = sums_step(*line.at(every, far))
    far = doubled(grid, every, bits[2])
    last = push_b.outer_rest()
    grad_tokens = to_blocks(*line.at(grad_x, grad_x_theirs))
    line.mark(far, last, grad_tokens)
    push_b.own_half()
    for bit in bits[3:]:
        every = sums_step(*line.at(every, far))
        far = doubled(grid, every, bit)
        line.mark(far)
    layer_out = to_blocks(*line.at(out_mine, out_theirs))
    grad_out = push_a.result(core, group_width, width // 2)
    every = sums_step(*line.at(every, far))
    sums, rest = every[:4], [every[4:]]
    for k in range(1, grid.blocks):
        pairs = [
            (d * grid.blocks + b, d * grid.blocks + (b - k) % grid.blocks)
            for d in range(grid.groups) for b in range(grid.blocks)
        ]
        far = lax.ppermute(every, AXES, pairs)
        sums, rest = sums + far[:4], rest + [far[4:]]
    both = jnp.stack([p.result(core, 0, group_width).reshape(-1, 2, 3, width // 4) for p in (push_a, push_b)], axis=1)
    grad_qkv = both.transpose(0, 3, 1, 2, 4).reshape(-1, 3 * width)
    rest = jnp.concatenate(rest).reshape(-1, 4, width)
    my_features = time_features(rest[:, 2, 0], group * t_rows + jnp.arange(t_rows, dtype=jnp.int32))
    grad_scales = rest[:, :2].reshape(-1, 2 * width)
    grad_time = lax.dot_general(
        my_features, grad_scales, (((0,), (0,)), ((), ())), precision=lax.Precision.HIGHEST
    )
    sums = lax.dynamic_slice_in_dim(sums, group * per, per, 1)
    return (
        layer_out, grad_tokens, grad_qkv, grad_out, grad_up, grad_down, grad_time,
        sums[0], sums[1], sums[2], sums[3],
    )


def solution(mesh):
    rows = P("dp", "blk", None)
    matrix = P("dp", None)
    vector = P("dp")
    return jax.shard_map(
        shards,
        mesh=mesh,
        in_specs=(rows, vector, vector) + (matrix,) * 5 + (vector,) * 4 + (rows,),
        out_specs=(rows, rows) + (matrix,) * 5 + (vector,) * 4,
        check_vma=False,
    )
```

time: 678 us -> 528 us (0.78)
  waiting for transfers between devices: 200 us -> 60.2 us
  Pallas kernels: 275 us -> 327 us
  local copies, waits for them, and re-layouts: 48.6 us -> 24.4 us
  starting transfers between devices: 96.2 us -> 77.1 us
  other arithmetic: 43.8 us -> 29.8 us
    ppermute x44 -> x45, waiting for transfers between devices: 167 us -> 53.9 us  [shift(): return lax.ppermute(v, AXES, pairs)]
    pallas_call x14 -> x31, Pallas kernels: 275 us -> 327 us  [the longest x4 69.5 us: attend_back(): call(functools.partial(attend_back_kernel, min(rows, 512)), 'attend_back'...]
    ppermute x11 -> x9, waiting for transfers between devices: 32.5 us -> 6.18 us  [the longest x8 6.18 us: doubled(): return lax.ppermute(v, AXES, pairs)]
    convert_element_type x23 -> x21, other arithmetic: 25.4 us -> 7.63 us  [the longest x4 3.89 us: outer(): plus(*self.line.at(self.terms[0] + seconds + self.first_in)).astype(BF16)]
    unnamed x113 -> x151, local copies, waits for them, and re-layouts: 24.2 us -> 7.22 us
    ppermute x44 -> x45, starting transfers between devices: 51.1 us -> 38 us  [shift(): return lax.ppermute(v, AXES, pairs)]
    another operation x14 -> x0, local copies, waits for them, and re-layouts: 7.62 us -> none  [the longest x6 2.32 us: rolled(): both = jnp.stack(list(parts) + list(parts[:-1]))]
    ppermute x11 -> x9, starting transfers between devices: 16.3 us -> 10.6 us  [the longest x8 9.8 us: doubled(): return lax.ppermute(v, AXES, pairs)]
  transfers between devices with their start and end apart: 83 -> 82, of which waited for: 26 -> 18; matrix products, arithmetic and copies ran while one was open for 13% -> 7% of each run, Pallas kernels for 20% -> 56%
where the time goes in v2:
time: 528 us; the launch traced here: 523 us
  Pallas kernels  327 us (62%)
  starting transfers between devices  77.1 us (15%)
  waiting for transfers between devices  60.2 us (11%)
  other arithmetic  29.8 us (6%)
  local copies, waits for them, and re-layouts  24.4 us (5%)
    pallas_call x4, Pallas kernels, attend_back(): call(functools.partial(attend_back_kernel, min(rows, 512)), 'attend_back'...  69.5 us
    ppermute x45, waiting for transfers between devices, shift(): return lax.ppermute(v, AXES, pairs)  53.9 us
    pallas_call x4, Pallas kernels, attend(): call(functools.partial(attend_kernel, min(rows, 512)), 'attend', (1,), [p...  46.4 us
    ppermute x45, starting transfers between devices, shift(): return lax.ppermute(v, AXES, pairs)  38 us
    pallas_call x2, Pallas kernels, norm_back(): call(functools.partial(norm_back_kernel, [w[1] for w in weights], starts,...  35.5 us
    pallas_call x4, Pallas kernels, heads_chunks(): call(functools.partial(heads_chunks_kernel, kept, more, came is not None)...  33.9 us
    ppermute x28, starting transfers between devices, swap(): return lax.ppermute(v, AXES, pairs)  28.5 us
    pallas_call x2, Pallas kernels, wide_chunks(): call(functools.partial(wide_chunks_kernel, grid.n0, kept, came is not Non...  21.1 us
  transfers between devices with their start and end apart: 82, of which 18 were waited for; matrix products, arithmetic and copies ran while one was open for 7% of the time, Pallas kernels for 56%

profile of v2, /device:TPU:1, one launch (start us, length us, event | category | flops | bytes accessed | tf_op | source)
XLA Modules:
  0.0 523.1 jit_solution(13700331744459759946)
XLA Ops:
  1.8 2.2 collective-permute-start.1
  4.0 2.3 collective-permute-start.2
  11.2 1.7 collective-permute-done.3.refs_3_
  13.0 3.1 collective-permute-start.5
  16.2 1.8 rolled.4.refs_5_.refs_0_
  19.7 2.7 pad_maximum_fusion.refs_0_.x
  27.9 3.8 collective-permute-start.11
  35.7 3.7 collective-permute-done.10.refs_8_.refs_3_
  40.7 2.7 collective-permute-start.14
  45.3 15.7 %collective-permute-done.16.refs_1_ = bf16[2,64,1280]{2,1,0:T(8,128)(2,1)S(1)} collective-permute-done((bf16[2,64,1280]{2,1,0:T(8,128)(2,1)S(1)}, bf16[2,64,1280]{2,1,0:T(8,128)(2,1)S(1)}, u32[]{:S(2)}, u32[]{:S(2)}) %collective-permute-start.16) | collective-permute-done | bytes 327712 | tf_op jit(solution)/shard_map/ppermute | solution.py:46
  66.3 2.0 rolled.5.refs_3_.refs_0_.refs_8_
  69.7 1.7 dynamic-slice_bitcast_fusion.12
  71.4 9.3 %qkv.2 = (bf16[1024,1024]{1,0:T(8,128)(2,1)}, bf16[1024,1024]{1,0:T(8,128)(2,1)}, bf16[1024,1536]{1,0:T(8,128)(2,1)}) custom-call(s32[24]{0:T(128)} %fusion.32.place, bf16[1024,1024]{1,0:T(8,128)(2,1)} %pad_maximum_fusion.refs_0_.x, f32[1,1024]{1,0:T(1,128)} %get-tuple-element.285.refs_1_.gain, f32[1,1024]{1,0:T(1,128)} %squeeze.128.refs_2_, ...), custom_call_target="tpu_custom_call" | custom-call | flops 3221225472 | bytes 12582912 | tf_op jit(solution)/shard_map/qkv/pallas_call | solution.py:219
  85.3 11.4 %attend.4 = (bf16[1024,256]{1,0:T(8,128)(2,1)}, f32[1024,128]{1,0:T(8,128)}) custom-call(bf16[1024,1536]{1,0:T(8,128)(2,1)} %get-tuple-element.293.q.kv, bf16[1024,1536]{1,0:T(8,128)(2,1)} %get-tuple-element.293.q.kv, f32[1,1024]{1,0:T(1,128)} %bitcast.279), custom_call_target="tpu_custom_call" | custom-call | flops 4294967296 | bytes 2097152 | tf_op jit(solution)/shard_map/attend/pallas_call | solution.py:262
  99.0 11.9 %attend.5 = (bf16[1024,256]{1,0:T(8,128)(2,1)}, f32[1024,128]{1,0:T(8,128)}) custom-call(bf16[1024,1536]{1,0:T(8,128)(2,1)} %get-tuple-element.293.q.kv, bf16[1024,1536]{1,0:T(8,128)(2,1)} %get-tuple-element.293.q.kv, f32[1,1024]{1,0:T(1,128)} %bitcast.280), custom_call_target="tpu_custom_call" | custom-call | flops 4294967296 | bytes 2097152 | tf_op jit(solution)/shard_map/attend/pallas_call | solution.py:262
  112.3 1.5 pad_maximum_fusion.1.refs_4_.grad.base
  113.8 2.1 collective-permute-done.27
  115.9 2.7 rolled.6.refs_0_
  119.5 8.6 %qkv.3.q.kv = bf16[1024,1536]{1,0:T(8,128)(2,1)} custom-call(s32[24]{0:T(128)} %fusion.32.place, bf16[1024,1024]{1,0:T(8,128)(2,1)} %get-tuple-element.310.refs_0_, f32[1024,128]{1,0:T(8,128)} %pad_maximum_fusion.3.refs_3_.refs_1_.cosine, f32[1024,128]{1,0:T(8,128)} %pad_maximum_fusion.4.refs_4_.refs_2_.sine, ...), custom_call_target="tpu_custom_call" | custom-call | flops 3221225472 | bytes 12582912 | tf_op jit(solution)/shard_map/qkv/pallas_call | solution.py:219
  128.2 4.6 collective-permute-done.28.refs_1_
  134.2 11.4 %attend.6 = (bf16[1024,256]{1,0:T(8,128)(2,1)}, f32[1024,128]{1,0:T(8,128)}) custom-call(bf16[1024,1536]{1,0:T(8,128)(2,1)} %qkv.3.q.kv, bf16[1024,1536]{1,0:T(8,128)(2,1)} %qkv.3.q.kv, f32[1,1024]{1,0:T(1,128)} %bitcast.281), custom_call_target="tpu_custom_call" | custom-call | flops 4294967296 | bytes 2097152 | tf_op jit(solution)/shard_map/attend/pallas_call | solution.py:262
  145.7 1.9 collective-permute-start.31
  149.1 11.6 %attend.7 = (bf16[1024,256]{1,0:T(8,128)(2,1)}, f32[1024,128]{1,0:T(8,128)}) custom-call(bf16[1024,1536]{1,0:T(8,128)(2,1)} %qkv.3.q.kv, bf16[1024,1536]{1,0:T(8,128)(2,1)} %qkv.3.q.kv, f32[1,1024]{1,0:T(1,128)} %bitcast.282), custom_call_target="tpu_custom_call" | custom-call | flops 4294967296 | bytes 2097152 | tf_op jit(solution)/shard_map/attend/pallas_call | solution.py:262
  160.7 14.0 %collective-permute-done.33.refs_1_ = bf16[2,256,512]{2,1,0:T(8,128)(2,1)S(1)} collective-permute-done((bf16[2,256,512]{2,1,0:T(8,128)(2,1)S(1)}, bf16[2,256,512]{2,1,0:T(8,128)(2,1)S(1)}, u32[]{:S(2)}, u32[]{:S(2)}) %collective-permute-start.33) | collective-permute-done | bytes 524320 | tf_op jit(solution)/shard_map/ppermute | solution.py:46
  175.5 2.4 rolled.7.refs_0_
  178.7 10.6 %out.1 = (bf16[1024,1024]{1,0:T(8,128)(2,1)}, bf16[1024,1024]{1,0:T(8,128)(2,1)}, bf16[1024,1024]{1,0:T(8,128)(2,1)}) custom-call(s32[24]{0:T(128)} %fusion.32.place, bf16[1024,1024]{1,0:T(8,128)(2,1)} %pad_maximum_fusion.refs_0_.x, f32[1,1024]{1,0:T(1,128)} %get-tuple-element.539.gain, f32[1,1024]{1,0:T(1,128)} %squeeze.126.bias, ...), custom_call_target="tpu_custom_call" | custom-call | flops 2147483648 | bytes 10485760 | tf_op jit(solution)/shard_map/out/pallas_call | solution.py:388
  189.3 2.6 collective-permute-done.36.refs_1_
  193.5 1.9 collective-permute-start.39
  195.4 21.1 %up.1 = (bf16[1024,4096]{1,0:T(8,128)(2,1)}, bf16[1024,4096]{1,0:T(8,128)(2,1)}) custom-call(s32[24]{0:T(128)} %fusion.32.place, bf16[1024,1024]{1,0:T(8,128)(2,1)} %get-tuple-element.338.normed, bf16[4,64,2048]{2,1,0:T(8,128)(2,1)} %rolled.6.refs_0_, bf16[4,64,2048]{2,1,0:T(8,128)(2,1)} %copy-done.63, bf16[4,64,2048]{2,1,0:T(8,128)(2,1)} %copy-done.64, ...), custom_call_target="tpu_custom_call" | custom-call | flops 8589934592 | bytes 25165824 | tf_op jit(solution)/shard_map/up/pallas_call | solution.py:429
  217.2 2.3 collective-permute-start.41
  219.6 9.7 %wide_chunks.2 = bf16[4,4,256,512]{3,2,1,0:T(8,128)(2,1)} custom-call(s32[24]{0:T(128)} %fusion.32.place, bf16[1024,4096]{1,0:T(8,128)(2,1)} %get-tuple-element.466.refs_0_.refs_1_.refs_2_.refs_3_.active, bf16[1024,4096]{1,0:T(8,128)(2,1)} %get-tuple-element.466.refs_0_.refs_1_.refs_2_.refs_3_.active, ...), custom_call_target="tpu_custom_call" | custom-call | flops 4294967296 | bytes 14680064 | tf_op jit(solution)/shard_map/wide_chunks/pallas_call | solution.py:721
  230.7 14.9 %hidden_back.1.b.refs_8_ = bf16[1024,4096]{1,0:T(8,128)(2,1)} custom-call(s32[24]{0:T(128)} %fusion.32.place, bf16[1024,1024]{1,0:T(8,128)(2,1)} %pad_maximum_fusion.1.refs_4_.grad.base, bf16[1024,4096]{1,0:T(8,128)(2,1)} %get-tuple-element.351.slope, bf16[4,256,512]{2,1,0:T(8,128)(2,1)} %rolled.7.refs_0_, bf16[4,256,512]{2,1,0:T(8,128)(2,1)} %copy-done.4, ...), custom_call_target="tpu_custom_call" | custom-call | flops 8589934592 | bytes 25165824 | tf_op jit(solution)/shard_map/hidden_back/pallas_call | solution.py:499
  245.6 11.3 %wide_chunks.3 = (bf16[4,256,512]{2,1,0:T(8,128)(2,1)}, bf16[4,256,512]{2,1,0:T(8,128)(2,1)}, bf16[4,256,512]{2,1,0:T(8,128)(2,1)}, bf16[4,256,512]{2,1,0:T(8,128)(2,1)}) custom-call(s32[24]{0:T(128)} %fusion.32.place, bf16[1024,4096]{1,0:T(8,128)(2,1)} %get-tuple-element.466.refs_0_.refs_1_.refs_2_.refs_3_.active, ...), custom_call_target="tpu_custom_call" | custom-call | flops 4294967296 | bytes 14680064 | tf_op jit(solution)/shard_map/wide_chunks/pallas_call | solution.py:721
  257.0 9.9 %row_chunks.2 = bf16[4,4,64,2048]{3,2,1,0:T(8,128)(2,1)} custom-call(s32[24]{0:T(128)} %fusion.32.place, bf16[1024,1024]{1,0:T(8,128)(2,1)} %get-tuple-element.368.a, bf16[1024,4096]{1,0:T(8,128)(2,1)} %hidden_back.1.b.refs_8_), custom_call_target="tpu_custom_call" | custom-call | flops 4294967296 | bytes 10485760 | tf_op jit(solution)/shard_map/row_chunks/pallas_call | solution.py:633
  268.8 20.5 %norm_back.2 = (bf16[1024,1024]{1,0:T(8,128)(2,1)}, f32[2,1024]{1,0:T(2,128)}) custom-call(s32[24]{0:T(128)} %fusion.32.place, bf16[1024,1024]{1,0:T(8,128)(2,1)} %get-tuple-element.467.x.middle, f32[1,1024]{1,0:T(1,128)} %get-tuple-element.539.gain, bf16[1024,1024]{1,0:T(8,128)(2,1)} %pad_maximum_fusion.1.refs_4_.grad.base, ...), custom_call_target="tpu_custom_call" | custom-call | flops 8589934592 | bytes 23068672 | tf_op jit(solution)/shard_map/norm_back/pallas_call | solution.py:551
  289.4 3.2 collective-permute-done.46
  293.7 10.0 %row_chunks.3 = (bf16[4,64,2048]{2,1,0:T(8,128)(2,1)}, bf16[4,64,2048]{2,1,0:T(8,128)(2,1)}, bf16[4,64,2048]{2,1,0:T(8,128)(2,1)}, bf16[4,64,2048]{2,1,0:T(8,128)(2,1)}) custom-call(s32[24]{0:T(128)} %fusion.32.place, bf16[1024,1024]{1,0:T(8,128)(2,1)} %get-tuple-element.368.a, bf16[1024,4096]{1,0:T(8,128)(2,1)} %hidden_back.1.b.refs_8_, ...), custom_call_target="tpu_custom_call" | custom-call | flops 4294967296 | bytes 10485760 | tf_op jit(solution)/shard_map/row_chunks/pallas_call | solution.py:633
  303.8 6.8 %heads_back.1.grad = bf16[1024,1024]{1,0:T(8,128)(2,1)} custom-call(s32[24]{0:T(128)} %fusion.32.place, bf16[1024,1024]{1,0:T(8,128)(2,1)} %get-tuple-element.415.grad.refs_6_.refs_7_.base, bf16[4,64,1280]{2,1,0:T(8,128)(2,1)} %rolled.5.refs_3_.refs_0_.refs_8_, bf16[4,64,1280]{2,1,0:T(8,128)(2,1)} %copy-done.11, bf16[4,64,1280]{2,1,0:T(8,128)(2,1)} %copy-done.12, ...), custom_call_target="tpu_custom_call" | custom-call | flops 2147483648 | bytes 6291456 | tf_op jit(solution)/shard_map/heads_back/pallas_call | solution.py:585
  311.2 1.6 add_convert_fusion.2
  313.0 17.3 %attend_back.4.refs_0_.refs_16_ = bf16[1024,768]{1,0:T(8,128)(2,1)} custom-call(bf16[1024,1536]{1,0:T(8,128)(2,1)} %get-tuple-element.293.q.kv, bf16[1024,1536]{1,0:T(8,128)(2,1)} %get-tuple-element.293.q.kv, bf16[1024,256]{1,0:T(8,128)(2,1)} %get-tuple-element.411.refs_8_.mixed.refs_2_.refs_3_, bf16[1024,1024]{1,0:T(8,128)(2,1)} %heads_back.1.grad, ...), custom_call_target="tpu_custom_call" | custom-call | flops 10737418240 | bytes 4194304 | tf_op jit(solution)/shard_map/attend_back/pallas_call | solution.py:345
  332.1 17.5 %attend_back.5.refs_1_.refs_17_ = bf16[1024,768]{1,0:T(8,128)(2,1)} custom-call(bf16[1024,1536]{1,0:T(8,128)(2,1)} %get-tuple-element.293.q.kv, bf16[1024,1536]{1,0:T(8,128)(2,1)} %get-tuple-element.293.q.kv, bf16[1024,256]{1,0:T(8,128)(2,1)} %get-tuple-element.412.refs_9_.mixed.refs_3_.refs_4_, bf16[1024,1024]{1,0:T(8,128)(2,1)} %heads_back.1.grad, ...), custom_call_target="tpu_custom_call" | custom-call | flops 10737418240 | bytes 4194304 | tf_op jit(solution)/shard_map/attend_back/pallas_call | solution.py:345
  349.8 2.3 collective-permute-start.51
  352.3 10.4 %heads_chunks.4 = bf16[4,4,64,1280]{3,2,1,0:T(8,128)(2,1)} custom-call(s32[24]{0:T(128)} %fusion.32.place, bf16[1024,1024]{1,0:T(8,128)(2,1)} %get-tuple-element.432.a, bf16[1024,768]{1,0:T(8,128)(2,1)} %attend_back.4.refs_0_.refs_16_, bf16[1024,768]{1,0:T(8,128)(2,1)} %attend_back.5.refs_1_.refs_17_, ...), custom_call_target="tpu_custom_call" | custom-call | flops 2684354560 | bytes 7340032 | tf_op jit(solution)/shard_map/heads_chunks/pallas_call | solution.py:679
  365.6 2.0 collective-permute-start.54
  367.6 1.8 add_convert_fusion
  369.6 2.0 collective-permute-start.55
  372.0 17.3 %attend_back.6.refs_0_.refs_18_ = bf16[1024,768]{1,0:T(8,128)(2,1)} custom-call(bf16[1024,1536]{1,0:T(8,128)(2,1)} %qkv.3.q.kv, bf16[1024,1536]{1,0:T(8,128)(2,1)} %qkv.3.q.kv, bf16[1024,256]{1,0:T(8,128)(2,1)} %get-tuple-element.413.refs_10_.refs_4_.mixed.refs_5_, bf16[1024,1024]{1,0:T(8,128)(2,1)} %heads_back.1.grad, f32[1024,128]{1,0:T(8,128)} %get-tuple-element.317.lse, ...), custom_call_target="tpu_custom_call" | custom-call | flops 10737418240 | bytes 4194304 | tf_op jit(solution)/shard_map/attend_back/pallas_call | solution.py:345
  389.3 1.6 copy-done.18
  390.9 10.8 %heads_chunks.5 = (bf16[4,64,1280]{2,1,0:T(8,128)(2,1)}, bf16[4,64,1280]{2,1,0:T(8,128)(2,1)}, bf16[4,64,1280]{2,1,0:T(8,128)(2,1)}, bf16[4,64,1280]{2,1,0:T(8,128)(2,1)}) custom-call(s32[24]{0:T(128)} %fusion.32.place, bf16[1024,1024]{1,0:T(8,128)(2,1)} %get-tuple-element.432.a, bf16[1024,768]{1,0:T(8,128)(2,1)} %attend_back.4.refs_0_.refs_16_, ...), custom_call_target="tpu_custom_call" | custom-call | flops 2684354560 | bytes 7340032 | tf_op jit(solution)/shard_map/heads_chunks/pallas_call | solution.py:679
  403.8 1.7 collective-permute-start.60
  405.5 17.4 %attend_back.7.refs_1_.refs_19_ = bf16[1024,768]{1,0:T(8,128)(2,1)} custom-call(bf16[1024,1536]{1,0:T(8,128)(2,1)} %qkv.3.q.kv, bf16[1024,1536]{1,0:T(8,128)(2,1)} %qkv.3.q.kv, bf16[1024,256]{1,0:T(8,128)(2,1)} %get-tuple-element.414.refs_11_.refs_5_.refs_6_.mixed, bf16[1024,1024]{1,0:T(8,128)(2,1)} %heads_back.1.grad, f32[1024,128]{1,0:T(8,128)} %get-tuple-element.320.lse, ...), custom_call_target="tpu_custom_call" | custom-call | flops 10737418240 | bytes 4194304 | tf_op jit(solution)/shard_map/attend_back/pallas_call | solution.py:345
  424.5 6.5 %heads_chunks.6 = bf16[4,4,64,768]{3,2,1,0:T(8,128)(2,1)} custom-call(s32[24]{0:T(128)} %fusion.32.place, bf16[1024,1024]{1,0:T(8,128)(2,1)} %get-tuple-element.432.a, bf16[1024,768]{1,0:T(8,128)(2,1)} %attend_back.6.refs_0_.refs_18_, bf16[1024,768]{1,0:T(8,128)(2,1)} %attend_back.7.refs_1_.refs_19_), custom_call_target="tpu_custom_call" | custom-call | flops 1610612736 | bytes 5242880 | tf_op jit(solution)/shard_map/heads_chunks/pallas_call | solution.py:679
  434.6 6.3 %heads_chunks.7 = (bf16[4,64,768]{2,1,0:T(8,128)(2,1)}, bf16[4,64,768]{2,1,0:T(8,128)(2,1)}, bf16[4,64,768]{2,1,0:T(8,128)(2,1)}, bf16[4,64,768]{2,1,0:T(8,128)(2,1)}) custom-call(s32[24]{0:T(128)} %fusion.32.place, bf16[1024,1024]{1,0:T(8,128)(2,1)} %get-tuple-element.432.a, bf16[1024,768]{1,0:T(8,128)(2,1)} %attend_back.6.refs_0_.refs_18_, ...), custom_call_target="tpu_custom_call" | custom-call | flops 1610612736 | bytes 5242880 | tf_op jit(solution)/shard_map/heads_chunks/pallas_call | solution.py:679
  442.3 1.6 slice_bitcast_fusion
  446.9 15.0 %norm_back.3 = (bf16[512,1024]{1,0:T(8,128)(2,1)}, bf16[512,1024]{1,0:T(8,128)(2,1)}, f32[2,1024]{1,0:T(2,128)}) custom-call(s32[24]{0:T(128)} %fusion.32.place, bf16[1024,1024]{1,0:T(8,128)(2,1)} %pad_maximum_fusion.refs_0_.x, f32[1,1024]{1,0:T(1,128)} %get-tuple-element.285.refs_1_.gain, bf16[1024,1024]{1,0:T(8,128)(2,1)} %get-tuple-element.415.grad.refs_6_.refs_7_.base, ...), custom_call_target="tpu_custom_call" | custom-call | flops 6442450944 | bytes 18874368 | tf_op jit(solution)/shard_map/norm_back/pallas_call | solution.py:551
  461.9 2.1 collective-permute-start.71
  465.1 1.6 collective-permute-start.68
  469.8 9.7 %down.2 = bf16[512,1024]{1,0:T(8,128)(2,1)} custom-call(s32[24]{0:T(128)} %fusion.32.place, bf16[1024,4096]{1,0:T(8,128)(2,1)} %get-tuple-element.466.refs_0_.refs_1_.refs_2_.refs_3_.active, bf16[1024,1024]{1,0:T(8,128)(2,1)} %get-tuple-element.467.x.middle, bf16[4,256,512]{2,1,0:T(8,128)(2,1)} %rolled.7.refs_0_, bf16[4,256,512]{2,1,0:T(8,128)(2,1)} %copy-done.4, ...), custom_call_target="tpu_custom_call" | custom-call | flops 4294967296 | bytes 12582912 | tf_op jit(solution)/shard_map/down/pallas_call | solution.py:468
  482.3 1.6 collective-permute-start.74
  483.9 9.5 %down.3 = bf16[512,1024]{1,0:T(8,128)(2,1)} custom-call(s32[24]{0:T(128)} %fusion.32.place, bf16[1024,4096]{1,0:T(8,128)(2,1)} %get-tuple-element.466.refs_0_.refs_1_.refs_2_.refs_3_.active, bf16[1024,1024]{1,0:T(8,128)(2,1)} %get-tuple-element.467.x.middle, bf16[4,256,512]{2,1,0:T(8,128)(2,1)} %rolled.7.refs_0_, bf16[4,256,512]{2,1,0:T(8,128)(2,1)} %copy-done.4, ...), custom_call_target="tpu_custom_call" | custom-call | flops 4294967296 | bytes 12582912 | tf_op jit(solution)/shard_map/down/pallas_call | solution.py:468
  499.2 3.2 maximum_select_fusion
  503.4 2.4 collective-permute-start.80
  507.1 4.6 collective-permute-done.79
  515.4 3.3 maximum_select_fusion.1
  (394 shorter events, 87.1 us)
Async XLA Ops:
  25.2 10.5 %collective-permute-start.8 = (bf16[4,8,2176]{2,1,0:T(8,128)(2,1)S(1)}, bf16[4,8,2176]{2,1,0:T(8,128)(2,1)S(1)}, u32[]{:S(2)}, u32[]{:S(2)}) collective-permute-start(bf16[4,8,2176]{2,1,0:T(8,128)(2,1)S(1)} %pad_maximum_fusion.12), channel_id=1, source_target_pairs={{0,2},{1,3},{2,0},{3,1},{4,6},{5,7},{6,4},{7,5},{8,10},{9,11},{10,... | collective-permute-start | bytes 417800 | tf_op jit(solution)/shard_map/ppermute | solution.py:866
  26.7 12.8 %collective-permute-start.10 = (bf16[4,64,768]{2,1,0:T(8,128)(2,1)}, bf16[4,64,768]{2,1,0:T(8,128)(2,1)}, u32[]{:S(2)}, u32[]{:S(2)}) collective-permute-start(bf16[4,64,768]{2,1,0:T(8,128)(2,1)} %collective-permute-done.6.refs_6_.refs_1_), channel_id=1, source_target_pairs={{0,4},{1,3},{2,6},{3,1},{4,0},{5,7},{6,2},{7,5},{8,12},{9,11},{10,... | collective-permute-start | bytes 1179656 | tf_op jit(solution)/shard_map/ppermute | solution.py:46
  27.9 11.5 %collective-permute-start.11 = (bf16[4,64,768]{2,1,0:T(8,128)(2,1)S(1)}, bf16[4,64,768]{2,1,0:T(8,128)(2,1)}, u32[]{:S(2)}, u32[]{:S(2)}) collective-permute-start(bf16[4,64,768]{2,1,0:T(8,128)(2,1)S(1)} %copy-done.39), channel_id=1, source_target_pairs={{0,1},{1,0},{2,3},{3,2},{4,5},{5,4},{6,7},{7,6},{8,9},{9,8},{10,11... | collective-permute-start | bytes 1179656 | tf_op jit(solution)/shard_map/ppermute | solution.py:53
  40.7 20.3 %collective-permute-start.14 = (bf16[4,64,768]{2,1,0:T(8,128)(2,1)}, bf16[4,64,768]{2,1,0:T(8,128)(2,1)S(1)}, u32[]{:S(2)}, u32[]{:S(2)}) collective-permute-start(bf16[4,64,768]{2,1,0:T(8,128)(2,1)} %collective-permute-done.9.refs_7_.refs_2_), channel_id=1, source_target_pairs={{0,1},{1,0},{2,3},{3,2},{4,5},{5,4},{6,7},{7,6},{8,9},{9,8},{10,11... | collective-permute-start | bytes 1179656 | tf_op jit(solution)/shard_map/ppermute | solution.py:53
  43.4 17.6 %collective-permute-start.15 = (bf16[4,64,768]{2,1,0:T(8,128)(2,1)}, bf16[4,64,768]{2,1,0:T(8,128)(2,1)S(1)}, u32[]{:S(2)}, u32[]{:S(2)}) collective-permute-start(bf16[4,64,768]{2,1,0:T(8,128)(2,1)} %collective-permute-done.10.refs_8_.refs_3_), channel_id=1, source_target_pairs={{0,1},{1,0},{2,3},{3,2},{4,5},{5,4},{6,7},{7,6},{8,9},{9,8},{10,11... | collective-permute-start | bytes 1179656 | tf_op jit(solution)/shard_map/ppermute | solution.py:53
  43.5 17.5 %collective-permute-start.16 = (bf16[2,64,1280]{2,1,0:T(8,128)(2,1)S(1)}, bf16[2,64,1280]{2,1,0:T(8,128)(2,1)S(1)}, u32[]{:S(2)}, u32[]{:S(2)}) collective-permute-start(bf16[2,64,1280]{2,1,0:T(8,128)(2,1)S(1)} %pad_maximum_fusion.8.refs_0_), channel_id=1, source_target_pairs={{0,16},{1,17},{2,18},{3,19},{4,20},{5,21},{6,22},{7,23},{8,24},{9,... | collective-permute-start | bytes 983048 | tf_op jit(solution)/shard_map/ppermute | solution.py:46
  43.6 20.1 %collective-permute-start.18 = (bf16[1,64,2048]{2,1,0:T(8,128)(2,1)S(1)}, bf16[1,64,2048]{2,1,0:T(8,128)(2,1)S(1)}, u32[]{:S(2)}, u32[]{:S(2)}) collective-permute-start(bf16[1,64,2048]{2,1,0:T(8,128)(2,1)S(1)} %dynamic-slice_bitcast_fusion.13), channel_id=1, source_target_pairs={{0,8},{1,9},{2,10},{3,11},{4,12},{5,13},{6,14},{7,15},{8,0},{9,1},... | collective-permute-start | bytes 786440 | tf_op jit(solution)/shard_map/ppermute | solution.py:46
  65.7 15.0 %collective-permute-start.19 = (bf16[512,1024]{1,0:T(8,128)(2,1)S(1)}, bf16[512,1024]{1,0:T(8,128)(2,1)S(1)}, u32[]{:S(2)}, u32[]{:S(2)}) collective-permute-start(bf16[512,1024]{1,0:T(8,128)(2,1)S(1)} %dynamic-slice_bitcast_fusion.1), channel_id=1, source_target_pairs={{0,1},{1,0},{2,3},{3,2},{4,5},{5,4},{6,7},{7,6},{8,9},{9,8},{10,11... | collective-permute-start | bytes 3145736 | tf_op jit(solution)/shard_map/ppermute | solution.py:53
  68.2 12.5 %collective-permute-start.17 = (bf16[4,64,1280]{2,1,0:T(8,128)(2,1)}, bf16[4,64,1280]{2,1,0:T(8,128)(2,1)S(1)}, u32[]{:S(2)}, u32[]{:S(2)}) collective-permute-start(bf16[4,64,1280]{2,1,0:T(8,128)(2,1)} %rolled.5.refs_3_.refs_0_.refs_8_), channel_id=1, source_target_pairs={{0,2},{1,5},{2,0},{3,7},{4,6},{5,1},{6,4},{7,3},{8,10},{9,13},{10,... | collective-permute-start | bytes 1966088 | tf_op jit(solution)/shard_map/ppermute | solution.py:46
  80.7 16.0 %collective-permute-start.20 = (bf16[4,64,1280]{2,1,0:T(8,128)(2,1)S(1)}, bf16[4,64,1280]{2,1,0:T(8,128)(2,1)S(1)}, u32[]{:S(2)}, u32[]{:S(2)}) collective-permute-start(bf16[4,64,1280]{2,1,0:T(8,128)(2,1)S(1)} %copy-done.3), channel_id=1, source_target_pairs={{0,4},{1,3},{2,6},{3,1},{4,0},{5,7},{6,2},{7,5},{8,12},{9,11},{10,... | collective-permute-start | bytes 1966088 | tf_op jit(solution)/shard_map/ppermute | solution.py:46
  81.1 16.6 %collective-permute-start.21 = (bf16[4,64,1280]{2,1,0:T(8,128)(2,1)S(1)}, bf16[4,64,1280]{2,1,0:T(8,128)(2,1)S(1)}, u32[]{:S(2)}, u32[]{:S(2)}) collective-permute-start(bf16[4,64,1280]{2,1,0:T(8,128)(2,1)S(1)} %collective-permute-done.17.refs_4_.refs_1_.refs_9_), channel_id=1, source_target_pairs={{0,4},{1,3},{2,6},{3,1},{4,0},{5,7},{6,2},{7,5},{8,12},{9,11},{10,... | collective-permute-start | bytes 1966088 | tf_op jit(solution)/shard_map/ppermute | solution.py:46
  82.3 15.4 %collective-permute-start.22 = (bf16[4,64,1280]{2,1,0:T(8,128)(2,1)S(1)}, bf16[4,64,1280]{2,1,0:T(8,128)(2,1)S(1)}, u32[]{:S(2)}, u32[]{:S(2)}) collective-permute-start(bf16[4,64,1280]{2,1,0:T(8,128)(2,1)S(1)} %copy-done.3), channel_id=1, source_target_pairs={{0,1},{1,0},{2,3},{3,2},{4,5},{5,4},{6,7},{7,6},{8,9},{9,8},{10,11... | collective-permute-start | bytes 1966088 | tf_op jit(solution)/shard_map/ppermute | solution.py:53
  83.2 14.5 %collective-permute-start.23 = (bf16[4,64,1280]{2,1,0:T(8,128)(2,1)S(1)}, bf16[4,64,1280]{2,1,0:T(8,128)(2,1)S(1)}, u32[]{:S(2)}, u32[]{:S(2)}) collective-permute-start(bf16[4,64,1280]{2,1,0:T(8,128)(2,1)S(1)} %collective-permute-done.17.refs_4_.refs_1_.refs_9_), channel_id=1, source_target_pairs={{0,1},{1,0},{2,3},{3,2},{4,5},{5,4},{6,7},{7,6},{8,9},{9,8},{10,11... | collective-permute-start | bytes 1966088 | tf_op jit(solution)/shard_map/ppermute | solution.py:53
  85.3 28.5 %collective-permute-start.26 = (bf16[2,64,2048]{2,1,0:T(8,128)(2,1)}, bf16[2,64,2048]{2,1,0:T(8,128)(2,1)}, u32[]{:S(2)}, u32[]{:S(2)}) collective-permute-start(bf16[2,64,2048]{2,1,0:T(8,128)(2,1)} %pad_maximum_fusion.5.refs_0_), channel_id=1, source_target_pairs={{0,16},{1,17},{2,18},{3,19},{4,20},{5,21},{6,22},{7,23},{8,24},{9,... | collective-permute-start | bytes 1572872 | tf_op jit(solution)/shard_map/ppermute | solution.py:46
  97.7 18.2 %collective-permute-start.24 = (bf16[4,64,1280]{2,1,0:T(8,128)(2,1)S(1)}, bf16[4,64,1280]{2,1,0:T(8,128)(2,1)S(1)}, u32[]{:S(2)}, u32[]{:S(2)}) collective-permute-start(bf16[4,64,1280]{2,1,0:T(8,128)(2,1)S(1)} %collective-permute-done.20.refs_5_.refs_2_.refs_10_), channel_id=1, source_target_pairs={{0,1},{1,0},{2,3},{3,2},{4,5},{5,4},{6,7},{7,6},{8,9},{9,8},{10,11... | collective-permute-start | bytes 1966088 | tf_op jit(solution)/shard_map/ppermute | solution.py:53
  98.8 17.0 %collective-permute-start.25 = (bf16[4,64,1280]{2,1,0:T(8,128)(2,1)S(1)}, bf16[4,64,1280]{2,1,0:T(8,128)(2,1)S(1)}, u32[]{:S(2)}, u32[]{:S(2)}) collective-permute-start(bf16[4,64,1280]{2,1,0:T(8,128)(2,1)S(1)} %collective-permute-done.21.refs_6_.refs_3_.refs_11_), channel_id=1, source_target_pairs={{0,1},{1,0},{2,3},{3,2},{4,5},{5,4},{6,7},{7,6},{8,9},{9,8},{10,11... | collective-permute-start | bytes 1966088 | tf_op jit(solution)/shard_map/ppermute | solution.py:53
  98.9 17.0 %collective-permute-start.27 = (bf16[1,256,512]{2,1,0:T(8,128)(2,1)}, bf16[1,256,512]{2,1,0:T(8,128)(2,1)}, u32[]{:S(2)}, u32[]{:S(2)}) collective-permute-start(bf16[1,256,512]{2,1,0:T(8,128)(2,1)} %dynamic-slice_bitcast_fusion.12), channel_id=1, source_target_pairs={{0,8},{1,9},{2,10},{3,11},{4,12},{5,13},{6,14},{7,15},{8,0},{9,1},... | collective-permute-start | bytes 786440 | tf_op jit(solution)/shard_map/ppermute | solution.py:46
  118.6 14.2 %collective-permute-start.28 = (bf16[4,64,2048]{2,1,0:T(8,128)(2,1)}, bf16[4,64,2048]{2,1,0:T(8,128)(2,1)S(1)}, u32[]{:S(2)}, u32[]{:S(2)}) collective-permute-start(bf16[4,64,2048]{2,1,0:T(8,128)(2,1)} %rolled.6.refs_0_), channel_id=1, source_target_pairs={{0,2},{1,5},{2,0},{3,7},{4,6},{5,1},{6,4},{7,3},{8,10},{9,13},{10,... | collective-permute-start | bytes 3145736 | tf_op jit(solution)/shard_map/ppermute | solution.py:46
  132.8 41.9 %collective-permute-start.29 = (bf16[4,64,2048]{2,1,0:T(8,128)(2,1)S(1)}, bf16[4,64,2048]{2,1,0:T(8,128)(2,1)S(1)}, u32[]{:S(2)}, u32[]{:S(2)}) collective-permute-start(bf16[4,64,2048]{2,1,0:T(8,128)(2,1)S(1)} %copy-done.27), channel_id=1, source_target_pairs={{0,4},{1,3},{2,6},{3,1},{4,0},{5,7},{6,2},{7,5},{8,12},{9,11},{10,... | collective-permute-start | bytes 3145736 | tf_op jit(solution)/shard_map/ppermute | solution.py:46
  134.0 40.7 %collective-permute-start.30 = (bf16[4,64,2048]{2,1,0:T(8,128)(2,1)S(1)}, bf16[4,64,2048]{2,1,0:T(8,128)(2,1)S(1)}, u32[]{:S(2)}, u32[]{:S(2)}) collective-permute-start(bf16[4,64,2048]{2,1,0:T(8,128)(2,1)S(1)} %collective-permute-done.28.refs_1_), channel_id=1, source_target_pairs={{0,4},{1,3},{2,6},{3,1},{4,0},{5,7},{6,2},{7,5},{8,12},{9,11},{10,... | collective-permute-start | bytes 3145736 | tf_op jit(solution)/shard_map/ppermute | solution.py:46
  145.7 29.0 %collective-permute-start.31 = (bf16[4,64,2048]{2,1,0:T(8,128)(2,1)S(1)}, bf16[4,64,2048]{2,1,0:T(8,128)(2,1)}, u32[]{:S(2)}, u32[]{:S(2)}) collective-permute-start(bf16[4,64,2048]{2,1,0:T(8,128)(2,1)S(1)} %copy-done.27), channel_id=1, source_target_pairs={{0,1},{1,0},{2,3},{3,2},{4,5},{5,4},{6,7},{7,6},{8,9},{9,8},{10,11... | collective-permute-start | bytes 3145736 | tf_op jit(solution)/shard_map/ppermute | solution.py:53
  147.6 27.1 %collective-permute-start.32 = (bf16[4,64,2048]{2,1,0:T(8,128)(2,1)S(1)}, bf16[4,64,2048]{2,1,0:T(8,128)(2,1)}, u32[]{:S(2)}, u32[]{:S(2)}) collective-permute-start(bf16[4,64,2048]{2,1,0:T(8,128)(2,1)S(1)} %collective-permute-done.28.refs_1_), channel_id=1, source_target_pairs={{0,1},{1,0},{2,3},{3,2},{4,5},{5,4},{6,7},{7,6},{8,9},{9,8},{10,11... | collective-permute-start | bytes 3145736 | tf_op jit(solution)/shard_map/ppermute | solution.py:53
  148.7 25.9 %collective-permute-start.33 = (bf16[2,256,512]{2,1,0:T(8,128)(2,1)S(1)}, bf16[2,256,512]{2,1,0:T(8,128)(2,1)S(1)}, u32[]{:S(2)}, u32[]{:S(2)}) collective-permute-start(bf16[2,256,512]{2,1,0:T(8,128)(2,1)S(1)} %pad_maximum_fusion.6.refs_0_), channel_id=1, source_target_pairs={{0,16},{1,17},{2,18},{3,19},{4,20},{5,21},{6,22},{7,23},{8,24},{9,... | collective-permute-start | bytes 1572872 | tf_op jit(solution)/shard_map/ppermute | solution.py:46
  174.7 14.6 %collective-permute-start.34 = (bf16[4,64,2048]{2,1,0:T(8,128)(2,1)S(1)}, bf16[4,64,2048]{2,1,0:T(8,128)(2,1)S(1)}, u32[]{:S(2)}, u32[]{:S(2)}) collective-permute-start(bf16[4,64,2048]{2,1,0:T(8,128)(2,1)S(1)} %collective-permute-done.29.refs_2_), channel_id=1, source_target_pairs={{0,1},{1,0},{2,3},{3,2},{4,5},{5,4},{6,7},{7,6},{8,9},{9,8},{10,11... | collective-permute-start | bytes 3145736 | tf_op jit(solution)/shard_map/ppermute | solution.py:53
  175.2 14.1 %collective-permute-start.35 = (bf16[4,64,2048]{2,1,0:T(8,128)(2,1)S(1)}, bf16[4,64,2048]{2,1,0:T(8,128)(2,1)}, u32[]{:S(2)}, u32[]{:S(2)}) collective-permute-start(bf16[4,64,2048]{2,1,0:T(8,128)(2,1)S(1)} %collective-permute-done.30.refs_3_), channel_id=1, source_target_pairs={{0,1},{1,0},{2,3},{3,2},{4,5},{5,4},{6,7},{7,6},{8,9},{9,8},{10,11... | collective-permute-start | bytes 3145736 | tf_op jit(solution)/shard_map/ppermute | solution.py:53
  177.8 14.2 %collective-permute-start.36 = (bf16[4,256,512]{2,1,0:T(8,128)(2,1)}, bf16[4,256,512]{2,1,0:T(8,128)(2,1)S(1)}, u32[]{:S(2)}, u32[]{:S(2)}) collective-permute-start(bf16[4,256,512]{2,1,0:T(8,128)(2,1)} %rolled.7.refs_0_), channel_id=1, source_target_pairs={{0,2},{1,5},{2,0},{3,7},{4,6},{5,1},{6,4},{7,3},{8,10},{9,13},{10,... | collective-permute-start | bytes 3145736 | tf_op jit(solution)/shard_map/ppermute | solution.py:46
  192.0 24.5 %collective-permute-start.37 = (bf16[4,256,512]{2,1,0:T(8,128)(2,1)S(1)}, bf16[4,256,512]{2,1,0:T(8,128)(2,1)S(1)}, u32[]{:S(2)}, u32[]{:S(2)}) collective-permute-start(bf16[4,256,512]{2,1,0:T(8,128)(2,1)S(1)} %copy-done.2), channel_id=1, source_target_pairs={{0,4},{1,3},{2,6},{3,1},{4,0},{5,7},{6,2},{7,5},{8,12},{9,11},{10,... | collective-permute-start | bytes 3145736 | tf_op jit(solution)/shard_map/ppermute | solution.py:46
  193.2 24.0 %collective-permute-start.38 = (bf16[4,256,512]{2,1,0:T(8,128)(2,1)S(1)}, bf16[4,256,512]{2,1,0:T(8,128)(2,1)S(1)}, u32[]{:S(2)}, u32[]{:S(2)}) collective-permute-start(bf16[4,256,512]{2,1,0:T(8,128)(2,1)S(1)} %collective-permute-done.36.refs_1_), channel_id=1, source_target_pairs={{0,4},{1,3},{2,6},{3,1},{4,0},{5,7},{6,2},{7,5},{8,12},{9,11},{10,... | collective-permute-start | bytes 3145736 | tf_op jit(solution)/shard_map/ppermute | solution.py:46
  193.5 23.7 %collective-permute-start.39 = (bf16[4,256,512]{2,1,0:T(8,128)(2,1)S(1)}, bf16[4,256,512]{2,1,0:T(8,128)(2,1)S(1)}, u32[]{:S(2)}, u32[]{:S(2)}) collective-permute-start(bf16[4,256,512]{2,1,0:T(8,128)(2,1)S(1)} %copy-done.2), channel_id=1, source_target_pairs={{0,1},{1,0},{2,3},{3,2},{4,5},{5,4},{6,7},{7,6},{8,9},{9,8},{10,11... | collective-permute-start | bytes 3145736 | tf_op jit(solution)/shard_map/ppermute | solution.py:53
  195.4 21.8 %collective-permute-start.40 = (bf16[4,256,512]{2,1,0:T(8,128)(2,1)S(1)}, bf16[4,256,512]{2,1,0:T(8,128)(2,1)}, u32[]{:S(2)}, u32[]{:S(2)}) collective-permute-start(bf16[4,256,512]{2,1,0:T(8,128)(2,1)S(1)} %collective-permute-done.36.refs_1_), channel_id=1, source_target_pairs={{0,1},{1,0},{2,3},{3,2},{4,5},{5,4},{6,7},{7,6},{8,9},{9,8},{10,11... | collective-permute-start | bytes 3145736 | tf_op jit(solution)/shard_map/ppermute | solution.py:53
  217.2 12.1 %collective-permute-start.41 = (bf16[4,256,512]{2,1,0:T(8,128)(2,1)S(1)}, bf16[4,256,512]{2,1,0:T(8,128)(2,1)S(1)}, u32[]{:S(2)}, u32[]{:S(2)}) collective-permute-start(bf16[4,256,512]{2,1,0:T(8,128)(2,1)S(1)} %collective-permute-done.37.refs_2_), channel_id=1, source_target_pairs={{0,1},{1,0},{2,3},{3,2},{4,5},{5,4},{6,7},{7,6},{8,9},{9,8},{10,11... | collective-permute-start | bytes 3145736 | tf_op jit(solution)/shard_map/ppermute | solution.py:53
  219.5 9.9 %collective-permute-start.42 = (bf16[4,256,512]{2,1,0:T(8,128)(2,1)S(1)}, bf16[4,256,512]{2,1,0:T(8,128)(2,1)S(1)}, u32[]{:S(2)}, u32[]{:S(2)}) collective-permute-start(bf16[4,256,512]{2,1,0:T(8,128)(2,1)S(1)} %collective-permute-done.38.refs_3_), channel_id=1, source_target_pairs={{0,1},{1,0},{2,3},{3,2},{4,5},{5,4},{6,7},{7,6},{8,9},{9,8},{10,11... | collective-permute-start | bytes 3145736 | tf_op jit(solution)/shard_map/ppermute | solution.py:53
  229.4 16.2 %collective-permute-start.43 = (bf16[4,4,256,512]{3,2,1,0:T(8,128)(2,1)}, bf16[4,4,256,512]{3,2,1,0:T(8,128)(2,1)}, u32[]{:S(2)}, u32[]{:S(2)}) collective-permute-start(bf16[4,4,256,512]{3,2,1,0:T(8,128)(2,1)} %wide_chunks.2), channel_id=1, source_target_pairs={{0,1},{1,0},{2,3},{3,2},{4,5},{5,4},{6,7},{7,6},{8,9},{9,8},{10,11... | collective-permute-start | bytes 12582920 | tf_op jit(solution)/shard_map/ppermute | solution.py:53
  266.9 25.7 %collective-permute-start.44 = (bf16[4,4,64,2048]{3,2,1,0:T(8,128)(2,1)}, bf16[4,4,64,2048]{3,2,1,0:T(8,128)(2,1)}, u32[]{:S(2)}, u32[]{:S(2)}) collective-permute-start(bf16[4,4,64,2048]{3,2,1,0:T(8,128)(2,1)} %row_chunks.2), channel_id=1, source_target_pairs={{0,1},{1,0},{2,3},{3,2},{4,5},{5,4},{6,7},{7,6},{8,9},{9,8},{10,11... | collective-permute-start | bytes 12582920 | tf_op jit(solution)/shard_map/ppermute | solution.py:53
  267.4 22.0 %collective-permute-start.45 = (bf16[4,256,512]{2,1,0:T(8,128)(2,1)S(1)}, bf16[4,256,512]{2,1,0:T(8,128)(2,1)S(1)}, u32[]{:S(2)}, u32[]{:S(2)}) collective-permute-start(bf16[4,256,512]{2,1,0:T(8,128)(2,1)S(1)} %copy-done.68), channel_id=1, source_target_pairs={{0,4},{1,3},{2,6},{3,1},{4,0},{5,7},{6,2},{7,5},{8,12},{9,11},{10,... | collective-permute-start | bytes 3145736 | tf_op jit(solution)/shard_map/ppermute | solution.py:46
  268.6 24.0 %collective-permute-start.46 = (bf16[4,256,512]{2,1,0:T(8,128)(2,1)S(1)}, bf16[4,256,512]{2,1,0:T(8,128)(2,1)S(1)}, u32[]{:S(2)}, u32[]{:S(2)}) collective-permute-start(bf16[4,256,512]{2,1,0:T(8,128)(2,1)S(1)} %copy-done.67), channel_id=1, source_target_pairs={{0,4},{1,3},{2,6},{3,1},{4,0},{5,7},{6,2},{7,5},{8,12},{9,11},{10,... | collective-permute-start | bytes 3145736 | tf_op jit(solution)/shard_map/ppermute | solution.py:46
  292.8 17.7 %collective-permute-start.47 = (bf16[4,256,512]{2,1,0:T(8,128)(2,1)S(1)}, bf16[4,256,512]{2,1,0:T(8,128)(2,1)}, u32[]{:S(2)}, u32[]{:S(2)}) collective-permute-start(bf16[4,256,512]{2,1,0:T(8,128)(2,1)S(1)} %add_convert_fusion.3), channel_id=1, source_target_pairs={{0,2},{1,5},{2,0},{3,7},{4,6},{5,1},{6,4},{7,3},{8,10},{9,13},{10,... | collective-permute-start | bytes 3145736 | tf_op jit(solution)/shard_map/ppermute | solution.py:46
  310.5 19.8 %collective-permute-start.49 = (bf16[4,64,2048]{2,1,0:T(8,128)(2,1)}, bf16[4,64,2048]{2,1,0:T(8,128)(2,1)S(1)}, u32[]{:S(2)}, u32[]{:S(2)}) collective-permute-start(bf16[4,64,2048]{2,1,0:T(8,128)(2,1)} %get-tuple-element.382), channel_id=1, source_target_pairs={{0,4},{1,3},{2,6},{3,1},{4,0},{5,7},{6,2},{7,5},{8,12},{9,11},{10,... | collective-permute-start | bytes 3145736 | tf_op jit(solution)/shard_map/ppermute | solution.py:46
  312.9 17.4 %collective-permute-start.48 = (bf16[256,512]{1,0:T(8,128)(2,1)S(1)}, bf16[256,512]{1,0:T(8,128)(2,1)S(1)}, u32[]{:S(2)}, u32[]{:S(2)}) collective-permute-start(bf16[256,512]{1,0:T(8,128)(2,1)S(1)} %get-tuple-element.512), channel_id=1, source_target_pairs={{0,16},{1,17},{2,18},{3,19},{4,20},{5,21},{6,22},{7,23},{8,24},{9,... | collective-permute-start | bytes 786440 | tf_op jit(solution)/shard_map/ppermute | solution.py:46
  330.8 18.8 %collective-permute-start.50 = (bf16[4,64,2048]{2,1,0:T(8,128)(2,1)S(1)}, bf16[4,64,2048]{2,1,0:T(8,128)(2,1)S(1)}, u32[]{:S(2)}, u32[]{:S(2)}) collective-permute-start(bf16[4,64,2048]{2,1,0:T(8,128)(2,1)S(1)} %add_convert_fusion.1), channel_id=1, source_target_pairs={{0,2},{1,5},{2,0},{3,7},{4,6},{5,1},{6,4},{7,3},{8,10},{9,13},{10,... | collective-permute-start | bytes 3145736 | tf_op jit(solution)/shard_map/ppermute | solution.py:46
  349.6 15.1 %collective-permute-start.53 = (bf16[4,64,2048]{2,1,0:T(8,128)(2,1)}, bf16[4,64,2048]{2,1,0:T(8,128)(2,1)S(1)}, u32[]{:S(2)}, u32[]{:S(2)}) collective-permute-start(bf16[4,64,2048]{2,1,0:T(8,128)(2,1)} %get-tuple-element.398), channel_id=1, source_target_pairs={{0,4},{1,3},{2,6},{3,1},{4,0},{5,7},{6,2},{7,5},{8,12},{9,11},{10,... | collective-permute-start | bytes 3145736 | tf_op jit(solution)/shard_map/ppermute | solution.py:46
  349.8 13.4 %collective-permute-start.51 = (bf16[256,512]{1,0:T(8,128)(2,1)S(1)}, bf16[256,512]{1,0:T(8,128)(2,1)S(1)}, u32[]{:S(2)}, u32[]{:S(2)}) collective-permute-start(bf16[256,512]{1,0:T(8,128)(2,1)S(1)} %get-tuple-element.395), channel_id=1, source_target_pairs={{0,16},{1,17},{2,18},{3,19},{4,20},{5,21},{6,22},{7,23},{8,24},{9,... | collective-permute-start | bytes 786440 | tf_op jit(solution)/shard_map/ppermute | solution.py:46
  352.2 11.0 %collective-permute-start.52 = (bf16[256,512]{1,0:T(8,128)(2,1)S(1)}, bf16[256,512]{1,0:T(8,128)(2,1)S(1)}, u32[]{:S(2)}, u32[]{:S(2)}) collective-permute-start(bf16[256,512]{1,0:T(8,128)(2,1)S(1)} %add_convert_fusion.13), channel_id=1, source_target_pairs={{0,8},{1,9},{2,10},{3,11},{4,12},{5,13},{6,14},{7,15},{8,0},{9,1},... | collective-permute-start | bytes 786440 | tf_op jit(solution)/shard_map/ppermute | solution.py:46
  365.6 23.7 %collective-permute-start.54 = (bf16[4,4,64,1280]{3,2,1,0:T(8,128)(2,1)}, bf16[4,4,64,1280]{3,2,1,0:T(8,128)(2,1)S(1)}, u32[]{:S(2)}, u32[]{:S(2)}) collective-permute-start(bf16[4,4,64,1280]{3,2,1,0:T(8,128)(2,1)} %heads_chunks.4), channel_id=1, source_target_pairs={{0,1},{1,0},{2,3},{3,2},{4,5},{5,4},{6,7},{7,6},{8,9},{9,8},{10,11... | collective-permute-start | bytes 7864328 | tf_op jit(solution)/shard_map/ppermute | solution.py:53
  369.6 19.7 %collective-permute-start.55 = (bf16[64,2048]{1,0:T(8,128)(2,1)S(1)}, bf16[64,2048]{1,0:T(8,128)(2,1)S(1)}, u32[]{:S(2)}, u32[]{:S(2)}) collective-permute-start(bf16[64,2048]{1,0:T(8,128)(2,1)S(1)} %get-tuple-element.508), channel_id=1, source_target_pairs={{0,16},{1,17},{2,18},{3,19},{4,20},{5,21},{6,22},{7,23},{8,24},{9,... | collective-permute-start | bytes 786440 | tf_op jit(solution)/shard_map/ppermute | solution.py:46
  371.7 17.6 %collective-permute-start.56 = (bf16[256,512]{1,0:T(8,128)(2,1)S(1)}, bf16[256,512]{1,0:T(8,128)(2,1)S(1)}, u32[]{:S(2)}, u32[]{:S(2)}) collective-permute-start(bf16[256,512]{1,0:T(8,128)(2,1)S(1)} %get-tuple-element.496), channel_id=1, source_target_pairs={{0,1},{1,0},{2,3},{3,2},{4,5},{5,4},{6,7},{7,6},{8,9},{9,8},{10,11... | collective-permute-start | bytes 786440 | tf_op jit(solution)/shard_map/ppermute | solution.py:53
  401.7 21.2 %collective-permute-start.57 = (bf16[4,64,1280]{2,1,0:T(8,128)(2,1)}, bf16[4,64,1280]{2,1,0:T(8,128)(2,1)S(1)}, u32[]{:S(2)}, u32[]{:S(2)}) collective-permute-start(bf16[4,64,1280]{2,1,0:T(8,128)(2,1)} %get-tuple-element.421), channel_id=1, source_target_pairs={{0,4},{1,3},{2,6},{3,1},{4,0},{5,7},{6,2},{7,5},{8,12},{9,11},{10,... | collective-permute-start | bytes 1966088 | tf_op jit(solution)/shard_map/ppermute | solution.py:46
  402.9 20.1 %collective-permute-start.58 = (bf16[4,64,1280]{2,1,0:T(8,128)(2,1)}, bf16[4,64,1280]{2,1,0:T(8,128)(2,1)S(1)}, u32[]{:S(2)}, u32[]{:S(2)}) collective-permute-start(bf16[4,64,1280]{2,1,0:T(8,128)(2,1)} %get-tuple-element.422), channel_id=1, source_target_pairs={{0,4},{1,3},{2,6},{3,1},{4,0},{5,7},{6,2},{7,5},{8,12},{9,11},{10,... | collective-permute-start | bytes 1966088 | tf_op jit(solution)/shard_map/ppermute | solution.py:46
  403.2 19.7 %collective-permute-start.59 = (bf16[64,2048]{1,0:T(8,128)(2,1)S(1)}, bf16[64,2048]{1,0:T(8,128)(2,1)S(1)}, u32[]{:S(2)}, u32[]{:S(2)}) collective-permute-start(bf16[64,2048]{1,0:T(8,128)(2,1)S(1)} %get-tuple-element.423), channel_id=1, source_target_pairs={{0,16},{1,17},{2,18},{3,19},{4,20},{5,21},{6,22},{7,23},{8,24},{9,... | collective-permute-start | bytes 786440 | tf_op jit(solution)/shard_map/ppermute | solution.py:46
  403.8 19.1 %collective-permute-start.60 = (bf16[64,2048]{1,0:T(8,128)(2,1)S(1)}, bf16[64,2048]{1,0:T(8,128)(2,1)S(1)}, u32[]{:S(2)}, u32[]{:S(2)}) collective-permute-start(bf16[64,2048]{1,0:T(8,128)(2,1)S(1)} %add_convert_fusion.11), channel_id=1, source_target_pairs={{0,8},{1,9},{2,10},{3,11},{4,12},{5,13},{6,14},{7,15},{8,0},{9,1},... | collective-permute-start | bytes 786440 | tf_op jit(solution)/shard_map/ppermute | solution.py:46
  431.0 11.3 %collective-permute-start.62 = (bf16[4,4,64,768]{3,2,1,0:T(8,128)(2,1)}, bf16[4,4,64,768]{3,2,1,0:T(8,128)(2,1)}, u32[]{:S(2)}, u32[]{:S(2)}) collective-permute-start(bf16[4,4,64,768]{3,2,1,0:T(8,128)(2,1)} %heads_chunks.6), channel_id=1, source_target_pairs={{0,1},{1,0},{2,3},{3,2},{4,5},{5,4},{6,7},{7,6},{8,9},{9,8},{10,11... | collective-permute-start | bytes 4718600 | tf_op jit(solution)/shard_map/ppermute | solution.py:53
  432.5 9.8 %collective-permute-start.63 = (bf16[4,64,1280]{2,1,0:T(8,128)(2,1)S(1)}, bf16[4,64,1280]{2,1,0:T(8,128)(2,1)S(1)}, u32[]{:S(2)}, u32[]{:S(2)}) collective-permute-start(bf16[4,64,1280]{2,1,0:T(8,128)(2,1)S(1)} %add_convert_fusion.5), channel_id=1, source_target_pairs={{0,2},{1,5},{2,0},{3,7},{4,6},{5,1},{6,4},{7,3},{8,10},{9,13},{10,... | collective-permute-start | bytes 1966088 | tf_op jit(solution)/shard_map/ppermute | solution.py:46
  444.0 17.9 %collective-permute-start.64 = (bf16[4,64,768]{2,1,0:T(8,128)(2,1)S(1)}, bf16[4,64,768]{2,1,0:T(8,128)(2,1)S(1)}, u32[]{:S(2)}, u32[]{:S(2)}) collective-permute-start(bf16[4,64,768]{2,1,0:T(8,128)(2,1)S(1)} %add_convert_fusion.9), channel_id=1, source_target_pairs={{0,4},{1,3},{2,6},{3,1},{4,0},{5,7},{6,2},{7,5},{8,12},{9,11},{10,... | collective-permute-start | bytes 1179656 | tf_op jit(solution)/shard_map/ppermute | solution.py:46
  445.3 16.5 %collective-permute-start.65 = (bf16[4,64,768]{2,1,0:T(8,128)(2,1)S(1)}, bf16[4,64,768]{2,1,0:T(8,128)(2,1)S(1)}, u32[]{:S(2)}, u32[]{:S(2)}) collective-permute-start(bf16[4,64,768]{2,1,0:T(8,128)(2,1)S(1)} %add_convert_fusion.8), channel_id=1, source_target_pairs={{0,4},{1,3},{2,6},{3,1},{4,0},{5,7},{6,2},{7,5},{8,12},{9,11},{10,... | collective-permute-start | bytes 1179656 | tf_op jit(solution)/shard_map/ppermute | solution.py:46
  446.0 15.9 %collective-permute-start.66 = (bf16[64,1280]{1,0:T(8,128)(2,1)S(1)}, bf16[64,1280]{1,0:T(8,128)(2,1)S(1)}, u32[]{:S(2)}, u32[]{:S(2)}) collective-permute-start(bf16[64,1280]{1,0:T(8,128)(2,1)S(1)} %get-tuple-element.516), channel_id=1, source_target_pairs={{0,16},{1,17},{2,18},{3,19},{4,20},{5,21},{6,22},{7,23},{8,24},{9,... | collective-permute-start | bytes 491528 | tf_op jit(solution)/shard_map/ppermute | solution.py:46
  461.9 17.6 %collective-permute-start.71 = (bf16[512,1024]{1,0:T(8,128)(2,1)}, bf16[512,1024]{1,0:T(8,128)(2,1)S(1)}, u32[]{:S(2)}, u32[]{:S(2)}) collective-permute-start(bf16[512,1024]{1,0:T(8,128)(2,1)} %get-tuple-element.465), channel_id=1, source_target_pairs={{0,1},{1,0},{2,3},{3,2},{4,5},{5,4},{6,7},{7,6},{8,9},{9,8},{10,11... | collective-permute-start | bytes 3145736 | tf_op jit(solution)/shard_map/ppermute | solution.py:53
  464.2 15.3 %collective-permute-start.67 = (bf16[4,64,768]{2,1,0:T(8,128)(2,1)S(1)}, bf16[4,64,768]{2,1,0:T(8,128)(2,1)S(1)}, u32[]{:S(2)}, u32[]{:S(2)}) collective-permute-start(bf16[4,64,768]{2,1,0:T(8,128)(2,1)S(1)} %add_convert_fusion.7), channel_id=1, source_target_pairs={{0,2},{1,5},{2,0},{3,7},{4,6},{5,1},{6,4},{7,3},{8,10},{9,13},{10,... | collective-permute-start | bytes 1179656 | tf_op jit(solution)/shard_map/ppermute | solution.py:46
  465.1 14.4 %collective-permute-start.68 = (bf16[64,1280]{1,0:T(8,128)(2,1)S(1)}, bf16[64,1280]{1,0:T(8,128)(2,1)S(1)}, u32[]{:S(2)}, u32[]{:S(2)}) collective-permute-start(bf16[64,1280]{1,0:T(8,128)(2,1)S(1)} %get-tuple-element.459), channel_id=1, source_target_pairs={{0,16},{1,17},{2,18},{3,19},{4,20},{5,21},{6,22},{7,23},{8,24},{9,... | collective-permute-start | bytes 491528 | tf_op jit(solution)/shard_map/ppermute | solution.py:46
  466.7 12.8 %collective-permute-start.69 = (bf16[64,1280]{1,0:T(8,128)(2,1)S(1)}, bf16[64,1280]{1,0:T(8,128)(2,1)S(1)}, u32[]{:S(2)}, u32[]{:S(2)}) collective-permute-start(bf16[64,1280]{1,0:T(8,128)(2,1)S(1)} %add_convert_fusion.15), channel_id=1, source_target_pairs={{0,8},{1,9},{2,10},{3,11},{4,12},{5,13},{6,14},{7,15},{8,0},{9,1},... | collective-permute-start | bytes 491528 | tf_op jit(solution)/shard_map/ppermute | solution.py:46
  468.2 11.2 %collective-permute-start.70 = (f32[8,1024]{1,0:T(8,128)}, f32[8,1024]{1,0:T(8,128)S(1)}, u32[]{:S(2)}, u32[]{:S(2)}) collective-permute-start(f32[8,1024]{1,0:T(8,128)} %sums.1), channel_id=1, source_target_pairs={{0,16},{1,17},{2,18},{3,19},{4,20},{5,21},{6,22},{7,23},{8,24},{9,... | collective-permute-start | bytes 98312 | tf_op jit(solution)/shard_map/ppermute | solution.py:866
  479.6 13.8 %collective-permute-start.75 = (bf16[64,1280]{1,0:T(8,128)(2,1)S(1)}, bf16[64,1280]{1,0:T(8,128)(2,1)S(1)}, u32[]{:S(2)}, u32[]{:S(2)}) collective-permute-start(bf16[64,1280]{1,0:T(8,128)(2,1)S(1)} %add_convert_fusion.14), channel_id=1, source_target_pairs={{0,1},{1,0},{2,3},{3,2},{4,5},{5,4},{6,7},{7,6},{8,9},{9,8},{10,11... | collective-permute-start | bytes 491528 | tf_op jit(solution)/shard_map/ppermute | solution.py:53
  481.1 13.4 %collective-permute-start.72 = (bf16[512,1024]{1,0:T(8,128)(2,1)}, bf16[512,1024]{1,0:T(8,128)(2,1)S(1)}, u32[]{:S(2)}, u32[]{:S(2)}) collective-permute-start(bf16[512,1024]{1,0:T(8,128)(2,1)} %down.2), channel_id=1, source_target_pairs={{0,1},{1,0},{2,3},{3,2},{4,5},{5,4},{6,7},{7,6},{8,9},{9,8},{10,11... | collective-permute-start | bytes 3145736 | tf_op jit(solution)/shard_map/ppermute | solution.py:53
  481.3 13.2 %collective-permute-start.73 = (f32[12,1024]{1,0:T(8,128)S(1)}, f32[12,1024]{1,0:T(8,128)}, u32[]{:S(2)}, u32[]{:S(2)}) collective-permute-start(f32[12,1024]{1,0:T(8,128)S(1)} %pad_maximum_fusion.15), channel_id=1, source_target_pairs={{0,8},{1,9},{2,10},{3,11},{4,12},{5,13},{6,14},{7,15},{8,0},{9,1},... | collective-permute-start | bytes 147464 | tf_op jit(solution)/shard_map/ppermute | solution.py:866
  482.3 12.2 %collective-permute-start.74 = (bf16[64,768]{1,0:T(8,128)(2,1)S(1)}, bf16[64,768]{1,0:T(8,128)(2,1)}, u32[]{:S(2)}, u32[]{:S(2)}) collective-permute-start(bf16[64,768]{1,0:T(8,128)(2,1)S(1)} %get-tuple-element.524), channel_id=1, source_target_pairs={{0,16},{1,17},{2,18},{3,19},{4,20},{5,21},{6,22},{7,23},{8,24},{9,... | collective-permute-start | bytes 294920 | tf_op jit(solution)/shard_map/ppermute | solution.py:46
  (92 other events, 813.8 us)

commit v3 on v2

--- a/solution.py
+++ b/solution.py
@@ -20,7 +20,9 @@
 LANES = 128
 ROWS = 256
 VMEM_LIMIT = 58 << 20
-ANY = pl.BlockSpec(memory_space=pl.ANY)
+ROOM = 14 << 20
+ANY = pl.BlockSpec(memory_space=pltpu.HBM)
+TIGHT = ("qkv", "attend", "attend_back", "heads_chunks", "heads_back", "rolled", "out")
 
 
 class Grid:
@@ -35,13 +37,13 @@
     def join(self, z, a, b):
         return (z * self.n + a) * self.n + b
 
-    def shift(self, v, phase, k):
+    def shift(self, v, phase, k, flip=False):
         pairs = []
         for d in range(self.groups):
             for b in range(self.blocks):
                 at = list(self.coords(d))
                 axis = 0 if phase == 0 else (3 - phase if b % 2 == 0 else phase)
-                at[axis] = (at[axis] - k) % self.n if axis else at[axis] ^ k
+                at[axis] = at[axis] ^ k if flip else (at[axis] - k) % (self.n if axis else self.n0)
                 pairs.append((d * self.blocks + b, self.join(*at) * self.blocks + b))
         return lax.ppermute(v, AXES, pairs)
 
@@ -85,14 +87,35 @@
 SCALARS = pl.BlockSpec(memory_space=pltpu.SMEM)
 
 
-def call(kernel, name, grid, ins, outs, shapes, scratch, flops, moved, prefetch=0):
+def vmem_bytes(specs, types, scratch, room):
+    total = room
+    for block, dtype in zip(specs, types):
+        if block.block_shape is not None:
+            rows = math.prod(block.block_shape[:-1])
+            total += 2 * rows * max(block.block_shape[-1], LANES) * np.dtype(dtype).itemsize
+    for v in scratch:
+        if len(v.shape) > 1:
+            total += math.prod(v.shape) * np.dtype(v.dtype).itemsize
+    return min(total, VMEM_LIMIT)
+
+
+def call(kernel, name, grid, ins, outs, shapes, scratch, flops, moved, prefetch=0, room=ROOM):
+    def run(*args):
+        types = [v.dtype for v in args[prefetch:]] + [t for _, t in shapes]
+        limit = vmem_bytes(list(ins) + list(outs), types, scratch, room) if name in TIGHT else VMEM_LIMIT
+        return kernel_call(kernel, name, grid, ins, outs, shapes, scratch, flops, moved, prefetch, limit)(*args)
+
+    return run
+
+
+def kernel_call(kernel, name, grid, ins, outs, shapes, scratch, flops, moved, prefetch, limit):
     return pl.pallas_call(
         kernel,
         grid_spec=pltpu.PrefetchScalarGridSpec(
             num_scalar_prefetch=prefetch, grid=grid, in_specs=ins, out_specs=outs, scratch_shapes=scratch
         ),
         out_shape=[jax.ShapeDtypeStruct(s, t) for s, t in shapes],
-        compiler_params=pltpu.CompilerParams(vmem_limit_bytes=VMEM_LIMIT),
+        compiler_params=pltpu.CompilerParams(vmem_limit_bytes=limit),
         cost_estimate=pl.CostEstimate(flops=flops, bytes_accessed=moved, transcendentals=0),
         name=name,
     )
@@ -153,7 +176,7 @@
     k, out = 0, refs[-1]
     for part in refs[:-1]:
         for i in range(part.shape[0]):
-            out[place[0] ^ k] = part[i]
+            out[lax.rem(place[0] + k, out.shape[0])] = part[i]
             k += 1
 
 
@@ -217,7 +240,7 @@
         outs = [whole((rows, width)), whole((width, rows))] + outs
         shapes = [((rows, width), BF16), ((width, rows), BF16)] + shapes
     return call(
-        functools.partial(qkv_kernel, len(pieces), span, first), "qkv", (2,),
+        functools.partial(qkv_kernel, len(pieces), span, first), "qkv_first" if first else "qkv", (2,),
         [SCALARS] + [whole(v.shape) for v in source] + [whole((rows, LANES))] * 2 + [ANY] * len(pieces),
         outs, shapes,
         [pltpu.VMEM(matrix_shape(grid, weight), BF16), pltpu.SemaphoreType.DMA((2,))],
@@ -396,16 +419,17 @@
     )(places, x, gain, bias, *pieces, *mixed)
 
 
-def up_kernel(count, span, block, place, normed, *refs):
+def up_kernel(count, span, block, side, place, normed, *refs):
     pieces = refs[:count]
-    active, slope, matrix, sems = refs[count:]
-    j = pl.program_id(0)
+    active, slope, matrix, sems = refs[-4:]
+    j, steps = pl.program_id(0), pl.num_programs(0)
 
     @pl.when(j == 0)
     def _():
-        start_blocks(place, pieces, span, matrix, sems, block)
-
-    start = pl.multiple_of(j * block, block)
+        for i in range(span[1] // block):
+            fetch(place, pieces, span, matrix, sems.at[i], side, i * block, block)
+
+    start = pl.multiple_of((side * steps + j) * block, block)
     arrived(matrix, sems.at[j], start, block)
     weight = columns(matrix, start, block)
     root = math.sqrt(2.0 / math.pi)
@@ -421,18 +445,26 @@
         ).astype(BF16)
 
 
-def up_product(grid, places, normed, weight, block=512):
+def up_product(grid, places, normed, weight, side, before=(), block=512):
     rows, width = normed.shape
     pieces, span = weight
-    full = 2 * span[1]
-    out = spec((rows, block), lambda j: (0, j))
-    return call(
-        functools.partial(up_kernel, len(pieces), span, block), "up", (full // block,),
-        [SCALARS, whole(normed.shape)] + [ANY] * len(pieces),
-        [out, out], [((rows, full), BF16)] * 2,
-        [pltpu.VMEM(matrix_shape(grid, weight), BF16), pltpu.SemaphoreType.DMA((full // block,))],
-        2 * rows * width * full, 2 * width * full + 4 * rows * full,
-    )(places, normed, *pieces)
+    full, per = 2 * span[1], span[1] // block
+    out = spec((rows, block), lambda j: (0, side * per + j))
+    kernel = functools.partial(up_kernel, len(pieces), span, block, side)
+    return pl.pallas_call(
+        kernel,
+        grid=(per,),
+        in_specs=[SCALARS, whole(normed.shape)] + [ANY] * (len(pieces) + len(before)),
+        out_specs=[out, out],
+        out_shape=[jax.ShapeDtypeStruct((rows, full), BF16)] * 2,
+        scratch_shapes=[pltpu.VMEM(matrix_shape(grid, weight), BF16), pltpu.SemaphoreType.DMA((per,))],
+        input_output_aliases={2 + len(pieces) + i: i for i in range(len(before))},
+        compiler_params=pltpu.CompilerParams(vmem_limit_bytes=VMEM_LIMIT),
+        cost_estimate=pl.CostEstimate(
+            flops=rows * width * full, bytes_accessed=width * full + 2 * rows * full, transcendentals=0
+        ),
+        name="up",
+    )(places, normed, *pieces, *before)
 
 
 def start_levels(place, pieces, span, matrix, sems):
@@ -555,7 +587,7 @@
         [((rows // outs, width), BF16)] * outs + [((2, width), F32)],
         [pltpu.VMEM((*outer, full), BF16), pltpu.VMEM((len(starts), rows, block), BF16),
          pltpu.VMEM(x.shape, F32), pltpu.SemaphoreType.DMA((len(starts),)), pltpu.SemaphoreType.DMA((len(starts),))],
-        2 * rows * width * full, 2 * width * full + 2 * rows * full + 6 * rows * width,
+        2 * rows * width * full, 2 * width * full + 2 * rows * full + 6 * rows * width, room=24 << 20,
     )(places, x, gain, base, *[v for w in weights for v in w[0]], *grads)
 
 
@@ -743,7 +775,7 @@
     def __init__(self, grid, line, mine):
         self.grid, self.line, self.mine = grid, line, mine[None]
         self.parts = [self.mine]
-        self.place = grid.coords(lax.axis_index("dp"))[0]
+        self.place, self.column = grid.coords(lax.axis_index("dp"))[0], None
 
     def outer(self):
         self.mine = self.line.at(self.mine)
@@ -751,15 +783,18 @@
         return self.parts[1:]
 
     def outer_step(self):
-        held = self.parts[0] if len(self.parts) == 1 else jnp.concatenate(self.line.at(self.parts))
-        if held.shape[0] == self.grid.n0:
+        if len(self.parts) == self.grid.n0:
             return ()
-        held = self.line.at(held)
-        self.parts = [held, self.grid.shift(held, 0, held.shape[0])]
-        return self.parts[1:]
+        self.parts.append(self.grid.shift(self.line.at(self.parts[-1]), 0, 1))
+        return self.parts[-1]
+
+    def prepare(self):
+        self.column = rolled(self.line.at(self.parts), self.place)
 
     def inner(self):
-        column = self.line.at(rolled(self.line.at(self.parts), self.place))
+        if self.column is None:
+            self.prepare()
+        column = self.line.at(self.column)
         self.level = [column] + [self.grid.shift(column, 1, k) for k in range(1, self.grid.n)]
         self.pieces, self.swapped = list(self.level), {}
         return self.level[1:]
@@ -824,11 +859,11 @@
         here, there = pick(total, z // size), pick(total, 1 - z // size)
         self.on, self.mine = 1 - z % size, z % size
         if size == 1:
-            self.own, self.far = [here[0]], [self.grid.shift(there[0], 0, 1)]
+            self.own, self.far = [here[0]], [self.grid.shift(there[0], 0, 1, True)]
             return self.far
         self.own = [pick(here, self.mine)]
         self.onward, self.rest = pick(here, self.on), pick(there, self.mine)
-        self.far_on = self.grid.shift(pick(there, self.on), 0, size)
+        self.far_on = self.grid.shift(pick(there, self.on), 0, size, True)
         self.far = []
         return [self.far_on, self.rest]
 
@@ -836,7 +871,7 @@
         if self.grid.n0 == 2:
             return ()
         rest, onward = self.line.at(self.rest, [self.onward, self.far_on])
-        self.far = [self.grid.shift(rest, 0, 2), self.grid.shift(plus(*onward).astype(BF16), 0, 1)]
+        self.far = [self.grid.shift(rest, 0, 2, True), self.grid.shift(plus(*onward).astype(BF16), 0, 1, True)]
         return self.far
 
     def own_half(self):
@@ -955,8 +990,8 @@
     line.mark(moved, more, far, x)
 
     moved = heads_a.last()
-    swaps = heads_a.swap(0, 1)
-    later = heads_b.outer_step()
+    swaps = heads_a.swap(0)
+    more = heads_b.outer_step()
     small, far = small_step(line.at(small), bits[2])
     in_block = jnp.arange(block_len, dtype=jnp.int32)
     my_places = jnp.concatenate([core * block_len + in_block, (1 - core) * block_len + in_block])
@@ -973,17 +1008,17 @@
     length = lax.dynamic_index_in_dim(line.at(lengths), core, 0, keepdims=False)
     mask = jnp.where(key_places < length, 0.0, MASKED).astype(F32)
     mask_column = mask[:, None].astype(BF16)
-    line.mark(moved, swaps, far, tables, mask_column)
-
-    swaps = heads_a.swap(2, 3)
-    up_more = up_w.outer_step()
+    line.mark(moved, swaps, more, far, tables, mask_column)
+
+    swaps = heads_a.swap(1, 2, 3)
+    more = heads_b.outer_step()
     for bit in bits[3:]:
         small, far = small_step(line.at(small), bit)
     my_time = lax.dynamic_slice_in_dim(time_index, core, 1, 0)
     index = jnp.arange(TF, dtype=jnp.int32)
     reach = jnp.asarray(reach)
     features = line.at(time_features(my_time, (group ^ reach[index // t_rows]) * t_rows + index % t_rows))
-    line.mark(swaps, far, features, later)
+    line.mark(swaps, far, features, more)
     small = line.at(small)
     time_matrix = small[:, :, :t_cols].reshape(TF, t_cols).astype(F32)
     norms = small[:, : 4 * per // LANES, t_cols:].reshape(grid.groups, 4 * per).astype(F32)
@@ -997,66 +1032,81 @@
     scale1, scale2 = scales[:, :width], scales[:, width:]
     eff1, eff2 = gain1 * scale1, gain2 * scale2
     moved = heads_b.inner()
-    line.mark(eff1, eff2, bias1, bias2, up_more)
+    more = up_w.outer_step()
+    line.mark(eff1, eff2, bias1, bias2)
 
     def gathered(v):
         if ranks == 1:
             return v
         return lax.all_gather(v, "blk", axis=0, tiled=True, axis_index_groups=rank_groups(grid))
 
-    later = up_w.outer_step()
-    theirs = swapped(line.at(cotangent))
     normed1, normed1_t, packed_a = qkv_product(grid, at, line.at((x, eff1, bias1)), *tables, heads_a.weight())
     wide_a = gathered(packed_a)
-    line.mark(packed_a, moved, theirs)
+    line.mark(packed_a, moved, more)
 
     moved = heads_b.last()
     swaps = heads_b.swap(0, 1)
+    more = up_w.outer_step()
     att = {}
     packed_a, mask = line.at(packed_a, mask)
     if ranks == 1:
         wide_a = packed_a
     att[0, 0] = attend(0, packed_a, wide_a, mask[None])
-    line.mark(att[0, 0], moved, swaps)
+    line.mark(att[0, 0], swaps, more)
+
+    more = up_w.outer_step()
+    att[0, 1] = attend(1, packed_a, wide_a, line.at(mask)[None])
+    line.mark(att[0, 1], moved, more)
 
     swaps = heads_b.swap(2, 3)
+    theirs = swapped(line.at(cotangent))
+    up_w.prepare()
+    line.mark(swaps, up_w.column)
+
+    moved = up_w.inner()
+    more = down_w.outer_step()
+    (packed_b,) = qkv_product(grid, at, (line.at(normed1),), *tables, heads_b.weight(0, group_width))
+    wide_b = gathered(packed_b)
+    line.mark(packed_b, theirs, more)
+
     more = down_w.outer_step()
     cot = joined(*line.at(cotangent, theirs))
-    att[0, 1] = attend(1, packed_a, wide_a, line.at(mask)[None])
-    line.mark(att[0, 1], swaps, cot, later, more)
-
-    moved = up_w.inner()
-    later = down_w.outer_step()
-    (packed_b,) = qkv_product(grid, at, (line.at(normed1),), *tables, heads_b.weight(0, group_width))
-    wide_b = gathered(packed_b)
-    line.mark(packed_b, moved)
-
-    moved = up_w.last()
     packed_b, mask = line.at(packed_b, mask)
     if ranks == 1:
         wide_b = packed_b
     att[1, 0] = attend(0, packed_b, wide_b, mask[None])
-    line.mark(att[1, 0])
-
+    line.mark(att[1, 0], moved, more, cot)
+
+    moved = up_w.last()
     swaps = up_w.swap(0, 1)
+    more = down_w.outer_step()
     att[1, 1] = attend(1, packed_b, wide_b, line.at(mask)[None])
     mixed = [att[i][0] for i in ((0, 0), (0, 1), (1, 0), (1, 1))]
-    line.mark(att[1, 1], moved, swaps, later)
-
-    swaps = up_w.swap(2, 3)
-    moved = down_w.inner()
+    line.mark(att[1, 1], swaps, more)
+
     out_weight = heads_b.weight(group_width, width // 2)
     middle, normed2, normed2_t = out_product(grid, at, line.at(mixed), x, eff2, bias2, out_weight)
-    line.mark(normed2, swaps, moved)
+    line.mark(normed2, moved)
+
+    swaps = up_w.swap(2, 3)
+    down_w.prepare()
+    line.mark(swaps, down_w.column)
+
+    moved = down_w.inner()
+    normed2 = line.at(normed2)
+    hidden = up_product(grid, at, normed2, up_w.weight(), 0)
+    line.mark(hidden, moved)
 
     moved = down_w.last()
     swaps = down_w.swap(0, 1)
-    active, slope = up_product(grid, at, line.at(normed2), up_w.weight())
-    line.mark(active, moved, swaps)
+    active, slope = up_product(grid, at, line.at(normed2), up_w.weight(), 1, hidden)
+    line.mark(active, swaps)
+
+    (sent,) = wide_chunks(grid, at, False, *line.at(active, cot))
+    line.mark(sent, moved)
 
     swaps = down_w.swap(2, 3)
-    (sent,) = wide_chunks(grid, at, False, *line.at(active, cot))
-    line.mark(sent, swaps)
+    line.mark(swaps)
 
     push_down = Push(grid, line, line.at(sent))
     grad_hidden = hidden_back(grid, at, *line.at(cot, slope), down_w.weight())

time: 528 us -> 482 us (0.913)
  Pallas kernels: 327 us -> 276 us
  local copies, waits for them, and re-layouts: 24.4 us -> 33.2 us
  waiting for transfers between devices: 60.2 us -> 52.3 us
    pallas_call x31 -> x32, Pallas kernels: 327 us -> 276 us  [the longest x30 251 us: run(): kernel_call(kernel, name, grid, ins, outs, shapes, scratch, flops, moved,...]
    ppermute x45 -> x48, waiting for transfers between devices: 53.9 us -> 23.4 us  [shift(): return lax.ppermute(v, AXES, pairs)]
    ppermute x8, waiting for transfers between devices: 6.18 us -> 18.7 us  [doubled(): return lax.ppermute(v, AXES, pairs)]
    unnamed x151 -> x249, local copies, waits for them, and re-layouts: 7.22 us -> 17.9 us
    ppermute x28, waiting for transfers between devices: 0.08 us -> 10.2 us  [swap(): return lax.ppermute(v, AXES, pairs)]
    ppermute x45 -> x48, starting transfers between devices: 38 us -> 46.4 us  [shift(): return lax.ppermute(v, AXES, pairs)]
  transfers between devices with their start and end apart: 82 -> 85, of which waited for: 18 -> 20; matrix products, arithmetic and copies ran while one was open for 7% -> 8% of each run, Pallas kernels for 56% -> 52%
where the time goes in v3:
time: 482 us; the launch traced here: 475 us
  Pallas kernels  276 us (57%)
  starting transfers between devices  78.7 us (16%)
  waiting for transfers between devices  52.3 us (11%)
  local copies, waits for them, and re-layouts  33.2 us (7%)
  other arithmetic  29.5 us (6%)
    pallas_call x30, Pallas kernels, run(): kernel_call(kernel, name, grid, ins, outs, shapes, scratch, flops, moved,...  251 us
    ppermute x48, starting transfers between devices, shift(): return lax.ppermute(v, AXES, pairs)  46.4 us
    pallas_call x2, Pallas kernels, up_product(): pl.pallas_call(kernel, grid=(per,), in_specs=[SCALARS, whole(normed.shape...  25.3 us
    ppermute x28, starting transfers between devices, swap(): return lax.ppermute(v, AXES, pairs)  24.1 us
    ppermute x48, waiting for transfers between devices, shift(): return lax.ppermute(v, AXES, pairs)  23.4 us
    ppermute x8, waiting for transfers between devices, doubled(): return lax.ppermute(v, AXES, pairs)  18.7 us
    unnamed x249, local copies, waits for them, and re-layouts  17.9 us
    ppermute x28, waiting for transfers between devices, swap(): return lax.ppermute(v, AXES, pairs)  10.2 us
  transfers between devices with their start and end apart: 85, of which 20 were waited for; matrix products, arithmetic and copies ran while one was open for 8% of the time, Pallas kernels for 52%

profile of v3, /device:TPU:1, one launch (start us, length us, event | category | flops | bytes accessed | tf_op | source)
XLA Modules:
  0.0 475.0 jit_solution(1107996649016780097)
XLA Ops:
  1.8 4.2 collective-permute-start.1
  7.5 1.5 collective-permute-start
  9.1 2.3 collective-permute-start.4
  12.8 3.1 collective-permute-done.4
  18.0 2.8 pad_maximum_fusion.refs_0_.x
  21.9 1.5 collective-permute-done.6.refs_6_.refs_1_
  23.4 3.9 collective-permute-start.12
  35.2 5.9 %collective-permute-done.8 = bf16[4,8,2176]{2,1,0:T(8,128)(2,1)S(1)} collective-permute-done((bf16[4,8,2176]{2,1,0:T(8,128)(2,1)S(1)}, bf16[4,8,2176]{2,1,0:T(8,128)(2,1)S(1)}, u32[]{:S(2)}, u32[]{:S(2)}) %collective-permute-start.8) | collective-permute-done | bytes 139296 | tf_op jit(solution)/shard_map/ppermute | solution.py:901
  45.3 4.0 collective-permute-done.13
  53.7 1.9 collective-permute-start.19
  55.5 9.1 %qkv_first.1 = (bf16[1024,1024]{1,0:T(8,128)(2,1)}, bf16[1024,1024]{1,0:T(8,128)(2,1)}, bf16[1024,1536]{1,0:T(8,128)(2,1)}) custom-call(s32[24]{0:T(128)} %fusion.32.place, bf16[1024,1024]{1,0:T(8,128)(2,1)} %pad_maximum_fusion.refs_0_.x, f32[1,1024]{1,0:T(1,128)} %get-tuple-element.290.refs_1_.gain, f32[1,1024]{1,0:T(1,128)} %squeeze.128.refs_2_, ...), custom_call_target="tpu_custom_call" | custom-call | flops 3221225472 | bytes 12582912 | tf_op jit(solution)/shard_map/qkv_first/pallas_call | solution.py:106
  64.7 3.0 collective-permute-start.22
  70.2 1.9 copy-done.57
  72.1 8.8 %attend.4 = (bf16[1024,256]{1,0:T(8,128)(2,1)S(1)}, f32[1024,128]{1,0:T(8,128)S(1)}) custom-call(bf16[1024,1536]{1,0:T(8,128)(2,1)S(1)} %copy-done.57, bf16[1024,1536]{1,0:T(8,128)(2,1)S(1)} %copy-done.57, f32[1,1024]{1,0:T(1,128)S(1)} %bitcast.263), custom_call_target="tpu_custom_call" | custom-call | flops 4294967296 | bytes 2097152 | tf_op jit(solution)/shard_map/attend/pallas_call | solution.py:106
  81.8 8.8 %attend.5 = (bf16[1024,256]{1,0:T(8,128)(2,1)S(1)}, f32[1024,128]{1,0:T(8,128)S(1)}) custom-call(bf16[1024,1536]{1,0:T(8,128)(2,1)S(1)} %copy-done.57, bf16[1024,1536]{1,0:T(8,128)(2,1)S(1)} %copy-done.57, f32[1,1024]{1,0:T(1,128)S(1)} %bitcast.264), custom_call_target="tpu_custom_call" | custom-call | flops 4294967296 | bytes 2097152 | tf_op jit(solution)/shard_map/attend/pallas_call | solution.py:106
  95.7 2.3 collective-permute-start.29
  98.0 5.2 %qkv.1.q.kv = bf16[1024,1536]{1,0:T(8,128)(2,1)S(1)} custom-call(s32[24]{0:T(128)S(1)} %copy-done.50, bf16[1024,1024]{1,0:T(8,128)(2,1)S(1)} %copy-done.56, f32[1024,128]{1,0:T(8,128)S(1)} %copy-done.41, f32[1024,128]{1,0:T(8,128)S(1)} %copy-done.44, bf16[4,64,1280]{2,1,0:T(8,128)(2,1)S(1)} %rolled.5.refs_3_.refs_0_.refs_8_, ...), custom_call_target="tpu_custom_call" | custom-call | flops 3221225472 | bytes 12582912 | tf_op jit(solution)/shard_map/qkv/pallas_call | solution.py:106
  103.2 4.1 collective-permute-start.31
  107.3 8.8 %attend.6 = (bf16[1024,256]{1,0:T(8,128)(2,1)S(1)}, f32[1024,128]{1,0:T(8,128)S(1)}) custom-call(bf16[1024,1536]{1,0:T(8,128)(2,1)S(1)} %qkv.1.q.kv, bf16[1024,1536]{1,0:T(8,128)(2,1)S(1)} %qkv.1.q.kv, f32[1,1024]{1,0:T(1,128)S(1)} %bitcast.265), custom_call_target="tpu_custom_call" | custom-call | flops 4294967296 | bytes 2097152 | tf_op jit(solution)/shard_map/attend/pallas_call | solution.py:106
  116.3 1.5 pad_maximum_fusion.1.refs_4_.grad.base
  117.8 1.9 collective-permute-start.32
  121.3 8.8 %attend.7 = (bf16[1024,256]{1,0:T(8,128)(2,1)S(1)}, f32[1024,128]{1,0:T(8,128)S(1)}) custom-call(bf16[1024,1536]{1,0:T(8,128)(2,1)S(1)} %qkv.1.q.kv, bf16[1024,1536]{1,0:T(8,128)(2,1)S(1)} %qkv.1.q.kv, f32[1,1024]{1,0:T(1,128)S(1)} %bitcast.266), custom_call_target="tpu_custom_call" | custom-call | flops 4294967296 | bytes 2097152 | tf_op jit(solution)/shard_map/attend/pallas_call | solution.py:106
  132.1 7.8 %out.1 = (bf16[1024,1024]{1,0:T(8,128)(2,1)S(1)}, bf16[1024,1024]{1,0:T(8,128)(2,1)S(1)}, bf16[1024,1024]{1,0:T(8,128)(2,1)}) custom-call(s32[24]{0:T(128)S(1)} %copy-done.50, bf16[1024,1024]{1,0:T(8,128)(2,1)} %pad_maximum_fusion.refs_0_.x, f32[1,1024]{1,0:T(1,128)S(1)} %get-tuple-element.551.gain, f32[1,1024]{1,0:T(1,128)S(1)} %squeeze.126.bias, ...), custom_call_target="tpu_custom_call" | custom-call | flops 2147483648 | bytes 10485760 | tf_op jit(solution)/shard_map/out/pallas_call | solution.py:106
  141.3 3.7 collective-permute-done.36.refs_3_
  146.3 2.2 collective-permute-done.37.refs_6_
  148.5 1.5 collective-permute-done.38.refs_7_
  151.3 12.7 %up.2 = (bf16[1024,4096]{1,0:T(8,128)(2,1)}, bf16[1024,4096]{1,0:T(8,128)(2,1)}) custom-call(s32[24]{0:T(128)} %fusion.32.place, bf16[1024,1024]{1,0:T(8,128)(2,1)} %copy-done.36, bf16[4,64,2048]{2,1,0:T(8,128)(2,1)} %copy-done.19, bf16[4,64,2048]{2,1,0:T(8,128)(2,1)} %copy-done.79, bf16[4,64,2048]{2,1,0:T(8,128)(2,1)} %copy-done.84, ...), custom_call_target="tpu_custom_call" | custom-call | flops 4294967296 | bytes 12582912 | tf_op jit(solution)/shard_map/up/pallas_call | solution.py:454
  166.8 12.6 %up.3 = (bf16[1024,4096]{1,0:T(8,128)(2,1)}, bf16[1024,4096]{1,0:T(8,128)(2,1)}) custom-call(s32[24]{0:T(128)} %fusion.32.place, bf16[1024,1024]{1,0:T(8,128)(2,1)} %copy-done.36, bf16[4,64,2048]{2,1,0:T(8,128)(2,1)} %copy-done.19, bf16[4,64,2048]{2,1,0:T(8,128)(2,1)} %copy-done.79, ...), custom_call_target="tpu_custom_call", output_to_operand_aliasing={{0}: (10, {}), {1}: (11, {})} | custom-call | flops 4294967296 | bytes 12582912 | tf_op jit(solution)/shard_map/up/pallas_call | solution.py:454
  179.4 9.9 %wide_chunks.2 = bf16[4,4,256,512]{3,2,1,0:T(8,128)(2,1)} custom-call(s32[24]{0:T(128)} %fusion.32.place, bf16[1024,4096]{1,0:T(8,128)(2,1)} %get-tuple-element.478.refs_0_.refs_1_.refs_2_.refs_3_.active, bf16[1024,4096]{1,0:T(8,128)(2,1)} %get-tuple-element.478.refs_0_.refs_1_.refs_2_.refs_3_.active, ...), custom_call_target="tpu_custom_call" | custom-call | flops 4294967296 | bytes 14680064 | tf_op jit(solution)/shard_map/wide_chunks/pallas_call | solution.py:106
  191.9 3.7 collective-permute-done.44.refs_6_
  197.0 14.9 %hidden_back.1.b.refs_8_ = bf16[1024,4096]{1,0:T(8,128)(2,1)} custom-call(s32[24]{0:T(128)} %fusion.32.place, bf16[1024,1024]{1,0:T(8,128)(2,1)} %pad_maximum_fusion.1.refs_4_.grad.base, bf16[1024,4096]{1,0:T(8,128)(2,1)} %get-tuple-element.363.slope, bf16[4,256,512]{2,1,0:T(8,128)(2,1)} %copy-done.5, bf16[4,256,512]{2,1,0:T(8,128)(2,1)} %copy-done.67, ...), custom_call_target="tpu_custom_call" | custom-call | flops 8589934592 | bytes 25165824 | tf_op jit(solution)/shard_map/hidden_back/pallas_call | solution.py:106
  211.9 11.3 %wide_chunks.3 = (bf16[4,256,512]{2,1,0:T(8,128)(2,1)}, bf16[4,256,512]{2,1,0:T(8,128)(2,1)}, bf16[4,256,512]{2,1,0:T(8,128)(2,1)}, bf16[4,256,512]{2,1,0:T(8,128)(2,1)}) custom-call(s32[24]{0:T(128)} %fusion.32.place, bf16[1024,4096]{1,0:T(8,128)(2,1)} %get-tuple-element.478.refs_0_.refs_1_.refs_2_.refs_3_.active, ...), custom_call_target="tpu_custom_call" | custom-call | flops 4294967296 | bytes 14680064 | tf_op jit(solution)/shard_map/wide_chunks/pallas_call | solution.py:106
  223.2 9.7 %row_chunks.2 = bf16[4,4,64,2048]{3,2,1,0:T(8,128)(2,1)} custom-call(s32[24]{0:T(128)} %fusion.32.place, bf16[1024,1024]{1,0:T(8,128)(2,1)} %get-tuple-element.380.a, bf16[1024,4096]{1,0:T(8,128)(2,1)} %hidden_back.1.b.refs_8_), custom_call_target="tpu_custom_call" | custom-call | flops 4294967296 | bytes 10485760 | tf_op jit(solution)/shard_map/row_chunks/pallas_call | solution.py:106
  234.9 20.7 %norm_back.2 = (bf16[1024,1024]{1,0:T(8,128)(2,1)}, f32[2,1024]{1,0:T(2,128)}) custom-call(s32[24]{0:T(128)} %fusion.32.place, bf16[1024,1024]{1,0:T(8,128)(2,1)} %copy-done.6, f32[1,1024]{1,0:T(1,128)} %copy-done.52, bf16[1024,1024]{1,0:T(8,128)(2,1)} %pad_maximum_fusion.1.refs_4_.grad.base, bf16[4,64,2048]{2,1,0:T(8,128)(2,1)} %copy-done.19, ...), custom_call_target="tpu_custom_call" | custom-call | flops 8589934592 | bytes 23068672 | tf_op jit(solution)/shard_map/norm_back/pallas_call | solution.py:106
  255.5 3.0 collective-permute-done.49
  261.2 10.5 %row_chunks.3 = (bf16[4,64,2048]{2,1,0:T(8,128)(2,1)}, bf16[4,64,2048]{2,1,0:T(8,128)(2,1)}, bf16[4,64,2048]{2,1,0:T(8,128)(2,1)}, bf16[4,64,2048]{2,1,0:T(8,128)(2,1)}) custom-call(s32[24]{0:T(128)} %fusion.32.place, bf16[1024,1024]{1,0:T(8,128)(2,1)} %get-tuple-element.380.a, bf16[1024,4096]{1,0:T(8,128)(2,1)} %hidden_back.1.b.refs_8_, ...), custom_call_target="tpu_custom_call" | custom-call | flops 4294967296 | bytes 10485760 | tf_op jit(solution)/shard_map/row_chunks/pallas_call | solution.py:106
  274.0 3.9 heads_back.1.grad
  278.3 2.1 add_convert_fusion.2
  282.0 13.9 %attend_back.4.refs_0_.refs_16_ = bf16[1024,768]{1,0:T(8,128)(2,1)S(1)} custom-call(bf16[1024,1536]{1,0:T(8,128)(2,1)S(1)} %copy-done.58, bf16[1024,1536]{1,0:T(8,128)(2,1)S(1)} %copy-done.58, bf16[1024,256]{1,0:T(8,128)(2,1)S(1)} %copy-done.12, bf16[1024,1024]{1,0:T(8,128)(2,1)S(1)} %heads_back.1.grad, f32[1024,128]{1,0:T(8,128)S(1)} %copy-done.66, ...), custom_call_target="tpu_custom_call" | custom-call | flops 10737418240 | bytes 4194304 | tf_op jit(solution)/shard_map/attend_back/pallas_call | solution.py:106
  297.7 13.7 %attend_back.5.refs_1_.refs_17_ = bf16[1024,768]{1,0:T(8,128)(2,1)S(1)} custom-call(bf16[1024,1536]{1,0:T(8,128)(2,1)S(1)} %copy-done.58, bf16[1024,1536]{1,0:T(8,128)(2,1)S(1)} %copy-done.58, bf16[1024,256]{1,0:T(8,128)(2,1)S(1)} %copy-done.14, bf16[1024,1024]{1,0:T(8,128)(2,1)S(1)} %heads_back.1.grad, f32[1024,128]{1,0:T(8,128)S(1)} %copy-done.64, ...), custom_call_target="tpu_custom_call" | custom-call | flops 10737418240 | bytes 4194304 | tf_op jit(solution)/shard_map/attend_back/pallas_call | solution.py:106
  313.7 6.0 %heads_chunks.4 = bf16[4,4,64,1280]{3,2,1,0:T(8,128)(2,1)} custom-call(s32[24]{0:T(128)S(1)} %copy-done.51, bf16[1024,1024]{1,0:T(8,128)(2,1)S(1)} %copy-done.3, bf16[1024,768]{1,0:T(8,128)(2,1)S(1)} %attend_back.4.refs_0_.refs_16_, bf16[1024,768]{1,0:T(8,128)(2,1)S(1)} %attend_back.5.refs_1_.refs_17_, bf16[1024,256]{1,0:T(8,128)(2,1)S(1)} %copy-done.12, ...), custom_call_target="tpu_custom_call" | custom-call | flops 2684354560 | bytes 7340032 | tf_op jit(solution)/shard_map/heads_chunks/pallas_call | solution.py:106
  319.7 6.3 %collective-permute-done.54 = bf16[256,512]{1,0:T(8,128)(2,1)S(1)} collective-permute-done((bf16[256,512]{1,0:T(8,128)(2,1)S(1)}, bf16[256,512]{1,0:T(8,128)(2,1)S(1)}, u32[]{:S(2)}, u32[]{:S(2)}) %collective-permute-start.54) | collective-permute-done | bytes 262176 | tf_op jit(solution)/shard_map/ppermute | solution.py:48
  326.0 2.1 collective-permute-start.57
  328.1 1.7 add_convert_fusion
  333.3 13.8 %attend_back.6.refs_0_.refs_18_ = bf16[1024,768]{1,0:T(8,128)(2,1)S(1)} custom-call(bf16[1024,1536]{1,0:T(8,128)(2,1)S(1)} %copy-done.54, bf16[1024,1536]{1,0:T(8,128)(2,1)S(1)} %copy-done.54, bf16[1024,256]{1,0:T(8,128)(2,1)S(1)} %copy-done.16, bf16[1024,1024]{1,0:T(8,128)(2,1)S(1)} %heads_back.1.grad, f32[1024,128]{1,0:T(8,128)S(1)} %copy-done.62, ...), custom_call_target="tpu_custom_call" | custom-call | flops 10737418240 | bytes 4194304 | tf_op jit(solution)/shard_map/attend_back/pallas_call | solution.py:106
  349.4 9.1 %heads_chunks.5 = (bf16[4,64,1280]{2,1,0:T(8,128)(2,1)S(1)}, bf16[4,64,1280]{2,1,0:T(8,128)(2,1)S(1)}, bf16[4,64,1280]{2,1,0:T(8,128)(2,1)S(1)}, bf16[4,64,1280]{2,1,0:T(8,128)(2,1)S(1)}) custom-call(s32[24]{0:T(128)S(1)} %copy-done.51, bf16[1024,1024]{1,0:T(8,128)(2,1)} %get-tuple-element.444.a, bf16[1024,768]{1,0:T(8,128)(2,1)} %copy-done.7, ...), custom_call_target="tpu_custom_call" | custom-call | flops 2684354560 | bytes 7340032 | tf_op jit(solution)/shard_map/heads_chunks/pallas_call | solution.py:106
  361.2 1.9 copy-done.55
  363.1 13.8 %attend_back.7.refs_1_.refs_19_ = bf16[1024,768]{1,0:T(8,128)(2,1)S(1)} custom-call(bf16[1024,1536]{1,0:T(8,128)(2,1)S(1)} %copy-done.55, bf16[1024,1536]{1,0:T(8,128)(2,1)S(1)} %copy-done.55, bf16[1024,256]{1,0:T(8,128)(2,1)S(1)} %copy-done.18, bf16[1024,1024]{1,0:T(8,128)(2,1)S(1)} %copy-done.35, f32[1024,128]{1,0:T(8,128)S(1)} %copy-done.60, ...), custom_call_target="tpu_custom_call" | custom-call | flops 10737418240 | bytes 4194304 | tf_op jit(solution)/shard_map/attend_back/pallas_call | solution.py:106
  379.2 3.8 heads_chunks.6
  387.8 2.5 heads_chunks.7
  391.5 4.6 collective-permute-done.66
  396.1 1.6 slice_bitcast_fusion
  401.2 15.0 %norm_back.3 = (bf16[512,1024]{1,0:T(8,128)(2,1)}, bf16[512,1024]{1,0:T(8,128)(2,1)}, f32[2,1024]{1,0:T(2,128)}) custom-call(s32[24]{0:T(128)} %fusion.32.place, bf16[1024,1024]{1,0:T(8,128)(2,1)} %pad_maximum_fusion.refs_0_.x, f32[1,1024]{1,0:T(1,128)} %get-tuple-element.290.refs_1_.gain, bf16[1024,1024]{1,0:T(8,128)(2,1)} %get-tuple-element.427.grad.refs_6_.refs_7_.base, ...), custom_call_target="tpu_custom_call" | custom-call | flops 6442450944 | bytes 18874368 | tf_op jit(solution)/shard_map/norm_back/pallas_call | solution.py:106
  416.2 2.2 collective-permute-start.74
  420.0 1.8 collective-permute-start.72
  424.5 9.6 %down.2 = bf16[512,1024]{1,0:T(8,128)(2,1)} custom-call(s32[24]{0:T(128)} %fusion.32.place, bf16[1024,4096]{1,0:T(8,128)(2,1)} %get-tuple-element.478.refs_0_.refs_1_.refs_2_.refs_3_.active, bf16[1024,1024]{1,0:T(8,128)(2,1)} %copy-done.6, bf16[4,256,512]{2,1,0:T(8,128)(2,1)} %copy-done.5, bf16[4,256,512]{2,1,0:T(8,128)(2,1)} %copy-done.67, ...), custom_call_target="tpu_custom_call" | custom-call | flops 4294967296 | bytes 12582912 | tf_op jit(solution)/shard_map/down/pallas_call | solution.py:106
  434.3 1.9 collective-permute-start.78
  437.7 9.4 %down.3 = bf16[512,1024]{1,0:T(8,128)(2,1)} custom-call(s32[24]{0:T(128)} %fusion.32.place, bf16[1024,4096]{1,0:T(8,128)(2,1)} %get-tuple-element.478.refs_0_.refs_1_.refs_2_.refs_3_.active, bf16[1024,1024]{1,0:T(8,128)(2,1)} %copy-done.6, bf16[4,256,512]{2,1,0:T(8,128)(2,1)} %copy-done.5, bf16[4,256,512]{2,1,0:T(8,128)(2,1)} %copy-done.67, ...), custom_call_target="tpu_custom_call" | custom-call | flops 4294967296 | bytes 12582912 | tf_op jit(solution)/shard_map/down/pallas_call | solution.py:106
  451.3 1.5 collective-permute-start.81
  452.8 1.6 maximum_select_fusion
  454.5 1.8 collective-permute-done.81
  459.1 4.6 collective-permute-done.82
  466.0 1.5 reshape.347
  467.5 3.3 maximum_select_fusion.1
  (496 shorter events, 96.3 us)
Async XLA Ops:
  1.8 14.1 %collective-permute-start.1 = (bf16[1,64,768]{2,1,0:T(8,128)(2,1)S(1)}, bf16[1,64,768]{2,1,0:T(8,128)(2,1)S(1)}, u32[]{:S(2)}, u32[]{:S(2)}) collective-permute-start(bf16[1,64,768]{2,1,0:T(8,128)(2,1)S(1)} %maximum_bitcast_fusion.2.refs_0_), channel_id=1, source_target_pairs={{0,24},{1,25},{2,26},{3,27},{4,28},{5,29},{6,30},{7,31},{8,0},{9,1... | collective-permute-start | bytes 294920 | tf_op jit(solution)/shard_map/ppermute | solution.py:48
  6.0 10.0 %collective-permute-start.2 = (bf16[1,64,768]{2,1,0:T(8,128)(2,1)S(1)}, bf16[1,64,768]{2,1,0:T(8,128)(2,1)S(1)}, u32[]{:S(2)}, u32[]{:S(2)}) collective-permute-start(bf16[1,64,768]{2,1,0:T(8,128)(2,1)S(1)} %maximum_bitcast_fusion.2.refs_0_), channel_id=1, source_target_pairs={{0,16},{1,17},{2,18},{3,19},{4,20},{5,21},{6,22},{7,23},{8,24},{9,... | collective-permute-start | bytes 294920 | tf_op jit(solution)/shard_map/ppermute | solution.py:48
  6.0 10.0 %collective-permute-start.3 = (bf16[1,64,768]{2,1,0:T(8,128)(2,1)S(1)}, bf16[1,64,768]{2,1,0:T(8,128)(2,1)S(1)}, u32[]{:S(2)}, u32[]{:S(2)}) collective-permute-start(bf16[1,64,768]{2,1,0:T(8,128)(2,1)S(1)} %maximum_bitcast_fusion.2.refs_0_), channel_id=1, source_target_pairs={{0,8},{1,9},{2,10},{3,11},{4,12},{5,13},{6,14},{7,15},{8,16},{9,17... | collective-permute-start | bytes 294920 | tf_op jit(solution)/shard_map/ppermute | solution.py:48
  7.5 8.5 %collective-permute-start = (bf16[512,1024]{1,0:T(8,128)(2,1)}, bf16[512,1024]{1,0:T(8,128)(2,1)}, u32[]{:S(2)}, u32[]{:S(2)}) collective-permute-start(bf16[512,1024]{1,0:T(8,128)(2,1)} %dynamic-slice_bitcast_fusion.3), channel_id=1, source_target_pairs={{0,1},{1,0},{2,3},{3,2},{4,5},{5,4},{6,7},{7,6},{8,9},{9,8},{10,11... | collective-permute-start | bytes 3145736 | tf_op jit(solution)/shard_map/ppermute | solution.py:55
  23.4 17.7 %collective-permute-start.12 = (bf16[1,64,1280]{2,1,0:T(8,128)(2,1)S(1)}, bf16[1,64,1280]{2,1,0:T(8,128)(2,1)S(1)}, u32[]{:S(2)}, u32[]{:S(2)}) collective-permute-start(bf16[1,64,1280]{2,1,0:T(8,128)(2,1)S(1)} %collective-permute-done.7.refs_1_), channel_id=1, source_target_pairs={{0,24},{1,25},{2,26},{3,27},{4,28},{5,29},{6,30},{7,31},{8,0},{9,1... | collective-permute-start | bytes 491528 | tf_op jit(solution)/shard_map/ppermute | solution.py:48
  27.3 13.9 %collective-permute-start.9 = (bf16[4,64,768]{2,1,0:T(8,128)(2,1)S(1)}, bf16[4,64,768]{2,1,0:T(8,128)(2,1)S(1)}, u32[]{:S(2)}, u32[]{:S(2)}) collective-permute-start(bf16[4,64,768]{2,1,0:T(8,128)(2,1)S(1)} %rolled.4.refs_5_.refs_0_), channel_id=1, source_target_pairs={{0,4},{1,3},{2,6},{3,1},{4,0},{5,7},{6,2},{7,5},{8,12},{9,11},{10,... | collective-permute-start | bytes 1179656 | tf_op jit(solution)/shard_map/ppermute | solution.py:48
  28.5 12.7 %collective-permute-start.10 = (bf16[4,64,768]{2,1,0:T(8,128)(2,1)}, bf16[4,64,768]{2,1,0:T(8,128)(2,1)}, u32[]{:S(2)}, u32[]{:S(2)}) collective-permute-start(bf16[4,64,768]{2,1,0:T(8,128)(2,1)} %collective-permute-done.6.refs_6_.refs_1_), channel_id=1, source_target_pairs={{0,4},{1,3},{2,6},{3,1},{4,0},{5,7},{6,2},{7,5},{8,12},{9,11},{10,... | collective-permute-start | bytes 1179656 | tf_op jit(solution)/shard_map/ppermute | solution.py:48
  28.8 12.4 %collective-permute-start.11 = (bf16[4,64,768]{2,1,0:T(8,128)(2,1)S(1)}, bf16[4,64,768]{2,1,0:T(8,128)(2,1)}, u32[]{:S(2)}, u32[]{:S(2)}) collective-permute-start(bf16[4,64,768]{2,1,0:T(8,128)(2,1)S(1)} %rolled.4.refs_5_.refs_0_), channel_id=1, source_target_pairs={{0,1},{1,0},{2,3},{3,2},{4,5},{5,4},{6,7},{7,6},{8,9},{9,8},{10,11... | collective-permute-start | bytes 1179656 | tf_op jit(solution)/shard_map/ppermute | solution.py:55
  30.1 11.0 %collective-permute-start.8 = (bf16[4,8,2176]{2,1,0:T(8,128)(2,1)S(1)}, bf16[4,8,2176]{2,1,0:T(8,128)(2,1)S(1)}, u32[]{:S(2)}, u32[]{:S(2)}) collective-permute-start(bf16[4,8,2176]{2,1,0:T(8,128)(2,1)S(1)} %pad_maximum_fusion.9), channel_id=1, source_target_pairs={{0,2},{1,3},{2,0},{3,1},{4,6},{5,7},{6,4},{7,5},{8,10},{9,11},{10,... | collective-permute-start | bytes 417800 | tf_op jit(solution)/shard_map/ppermute | solution.py:901
  41.2 8.1 %collective-permute-start.13 = (bf16[8,8,2176]{2,1,0:T(8,128)(2,1)S(1)}, bf16[8,8,2176]{2,1,0:T(8,128)(2,1)S(1)}, u32[]{:S(2)}, u32[]{:S(2)}) collective-permute-start(bf16[8,8,2176]{2,1,0:T(8,128)(2,1)S(1)} %pad_maximum_fusion.7), channel_id=1, source_target_pairs={{0,4},{1,5},{2,6},{3,7},{4,0},{5,1},{6,2},{7,3},{8,12},{9,13},{10,... | collective-permute-start | bytes 835592 | tf_op jit(solution)/shard_map/ppermute | solution.py:901
  51.6 13.1 %collective-permute-start.18 = (bf16[4,64,1280]{2,1,0:T(8,128)(2,1)S(1)}, bf16[4,64,1280]{2,1,0:T(8,128)(2,1)S(1)}, u32[]{:S(2)}, u32[]{:S(2)}) collective-permute-start(bf16[4,64,1280]{2,1,0:T(8,128)(2,1)S(1)} %rolled.5.refs_3_.refs_0_.refs_8_), channel_id=1, source_target_pairs={{0,2},{1,5},{2,0},{3,7},{4,6},{5,1},{6,4},{7,3},{8,10},{9,13},{10,... | collective-permute-start | bytes 1966088 | tf_op jit(solution)/shard_map/ppermute | solution.py:48
  53.7 11.0 %collective-permute-start.19 = (bf16[1,64,2048]{2,1,0:T(8,128)(2,1)S(1)}, bf16[1,64,2048]{2,1,0:T(8,128)(2,1)S(1)}, u32[]{:S(2)}, u32[]{:S(2)}) collective-permute-start(bf16[1,64,2048]{2,1,0:T(8,128)(2,1)S(1)} %dynamic-slice_bitcast_fusion.13.refs_0_), channel_id=1, source_target_pairs={{0,24},{1,25},{2,26},{3,27},{4,28},{5,29},{6,30},{7,31},{8,0},{9,1... | collective-permute-start | bytes 786440 | tf_op jit(solution)/shard_map/ppermute | solution.py:48
  64.7 17.0 %collective-permute-start.22 = (bf16[4,64,1280]{2,1,0:T(8,128)(2,1)S(1)}, bf16[4,64,1280]{2,1,0:T(8,128)(2,1)S(1)}, u32[]{:S(2)}, u32[]{:S(2)}) collective-permute-start(bf16[4,64,1280]{2,1,0:T(8,128)(2,1)S(1)} %rolled.5.refs_3_.refs_0_.refs_8_), channel_id=1, source_target_pairs={{0,1},{1,0},{2,3},{3,2},{4,5},{5,4},{6,7},{7,6},{8,9},{9,8},{10,11... | collective-permute-start | bytes 1966088 | tf_op jit(solution)/shard_map/ppermute | solution.py:55
  67.7 14.0 %collective-permute-start.23 = (bf16[4,64,1280]{2,1,0:T(8,128)(2,1)S(1)}, bf16[4,64,1280]{2,1,0:T(8,128)(2,1)S(1)}, u32[]{:S(2)}, u32[]{:S(2)}) collective-permute-start(bf16[4,64,1280]{2,1,0:T(8,128)(2,1)S(1)} %collective-permute-done.18.refs_4_.refs_1_.refs_9_), channel_id=1, source_target_pairs={{0,1},{1,0},{2,3},{3,2},{4,5},{5,4},{6,7},{7,6},{8,9},{9,8},{10,11... | collective-permute-start | bytes 1966088 | tf_op jit(solution)/shard_map/ppermute | solution.py:55
  68.4 23.0 %collective-permute-start.20 = (bf16[4,64,1280]{2,1,0:T(8,128)(2,1)S(1)}, bf16[4,64,1280]{2,1,0:T(8,128)(2,1)S(1)}, u32[]{:S(2)}, u32[]{:S(2)}) collective-permute-start(bf16[4,64,1280]{2,1,0:T(8,128)(2,1)S(1)} %rolled.5.refs_3_.refs_0_.refs_8_), channel_id=1, source_target_pairs={{0,4},{1,3},{2,6},{3,1},{4,0},{5,7},{6,2},{7,5},{8,12},{9,11},{10,... | collective-permute-start | bytes 1966088 | tf_op jit(solution)/shard_map/ppermute | solution.py:48
  68.7 13.0 %collective-permute-start.24 = (bf16[1,64,2048]{2,1,0:T(8,128)(2,1)S(1)}, bf16[1,64,2048]{2,1,0:T(8,128)(2,1)S(1)}, u32[]{:S(2)}, u32[]{:S(2)}) collective-permute-start(bf16[1,64,2048]{2,1,0:T(8,128)(2,1)S(1)} %collective-permute-done.19.refs_1_), channel_id=1, source_target_pairs={{0,24},{1,25},{2,26},{3,27},{4,28},{5,29},{6,30},{7,31},{8,0},{9,1... | collective-permute-start | bytes 786440 | tf_op jit(solution)/shard_map/ppermute | solution.py:48
  68.9 22.6 %collective-permute-start.21 = (bf16[4,64,1280]{2,1,0:T(8,128)(2,1)S(1)}, bf16[4,64,1280]{2,1,0:T(8,128)(2,1)S(1)}, u32[]{:S(2)}, u32[]{:S(2)}) collective-permute-start(bf16[4,64,1280]{2,1,0:T(8,128)(2,1)S(1)} %collective-permute-done.18.refs_4_.refs_1_.refs_9_), channel_id=1, source_target_pairs={{0,4},{1,3},{2,6},{3,1},{4,0},{5,7},{6,2},{7,5},{8,12},{9,11},{10,... | collective-permute-start | bytes 1966088 | tf_op jit(solution)/shard_map/ppermute | solution.py:48
  81.7 9.7 %collective-permute-start.25 = (bf16[1,64,2048]{2,1,0:T(8,128)(2,1)S(1)}, bf16[1,64,2048]{2,1,0:T(8,128)(2,1)S(1)}, u32[]{:S(2)}, u32[]{:S(2)}) collective-permute-start(bf16[1,64,2048]{2,1,0:T(8,128)(2,1)S(1)} %collective-permute-done.24.refs_2_), channel_id=1, source_target_pairs={{0,24},{1,25},{2,26},{3,27},{4,28},{5,29},{6,30},{7,31},{8,0},{9,1... | collective-permute-start | bytes 786440 | tf_op jit(solution)/shard_map/ppermute | solution.py:48
  93.0 10.2 %collective-permute-start.28 = (bf16[512,1024]{1,0:T(8,128)(2,1)S(1)}, bf16[512,1024]{1,0:T(8,128)(2,1)S(1)}, u32[]{:S(2)}, u32[]{:S(2)}) collective-permute-start(bf16[512,1024]{1,0:T(8,128)(2,1)S(1)} %dynamic-slice_bitcast_fusion.1), channel_id=1, source_target_pairs={{0,1},{1,0},{2,3},{3,2},{4,5},{5,4},{6,7},{7,6},{8,9},{9,8},{10,11... | collective-permute-start | bytes 3145736 | tf_op jit(solution)/shard_map/ppermute | solution.py:55
  95.5 22.3 %collective-permute-start.30 = (bf16[4,64,2048]{2,1,0:T(8,128)(2,1)S(1)}, bf16[4,64,2048]{2,1,0:T(8,128)(2,1)S(1)}, u32[]{:S(2)}, u32[]{:S(2)}) collective-permute-start(bf16[4,64,2048]{2,1,0:T(8,128)(2,1)S(1)} %rolled.6.refs_0_), channel_id=1, source_target_pairs={{0,2},{1,5},{2,0},{3,7},{4,6},{5,1},{6,4},{7,3},{8,10},{9,13},{10,... | collective-permute-start | bytes 3145736 | tf_op jit(solution)/shard_map/ppermute | solution.py:48
  95.7 7.5 %collective-permute-start.29 = (bf16[1,256,512]{2,1,0:T(8,128)(2,1)S(1)}, bf16[1,256,512]{2,1,0:T(8,128)(2,1)S(1)}, u32[]{:S(2)}, u32[]{:S(2)}) collective-permute-start(bf16[1,256,512]{2,1,0:T(8,128)(2,1)S(1)} %dynamic-slice_bitcast_fusion.12.refs_0_), channel_id=1, source_target_pairs={{0,24},{1,25},{2,26},{3,27},{4,28},{5,29},{6,30},{7,31},{8,0},{9,1... | collective-permute-start | bytes 786440 | tf_op jit(solution)/shard_map/ppermute | solution.py:48
  103.2 14.6 %collective-permute-start.31 = (bf16[1,256,512]{2,1,0:T(8,128)(2,1)S(1)}, bf16[1,256,512]{2,1,0:T(8,128)(2,1)S(1)}, u32[]{:S(2)}, u32[]{:S(2)}) collective-permute-start(bf16[1,256,512]{2,1,0:T(8,128)(2,1)S(1)} %collective-permute-done.29.refs_1_), channel_id=1, source_target_pairs={{0,24},{1,25},{2,26},{3,27},{4,28},{5,29},{6,30},{7,31},{8,0},{9,1... | collective-permute-start | bytes 786440 | tf_op jit(solution)/shard_map/ppermute | solution.py:48
  117.8 13.2 %collective-permute-start.32 = (bf16[4,64,2048]{2,1,0:T(8,128)(2,1)S(1)}, bf16[4,64,2048]{2,1,0:T(8,128)(2,1)S(1)}, u32[]{:S(2)}, u32[]{:S(2)}) collective-permute-start(bf16[4,64,2048]{2,1,0:T(8,128)(2,1)S(1)} %rolled.6.refs_0_), channel_id=1, source_target_pairs={{0,1},{1,0},{2,3},{3,2},{4,5},{5,4},{6,7},{7,6},{8,9},{9,8},{10,11... | collective-permute-start | bytes 3145736 | tf_op jit(solution)/shard_map/ppermute | solution.py:55
  119.7 11.3 %collective-permute-start.33 = (bf16[4,64,2048]{2,1,0:T(8,128)(2,1)S(1)}, bf16[4,64,2048]{2,1,0:T(8,128)(2,1)S(1)}, u32[]{:S(2)}, u32[]{:S(2)}) collective-permute-start(bf16[4,64,2048]{2,1,0:T(8,128)(2,1)S(1)} %collective-permute-done.30.refs_1_), channel_id=1, source_target_pairs={{0,1},{1,0},{2,3},{3,2},{4,5},{5,4},{6,7},{7,6},{8,9},{9,8},{10,11... | collective-permute-start | bytes 3145736 | tf_op jit(solution)/shard_map/ppermute | solution.py:55
  119.8 21.5 %collective-permute-start.35 = (bf16[4,64,2048]{2,1,0:T(8,128)(2,1)S(1)}, bf16[4,64,2048]{2,1,0:T(8,128)(2,1)S(1)}, u32[]{:S(2)}, u32[]{:S(2)}) collective-permute-start(bf16[4,64,2048]{2,1,0:T(8,128)(2,1)S(1)} %rolled.6.refs_0_), channel_id=1, source_target_pairs={{0,4},{1,3},{2,6},{3,1},{4,0},{5,7},{6,2},{7,5},{8,12},{9,11},{10,... | collective-permute-start | bytes 3145736 | tf_op jit(solution)/shard_map/ppermute | solution.py:48
  120.0 24.9 %collective-permute-start.36 = (bf16[4,64,2048]{2,1,0:T(8,128)(2,1)S(1)}, bf16[4,64,2048]{2,1,0:T(8,128)(2,1)S(1)}, u32[]{:S(2)}, u32[]{:S(2)}) collective-permute-start(bf16[4,64,2048]{2,1,0:T(8,128)(2,1)S(1)} %collective-permute-done.30.refs_1_), channel_id=1, source_target_pairs={{0,4},{1,3},{2,6},{3,1},{4,0},{5,7},{6,2},{7,5},{8,12},{9,11},{10,... | collective-permute-start | bytes 3145736 | tf_op jit(solution)/shard_map/ppermute | solution.py:48
  121.3 9.7 %collective-permute-start.34 = (bf16[1,256,512]{2,1,0:T(8,128)(2,1)S(1)}, bf16[1,256,512]{2,1,0:T(8,128)(2,1)S(1)}, u32[]{:S(2)}, u32[]{:S(2)}) collective-permute-start(bf16[1,256,512]{2,1,0:T(8,128)(2,1)S(1)} %collective-permute-done.31.refs_2_), channel_id=1, source_target_pairs={{0,24},{1,25},{2,26},{3,27},{4,28},{5,29},{6,30},{7,31},{8,0},{9,1... | collective-permute-start | bytes 786440 | tf_op jit(solution)/shard_map/ppermute | solution.py:48
  150.1 13.9 %collective-permute-start.39 = (bf16[4,256,512]{2,1,0:T(8,128)(2,1)S(1)}, bf16[4,256,512]{2,1,0:T(8,128)(2,1)S(1)}, u32[]{:S(2)}, u32[]{:S(2)}) collective-permute-start(bf16[4,256,512]{2,1,0:T(8,128)(2,1)S(1)} %rolled.7.refs_0_), channel_id=1, source_target_pairs={{0,2},{1,5},{2,0},{3,7},{4,6},{5,1},{6,4},{7,3},{8,10},{9,13},{10,... | collective-permute-start | bytes 3145736 | tf_op jit(solution)/shard_map/ppermute | solution.py:48
  164.0 15.4 %collective-permute-start.41 = (bf16[4,256,512]{2,1,0:T(8,128)(2,1)S(1)}, bf16[4,256,512]{2,1,0:T(8,128)(2,1)S(1)}, u32[]{:S(2)}, u32[]{:S(2)}) collective-permute-start(bf16[4,256,512]{2,1,0:T(8,128)(2,1)S(1)} %rolled.7.refs_0_), channel_id=1, source_target_pairs={{0,1},{1,0},{2,3},{3,2},{4,5},{5,4},{6,7},{7,6},{8,9},{9,8},{10,11... | collective-permute-start | bytes 3145736 | tf_op jit(solution)/shard_map/ppermute | solution.py:55
  165.3 14.1 %collective-permute-start.42 = (bf16[4,256,512]{2,1,0:T(8,128)(2,1)S(1)}, bf16[4,256,512]{2,1,0:T(8,128)(2,1)S(1)}, u32[]{:S(2)}, u32[]{:S(2)}) collective-permute-start(bf16[4,256,512]{2,1,0:T(8,128)(2,1)S(1)} %collective-permute-done.39.refs_1_), channel_id=1, source_target_pairs={{0,1},{1,0},{2,3},{3,2},{4,5},{5,4},{6,7},{7,6},{8,9},{9,8},{10,11... | collective-permute-start | bytes 3145736 | tf_op jit(solution)/shard_map/ppermute | solution.py:55
  165.3 24.1 %collective-permute-start.40 = (bf16[4,256,512]{2,1,0:T(8,128)(2,1)S(1)}, bf16[4,256,512]{2,1,0:T(8,128)(2,1)S(1)}, u32[]{:S(2)}, u32[]{:S(2)}) collective-permute-start(bf16[4,256,512]{2,1,0:T(8,128)(2,1)S(1)} %rolled.7.refs_0_), channel_id=1, source_target_pairs={{0,4},{1,3},{2,6},{3,1},{4,0},{5,7},{6,2},{7,5},{8,12},{9,11},{10,... | collective-permute-start | bytes 3145736 | tf_op jit(solution)/shard_map/ppermute | solution.py:48
  165.5 25.0 %collective-permute-start.43 = (bf16[4,256,512]{2,1,0:T(8,128)(2,1)S(1)}, bf16[4,256,512]{2,1,0:T(8,128)(2,1)}, u32[]{:S(2)}, u32[]{:S(2)}) collective-permute-start(bf16[4,256,512]{2,1,0:T(8,128)(2,1)S(1)} %collective-permute-done.39.refs_1_), channel_id=1, source_target_pairs={{0,4},{1,3},{2,6},{3,1},{4,0},{5,7},{6,2},{7,5},{8,12},{9,11},{10,... | collective-permute-start | bytes 3145736 | tf_op jit(solution)/shard_map/ppermute | solution.py:48
  195.9 16.0 %collective-permute-start.46 = (bf16[4,4,256,512]{3,2,1,0:T(8,128)(2,1)}, bf16[4,4,256,512]{3,2,1,0:T(8,128)(2,1)}, u32[]{:S(2)}, u32[]{:S(2)}) collective-permute-start(bf16[4,4,256,512]{3,2,1,0:T(8,128)(2,1)} %wide_chunks.2), channel_id=1, source_target_pairs={{0,1},{1,0},{2,3},{3,2},{4,5},{5,4},{6,7},{7,6},{8,9},{9,8},{10,11... | collective-permute-start | bytes 12582920 | tf_op jit(solution)/shard_map/ppermute | solution.py:55
  233.0 25.6 %collective-permute-start.47 = (bf16[4,4,64,2048]{3,2,1,0:T(8,128)(2,1)}, bf16[4,4,64,2048]{3,2,1,0:T(8,128)(2,1)}, u32[]{:S(2)}, u32[]{:S(2)}) collective-permute-start(bf16[4,4,64,2048]{3,2,1,0:T(8,128)(2,1)} %row_chunks.2), channel_id=1, source_target_pairs={{0,1},{1,0},{2,3},{3,2},{4,5},{5,4},{6,7},{7,6},{8,9},{9,8},{10,11... | collective-permute-start | bytes 12582920 | tf_op jit(solution)/shard_map/ppermute | solution.py:55
  233.4 22.1 %collective-permute-start.48 = (bf16[4,256,512]{2,1,0:T(8,128)(2,1)S(1)}, bf16[4,256,512]{2,1,0:T(8,128)(2,1)S(1)}, u32[]{:S(2)}, u32[]{:S(2)}) collective-permute-start(bf16[4,256,512]{2,1,0:T(8,128)(2,1)S(1)} %copy-done.115), channel_id=1, source_target_pairs={{0,4},{1,3},{2,6},{3,1},{4,0},{5,7},{6,2},{7,5},{8,12},{9,11},{10,... | collective-permute-start | bytes 3145736 | tf_op jit(solution)/shard_map/ppermute | solution.py:48
  233.7 24.9 %collective-permute-start.49 = (bf16[4,256,512]{2,1,0:T(8,128)(2,1)S(1)}, bf16[4,256,512]{2,1,0:T(8,128)(2,1)S(1)}, u32[]{:S(2)}, u32[]{:S(2)}) collective-permute-start(bf16[4,256,512]{2,1,0:T(8,128)(2,1)S(1)} %copy-done.114), channel_id=1, source_target_pairs={{0,4},{1,3},{2,6},{3,1},{4,0},{5,7},{6,2},{7,5},{8,12},{9,11},{10,... | collective-permute-start | bytes 3145736 | tf_op jit(solution)/shard_map/ppermute | solution.py:48
  259.9 18.0 %collective-permute-start.50 = (bf16[4,256,512]{2,1,0:T(8,128)(2,1)}, bf16[4,256,512]{2,1,0:T(8,128)(2,1)}, u32[]{:S(2)}, u32[]{:S(2)}) collective-permute-start(bf16[4,256,512]{2,1,0:T(8,128)(2,1)} %add_convert_fusion.3), channel_id=1, source_target_pairs={{0,2},{1,5},{2,0},{3,7},{4,6},{5,1},{6,4},{7,3},{8,10},{9,13},{10,... | collective-permute-start | bytes 3145736 | tf_op jit(solution)/shard_map/ppermute | solution.py:48
  278.0 18.0 %collective-permute-start.52 = (bf16[4,64,2048]{2,1,0:T(8,128)(2,1)S(1)}, bf16[4,64,2048]{2,1,0:T(8,128)(2,1)S(1)}, u32[]{:S(2)}, u32[]{:S(2)}) collective-permute-start(bf16[4,64,2048]{2,1,0:T(8,128)(2,1)S(1)} %copy-done.113), channel_id=1, source_target_pairs={{0,4},{1,3},{2,6},{3,1},{4,0},{5,7},{6,2},{7,5},{8,12},{9,11},{10,... | collective-permute-start | bytes 3145736 | tf_op jit(solution)/shard_map/ppermute | solution.py:48
  280.5 15.4 %collective-permute-start.51 = (bf16[256,512]{1,0:T(8,128)(2,1)S(1)}, bf16[256,512]{1,0:T(8,128)(2,1)S(1)}, u32[]{:S(2)}, u32[]{:S(2)}) collective-permute-start(bf16[256,512]{1,0:T(8,128)(2,1)S(1)} %get-tuple-element.524), channel_id=1, source_target_pairs={{0,16},{1,17},{2,18},{3,19},{4,20},{5,21},{6,22},{7,23},{8,24},{9,... | collective-permute-start | bytes 786440 | tf_op jit(solution)/shard_map/ppermute | solution.py:48
  296.4 15.1 %collective-permute-start.53 = (bf16[4,64,2048]{2,1,0:T(8,128)(2,1)S(1)}, bf16[4,64,2048]{2,1,0:T(8,128)(2,1)S(1)}, u32[]{:S(2)}, u32[]{:S(2)}) collective-permute-start(bf16[4,64,2048]{2,1,0:T(8,128)(2,1)S(1)} %add_convert_fusion.1), channel_id=1, source_target_pairs={{0,2},{1,5},{2,0},{3,7},{4,6},{5,1},{6,4},{7,3},{8,10},{9,13},{10,... | collective-permute-start | bytes 3145736 | tf_op jit(solution)/shard_map/ppermute | solution.py:48
  311.4 14.6 %collective-permute-start.56 = (bf16[4,64,2048]{2,1,0:T(8,128)(2,1)}, bf16[4,64,2048]{2,1,0:T(8,128)(2,1)}, u32[]{:S(2)}, u32[]{:S(2)}) collective-permute-start(bf16[4,64,2048]{2,1,0:T(8,128)(2,1)} %get-tuple-element.410), channel_id=1, source_target_pairs={{0,4},{1,3},{2,6},{3,1},{4,0},{5,7},{6,2},{7,5},{8,12},{9,11},{10,... | collective-permute-start | bytes 3145736 | tf_op jit(solution)/shard_map/ppermute | solution.py:48
  312.4 13.6 %collective-permute-start.54 = (bf16[256,512]{1,0:T(8,128)(2,1)S(1)}, bf16[256,512]{1,0:T(8,128)(2,1)S(1)}, u32[]{:S(2)}, u32[]{:S(2)}) collective-permute-start(bf16[256,512]{1,0:T(8,128)(2,1)S(1)} %get-tuple-element.407), channel_id=1, source_target_pairs={{0,16},{1,17},{2,18},{3,19},{4,20},{5,21},{6,22},{7,23},{8,24},{9,... | collective-permute-start | bytes 786440 | tf_op jit(solution)/shard_map/ppermute | solution.py:48
  313.5 12.4 %collective-permute-start.55 = (bf16[256,512]{1,0:T(8,128)(2,1)S(1)}, bf16[256,512]{1,0:T(8,128)(2,1)S(1)}, u32[]{:S(2)}, u32[]{:S(2)}) collective-permute-start(bf16[256,512]{1,0:T(8,128)(2,1)S(1)} %add_convert_fusion.13), channel_id=1, source_target_pairs={{0,8},{1,9},{2,10},{3,11},{4,12},{5,13},{6,14},{7,15},{8,0},{9,1},... | collective-permute-start | bytes 786440 | tf_op jit(solution)/shard_map/ppermute | solution.py:48
  326.0 21.1 %collective-permute-start.57 = (bf16[4,4,64,1280]{3,2,1,0:T(8,128)(2,1)}, bf16[4,4,64,1280]{3,2,1,0:T(8,128)(2,1)S(1)}, u32[]{:S(2)}, u32[]{:S(2)}) collective-permute-start(bf16[4,4,64,1280]{3,2,1,0:T(8,128)(2,1)} %heads_chunks.4), channel_id=1, source_target_pairs={{0,1},{1,0},{2,3},{3,2},{4,5},{5,4},{6,7},{7,6},{8,9},{9,8},{10,11... | collective-permute-start | bytes 7864328 | tf_op jit(solution)/shard_map/ppermute | solution.py:55
  330.7 16.4 %collective-permute-start.58 = (bf16[64,2048]{1,0:T(8,128)(2,1)S(1)}, bf16[64,2048]{1,0:T(8,128)(2,1)S(1)}, u32[]{:S(2)}, u32[]{:S(2)}) collective-permute-start(bf16[64,2048]{1,0:T(8,128)(2,1)S(1)} %get-tuple-element.520), channel_id=1, source_target_pairs={{0,16},{1,17},{2,18},{3,19},{4,20},{5,21},{6,22},{7,23},{8,24},{9,... | collective-permute-start | bytes 786440 | tf_op jit(solution)/shard_map/ppermute | solution.py:48
  333.0 14.1 %collective-permute-start.59 = (bf16[256,512]{1,0:T(8,128)(2,1)S(1)}, bf16[256,512]{1,0:T(8,128)(2,1)}, u32[]{:S(2)}, u32[]{:S(2)}) collective-permute-start(bf16[256,512]{1,0:T(8,128)(2,1)S(1)} %get-tuple-element.508), channel_id=1, source_target_pairs={{0,1},{1,0},{2,3},{3,2},{4,5},{5,4},{6,7},{7,6},{8,9},{9,8},{10,11... | collective-permute-start | bytes 786440 | tf_op jit(solution)/shard_map/ppermute | solution.py:55
  358.5 18.5 %collective-permute-start.60 = (bf16[4,64,1280]{2,1,0:T(8,128)(2,1)S(1)}, bf16[4,64,1280]{2,1,0:T(8,128)(2,1)S(1)}, u32[]{:S(2)}, u32[]{:S(2)}) collective-permute-start(bf16[4,64,1280]{2,1,0:T(8,128)(2,1)S(1)} %get-tuple-element.433), channel_id=1, source_target_pairs={{0,4},{1,3},{2,6},{3,1},{4,0},{5,7},{6,2},{7,5},{8,12},{9,11},{10,... | collective-permute-start | bytes 1966088 | tf_op jit(solution)/shard_map/ppermute | solution.py:48
  359.5 17.5 %collective-permute-start.61 = (bf16[4,64,1280]{2,1,0:T(8,128)(2,1)S(1)}, bf16[4,64,1280]{2,1,0:T(8,128)(2,1)S(1)}, u32[]{:S(2)}, u32[]{:S(2)}) collective-permute-start(bf16[4,64,1280]{2,1,0:T(8,128)(2,1)S(1)} %get-tuple-element.434), channel_id=1, source_target_pairs={{0,4},{1,3},{2,6},{3,1},{4,0},{5,7},{6,2},{7,5},{8,12},{9,11},{10,... | collective-permute-start | bytes 1966088 | tf_op jit(solution)/shard_map/ppermute | solution.py:48
  360.0 16.9 %collective-permute-start.62 = (bf16[64,2048]{1,0:T(8,128)(2,1)}, bf16[64,2048]{1,0:T(8,128)(2,1)S(1)}, u32[]{:S(2)}, u32[]{:S(2)}) collective-permute-start(bf16[64,2048]{1,0:T(8,128)(2,1)} %get-tuple-element.435), channel_id=1, source_target_pairs={{0,16},{1,17},{2,18},{3,19},{4,20},{5,21},{6,22},{7,23},{8,24},{9,... | collective-permute-start | bytes 786440 | tf_op jit(solution)/shard_map/ppermute | solution.py:48
  361.1 15.8 %collective-permute-start.63 = (bf16[64,2048]{1,0:T(8,128)(2,1)S(1)}, bf16[64,2048]{1,0:T(8,128)(2,1)S(1)}, u32[]{:S(2)}, u32[]{:S(2)}) collective-permute-start(bf16[64,2048]{1,0:T(8,128)(2,1)S(1)} %add_convert_fusion.11), channel_id=1, source_target_pairs={{0,8},{1,9},{2,10},{3,11},{4,12},{5,13},{6,14},{7,15},{8,0},{9,1},... | collective-permute-start | bytes 786440 | tf_op jit(solution)/shard_map/ppermute | solution.py:48
  383.7 12.3 %collective-permute-start.65 = (bf16[4,4,64,768]{3,2,1,0:T(8,128)(2,1)}, bf16[4,4,64,768]{3,2,1,0:T(8,128)(2,1)}, u32[]{:S(2)}, u32[]{:S(2)}) collective-permute-start(bf16[4,4,64,768]{3,2,1,0:T(8,128)(2,1)} %heads_chunks.6), channel_id=1, source_target_pairs={{0,1},{1,0},{2,3},{3,2},{4,5},{5,4},{6,7},{7,6},{8,9},{9,8},{10,11... | collective-permute-start | bytes 4718600 | tf_op jit(solution)/shard_map/ppermute | solution.py:55
  386.3 9.8 %collective-permute-start.66 = (bf16[4,64,1280]{2,1,0:T(8,128)(2,1)S(1)}, bf16[4,64,1280]{2,1,0:T(8,128)(2,1)S(1)}, u32[]{:S(2)}, u32[]{:S(2)}) collective-permute-start(bf16[4,64,1280]{2,1,0:T(8,128)(2,1)S(1)} %add_convert_fusion.5), channel_id=1, source_target_pairs={{0,2},{1,5},{2,0},{3,7},{4,6},{5,1},{6,4},{7,3},{8,10},{9,13},{10,... | collective-permute-start | bytes 1966088 | tf_op jit(solution)/shard_map/ppermute | solution.py:48
  397.7 18.5 %collective-permute-start.67 = (bf16[4,64,768]{2,1,0:T(8,128)(2,1)S(1)}, bf16[4,64,768]{2,1,0:T(8,128)(2,1)S(1)}, u32[]{:S(2)}, u32[]{:S(2)}) collective-permute-start(bf16[4,64,768]{2,1,0:T(8,128)(2,1)S(1)} %add_convert_fusion.9), channel_id=1, source_target_pairs={{0,4},{1,3},{2,6},{3,1},{4,0},{5,7},{6,2},{7,5},{8,12},{9,11},{10,... | collective-permute-start | bytes 1179656 | tf_op jit(solution)/shard_map/ppermute | solution.py:48
  398.8 17.4 %collective-permute-start.68 = (bf16[4,64,768]{2,1,0:T(8,128)(2,1)S(1)}, bf16[4,64,768]{2,1,0:T(8,128)(2,1)S(1)}, u32[]{:S(2)}, u32[]{:S(2)}) collective-permute-start(bf16[4,64,768]{2,1,0:T(8,128)(2,1)S(1)} %add_convert_fusion.8), channel_id=1, source_target_pairs={{0,4},{1,3},{2,6},{3,1},{4,0},{5,7},{6,2},{7,5},{8,12},{9,11},{10,... | collective-permute-start | bytes 1179656 | tf_op jit(solution)/shard_map/ppermute | solution.py:48
  399.7 16.4 %collective-permute-start.69 = (bf16[64,1280]{1,0:T(8,128)(2,1)S(1)}, bf16[64,1280]{1,0:T(8,128)(2,1)S(1)}, u32[]{:S(2)}, u32[]{:S(2)}) collective-permute-start(bf16[64,1280]{1,0:T(8,128)(2,1)S(1)} %get-tuple-element.528), channel_id=1, source_target_pairs={{0,16},{1,17},{2,18},{3,19},{4,20},{5,21},{6,22},{7,23},{8,24},{9,... | collective-permute-start | bytes 491528 | tf_op jit(solution)/shard_map/ppermute | solution.py:48
  416.2 18.0 %collective-permute-start.74 = (bf16[512,1024]{1,0:T(8,128)(2,1)}, bf16[512,1024]{1,0:T(8,128)(2,1)S(1)}, u32[]{:S(2)}, u32[]{:S(2)}) collective-permute-start(bf16[512,1024]{1,0:T(8,128)(2,1)} %get-tuple-element.477), channel_id=1, source_target_pairs={{0,1},{1,0},{2,3},{3,2},{4,5},{5,4},{6,7},{7,6},{8,9},{9,8},{10,11... | collective-permute-start | bytes 3145736 | tf_op jit(solution)/shard_map/ppermute | solution.py:55
  418.6 15.6 %collective-permute-start.70 = (bf16[4,64,768]{2,1,0:T(8,128)(2,1)S(1)}, bf16[4,64,768]{2,1,0:T(8,128)(2,1)S(1)}, u32[]{:S(2)}, u32[]{:S(2)}) collective-permute-start(bf16[4,64,768]{2,1,0:T(8,128)(2,1)S(1)} %add_convert_fusion.7), channel_id=1, source_target_pairs={{0,2},{1,5},{2,0},{3,7},{4,6},{5,1},{6,4},{7,3},{8,10},{9,13},{10,... | collective-permute-start | bytes 1179656 | tf_op jit(solution)/shard_map/ppermute | solution.py:48
  418.9 15.3 %collective-permute-start.71 = (bf16[64,1280]{1,0:T(8,128)(2,1)S(1)}, bf16[64,1280]{1,0:T(8,128)(2,1)S(1)}, u32[]{:S(2)}, u32[]{:S(2)}) collective-permute-start(bf16[64,1280]{1,0:T(8,128)(2,1)S(1)} %get-tuple-element.471), channel_id=1, source_target_pairs={{0,16},{1,17},{2,18},{3,19},{4,20},{5,21},{6,22},{7,23},{8,24},{9,... | collective-permute-start | bytes 491528 | tf_op jit(solution)/shard_map/ppermute | solution.py:48
  420.0 14.2 %collective-permute-start.72 = (bf16[64,1280]{1,0:T(8,128)(2,1)S(1)}, bf16[64,1280]{1,0:T(8,128)(2,1)S(1)}, u32[]{:S(2)}, u32[]{:S(2)}) collective-permute-start(bf16[64,1280]{1,0:T(8,128)(2,1)S(1)} %add_convert_fusion.15), channel_id=1, source_target_pairs={{0,8},{1,9},{2,10},{3,11},{4,12},{5,13},{6,14},{7,15},{8,0},{9,1},... | collective-permute-start | bytes 491528 | tf_op jit(solution)/shard_map/ppermute | solution.py:48
  423.2 11.0 %collective-permute-start.73 = (f32[8,1024]{1,0:T(8,128)}, f32[8,1024]{1,0:T(8,128)S(1)}, u32[]{:S(2)}, u32[]{:S(2)}) collective-permute-start(f32[8,1024]{1,0:T(8,128)} %sums.1), channel_id=1, source_target_pairs={{0,16},{1,17},{2,18},{3,19},{4,20},{5,21},{6,22},{7,23},{8,24},{9,... | collective-permute-start | bytes 98312 | tf_op jit(solution)/shard_map/ppermute | solution.py:901
  434.3 13.0 %collective-permute-start.78 = (bf16[64,1280]{1,0:T(8,128)(2,1)S(1)}, bf16[64,1280]{1,0:T(8,128)(2,1)S(1)}, u32[]{:S(2)}, u32[]{:S(2)}) collective-permute-start(bf16[64,1280]{1,0:T(8,128)(2,1)S(1)} %add_convert_fusion.14), channel_id=1, source_target_pairs={{0,1},{1,0},{2,3},{3,2},{4,5},{5,4},{6,7},{7,6},{8,9},{9,8},{10,11... | collective-permute-start | bytes 491528 | tf_op jit(solution)/shard_map/ppermute | solution.py:55
  436.2 12.2 %collective-permute-start.75 = (bf16[512,1024]{1,0:T(8,128)(2,1)}, bf16[512,1024]{1,0:T(8,128)(2,1)}, u32[]{:S(2)}, u32[]{:S(2)}) collective-permute-start(bf16[512,1024]{1,0:T(8,128)(2,1)} %down.2), channel_id=1, source_target_pairs={{0,1},{1,0},{2,3},{3,2},{4,5},{5,4},{6,7},{7,6},{8,9},{9,8},{10,11... | collective-permute-start | bytes 3145736 | tf_op jit(solution)/shard_map/ppermute | solution.py:55
  436.3 12.0 %collective-permute-start.76 = (f32[12,1024]{1,0:T(8,128)S(1)}, f32[12,1024]{1,0:T(8,128)S(1)}, u32[]{:S(2)}, u32[]{:S(2)}) collective-permute-start(f32[12,1024]{1,0:T(8,128)S(1)} %pad_maximum_fusion.12), channel_id=1, source_target_pairs={{0,8},{1,9},{2,10},{3,11},{4,12},{5,13},{6,14},{7,15},{8,0},{9,1},... | collective-permute-start | bytes 147464 | tf_op jit(solution)/shard_map/ppermute | solution.py:901
  436.7 11.7 %collective-permute-start.77 = (bf16[64,768]{1,0:T(8,128)(2,1)S(1)}, bf16[64,768]{1,0:T(8,128)(2,1)}, u32[]{:S(2)}, u32[]{:S(2)}) collective-permute-start(bf16[64,768]{1,0:T(8,128)(2,1)S(1)} %get-tuple-element.536), channel_id=1, source_target_pairs={{0,16},{1,17},{2,18},{3,19},{4,20},{5,21},{6,22},{7,23},{8,24},{9,... | collective-permute-start | bytes 294920 | tf_op jit(solution)/shard_map/ppermute | solution.py:48
  (144 other events, 1616.8 us)

commit v4 on v3

--- a/solution.py
+++ b/solution.py
@@ -226,7 +226,7 @@
                 if t < 2:
                     piece = turned(piece, cosine[at, :], sine[at, :])
                 if t == 0:
-                    piece = piece * HD ** (-0.5)
+                    piece = piece * (HD ** (-0.5) / math.log(2.0))
                 packed[at, t * part + c : t * part + c + LANES] = piece.astype(BF16)
 
 
@@ -250,41 +250,37 @@
 
 def attend_kernel(step, q, kv, mask, mixed, lse):
     lane = lax.broadcasted_iota(jnp.int32, (1, LANES), 1)
-    zero = jnp.zeros((), BF16)
+    zero, one = jnp.zeros((), BF16), jnp.ones((), BF16)
     mine = [lane < HD, lane >= HD]
+    spare = [lane == HD, lane == 0]
     part = q.shape[1] // 3
     away = mask[...]
-
     lse[...] = jnp.zeros_like(lse)
     for c in range(0, part, LANES):
-        keys = [jnp.where(m, kv[:, part + c : part + c + LANES], zero) for m in mine]
-        values = [jnp.where(m, kv[:, 2 * part + c : 2 * part + c + LANES], zero) for m in mine]
-
-        def body(i, _):
-            rows = pl.ds(pl.multiple_of(i * step, step), step)
+        k, v = kv[:, part + c : part + c + LANES], kv[:, 2 * part + c : 2 * part + c + LANES]
+        keys = [jnp.where(spare[h], away, jnp.where(mine[h], k, zero)) for h in range(2)]
+        values = [jnp.where(spare[h], one, jnp.where(mine[h], v, zero)) for h in range(2)]
+        for r in range(0, q.shape[0], step):
+            rows = slice(r, r + step)
             queries, kept = q[rows, c : c + LANES], lse[rows, :]
-            out = None
+            scores = [dot(jnp.where(spare[h], one, queries), keys[h], 1, 1) for h in range(2)]
+            outs = []
             for h in range(2):
-                scores = dot(queries, keys[h], 1, 1) + away
-                top = jnp.max(scores, axis=-1, keepdims=True)
-                weights = jnp.exp(scores - top)
-                total = jnp.sum(weights, axis=-1, keepdims=True)
-                product = dot(weights.astype(BF16), values[h]) * (1.0 / total)
-                out = product if out is None else out + product
-                kept = jnp.where(lane == c // HD + h, top + jnp.log(total), kept)
+                top = jnp.max(scores[h], axis=-1, keepdims=True)
+                product = dot(jnp.exp2(scores[h] - top).astype(BF16), values[h])
+                total = jnp.sum(jnp.where(spare[h], product, 0.0), axis=-1, keepdims=True)
+                outs.append(product * (1.0 / total))
+                kept = jnp.where(lane == c // HD + h, top + jnp.log2(total), kept)
             lse[rows, :] = kept
-            mixed[rows, c : c + LANES] = out.astype(BF16)
-            return 0
-
-        lax.fori_loop(0, q.shape[0] // step, body, 0)
+            mixed[rows, c : c + LANES] = jnp.where(mine[0], outs[0], outs[1]).astype(BF16)
 
 
 def attend(half, q, kv, mask):
     rows, width, places = q.shape[0], q.shape[1] // 6, kv.shape[0]
     part = lambda v: spec((v.shape[0], 3 * width), lambda p: (0, half))
     return call(
-        functools.partial(attend_kernel, min(rows, 512)), "attend", (1,),
-        [part(q), part(kv), whole((1, places))],
+        functools.partial(attend_kernel, min(rows, 256)), "attend", (1,),
+        [part(q), part(kv), whole((places, 1))],
         [whole((rows, width)), whole((rows, LANES))],
         [((rows, width), BF16), ((rows, LANES), F32)], [],
         16 * rows * places * width, 8 * rows * width,
@@ -321,38 +317,37 @@
             keys.append(own)
             keys_more.append(jnp.where(ones, one, jnp.where(lane == spare[h] + 3, mask[...], own)))
             values_more.append(jnp.where(ones, one, jnp.where(mine[h], v, zero)))
-        key_sum[...] = jnp.zeros_like(key_sum)
-        value_sum[...] = jnp.zeros_like(value_sum)
-
-        def body(i, _):
-            rows = pl.ds(pl.multiple_of(i * step, step), step)
+        for r in range(0, q.shape[0], step):
+            rows = slice(r, r + step)
             queries, grads = q[rows, c : c + LANES], grad[rows, c : c + LANES]
             kept = lse[rows, :]
             product = grads.astype(F32) * mixed[rows, c : c + LANES].astype(F32)
-            total = None
+            own_q, own_g, scores, grad_probs = [], [], [], []
             for h in range(2):
                 delta = jnp.sum(jnp.where(mine[h], product, 0.0), axis=-1, keepdims=True)
-                head = c // HD + h
-                log_sum = jnp.sum(jnp.where(lane == head, kept, 0.0), axis=-1, keepdims=True)
-                own_q = jnp.where(mine[h], queries, zero)
-                own_g = jnp.where(mine[h], grads, zero)
-                more_q = jnp.where(lane == spare[h] + 3, one, own_q)
-                more_g = own_g
+                log_sum = jnp.sum(jnp.where(lane == c // HD + h, kept, 0.0), axis=-1, keepdims=True)
+                own_q.append(jnp.where(mine[h], queries, zero))
+                own_g.append(jnp.where(mine[h], grads, zero))
+                more_q, more_g = jnp.where(lane == spare[h] + 3, one, own_q[h]), own_g[h]
                 for t, (a, b) in enumerate(zip(thirds(-log_sum), thirds(-delta))):
                     more_q = jnp.where(lane == spare[h] + t, a, more_q)
                     more_g = jnp.where(lane == spare[h] + t, b, more_g)
-                probs = jnp.exp(dot(keys_more[h], more_q, 1, 1))
-                grad_scores = (probs * dot(values_more[h], more_g, 1, 1)).astype(BF16)
-                value_sum[...] += dot(probs.astype(BF16), own_g)
-                key_sum[...] += dot(grad_scores, own_q)
-                product_q = dot(keys[h], grad_scores, 0, 0)
-                total = product_q if total is None else total + product_q
-            grad_q = turned(total.T, cosine[rows, :], -sine[rows, :]) * HD ** (-0.5)
+                scores.append(dot(keys_more[h], more_q, 1, 1))
+                grad_probs.append(dot(values_more[h], more_g, 1, 1))
+            sums = []
+            for h in range(2):
+                probs = jnp.exp2(scores[h])
+                grad_scores = (probs * grad_probs[h]).astype(BF16)
+                sums.append((
+                    dot(probs.astype(BF16), own_g[h]), dot(grad_scores, own_q[h]), dot(keys[h], grad_scores, 0, 0)
+                ))
+            for_v, for_k, for_q = [a + b for a, b in zip(*sums)]
+            value_sum[...] = for_v if r == 0 else value_sum[...] + for_v
+            key_sum[...] = for_k if r == 0 else key_sum[...] + for_k
+            grad_q = turned(for_q.T, cosine[rows, :], -sine[rows, :]) * HD ** (-0.5)
             out_q[rows, c : c + LANES] = grad_q.astype(BF16)
-            return 0
-
-        lax.fori_loop(0, q.shape[0] // step, body, 0)
-        out_kv[:, before + c : before + c + LANES] = turned(key_sum[...], key_cos[...], -key_sin[...]).astype(BF16)
+        grad_k = turned(key_sum[...], key_cos[...], -key_sin[...]) * math.log(2.0)
+        out_kv[:, before + c : before + c + LANES] = grad_k.astype(BF16)
         out_kv[:, before + part + c : before + part + c + LANES] = value_sum[...].astype(BF16)
 
 
@@ -366,7 +361,7 @@
     else:
         shapes = [((rows, width), BF16), ((places, 2 * width), BF16)]
     return call(
-        functools.partial(attend_back_kernel, min(rows, 512)), "attend_back", (1,),
+        functools.partial(attend_back_kernel, min(rows, 256)), "attend_back", (1,),
         [column(rows, 3 * width, half), column(places, 3 * width, half), whole((rows, width)),
          column(rows, width, 2 * group + half), whole((rows, LANES)), whole((places, 1))]
         + [whole((rows, LANES))] * 2 + [whole((places, LANES))] * len(more),
@@ -433,15 +428,15 @@
     arrived(matrix, sems.at[j], start, block)
     weight = columns(matrix, start, block)
     root = math.sqrt(2.0 / math.pi)
-    for r in range(0, normed.shape[0], ROWS):
-        rows = slice(r, r + ROWS)
+    for r in range(0, normed.shape[0], ROWS // 2):
+        rows = slice(r, r + ROWS // 2)
         h = dot(normed[rows, :], weight)
         square = h * h
-        t = jnp.tanh(h * (root + (root * 0.044715) * square))
-        half = 0.5 + 0.5 * t
-        active[rows, :] = (h * half).astype(BF16)
+        half = 0.5 + 0.5 * jnp.tanh(h * (root + (root * 0.044715) * square))
+        result = h * half
+        active[rows, :] = result.astype(BF16)
         slope[rows, :] = (
-            half + (h * half) * (1.0 - t) * (root + (3.0 * 0.044715 * root) * square)
+            half + result * (1.0 - half) * (2.0 * root + (6.0 * 0.044715 * root) * square)
         ).astype(BF16)
 
 
@@ -537,11 +532,12 @@
     )(places, grad, slope, *pieces)[0]
 
 
-def norm_back_kernel(spans, starts, count, count_outs, place, x, gain, base, *refs):
-    pieces, grads, outs = refs[: count * len(spans)], refs[count * len(spans) : -6 - count_outs], refs[-6 - count_outs :]
-    *outs, sums, matrix, taken, total, sems, grad_sems = outs
+def norm_back_kernel(spans, starts, count, count_outs, place, gain, x_far, base_far, *refs):
+    pieces, grads, outs = refs[: count * len(spans)], refs[count * len(spans) : -9 - count_outs], refs[-9 - count_outs :]
+    *outs, sums, matrix, taken, total, x, base, sems, grad_sems, row_sems = outs
     block = taken.shape[-1]
     full = matrix.shape[-1] // len(spans)
+    last = len(starts) - 1
 
     def grad_copy(i):
         which, start = starts[i]
@@ -553,24 +549,32 @@
             which = i * block // full
             part = matrix.at[:, :, :, :, pl.ds(which * full, full)]
             start_blocks(place, pieces[count * which : count * (which + 1)], spans[which], part, sems, block, i)
+    copies = [pltpu.make_async_copy(x_far, x, row_sems.at[0]), pltpu.make_async_copy(base_far, base, row_sems.at[1])]
+    for v in copies:
+        v.start()
     for i in range(len(starts)):
         grad_copy(i).wait()
         arrived(matrix, sems.at[i], i * block, block)
-        product = dot(taken[i], columns(matrix, i * block, block), 1, 1)
-        total[...] = product if i == 0 else total[...] + product
+        if i < last:
+            product = dot(taken[i], columns(matrix, i * block, block), 1, 1)
+            total[...] = product if i == 0 else total[...] + product
+    for v in copies:
+        v.wait()
+    weight = columns(matrix, last * block, block)
     added = [jnp.zeros((1, x.shape[1]), F32)] * 2
     each = x.shape[0] // count_outs
-    for r in range(0, x.shape[0], min(ROWS, each)):
-        rows = slice(r, r + min(ROWS, each))
+    size = min(ROWS, each)
+    for r in range(0, x.shape[0], size):
+        rows = slice(r, r + size)
+        back = total[rows, :] + dot(taken[last, rows, :], weight, 1, 1)
         hat, inverse = normalized(x[rows, :].astype(F32))
-        back = total[rows, :]
         added[0] = added[0] + jnp.sum(back * hat, axis=0, keepdims=True)
         added[1] = added[1] + jnp.sum(back, axis=0, keepdims=True)
         inner = back * gain[...]
         mean = jnp.mean(inner, axis=-1, keepdims=True)
         lean = jnp.mean(inner * hat, axis=-1, keepdims=True)
         result = (base[rows, :].astype(F32) + inverse * (inner - mean - hat * lean)).astype(BF16)
-        outs[r // each][r % each : r % each + result.shape[0], :] = result
+        outs[r // each][r % each : r % each + size, :] = result
     sums[...] = jnp.concatenate(added, axis=0)
 
 
@@ -580,15 +584,16 @@
     *outer, cols = matrix_shape(grid, weights[0])
     full = cols * len(weights)
     count = len(weights[0][0])
+    semaphores = [pltpu.SemaphoreType.DMA((n,)) for n in (len(starts), len(starts), 2)]
     return call(
         functools.partial(norm_back_kernel, [w[1] for w in weights], starts, count, outs), "norm_back", (1,),
-        [SCALARS, whole(x.shape), whole((1, width)), whole(x.shape)] + [ANY] * (len(weights) * count + len(grads)),
+        [SCALARS, whole((1, width))] + [ANY] * (2 + len(weights) * count + len(grads)),
         [whole((rows // outs, width))] * outs + [whole((2, width))],
         [((rows // outs, width), BF16)] * outs + [((2, width), F32)],
-        [pltpu.VMEM((*outer, full), BF16), pltpu.VMEM((len(starts), rows, block), BF16),
-         pltpu.VMEM(x.shape, F32), pltpu.SemaphoreType.DMA((len(starts),)), pltpu.SemaphoreType.DMA((len(starts),))],
-        2 * rows * width * full, 2 * width * full + 2 * rows * full + 6 * rows * width, room=24 << 20,
-    )(places, x, gain, base, *[v for w in weights for v in w[0]], *grads)
+        [pltpu.VMEM((*outer, full), BF16), pltpu.VMEM((len(starts), rows, block), BF16), pltpu.VMEM(x.shape, F32),
+         pltpu.VMEM(x.shape, BF16), pltpu.VMEM(x.shape, BF16)] + semaphores,
+        2 * rows * width * full, 2 * width * full + 2 * rows * full + 6 * rows * width,
+    )(places, gain, x, base, *[v for w in weights for v in w[0]], *grads)
 
 
 def heads_back_kernel(count, span, block, place, grad, *refs):
@@ -1006,9 +1011,8 @@
     if ranks > 1:
         key_tables = [jnp.concatenate([v for r in range(ranks) for v in table_of(t, r)]) for t in full_tables]
     length = lax.dynamic_index_in_dim(line.at(lengths), core, 0, keepdims=False)
-    mask = jnp.where(key_places < length, 0.0, MASKED).astype(F32)
-    mask_column = mask[:, None].astype(BF16)
-    line.mark(moved, swaps, more, far, tables, mask_column)
+    mask = jnp.where(key_places < length, 0.0, MASKED).astype(BF16)[:, None]
+    line.mark(moved, swaps, more, far, tables, mask)
 
     swaps = heads_a.swap(1, 2, 3)
     more = heads_b.outer_step()
@@ -1051,11 +1055,11 @@
     packed_a, mask = line.at(packed_a, mask)
     if ranks == 1:
         wide_a = packed_a
-    att[0, 0] = attend(0, packed_a, wide_a, mask[None])
+    att[0, 0] = attend(0, packed_a, wide_a, mask)
     line.mark(att[0, 0], swaps, more)
 
     more = up_w.outer_step()
-    att[0, 1] = attend(1, packed_a, wide_a, line.at(mask)[None])
+    att[0, 1] = attend(1, packed_a, wide_a, line.at(mask))
     line.mark(att[0, 1], moved, more)
 
     swaps = heads_b.swap(2, 3)
@@ -1074,13 +1078,13 @@
     packed_b, mask = line.at(packed_b, mask)
     if ranks == 1:
         wide_b = packed_b
-    att[1, 0] = attend(0, packed_b, wide_b, mask[None])
+    att[1, 0] = attend(0, packed_b, wide_b, mask)
     line.mark(att[1, 0], moved, more, cot)
 
     moved = up_w.last()
     swaps = up_w.swap(0, 1)
     more = down_w.outer_step()
-    att[1, 1] = attend(1, packed_b, wide_b, line.at(mask)[None])
+    att[1, 1] = attend(1, packed_b, wide_b, line.at(mask))
     mixed = [att[i][0] for i in ((0, 0), (0, 1), (1, 0), (1, 1))]
     line.mark(att[1, 1], swaps, more)
 
@@ -1121,7 +1125,7 @@
 
     push_up = Push(grid, line, line.at(sent))
     down += push_down.second(False)
-    grad_middle, sums2 = norm_back(grid, at, line.at((grad_hidden,)), middle, eff2, cot, (up_w.weight(),), 512)
+    grad_middle, sums2 = norm_back(grid, at, line.at((grad_hidden,)), middle, eff2, cot, (up_w.weight(),), 1024)
     line.mark(grad_middle, down, push_up.came)
 
     down = push_down.first()
@@ -1134,7 +1138,7 @@
     def back(group, half, grad_heads):
         packed, wide = ((packed_a, wide_a), (packed_b, wide_b))[group]
         mixed, lse = att[group, half]
-        parts = attend_back(group, half, packed, wide, mixed, grad_heads, lse, mask_column, tables, key_tables)
+        parts = attend_back(group, half, packed, wide, mixed, grad_heads, lse, mask, tables, key_tables)
         if ranks == 1:
             return parts[0]
         rest = lax.psum_scatter(

time: 482 us -> 466 us (0.967)
  Pallas kernels: 276 us -> 247 us
  waiting for transfers between devices: 52.3 us -> 70.6 us
    pallas_call x30, Pallas kernels: 251 us -> 222 us  [run(): kernel_call(kernel, name, grid, ins, outs, shapes, scratch, flops, moved,...]
    ppermute x48, waiting for transfers between devices: 23.4 us -> 40.7 us  [shift(): return lax.ppermute(v, AXES, pairs)]
  transfers between devices with their start and end apart: 85 -> 85, of which waited for: 20 -> 29; matrix products, arithmetic and copies ran while one was open for 8% -> 7% of each run, Pallas kernels for 52% -> 47%
where the time goes in v4:
time: 466 us; the launch traced here: 459 us
  Pallas kernels  247 us (53%)
  starting transfers between devices  78.5 us (17%)
  waiting for transfers between devices  70.6 us (15%)
  local copies, waits for them, and re-layouts  29.7 us (6%)
  other arithmetic  28.5 us (6%)
    pallas_call x30, Pallas kernels, run(): kernel_call(kernel, name, grid, ins, outs, shapes, scratch, flops, moved,...  222 us
    ppermute x48, starting transfers between devices, shift(): return lax.ppermute(v, AXES, pairs)  43.2 us
    ppermute x48, waiting for transfers between devices, shift(): return lax.ppermute(v, AXES, pairs)  40.7 us
    ppermute x28, starting transfers between devices, swap(): return lax.ppermute(v, AXES, pairs)  26.3 us
    pallas_call x2, Pallas kernels, up_product(): pl.pallas_call(kernel, grid=(per,), in_specs=[SCALARS, whole(normed.shape...  24.5 us
    ppermute x8, waiting for transfers between devices, doubled(): return lax.ppermute(v, AXES, pairs)  19.4 us
    unnamed x249, local copies, waits for them, and re-layouts  15 us
    ppermute x28, waiting for transfers between devices, swap(): return lax.ppermute(v, AXES, pairs)  10.5 us
  transfers between devices with their start and end apart: 85, of which 29 were waited for; matrix products, arithmetic and copies ran while one was open for 7% of the time, Pallas kernels for 47%

profile of v4, /device:TPU:1, one launch (start us, length us, event | category | flops | bytes accessed | tf_op | source)
XLA Modules:
  0.0 459.2 jit_solution(6957223622975407905)
XLA Ops:
  1.8 4.2 collective-permute-start.1
  9.1 2.3 collective-permute-start.4
  12.8 3.1 collective-permute-done.4
  18.0 2.8 pad_maximum_fusion.refs_0_.x.x_far
  23.4 3.9 collective-permute-start.12
  34.5 6.6 %collective-permute-done.8 = bf16[4,8,2176]{2,1,0:T(8,128)(2,1)S(1)} collective-permute-done((bf16[4,8,2176]{2,1,0:T(8,128)(2,1)S(1)}, bf16[4,8,2176]{2,1,0:T(8,128)(2,1)S(1)}, u32[]{:S(2)}, u32[]{:S(2)}) %collective-permute-start.8) | collective-permute-done | bytes 139296 | tf_op jit(solution)/shard_map/ppermute | solution.py:906
  45.3 4.0 collective-permute-done.13
  53.6 1.9 collective-permute-start.19
  55.5 9.1 %qkv_first.1 = (bf16[1024,1024]{1,0:T(8,128)(2,1)}, bf16[1024,1024]{1,0:T(8,128)(2,1)}, bf16[1024,1536]{1,0:T(8,128)(2,1)}) custom-call(s32[24]{0:T(128)} %fusion.31.place, bf16[1024,1024]{1,0:T(8,128)(2,1)} %pad_maximum_fusion.refs_0_.x.x_far, f32[1,1024]{1,0:T(1,128)} %get-tuple-element.290.refs_1_.gain, f32[1,1024]{1,0:T(1,128)} %squeeze.128.refs_2_, ...), custom_call_target="tpu_custom_call" | custom-call | flops 3221225472 | bytes 12582912 | tf_op jit(solution)/shard_map/qkv_first/pallas_call | solution.py:106
  64.6 3.0 collective-permute-start.22
  69.4 1.9 copy-done.58
  71.2 5.7 %attend.4 = (bf16[1024,256]{1,0:T(8,128)(2,1)S(1)}, f32[1024,128]{1,0:T(8,128)S(1)}) custom-call(bf16[1024,1536]{1,0:T(8,128)(2,1)S(1)} %copy-done.58, bf16[1024,1536]{1,0:T(8,128)(2,1)S(1)} %copy-done.58, bf16[1024,1]{1,0:T(8,128)(2,1)S(1)} %copy.48.mask), custom_call_target="tpu_custom_call" | custom-call | flops 4294967296 | bytes 2097152 | tf_op jit(solution)/shard_map/attend/pallas_call | solution.py:106
  78.1 5.8 %attend.5 = (bf16[1024,256]{1,0:T(8,128)(2,1)S(1)}, f32[1024,128]{1,0:T(8,128)S(1)}) custom-call(bf16[1024,1536]{1,0:T(8,128)(2,1)S(1)} %copy-done.58, bf16[1024,1536]{1,0:T(8,128)(2,1)S(1)} %copy-done.58, bf16[1024,1]{1,0:T(8,128)(2,1)S(1)} %copy.48.mask), custom_call_target="tpu_custom_call" | custom-call | flops 4294967296 | bytes 2097152 | tf_op jit(solution)/shard_map/attend/pallas_call | solution.py:106
  84.9 2.0 collective-permute-start.26
  89.8 1.9 collective-permute-start.29
  91.7 5.2 %qkv.1.q.kv = bf16[1024,1536]{1,0:T(8,128)(2,1)S(1)} custom-call(s32[24]{0:T(128)S(1)} %copy-done.51, bf16[1024,1024]{1,0:T(8,128)(2,1)S(1)} %copy-done.57, f32[1024,128]{1,0:T(8,128)S(1)} %copy-done.41, f32[1024,128]{1,0:T(8,128)S(1)} %copy-done.44, bf16[4,64,1280]{2,1,0:T(8,128)(2,1)S(1)} %rolled.5.refs_3_.refs_0_.refs_8_, ...), custom_call_target="tpu_custom_call" | custom-call | flops 3221225472 | bytes 12582912 | tf_op jit(solution)/shard_map/qkv/pallas_call | solution.py:106
  97.0 3.1 collective-permute-start.31
  100.2 5.8 %attend.6 = (bf16[1024,256]{1,0:T(8,128)(2,1)S(1)}, f32[1024,128]{1,0:T(8,128)S(1)}) custom-call(bf16[1024,1536]{1,0:T(8,128)(2,1)S(1)} %qkv.1.q.kv, bf16[1024,1536]{1,0:T(8,128)(2,1)S(1)} %qkv.1.q.kv, bf16[1024,1]{1,0:T(8,128)(2,1)S(1)} %copy.48.mask), custom_call_target="tpu_custom_call" | custom-call | flops 4294967296 | bytes 2097152 | tf_op jit(solution)/shard_map/attend/pallas_call | solution.py:106
  107.6 2.8 collective-permute-start.32
  112.3 5.8 %attend.7 = (bf16[1024,256]{1,0:T(8,128)(2,1)S(1)}, f32[1024,128]{1,0:T(8,128)S(1)}) custom-call(bf16[1024,1536]{1,0:T(8,128)(2,1)S(1)} %qkv.1.q.kv, bf16[1024,1536]{1,0:T(8,128)(2,1)S(1)} %qkv.1.q.kv, bf16[1024,1]{1,0:T(8,128)(2,1)S(1)} %copy.48.mask), custom_call_target="tpu_custom_call" | custom-call | flops 4294967296 | bytes 2097152 | tf_op jit(solution)/shard_map/attend/pallas_call | solution.py:106
  118.9 8.4 %out.1 = (bf16[1024,1024]{1,0:T(8,128)(2,1)S(1)}, bf16[1024,1024]{1,0:T(8,128)(2,1)S(1)}, bf16[1024,1024]{1,0:T(8,128)(2,1)}) custom-call(s32[24]{0:T(128)S(1)} %copy-done.51, bf16[1024,1024]{1,0:T(8,128)(2,1)} %pad_maximum_fusion.refs_0_.x.x_far, f32[1,1024]{1,0:T(1,128)S(1)} %get-tuple-element.551.gain, f32[1,1024]{1,0:T(1,128)S(1)} %squeeze.126.bias, ...), custom_call_target="tpu_custom_call" | custom-call | flops 2147483648 | bytes 10485760 | tf_op jit(solution)/shard_map/out/pallas_call | solution.py:106
  128.6 7.0 %collective-permute-done.36.refs_3_ = bf16[4,64,2048]{2,1,0:T(8,128)(2,1)S(1)} collective-permute-done((bf16[4,64,2048]{2,1,0:T(8,128)(2,1)S(1)}, bf16[4,64,2048]{2,1,0:T(8,128)(2,1)S(1)}, u32[]{:S(2)}, u32[]{:S(2)}) %collective-permute-start.36) | collective-permute-done | bytes 1048608 | tf_op jit(solution)/shard_map/ppermute | solution.py:48
  137.0 2.2 collective-permute-done.37.refs_6_
  142.0 12.3 %up.2 = (bf16[1024,4096]{1,0:T(8,128)(2,1)}, bf16[1024,4096]{1,0:T(8,128)(2,1)}) custom-call(s32[24]{0:T(128)} %fusion.31.place, bf16[1024,1024]{1,0:T(8,128)(2,1)} %copy-done.36, bf16[4,64,2048]{2,1,0:T(8,128)(2,1)} %copy-done.19, bf16[4,64,2048]{2,1,0:T(8,128)(2,1)} %copy-done.80, bf16[4,64,2048]{2,1,0:T(8,128)(2,1)} %copy-done.85, ...), custom_call_target="tpu_custom_call" | custom-call | flops 4294967296 | bytes 12582912 | tf_op jit(solution)/shard_map/up/pallas_call | solution.py:449
  157.4 12.3 %up.3 = (bf16[1024,4096]{1,0:T(8,128)(2,1)}, bf16[1024,4096]{1,0:T(8,128)(2,1)}) custom-call(s32[24]{0:T(128)} %fusion.31.place, bf16[1024,1024]{1,0:T(8,128)(2,1)} %copy-done.36, bf16[4,64,2048]{2,1,0:T(8,128)(2,1)} %copy-done.19, bf16[4,64,2048]{2,1,0:T(8,128)(2,1)} %copy-done.80, ...), custom_call_target="tpu_custom_call", output_to_operand_aliasing={{0}: (10, {}), {1}: (11, {})} | custom-call | flops 4294967296 | bytes 12582912 | tf_op jit(solution)/shard_map/up/pallas_call | solution.py:449
  169.7 9.8 %wide_chunks.2 = bf16[4,4,256,512]{3,2,1,0:T(8,128)(2,1)} custom-call(s32[24]{0:T(128)} %fusion.31.place, bf16[1024,4096]{1,0:T(8,128)(2,1)} %get-tuple-element.478.refs_0_.refs_1_.refs_2_.refs_3_.active, bf16[1024,4096]{1,0:T(8,128)(2,1)} %get-tuple-element.478.refs_0_.refs_1_.refs_2_.refs_3_.active, ...), custom_call_target="tpu_custom_call" | custom-call | flops 4294967296 | bytes 14680064 | tf_op jit(solution)/shard_map/wide_chunks/pallas_call | solution.py:106
  179.5 1.7 collective-permute-done.43.refs_3_
  182.5 3.7 collective-permute-done.44.refs_6_
  187.6 14.9 %hidden_back.1.b.refs_8_ = bf16[1024,4096]{1,0:T(8,128)(2,1)} custom-call(s32[24]{0:T(128)} %fusion.31.place, bf16[1024,1024]{1,0:T(8,128)(2,1)} %pad_maximum_fusion.1.refs_4_.grad.base_far, bf16[1024,4096]{1,0:T(8,128)(2,1)} %get-tuple-element.363.slope, bf16[4,256,512]{2,1,0:T(8,128)(2,1)} %copy-done.5, bf16[4,256,512]{2,1,0:T(8,128)(2,1)} %copy-done.68, ...), custom_call_target="tpu_custom_call" | custom-call | flops 8589934592 | bytes 25165824 | tf_op jit(solution)/shard_map/hidden_back/pallas_call | solution.py:106
  202.5 11.7 %wide_chunks.3 = (bf16[4,256,512]{2,1,0:T(8,128)(2,1)}, bf16[4,256,512]{2,1,0:T(8,128)(2,1)}, bf16[4,256,512]{2,1,0:T(8,128)(2,1)}, bf16[4,256,512]{2,1,0:T(8,128)(2,1)}) custom-call(s32[24]{0:T(128)} %fusion.31.place, bf16[1024,4096]{1,0:T(8,128)(2,1)} %get-tuple-element.478.refs_0_.refs_1_.refs_2_.refs_3_.active, ...), custom_call_target="tpu_custom_call" | custom-call | flops 4294967296 | bytes 14680064 | tf_op jit(solution)/shard_map/wide_chunks/pallas_call | solution.py:106
  214.2 9.5 %row_chunks.2 = bf16[4,4,64,2048]{3,2,1,0:T(8,128)(2,1)} custom-call(s32[24]{0:T(128)} %fusion.31.place, bf16[1024,1024]{1,0:T(8,128)(2,1)} %get-tuple-element.380.a, bf16[1024,4096]{1,0:T(8,128)(2,1)} %hidden_back.1.b.refs_8_), custom_call_target="tpu_custom_call" | custom-call | flops 4294967296 | bytes 10485760 | tf_op jit(solution)/shard_map/row_chunks/pallas_call | solution.py:106
  225.6 16.4 %norm_back.2 = (bf16[1024,1024]{1,0:T(8,128)(2,1)}, f32[2,1024]{1,0:T(2,128)}) custom-call(s32[24]{0:T(128)} %fusion.31.place, f32[1,1024]{1,0:T(1,128)} %copy-done.53, bf16[1024,1024]{1,0:T(8,128)(2,1)} %copy-done.6, bf16[1024,1024]{1,0:T(8,128)(2,1)} %pad_maximum_fusion.1.refs_4_.grad.base_far, bf16[4,64,2048]{2,1,0:T(8,128)(2,1)} %copy-done.19, ...), custom_call_target="tpu_custom_call" | custom-call | flops 8589934592 | bytes 23068672 | tf_op jit(solution)/shard_map/norm_back/pallas_call | solution.py:106
  242.0 7.3 %collective-permute-done.49 = bf16[4,256,512]{2,1,0:T(8,128)(2,1)S(1)} collective-permute-done((bf16[4,256,512]{2,1,0:T(8,128)(2,1)S(1)}, bf16[4,256,512]{2,1,0:T(8,128)(2,1)S(1)}, u32[]{:S(2)}, u32[]{:S(2)}) %collective-permute-start.49) | collective-permute-done | bytes 1048608 | tf_op jit(solution)/shard_map/ppermute | solution.py:48
  251.9 10.6 %row_chunks.3 = (bf16[4,64,2048]{2,1,0:T(8,128)(2,1)}, bf16[4,64,2048]{2,1,0:T(8,128)(2,1)}, bf16[4,64,2048]{2,1,0:T(8,128)(2,1)}, bf16[4,64,2048]{2,1,0:T(8,128)(2,1)}) custom-call(s32[24]{0:T(128)} %fusion.31.place, bf16[1024,1024]{1,0:T(8,128)(2,1)} %get-tuple-element.380.a, bf16[1024,4096]{1,0:T(8,128)(2,1)} %hidden_back.1.b.refs_8_, ...), custom_call_target="tpu_custom_call" | custom-call | flops 4294967296 | bytes 10485760 | tf_op jit(solution)/shard_map/row_chunks/pallas_call | solution.py:106
  264.7 4.1 heads_back.1.grad
  270.0 1.8 add_convert_fusion.2
  273.4 11.1 %attend_back.4.refs_0_.refs_16_ = bf16[1024,768]{1,0:T(8,128)(2,1)S(1)} custom-call(bf16[1024,1536]{1,0:T(8,128)(2,1)S(1)} %copy-done.59, bf16[1024,1536]{1,0:T(8,128)(2,1)S(1)} %copy-done.59, bf16[1024,256]{1,0:T(8,128)(2,1)S(1)} %copy-done.12, bf16[1024,1024]{1,0:T(8,128)(2,1)S(1)} %heads_back.1.grad, f32[1024,128]{1,0:T(8,128)S(1)} %copy-done.67, ...), custom_call_target="tpu_custom_call" | custom-call | flops 10737418240 | bytes 4194304 | tf_op jit(solution)/shard_map/attend_back/pallas_call | solution.py:106
  284.5 2.0 collective-permute-done.51
  287.0 11.5 %attend_back.5.refs_1_.refs_17_ = bf16[1024,768]{1,0:T(8,128)(2,1)S(1)} custom-call(bf16[1024,1536]{1,0:T(8,128)(2,1)S(1)} %copy-done.59, bf16[1024,1536]{1,0:T(8,128)(2,1)S(1)} %copy-done.59, bf16[1024,256]{1,0:T(8,128)(2,1)S(1)} %copy-done.14, bf16[1024,1024]{1,0:T(8,128)(2,1)S(1)} %heads_back.1.grad, f32[1024,128]{1,0:T(8,128)S(1)} %copy-done.65, ...), custom_call_target="tpu_custom_call" | custom-call | flops 10737418240 | bytes 4194304 | tf_op jit(solution)/shard_map/attend_back/pallas_call | solution.py:106
  298.5 2.4 collective-permute-done.53
  303.1 6.0 %heads_chunks.4 = bf16[4,4,64,1280]{3,2,1,0:T(8,128)(2,1)} custom-call(s32[24]{0:T(128)S(1)} %copy-done.52, bf16[1024,1024]{1,0:T(8,128)(2,1)S(1)} %copy-done.3, bf16[1024,768]{1,0:T(8,128)(2,1)S(1)} %attend_back.4.refs_0_.refs_16_, bf16[1024,768]{1,0:T(8,128)(2,1)S(1)} %attend_back.5.refs_1_.refs_17_, bf16[1024,256]{1,0:T(8,128)(2,1)S(1)} %copy-done.12, ...), custom_call_target="tpu_custom_call" | custom-call | flops 2684354560 | bytes 7340032 | tf_op jit(solution)/shard_map/heads_chunks/pallas_call | solution.py:106
  309.1 6.0 %collective-permute-done.54 = bf16[256,512]{1,0:T(8,128)(2,1)S(1)} collective-permute-done((bf16[256,512]{1,0:T(8,128)(2,1)S(1)}, bf16[256,512]{1,0:T(8,128)(2,1)S(1)}, u32[]{:S(2)}, u32[]{:S(2)}) %collective-permute-start.54) | collective-permute-done | bytes 262176 | tf_op jit(solution)/shard_map/ppermute | solution.py:48
  315.2 2.2 collective-permute-start.57
  317.4 1.7 add_convert_fusion
  321.6 11.1 %attend_back.6.refs_0_.refs_18_ = bf16[1024,768]{1,0:T(8,128)(2,1)S(1)} custom-call(bf16[1024,1536]{1,0:T(8,128)(2,1)S(1)} %copy-done.55, bf16[1024,1536]{1,0:T(8,128)(2,1)S(1)} %copy-done.55, bf16[1024,256]{1,0:T(8,128)(2,1)S(1)} %copy-done.16, bf16[1024,1024]{1,0:T(8,128)(2,1)S(1)} %heads_back.1.grad, f32[1024,128]{1,0:T(8,128)S(1)} %copy-done.63, ...), custom_call_target="tpu_custom_call" | custom-call | flops 10737418240 | bytes 4194304 | tf_op jit(solution)/shard_map/attend_back/pallas_call | solution.py:106
  332.7 1.9 collective-permute-done.58
  336.8 9.1 %heads_chunks.5 = (bf16[4,64,1280]{2,1,0:T(8,128)(2,1)S(1)}, bf16[4,64,1280]{2,1,0:T(8,128)(2,1)S(1)}, bf16[4,64,1280]{2,1,0:T(8,128)(2,1)S(1)}, bf16[4,64,1280]{2,1,0:T(8,128)(2,1)S(1)}) custom-call(s32[24]{0:T(128)S(1)} %copy-done.52, bf16[1024,1024]{1,0:T(8,128)(2,1)} %get-tuple-element.444.a, bf16[1024,768]{1,0:T(8,128)(2,1)} %copy-done.7, ...), custom_call_target="tpu_custom_call" | custom-call | flops 2684354560 | bytes 7340032 | tf_op jit(solution)/shard_map/heads_chunks/pallas_call | solution.py:106
  349.1 1.9 copy-done.56
  351.0 11.1 %attend_back.7.refs_1_.refs_19_ = bf16[1024,768]{1,0:T(8,128)(2,1)S(1)} custom-call(bf16[1024,1536]{1,0:T(8,128)(2,1)S(1)} %copy-done.56, bf16[1024,1536]{1,0:T(8,128)(2,1)S(1)} %copy-done.56, bf16[1024,256]{1,0:T(8,128)(2,1)S(1)} %copy-done.18, bf16[1024,1024]{1,0:T(8,128)(2,1)S(1)} %copy-done.35, f32[1024,128]{1,0:T(8,128)S(1)} %copy-done.61, ...), custom_call_target="tpu_custom_call" | custom-call | flops 10737418240 | bytes 4194304 | tf_op jit(solution)/shard_map/attend_back/pallas_call | solution.py:106
  363.8 1.7 collective-permute-start.64
  365.5 3.8 heads_chunks.6
  373.9 2.5 heads_chunks.7
  377.6 4.8 %collective-permute-done.66 = bf16[4,64,1280]{2,1,0:T(8,128)(2,1)S(1)} collective-permute-done((bf16[4,64,1280]{2,1,0:T(8,128)(2,1)S(1)}, bf16[4,64,1280]{2,1,0:T(8,128)(2,1)S(1)}, u32[]{:S(2)}, u32[]{:S(2)}) %collective-permute-start.66) | collective-permute-done | bytes 655392 | tf_op jit(solution)/shard_map/ppermute | solution.py:48
  386.2 12.9 %norm_back.3 = (bf16[512,1024]{1,0:T(8,128)(2,1)}, bf16[512,1024]{1,0:T(8,128)(2,1)}, f32[2,1024]{1,0:T(2,128)}) custom-call(s32[24]{0:T(128)} %fusion.31.place, f32[1,1024]{1,0:T(1,128)} %get-tuple-element.290.refs_1_.gain, bf16[1024,1024]{1,0:T(8,128)(2,1)} %pad_maximum_fusion.refs_0_.x.x_far, ...), custom_call_target="tpu_custom_call" | custom-call | flops 6442450944 | bytes 18874368 | tf_op jit(solution)/shard_map/norm_back/pallas_call | solution.py:106
  399.1 2.3 collective-permute-start.74
  401.6 2.4 collective-permute-start.71
  405.5 1.7 collective-permute-start.73
  407.3 9.6 %down.2 = bf16[512,1024]{1,0:T(8,128)(2,1)} custom-call(s32[24]{0:T(128)} %fusion.31.place, bf16[1024,4096]{1,0:T(8,128)(2,1)} %get-tuple-element.478.refs_0_.refs_1_.refs_2_.refs_3_.active, bf16[1024,1024]{1,0:T(8,128)(2,1)} %copy-done.6, bf16[4,256,512]{2,1,0:T(8,128)(2,1)} %copy-done.5, bf16[4,256,512]{2,1,0:T(8,128)(2,1)} %copy-done.68, ...), custom_call_target="tpu_custom_call" | custom-call | flops 4294967296 | bytes 12582912 | tf_op jit(solution)/shard_map/down/pallas_call | solution.py:106
  419.0 2.0 collective-permute-start.77
  421.0 9.4 %down.3 = bf16[512,1024]{1,0:T(8,128)(2,1)} custom-call(s32[24]{0:T(128)} %fusion.31.place, bf16[1024,4096]{1,0:T(8,128)(2,1)} %get-tuple-element.478.refs_0_.refs_1_.refs_2_.refs_3_.active, bf16[1024,1024]{1,0:T(8,128)(2,1)} %copy-done.6, bf16[4,256,512]{2,1,0:T(8,128)(2,1)} %copy-done.5, bf16[4,256,512]{2,1,0:T(8,128)(2,1)} %copy-done.68, ...), custom_call_target="tpu_custom_call" | custom-call | flops 4294967296 | bytes 12582912 | tf_op jit(solution)/shard_map/down/pallas_call | solution.py:106
  437.4 2.7 collective-permute-done.80
  440.2 1.9 collective-permute-start.83
  443.3 4.6 %collective-permute-done.82 = f32[36,1024]{1,0:T(8,128)S(1)} collective-permute-done((f32[36,1024]{1,0:T(8,128)S(1)}, f32[36,1024]{1,0:T(8,128)S(1)}, u32[]{:S(2)}, u32[]{:S(2)}) %collective-permute-start.82) | collective-permute-done | bytes 147488 | tf_op jit(solution)/shard_map/ppermute | solution.py:906
  451.7 3.3 maximum_select_fusion.1
  (496 shorter events, 97.9 us)
Async XLA Ops:
  1.8 14.1 %collective-permute-start.1 = (bf16[1,64,768]{2,1,0:T(8,128)(2,1)S(1)}, bf16[1,64,768]{2,1,0:T(8,128)(2,1)S(1)}, u32[]{:S(2)}, u32[]{:S(2)}) collective-permute-start(bf16[1,64,768]{2,1,0:T(8,128)(2,1)S(1)} %maximum_bitcast_fusion.2.refs_0_), channel_id=1, source_target_pairs={{0,24},{1,25},{2,26},{3,27},{4,28},{5,29},{6,30},{7,31},{8,0},{9,1... | collective-permute-start | bytes 294920 | tf_op jit(solution)/shard_map/ppermute | solution.py:48
  6.0 10.0 %collective-permute-start.2 = (bf16[1,64,768]{2,1,0:T(8,128)(2,1)S(1)}, bf16[1,64,768]{2,1,0:T(8,128)(2,1)S(1)}, u32[]{:S(2)}, u32[]{:S(2)}) collective-permute-start(bf16[1,64,768]{2,1,0:T(8,128)(2,1)S(1)} %maximum_bitcast_fusion.2.refs_0_), channel_id=1, source_target_pairs={{0,16},{1,17},{2,18},{3,19},{4,20},{5,21},{6,22},{7,23},{8,24},{9,... | collective-permute-start | bytes 294920 | tf_op jit(solution)/shard_map/ppermute | solution.py:48
  6.0 10.0 %collective-permute-start.3 = (bf16[1,64,768]{2,1,0:T(8,128)(2,1)S(1)}, bf16[1,64,768]{2,1,0:T(8,128)(2,1)S(1)}, u32[]{:S(2)}, u32[]{:S(2)}) collective-permute-start(bf16[1,64,768]{2,1,0:T(8,128)(2,1)S(1)} %maximum_bitcast_fusion.2.refs_0_), channel_id=1, source_target_pairs={{0,8},{1,9},{2,10},{3,11},{4,12},{5,13},{6,14},{7,15},{8,16},{9,17... | collective-permute-start | bytes 294920 | tf_op jit(solution)/shard_map/ppermute | solution.py:48
  7.5 8.5 %collective-permute-start = (bf16[512,1024]{1,0:T(8,128)(2,1)}, bf16[512,1024]{1,0:T(8,128)(2,1)}, u32[]{:S(2)}, u32[]{:S(2)}) collective-permute-start(bf16[512,1024]{1,0:T(8,128)(2,1)} %dynamic-slice_bitcast_fusion.3), channel_id=1, source_target_pairs={{0,1},{1,0},{2,3},{3,2},{4,5},{5,4},{6,7},{7,6},{8,9},{9,8},{10,11... | collective-permute-start | bytes 3145736 | tf_op jit(solution)/shard_map/ppermute | solution.py:55
  16.3 7.1 %collective-permute-start.6 = (bf16[4,64,768]{2,1,0:T(8,128)(2,1)S(1)}, bf16[4,64,768]{2,1,0:T(8,128)(2,1)}, u32[]{:S(2)}, u32[]{:S(2)}) collective-permute-start(bf16[4,64,768]{2,1,0:T(8,128)(2,1)S(1)} %rolled.4.refs_5_.refs_0_), channel_id=1, source_target_pairs={{0,2},{1,5},{2,0},{3,7},{4,6},{5,1},{6,4},{7,3},{8,10},{9,13},{10,... | collective-permute-start | bytes 1179656 | tf_op jit(solution)/shard_map/ppermute | solution.py:48
  23.4 17.7 %collective-permute-start.12 = (bf16[1,64,1280]{2,1,0:T(8,128)(2,1)S(1)}, bf16[1,64,1280]{2,1,0:T(8,128)(2,1)S(1)}, u32[]{:S(2)}, u32[]{:S(2)}) collective-permute-start(bf16[1,64,1280]{2,1,0:T(8,128)(2,1)S(1)} %collective-permute-done.7.refs_1_), channel_id=1, source_target_pairs={{0,24},{1,25},{2,26},{3,27},{4,28},{5,29},{6,30},{7,31},{8,0},{9,1... | collective-permute-start | bytes 491528 | tf_op jit(solution)/shard_map/ppermute | solution.py:48
  27.3 13.9 %collective-permute-start.9 = (bf16[4,64,768]{2,1,0:T(8,128)(2,1)S(1)}, bf16[4,64,768]{2,1,0:T(8,128)(2,1)}, u32[]{:S(2)}, u32[]{:S(2)}) collective-permute-start(bf16[4,64,768]{2,1,0:T(8,128)(2,1)S(1)} %rolled.4.refs_5_.refs_0_), channel_id=1, source_target_pairs={{0,4},{1,3},{2,6},{3,1},{4,0},{5,7},{6,2},{7,5},{8,12},{9,11},{10,... | collective-permute-start | bytes 1179656 | tf_op jit(solution)/shard_map/ppermute | solution.py:48
  28.5 12.7 %collective-permute-start.10 = (bf16[4,64,768]{2,1,0:T(8,128)(2,1)}, bf16[4,64,768]{2,1,0:T(8,128)(2,1)}, u32[]{:S(2)}, u32[]{:S(2)}) collective-permute-start(bf16[4,64,768]{2,1,0:T(8,128)(2,1)} %collective-permute-done.6.refs_6_.refs_1_), channel_id=1, source_target_pairs={{0,4},{1,3},{2,6},{3,1},{4,0},{5,7},{6,2},{7,5},{8,12},{9,11},{10,... | collective-permute-start | bytes 1179656 | tf_op jit(solution)/shard_map/ppermute | solution.py:48
  28.8 12.4 %collective-permute-start.11 = (bf16[4,64,768]{2,1,0:T(8,128)(2,1)S(1)}, bf16[4,64,768]{2,1,0:T(8,128)(2,1)}, u32[]{:S(2)}, u32[]{:S(2)}) collective-permute-start(bf16[4,64,768]{2,1,0:T(8,128)(2,1)S(1)} %rolled.4.refs_5_.refs_0_), channel_id=1, source_target_pairs={{0,1},{1,0},{2,3},{3,2},{4,5},{5,4},{6,7},{7,6},{8,9},{9,8},{10,11... | collective-permute-start | bytes 1179656 | tf_op jit(solution)/shard_map/ppermute | solution.py:55
  30.1 11.0 %collective-permute-start.8 = (bf16[4,8,2176]{2,1,0:T(8,128)(2,1)S(1)}, bf16[4,8,2176]{2,1,0:T(8,128)(2,1)S(1)}, u32[]{:S(2)}, u32[]{:S(2)}) collective-permute-start(bf16[4,8,2176]{2,1,0:T(8,128)(2,1)S(1)} %pad_maximum_fusion.9), channel_id=1, source_target_pairs={{0,2},{1,3},{2,0},{3,1},{4,6},{5,7},{6,4},{7,5},{8,10},{9,11},{10,... | collective-permute-start | bytes 417800 | tf_op jit(solution)/shard_map/ppermute | solution.py:906
  41.2 8.1 %collective-permute-start.13 = (bf16[8,8,2176]{2,1,0:T(8,128)(2,1)S(1)}, bf16[8,8,2176]{2,1,0:T(8,128)(2,1)S(1)}, u32[]{:S(2)}, u32[]{:S(2)}) collective-permute-start(bf16[8,8,2176]{2,1,0:T(8,128)(2,1)S(1)} %pad_maximum_fusion.7), channel_id=1, source_target_pairs={{0,4},{1,5},{2,6},{3,7},{4,0},{5,1},{6,2},{7,3},{8,12},{9,13},{10,... | collective-permute-start | bytes 835592 | tf_op jit(solution)/shard_map/ppermute | solution.py:906
  51.6 13.0 %collective-permute-start.18 = (bf16[4,64,1280]{2,1,0:T(8,128)(2,1)S(1)}, bf16[4,64,1280]{2,1,0:T(8,128)(2,1)S(1)}, u32[]{:S(2)}, u32[]{:S(2)}) collective-permute-start(bf16[4,64,1280]{2,1,0:T(8,128)(2,1)S(1)} %rolled.5.refs_3_.refs_0_.refs_8_), channel_id=1, source_target_pairs={{0,2},{1,5},{2,0},{3,7},{4,6},{5,1},{6,4},{7,3},{8,10},{9,13},{10,... | collective-permute-start | bytes 1966088 | tf_op jit(solution)/shard_map/ppermute | solution.py:48
  53.6 11.0 %collective-permute-start.19 = (bf16[1,64,2048]{2,1,0:T(8,128)(2,1)S(1)}, bf16[1,64,2048]{2,1,0:T(8,128)(2,1)S(1)}, u32[]{:S(2)}, u32[]{:S(2)}) collective-permute-start(bf16[1,64,2048]{2,1,0:T(8,128)(2,1)S(1)} %dynamic-slice_bitcast_fusion.13.refs_0_), channel_id=1, source_target_pairs={{0,24},{1,25},{2,26},{3,27},{4,28},{5,29},{6,30},{7,31},{8,0},{9,1... | collective-permute-start | bytes 786440 | tf_op jit(solution)/shard_map/ppermute | solution.py:48
  64.6 13.2 %collective-permute-start.22 = (bf16[4,64,1280]{2,1,0:T(8,128)(2,1)S(1)}, bf16[4,64,1280]{2,1,0:T(8,128)(2,1)S(1)}, u32[]{:S(2)}, u32[]{:S(2)}) collective-permute-start(bf16[4,64,1280]{2,1,0:T(8,128)(2,1)S(1)} %rolled.5.refs_3_.refs_0_.refs_8_), channel_id=1, source_target_pairs={{0,1},{1,0},{2,3},{3,2},{4,5},{5,4},{6,7},{7,6},{8,9},{9,8},{10,11... | collective-permute-start | bytes 1966088 | tf_op jit(solution)/shard_map/ppermute | solution.py:55
  67.6 10.2 %collective-permute-start.23 = (bf16[4,64,1280]{2,1,0:T(8,128)(2,1)S(1)}, bf16[4,64,1280]{2,1,0:T(8,128)(2,1)S(1)}, u32[]{:S(2)}, u32[]{:S(2)}) collective-permute-start(bf16[4,64,1280]{2,1,0:T(8,128)(2,1)S(1)} %collective-permute-done.18.refs_4_.refs_1_.refs_9_), channel_id=1, source_target_pairs={{0,1},{1,0},{2,3},{3,2},{4,5},{5,4},{6,7},{7,6},{8,9},{9,8},{10,11... | collective-permute-start | bytes 1966088 | tf_op jit(solution)/shard_map/ppermute | solution.py:55
  67.7 17.0 %collective-permute-start.20 = (bf16[4,64,1280]{2,1,0:T(8,128)(2,1)S(1)}, bf16[4,64,1280]{2,1,0:T(8,128)(2,1)S(1)}, u32[]{:S(2)}, u32[]{:S(2)}) collective-permute-start(bf16[4,64,1280]{2,1,0:T(8,128)(2,1)S(1)} %rolled.5.refs_3_.refs_0_.refs_8_), channel_id=1, source_target_pairs={{0,4},{1,3},{2,6},{3,1},{4,0},{5,7},{6,2},{7,5},{8,12},{9,11},{10,... | collective-permute-start | bytes 1966088 | tf_op jit(solution)/shard_map/ppermute | solution.py:48
  67.9 9.9 %collective-permute-start.24 = (bf16[1,64,2048]{2,1,0:T(8,128)(2,1)S(1)}, bf16[1,64,2048]{2,1,0:T(8,128)(2,1)S(1)}, u32[]{:S(2)}, u32[]{:S(2)}) collective-permute-start(bf16[1,64,2048]{2,1,0:T(8,128)(2,1)S(1)} %collective-permute-done.19.refs_1_), channel_id=1, source_target_pairs={{0,24},{1,25},{2,26},{3,27},{4,28},{5,29},{6,30},{7,31},{8,0},{9,1... | collective-permute-start | bytes 786440 | tf_op jit(solution)/shard_map/ppermute | solution.py:48
  68.1 16.6 %collective-permute-start.21 = (bf16[4,64,1280]{2,1,0:T(8,128)(2,1)S(1)}, bf16[4,64,1280]{2,1,0:T(8,128)(2,1)S(1)}, u32[]{:S(2)}, u32[]{:S(2)}) collective-permute-start(bf16[4,64,1280]{2,1,0:T(8,128)(2,1)S(1)} %collective-permute-done.18.refs_4_.refs_1_.refs_9_), channel_id=1, source_target_pairs={{0,4},{1,3},{2,6},{3,1},{4,0},{5,7},{6,2},{7,5},{8,12},{9,11},{10,... | collective-permute-start | bytes 1966088 | tf_op jit(solution)/shard_map/ppermute | solution.py:48
  87.1 10.0 %collective-permute-start.28 = (bf16[512,1024]{1,0:T(8,128)(2,1)S(1)}, bf16[512,1024]{1,0:T(8,128)(2,1)S(1)}, u32[]{:S(2)}, u32[]{:S(2)}) collective-permute-start(bf16[512,1024]{1,0:T(8,128)(2,1)S(1)} %dynamic-slice_bitcast_fusion.1), channel_id=1, source_target_pairs={{0,1},{1,0},{2,3},{3,2},{4,5},{5,4},{6,7},{7,6},{8,9},{9,8},{10,11... | collective-permute-start | bytes 3145736 | tf_op jit(solution)/shard_map/ppermute | solution.py:55
  89.6 18.0 %collective-permute-start.30 = (bf16[4,64,2048]{2,1,0:T(8,128)(2,1)S(1)}, bf16[4,64,2048]{2,1,0:T(8,128)(2,1)S(1)}, u32[]{:S(2)}, u32[]{:S(2)}) collective-permute-start(bf16[4,64,2048]{2,1,0:T(8,128)(2,1)S(1)} %rolled.6.refs_0_), channel_id=1, source_target_pairs={{0,2},{1,5},{2,0},{3,7},{4,6},{5,1},{6,4},{7,3},{8,10},{9,13},{10,... | collective-permute-start | bytes 3145736 | tf_op jit(solution)/shard_map/ppermute | solution.py:48
  89.8 7.2 %collective-permute-start.29 = (bf16[1,256,512]{2,1,0:T(8,128)(2,1)S(1)}, bf16[1,256,512]{2,1,0:T(8,128)(2,1)S(1)}, u32[]{:S(2)}, u32[]{:S(2)}) collective-permute-start(bf16[1,256,512]{2,1,0:T(8,128)(2,1)S(1)} %dynamic-slice_bitcast_fusion.12.refs_0_), channel_id=1, source_target_pairs={{0,24},{1,25},{2,26},{3,27},{4,28},{5,29},{6,30},{7,31},{8,0},{9,1... | collective-permute-start | bytes 786440 | tf_op jit(solution)/shard_map/ppermute | solution.py:48
  97.0 10.5 %collective-permute-start.31 = (bf16[1,256,512]{2,1,0:T(8,128)(2,1)S(1)}, bf16[1,256,512]{2,1,0:T(8,128)(2,1)S(1)}, u32[]{:S(2)}, u32[]{:S(2)}) collective-permute-start(bf16[1,256,512]{2,1,0:T(8,128)(2,1)S(1)} %collective-permute-done.29.refs_1_), channel_id=1, source_target_pairs={{0,24},{1,25},{2,26},{3,27},{4,28},{5,29},{6,30},{7,31},{8,0},{9,1... | collective-permute-start | bytes 786440 | tf_op jit(solution)/shard_map/ppermute | solution.py:48
  107.6 11.1 %collective-permute-start.32 = (bf16[4,64,2048]{2,1,0:T(8,128)(2,1)S(1)}, bf16[4,64,2048]{2,1,0:T(8,128)(2,1)S(1)}, u32[]{:S(2)}, u32[]{:S(2)}) collective-permute-start(bf16[4,64,2048]{2,1,0:T(8,128)(2,1)S(1)} %rolled.6.refs_0_), channel_id=1, source_target_pairs={{0,1},{1,0},{2,3},{3,2},{4,5},{5,4},{6,7},{7,6},{8,9},{9,8},{10,11... | collective-permute-start | bytes 3145736 | tf_op jit(solution)/shard_map/ppermute | solution.py:55
  110.4 8.4 %collective-permute-start.33 = (bf16[4,64,2048]{2,1,0:T(8,128)(2,1)S(1)}, bf16[4,64,2048]{2,1,0:T(8,128)(2,1)S(1)}, u32[]{:S(2)}, u32[]{:S(2)}) collective-permute-start(bf16[4,64,2048]{2,1,0:T(8,128)(2,1)S(1)} %collective-permute-done.30.refs_1_), channel_id=1, source_target_pairs={{0,1},{1,0},{2,3},{3,2},{4,5},{5,4},{6,7},{7,6},{8,9},{9,8},{10,11... | collective-permute-start | bytes 3145736 | tf_op jit(solution)/shard_map/ppermute | solution.py:55
  110.4 18.2 %collective-permute-start.35 = (bf16[4,64,2048]{2,1,0:T(8,128)(2,1)S(1)}, bf16[4,64,2048]{2,1,0:T(8,128)(2,1)S(1)}, u32[]{:S(2)}, u32[]{:S(2)}) collective-permute-start(bf16[4,64,2048]{2,1,0:T(8,128)(2,1)S(1)} %rolled.6.refs_0_), channel_id=1, source_target_pairs={{0,4},{1,3},{2,6},{3,1},{4,0},{5,7},{6,2},{7,5},{8,12},{9,11},{10,... | collective-permute-start | bytes 3145736 | tf_op jit(solution)/shard_map/ppermute | solution.py:48
  111.3 24.3 %collective-permute-start.36 = (bf16[4,64,2048]{2,1,0:T(8,128)(2,1)S(1)}, bf16[4,64,2048]{2,1,0:T(8,128)(2,1)S(1)}, u32[]{:S(2)}, u32[]{:S(2)}) collective-permute-start(bf16[4,64,2048]{2,1,0:T(8,128)(2,1)S(1)} %collective-permute-done.30.refs_1_), channel_id=1, source_target_pairs={{0,4},{1,3},{2,6},{3,1},{4,0},{5,7},{6,2},{7,5},{8,12},{9,11},{10,... | collective-permute-start | bytes 3145736 | tf_op jit(solution)/shard_map/ppermute | solution.py:48
  140.7 13.9 %collective-permute-start.39 = (bf16[4,256,512]{2,1,0:T(8,128)(2,1)S(1)}, bf16[4,256,512]{2,1,0:T(8,128)(2,1)S(1)}, u32[]{:S(2)}, u32[]{:S(2)}) collective-permute-start(bf16[4,256,512]{2,1,0:T(8,128)(2,1)S(1)} %rolled.7.refs_0_), channel_id=1, source_target_pairs={{0,2},{1,5},{2,0},{3,7},{4,6},{5,1},{6,4},{7,3},{8,10},{9,13},{10,... | collective-permute-start | bytes 3145736 | tf_op jit(solution)/shard_map/ppermute | solution.py:48
  154.7 15.0 %collective-permute-start.41 = (bf16[4,256,512]{2,1,0:T(8,128)(2,1)S(1)}, bf16[4,256,512]{2,1,0:T(8,128)(2,1)S(1)}, u32[]{:S(2)}, u32[]{:S(2)}) collective-permute-start(bf16[4,256,512]{2,1,0:T(8,128)(2,1)S(1)} %rolled.7.refs_0_), channel_id=1, source_target_pairs={{0,1},{1,0},{2,3},{3,2},{4,5},{5,4},{6,7},{7,6},{8,9},{9,8},{10,11... | collective-permute-start | bytes 3145736 | tf_op jit(solution)/shard_map/ppermute | solution.py:55
  155.9 13.8 %collective-permute-start.42 = (bf16[4,256,512]{2,1,0:T(8,128)(2,1)S(1)}, bf16[4,256,512]{2,1,0:T(8,128)(2,1)S(1)}, u32[]{:S(2)}, u32[]{:S(2)}) collective-permute-start(bf16[4,256,512]{2,1,0:T(8,128)(2,1)S(1)} %collective-permute-done.39.refs_1_), channel_id=1, source_target_pairs={{0,1},{1,0},{2,3},{3,2},{4,5},{5,4},{6,7},{7,6},{8,9},{9,8},{10,11... | collective-permute-start | bytes 3145736 | tf_op jit(solution)/shard_map/ppermute | solution.py:55
  155.9 23.6 %collective-permute-start.40 = (bf16[4,256,512]{2,1,0:T(8,128)(2,1)S(1)}, bf16[4,256,512]{2,1,0:T(8,128)(2,1)S(1)}, u32[]{:S(2)}, u32[]{:S(2)}) collective-permute-start(bf16[4,256,512]{2,1,0:T(8,128)(2,1)S(1)} %rolled.7.refs_0_), channel_id=1, source_target_pairs={{0,4},{1,3},{2,6},{3,1},{4,0},{5,7},{6,2},{7,5},{8,12},{9,11},{10,... | collective-permute-start | bytes 3145736 | tf_op jit(solution)/shard_map/ppermute | solution.py:48
  156.7 24.5 %collective-permute-start.43 = (bf16[4,256,512]{2,1,0:T(8,128)(2,1)S(1)}, bf16[4,256,512]{2,1,0:T(8,128)(2,1)}, u32[]{:S(2)}, u32[]{:S(2)}) collective-permute-start(bf16[4,256,512]{2,1,0:T(8,128)(2,1)S(1)} %collective-permute-done.39.refs_1_), channel_id=1, source_target_pairs={{0,4},{1,3},{2,6},{3,1},{4,0},{5,7},{6,2},{7,5},{8,12},{9,11},{10,... | collective-permute-start | bytes 3145736 | tf_op jit(solution)/shard_map/ppermute | solution.py:48
  186.5 16.0 %collective-permute-start.46 = (bf16[4,4,256,512]{3,2,1,0:T(8,128)(2,1)}, bf16[4,4,256,512]{3,2,1,0:T(8,128)(2,1)}, u32[]{:S(2)}, u32[]{:S(2)}) collective-permute-start(bf16[4,4,256,512]{3,2,1,0:T(8,128)(2,1)} %wide_chunks.2), channel_id=1, source_target_pairs={{0,1},{1,0},{2,3},{3,2},{4,5},{5,4},{6,7},{7,6},{8,9},{9,8},{10,11... | collective-permute-start | bytes 12582920 | tf_op jit(solution)/shard_map/ppermute | solution.py:55
  223.8 25.6 %collective-permute-start.47 = (bf16[4,4,64,2048]{3,2,1,0:T(8,128)(2,1)}, bf16[4,4,64,2048]{3,2,1,0:T(8,128)(2,1)}, u32[]{:S(2)}, u32[]{:S(2)}) collective-permute-start(bf16[4,4,64,2048]{3,2,1,0:T(8,128)(2,1)} %row_chunks.2), channel_id=1, source_target_pairs={{0,1},{1,0},{2,3},{3,2},{4,5},{5,4},{6,7},{7,6},{8,9},{9,8},{10,11... | collective-permute-start | bytes 12582920 | tf_op jit(solution)/shard_map/ppermute | solution.py:55
  224.1 17.8 %collective-permute-start.48 = (bf16[4,256,512]{2,1,0:T(8,128)(2,1)S(1)}, bf16[4,256,512]{2,1,0:T(8,128)(2,1)S(1)}, u32[]{:S(2)}, u32[]{:S(2)}) collective-permute-start(bf16[4,256,512]{2,1,0:T(8,128)(2,1)S(1)} %copy-done.116), channel_id=1, source_target_pairs={{0,4},{1,3},{2,6},{3,1},{4,0},{5,7},{6,2},{7,5},{8,12},{9,11},{10,... | collective-permute-start | bytes 3145736 | tf_op jit(solution)/shard_map/ppermute | solution.py:48
  224.9 24.3 %collective-permute-start.49 = (bf16[4,256,512]{2,1,0:T(8,128)(2,1)S(1)}, bf16[4,256,512]{2,1,0:T(8,128)(2,1)S(1)}, u32[]{:S(2)}, u32[]{:S(2)}) collective-permute-start(bf16[4,256,512]{2,1,0:T(8,128)(2,1)S(1)} %copy-done.115), channel_id=1, source_target_pairs={{0,4},{1,3},{2,6},{3,1},{4,0},{5,7},{6,2},{7,5},{8,12},{9,11},{10,... | collective-permute-start | bytes 3145736 | tf_op jit(solution)/shard_map/ppermute | solution.py:48
  250.6 18.3 %collective-permute-start.50 = (bf16[4,256,512]{2,1,0:T(8,128)(2,1)}, bf16[4,256,512]{2,1,0:T(8,128)(2,1)}, u32[]{:S(2)}, u32[]{:S(2)}) collective-permute-start(bf16[4,256,512]{2,1,0:T(8,128)(2,1)} %add_convert_fusion.3), channel_id=1, source_target_pairs={{0,2},{1,5},{2,0},{3,7},{4,6},{5,1},{6,4},{7,3},{8,10},{9,13},{10,... | collective-permute-start | bytes 3145736 | tf_op jit(solution)/shard_map/ppermute | solution.py:48
  268.9 17.6 %collective-permute-start.52 = (bf16[4,64,2048]{2,1,0:T(8,128)(2,1)S(1)}, bf16[4,64,2048]{2,1,0:T(8,128)(2,1)S(1)}, u32[]{:S(2)}, u32[]{:S(2)}) collective-permute-start(bf16[4,64,2048]{2,1,0:T(8,128)(2,1)S(1)} %copy-done.114), channel_id=1, source_target_pairs={{0,4},{1,3},{2,6},{3,1},{4,0},{5,7},{6,2},{7,5},{8,12},{9,11},{10,... | collective-permute-start | bytes 3145736 | tf_op jit(solution)/shard_map/ppermute | solution.py:48
  272.0 14.5 %collective-permute-start.51 = (bf16[256,512]{1,0:T(8,128)(2,1)S(1)}, bf16[256,512]{1,0:T(8,128)(2,1)S(1)}, u32[]{:S(2)}, u32[]{:S(2)}) collective-permute-start(bf16[256,512]{1,0:T(8,128)(2,1)S(1)} %get-tuple-element.524), channel_id=1, source_target_pairs={{0,16},{1,17},{2,18},{3,19},{4,20},{5,21},{6,22},{7,23},{8,24},{9,... | collective-permute-start | bytes 786440 | tf_op jit(solution)/shard_map/ppermute | solution.py:48
  286.9 14.0 %collective-permute-start.53 = (bf16[4,64,2048]{2,1,0:T(8,128)(2,1)S(1)}, bf16[4,64,2048]{2,1,0:T(8,128)(2,1)S(1)}, u32[]{:S(2)}, u32[]{:S(2)}) collective-permute-start(bf16[4,64,2048]{2,1,0:T(8,128)(2,1)S(1)} %add_convert_fusion.1), channel_id=1, source_target_pairs={{0,2},{1,5},{2,0},{3,7},{4,6},{5,1},{6,4},{7,3},{8,10},{9,13},{10,... | collective-permute-start | bytes 3145736 | tf_op jit(solution)/shard_map/ppermute | solution.py:48
  300.9 14.3 %collective-permute-start.56 = (bf16[4,64,2048]{2,1,0:T(8,128)(2,1)}, bf16[4,64,2048]{2,1,0:T(8,128)(2,1)}, u32[]{:S(2)}, u32[]{:S(2)}) collective-permute-start(bf16[4,64,2048]{2,1,0:T(8,128)(2,1)} %get-tuple-element.410), channel_id=1, source_target_pairs={{0,4},{1,3},{2,6},{3,1},{4,0},{5,7},{6,2},{7,5},{8,12},{9,11},{10,... | collective-permute-start | bytes 3145736 | tf_op jit(solution)/shard_map/ppermute | solution.py:48
  301.5 13.6 %collective-permute-start.54 = (bf16[256,512]{1,0:T(8,128)(2,1)S(1)}, bf16[256,512]{1,0:T(8,128)(2,1)S(1)}, u32[]{:S(2)}, u32[]{:S(2)}) collective-permute-start(bf16[256,512]{1,0:T(8,128)(2,1)S(1)} %get-tuple-element.407), channel_id=1, source_target_pairs={{0,16},{1,17},{2,18},{3,19},{4,20},{5,21},{6,22},{7,23},{8,24},{9,... | collective-permute-start | bytes 786440 | tf_op jit(solution)/shard_map/ppermute | solution.py:48
  301.5 13.5 %collective-permute-start.55 = (bf16[256,512]{1,0:T(8,128)(2,1)S(1)}, bf16[256,512]{1,0:T(8,128)(2,1)S(1)}, u32[]{:S(2)}, u32[]{:S(2)}) collective-permute-start(bf16[256,512]{1,0:T(8,128)(2,1)S(1)} %add_convert_fusion.13), channel_id=1, source_target_pairs={{0,8},{1,9},{2,10},{3,11},{4,12},{5,13},{6,14},{7,15},{8,0},{9,1},... | collective-permute-start | bytes 786440 | tf_op jit(solution)/shard_map/ppermute | solution.py:48
  315.2 19.4 %collective-permute-start.57 = (bf16[4,4,64,1280]{3,2,1,0:T(8,128)(2,1)}, bf16[4,4,64,1280]{3,2,1,0:T(8,128)(2,1)S(1)}, u32[]{:S(2)}, u32[]{:S(2)}) collective-permute-start(bf16[4,4,64,1280]{3,2,1,0:T(8,128)(2,1)} %heads_chunks.4), channel_id=1, source_target_pairs={{0,1},{1,0},{2,3},{3,2},{4,5},{5,4},{6,7},{7,6},{8,9},{9,8},{10,11... | collective-permute-start | bytes 7864328 | tf_op jit(solution)/shard_map/ppermute | solution.py:55
  320.0 14.6 %collective-permute-start.58 = (bf16[64,2048]{1,0:T(8,128)(2,1)S(1)}, bf16[64,2048]{1,0:T(8,128)(2,1)S(1)}, u32[]{:S(2)}, u32[]{:S(2)}) collective-permute-start(bf16[64,2048]{1,0:T(8,128)(2,1)S(1)} %get-tuple-element.520), channel_id=1, source_target_pairs={{0,16},{1,17},{2,18},{3,19},{4,20},{5,21},{6,22},{7,23},{8,24},{9,... | collective-permute-start | bytes 786440 | tf_op jit(solution)/shard_map/ppermute | solution.py:48
  321.3 13.3 %collective-permute-start.59 = (bf16[256,512]{1,0:T(8,128)(2,1)S(1)}, bf16[256,512]{1,0:T(8,128)(2,1)}, u32[]{:S(2)}, u32[]{:S(2)}) collective-permute-start(bf16[256,512]{1,0:T(8,128)(2,1)S(1)} %get-tuple-element.508), channel_id=1, source_target_pairs={{0,1},{1,0},{2,3},{3,2},{4,5},{5,4},{6,7},{7,6},{8,9},{9,8},{10,11... | collective-permute-start | bytes 786440 | tf_op jit(solution)/shard_map/ppermute | solution.py:55
  345.9 16.2 %collective-permute-start.60 = (bf16[4,64,1280]{2,1,0:T(8,128)(2,1)S(1)}, bf16[4,64,1280]{2,1,0:T(8,128)(2,1)S(1)}, u32[]{:S(2)}, u32[]{:S(2)}) collective-permute-start(bf16[4,64,1280]{2,1,0:T(8,128)(2,1)S(1)} %get-tuple-element.433), channel_id=1, source_target_pairs={{0,4},{1,3},{2,6},{3,1},{4,0},{5,7},{6,2},{7,5},{8,12},{9,11},{10,... | collective-permute-start | bytes 1966088 | tf_op jit(solution)/shard_map/ppermute | solution.py:48
  346.5 16.2 %collective-permute-start.61 = (bf16[4,64,1280]{2,1,0:T(8,128)(2,1)S(1)}, bf16[4,64,1280]{2,1,0:T(8,128)(2,1)S(1)}, u32[]{:S(2)}, u32[]{:S(2)}) collective-permute-start(bf16[4,64,1280]{2,1,0:T(8,128)(2,1)S(1)} %get-tuple-element.434), channel_id=1, source_target_pairs={{0,4},{1,3},{2,6},{3,1},{4,0},{5,7},{6,2},{7,5},{8,12},{9,11},{10,... | collective-permute-start | bytes 1966088 | tf_op jit(solution)/shard_map/ppermute | solution.py:48
  347.4 14.6 %collective-permute-start.62 = (bf16[64,2048]{1,0:T(8,128)(2,1)}, bf16[64,2048]{1,0:T(8,128)(2,1)S(1)}, u32[]{:S(2)}, u32[]{:S(2)}) collective-permute-start(bf16[64,2048]{1,0:T(8,128)(2,1)} %get-tuple-element.435), channel_id=1, source_target_pairs={{0,16},{1,17},{2,18},{3,19},{4,20},{5,21},{6,22},{7,23},{8,24},{9,... | collective-permute-start | bytes 786440 | tf_op jit(solution)/shard_map/ppermute | solution.py:48
  347.6 14.4 %collective-permute-start.63 = (bf16[64,2048]{1,0:T(8,128)(2,1)S(1)}, bf16[64,2048]{1,0:T(8,128)(2,1)S(1)}, u32[]{:S(2)}, u32[]{:S(2)}) collective-permute-start(bf16[64,2048]{1,0:T(8,128)(2,1)S(1)} %add_convert_fusion.11), channel_id=1, source_target_pairs={{0,8},{1,9},{2,10},{3,11},{4,12},{5,13},{6,14},{7,15},{8,0},{9,1},... | collective-permute-start | bytes 786440 | tf_op jit(solution)/shard_map/ppermute | solution.py:48
  370.1 12.3 %collective-permute-start.65 = (bf16[4,4,64,768]{3,2,1,0:T(8,128)(2,1)}, bf16[4,4,64,768]{3,2,1,0:T(8,128)(2,1)}, u32[]{:S(2)}, u32[]{:S(2)}) collective-permute-start(bf16[4,4,64,768]{3,2,1,0:T(8,128)(2,1)} %heads_chunks.6), channel_id=1, source_target_pairs={{0,1},{1,0},{2,3},{3,2},{4,5},{5,4},{6,7},{7,6},{8,9},{9,8},{10,11... | collective-permute-start | bytes 4718600 | tf_op jit(solution)/shard_map/ppermute | solution.py:55
  372.6 9.8 %collective-permute-start.66 = (bf16[4,64,1280]{2,1,0:T(8,128)(2,1)S(1)}, bf16[4,64,1280]{2,1,0:T(8,128)(2,1)S(1)}, u32[]{:S(2)}, u32[]{:S(2)}) collective-permute-start(bf16[4,64,1280]{2,1,0:T(8,128)(2,1)S(1)} %add_convert_fusion.5), channel_id=1, source_target_pairs={{0,2},{1,5},{2,0},{3,7},{4,6},{5,1},{6,4},{7,3},{8,10},{9,13},{10,... | collective-permute-start | bytes 1966088 | tf_op jit(solution)/shard_map/ppermute | solution.py:48
  384.1 15.0 %collective-permute-start.67 = (bf16[4,64,768]{2,1,0:T(8,128)(2,1)S(1)}, bf16[4,64,768]{2,1,0:T(8,128)(2,1)S(1)}, u32[]{:S(2)}, u32[]{:S(2)}) collective-permute-start(bf16[4,64,768]{2,1,0:T(8,128)(2,1)S(1)} %add_convert_fusion.9), channel_id=1, source_target_pairs={{0,4},{1,3},{2,6},{3,1},{4,0},{5,7},{6,2},{7,5},{8,12},{9,11},{10,... | collective-permute-start | bytes 1179656 | tf_op jit(solution)/shard_map/ppermute | solution.py:48
  384.4 14.7 %collective-permute-start.68 = (bf16[4,64,768]{2,1,0:T(8,128)(2,1)S(1)}, bf16[4,64,768]{2,1,0:T(8,128)(2,1)S(1)}, u32[]{:S(2)}, u32[]{:S(2)}) collective-permute-start(bf16[4,64,768]{2,1,0:T(8,128)(2,1)S(1)} %add_convert_fusion.8), channel_id=1, source_target_pairs={{0,4},{1,3},{2,6},{3,1},{4,0},{5,7},{6,2},{7,5},{8,12},{9,11},{10,... | collective-permute-start | bytes 1179656 | tf_op jit(solution)/shard_map/ppermute | solution.py:48
  386.1 13.0 %collective-permute-start.69 = (bf16[64,1280]{1,0:T(8,128)(2,1)S(1)}, bf16[64,1280]{1,0:T(8,128)(2,1)S(1)}, u32[]{:S(2)}, u32[]{:S(2)}) collective-permute-start(bf16[64,1280]{1,0:T(8,128)(2,1)S(1)} %get-tuple-element.528), channel_id=1, source_target_pairs={{0,16},{1,17},{2,18},{3,19},{4,20},{5,21},{6,22},{7,23},{8,24},{9,... | collective-permute-start | bytes 491528 | tf_op jit(solution)/shard_map/ppermute | solution.py:48
  399.1 17.8 %collective-permute-start.74 = (bf16[512,1024]{1,0:T(8,128)(2,1)}, bf16[512,1024]{1,0:T(8,128)(2,1)S(1)}, u32[]{:S(2)}, u32[]{:S(2)}) collective-permute-start(bf16[512,1024]{1,0:T(8,128)(2,1)} %get-tuple-element.477), channel_id=1, source_target_pairs={{0,1},{1,0},{2,3},{3,2},{4,5},{5,4},{6,7},{7,6},{8,9},{9,8},{10,11... | collective-permute-start | bytes 3145736 | tf_op jit(solution)/shard_map/ppermute | solution.py:55
  401.5 15.4 %collective-permute-start.70 = (bf16[4,64,768]{2,1,0:T(8,128)(2,1)S(1)}, bf16[4,64,768]{2,1,0:T(8,128)(2,1)S(1)}, u32[]{:S(2)}, u32[]{:S(2)}) collective-permute-start(bf16[4,64,768]{2,1,0:T(8,128)(2,1)S(1)} %add_convert_fusion.7), channel_id=1, source_target_pairs={{0,2},{1,5},{2,0},{3,7},{4,6},{5,1},{6,4},{7,3},{8,10},{9,13},{10,... | collective-permute-start | bytes 1179656 | tf_op jit(solution)/shard_map/ppermute | solution.py:48
  401.6 15.3 %collective-permute-start.71 = (bf16[64,1280]{1,0:T(8,128)(2,1)S(1)}, bf16[64,1280]{1,0:T(8,128)(2,1)S(1)}, u32[]{:S(2)}, u32[]{:S(2)}) collective-permute-start(bf16[64,1280]{1,0:T(8,128)(2,1)S(1)} %get-tuple-element.471), channel_id=1, source_target_pairs={{0,16},{1,17},{2,18},{3,19},{4,20},{5,21},{6,22},{7,23},{8,24},{9,... | collective-permute-start | bytes 491528 | tf_op jit(solution)/shard_map/ppermute | solution.py:48
  404.0 12.9 %collective-permute-start.72 = (bf16[64,1280]{1,0:T(8,128)(2,1)S(1)}, bf16[64,1280]{1,0:T(8,128)(2,1)S(1)}, u32[]{:S(2)}, u32[]{:S(2)}) collective-permute-start(bf16[64,1280]{1,0:T(8,128)(2,1)S(1)} %add_convert_fusion.15), channel_id=1, source_target_pairs={{0,8},{1,9},{2,10},{3,11},{4,12},{5,13},{6,14},{7,15},{8,0},{9,1},... | collective-permute-start | bytes 491528 | tf_op jit(solution)/shard_map/ppermute | solution.py:48
  405.5 11.4 %collective-permute-start.73 = (f32[8,1024]{1,0:T(8,128)}, f32[8,1024]{1,0:T(8,128)S(1)}, u32[]{:S(2)}, u32[]{:S(2)}) collective-permute-start(f32[8,1024]{1,0:T(8,128)} %sums.1), channel_id=1, source_target_pairs={{0,16},{1,17},{2,18},{3,19},{4,20},{5,21},{6,22},{7,23},{8,24},{9,... | collective-permute-start | bytes 98312 | tf_op jit(solution)/shard_map/ppermute | solution.py:906
  417.0 13.4 %collective-permute-start.78 = (bf16[64,1280]{1,0:T(8,128)(2,1)S(1)}, bf16[64,1280]{1,0:T(8,128)(2,1)S(1)}, u32[]{:S(2)}, u32[]{:S(2)}) collective-permute-start(bf16[64,1280]{1,0:T(8,128)(2,1)S(1)} %add_convert_fusion.14), channel_id=1, source_target_pairs={{0,1},{1,0},{2,3},{3,2},{4,5},{5,4},{6,7},{7,6},{8,9},{9,8},{10,11... | collective-permute-start | bytes 491528 | tf_op jit(solution)/shard_map/ppermute | solution.py:55
  418.5 13.1 %collective-permute-start.75 = (bf16[512,1024]{1,0:T(8,128)(2,1)}, bf16[512,1024]{1,0:T(8,128)(2,1)}, u32[]{:S(2)}, u32[]{:S(2)}) collective-permute-start(bf16[512,1024]{1,0:T(8,128)(2,1)} %down.2), channel_id=1, source_target_pairs={{0,1},{1,0},{2,3},{3,2},{4,5},{5,4},{6,7},{7,6},{8,9},{9,8},{10,11... | collective-permute-start | bytes 3145736 | tf_op jit(solution)/shard_map/ppermute | solution.py:55
  418.7 12.9 %collective-permute-start.76 = (f32[12,1024]{1,0:T(8,128)S(1)}, f32[12,1024]{1,0:T(8,128)S(1)}, u32[]{:S(2)}, u32[]{:S(2)}) collective-permute-start(f32[12,1024]{1,0:T(8,128)S(1)} %pad_maximum_fusion.12), channel_id=1, source_target_pairs={{0,8},{1,9},{2,10},{3,11},{4,12},{5,13},{6,14},{7,15},{8,0},{9,1},... | collective-permute-start | bytes 147464 | tf_op jit(solution)/shard_map/ppermute | solution.py:906
  419.0 12.6 %collective-permute-start.77 = (bf16[64,768]{1,0:T(8,128)(2,1)S(1)}, bf16[64,768]{1,0:T(8,128)(2,1)}, u32[]{:S(2)}, u32[]{:S(2)}) collective-permute-start(bf16[64,768]{1,0:T(8,128)(2,1)S(1)} %get-tuple-element.536), channel_id=1, source_target_pairs={{0,16},{1,17},{2,18},{3,19},{4,20},{5,21},{6,22},{7,23},{8,24},{9,... | collective-permute-start | bytes 294920 | tf_op jit(solution)/shard_map/ppermute | solution.py:48
  433.0 7.1 %collective-permute-start.80 = (bf16[64,768]{1,0:T(8,128)(2,1)S(1)}, bf16[64,768]{1,0:T(8,128)(2,1)S(1)}, u32[]{:S(2)}, u32[]{:S(2)}) collective-permute-start(bf16[64,768]{1,0:T(8,128)(2,1)S(1)} %get-tuple-element.492), channel_id=1, source_target_pairs={{0,16},{1,17},{2,18},{3,19},{4,20},{5,21},{6,22},{7,23},{8,24},{9,... | collective-permute-start | bytes 294920 | tf_op jit(solution)/shard_map/ppermute | solution.py:48
  (144 other events, 1596.0 us)

commit v5 on v4

--- a/solution.py
+++ b/solution.py
@@ -22,7 +22,7 @@
 VMEM_LIMIT = 58 << 20
 ROOM = 14 << 20
 ANY = pl.BlockSpec(memory_space=pltpu.HBM)
-TIGHT = ("qkv", "attend", "attend_back", "heads_chunks", "heads_back", "rolled", "out")
+TIGHT = ("qkv", "attend", "attend_back", "heads_chunks", "heads_back", "rolled", "out", "to_blocks", "heads_grads", "sums", "last_sums")
 
 
 class Grid:
@@ -921,6 +921,94 @@
     return np.tile(cosine, (1, 4)).astype(np.float32), np.tile(np.concatenate([-sine, sine], 1), (1, 2)).astype(np.float32)
 
 
+def to_blocks_kernel(place, mine, theirs, out):
+    j = pl.program_id(0)
+
+    @pl.when(j == 0)
+    def _():
+        out[0] = mine[...]
+
+    @pl.when(j == 1)
+    def _():
+        out[0] = theirs[...]
+
+
+def to_blocks(places, mine, theirs):
+    shape = (2,) + mine.shape
+    return call(
+        to_blocks_kernel, "to_blocks", (2,), [whole(mine.shape)] * 2,
+        [spec((1,) + mine.shape, lambda j, place: (jnp.where(j == 0, place[2], 1 - place[2]), 0, 0))],
+        [(shape, mine.dtype)], [], 0, 4 * math.prod(shape), prefetch=1,
+    )(places, mine, theirs)[0]
+
+
+def heads_grads_kernel(place, *refs):
+    *parts, qkv, out = refs
+    width = out.shape[1]
+    quarter = width // 4
+
+    def put(order):
+        for g in range(2):
+            for half in range(2):
+                part = parts[2 * g + order[half]]
+                for t in range(3):
+                    to = (4 * t + 2 * g + half) * quarter
+                    qkv[:, to : to + quarter] = part[:, t * quarter : (t + 1) * quarter].astype(F32)
+        for half in range(2):
+            out[:, half * 2 * quarter : (half + 1) * 2 * quarter] = parts[order[half]][:, 3 * quarter :].astype(F32)
+
+    pl.when(place[2] == 0)(lambda: put((0, 1)))
+    pl.when(place[2] == 1)(lambda: put((1, 0)))
+
+
+def heads_grads(places, first, second, width):
+    parts = [*first, *second]
+    rows = parts[0].shape[0]
+    return call(
+        heads_grads_kernel, "heads_grads", (1,), [SCALARS] + [whole(v.shape) for v in parts],
+        [whole((rows, 3 * width)), whole((rows, width))], [((rows, 3 * width), F32), ((rows, width), F32)], [],
+        0, 24 * rows * width,
+    )(places, *parts)
+
+
+def last_sums_kernel(count, index, frequency, *refs):
+    *parts, sums, grad = refs
+    width = sums.shape[1]
+    lane = lax.broadcasted_iota(jnp.int32, (1, LANES), 1)
+    total, rows, gradient = None, grad.shape[0], [jnp.zeros((grad.shape[0], width), F32)] * 2
+    number = 0
+    for part in parts:
+        for first in range(0, count, LANES):
+            some = min(count - first, LANES)
+            times = jnp.zeros((1, LANES), F32)
+            for i in range(some):
+                start = (first + i) * width
+                times = jnp.where(lane == i, part[6:7, start : start + LANES], times)
+            angles = frequency[...] * times
+            features = jnp.where(index[...] < TF // 2, jnp.sin(angles), jnp.cos(angles))
+            for i in range(some):
+                start = (first + i) * width
+                value = part[:, start : start + width]
+                total = value if total is None else total + value
+                feature = jnp.sum(jnp.where(lane == i, features, 0.0), axis=1, keepdims=True)
+                for k in range(2):
+                    gradient[k] = gradient[k] + feature * value[4 + k : 5 + k, :]
+    sums[...] = total
+    for k in range(2):
+        grad[:, k * width : (k + 1) * width] = gradient[k]
+
+
+def last_sums(parts, index, width):
+    rows, half = index.shape[0], TF // 2
+    frequency = jnp.exp((index % half).astype(F32) * (-math.log(10000.0) / half))[:, None]
+    count = parts[0].shape[1] // width
+    return call(
+        functools.partial(last_sums_kernel, count), "last_sums", (1,),
+        [whole((rows, 1))] * 2 + [whole(v.shape) for v in parts], [whole((8, width)), whole((rows, 2 * width))],
+        [((8, width), F32), ((rows, 2 * width), F32)], [], 0, 4 * sum(math.prod(v.shape) for v in parts),
+    )(index[:, None], frequency, *parts)
+
+
 def sums_kernel(first, second, gain1, gain2, scale1, scale2, time, out):
     out[0:1, :] = first[0:1, :] * scale1[...]
     out[1:2, :] = first[1:2, :]
@@ -1124,7 +1212,7 @@
     line.mark(sent)
 
     push_up = Push(grid, line, line.at(sent))
-    down += push_down.second(False)
+    down_rest = push_down.second(False)
     grad_middle, sums2 = norm_back(grid, at, line.at((grad_hidden,)), middle, eff2, cot, (up_w.weight(),), 1024)
     line.mark(grad_middle, down, push_up.came)
 
@@ -1133,7 +1221,7 @@
     line.mark(kept)
 
     grad_heads = heads_back(grid, at, line.at(grad_middle), out_weight)
-    line.mark(grad_heads, down)
+    line.mark(grad_heads, down, down_rest)
 
     def back(group, half, grad_heads):
         packed, wide = ((packed_a, wide_a), (packed_b, wide_b))[group]
@@ -1158,98 +1246,81 @@
 
     up = push_up.second(False)
     (sent,) = heads_chunks(grid, at, False, *line.at(normed1_t, (back_a0, back_a1), mixed, grad_middle))
-    line.mark(sent, down, up)
+    line.mark(sent)
 
     push_a = Push(grid, line, line.at(sent))
+    back_b0 = back(1, 0, line.at(grad_heads))
+    line.mark(back_b0, up, push_a.came, down)
+
     up = push_up.outer()
     down = push_down.own_half()
-    back_b0 = back(1, 0, line.at(grad_heads))
-    line.mark(back_b0, up, push_a.came, down)
-
-    up = push_up.outer_rest()
     kept = heads_chunks(grid, at, True, *line.at(normed1_t, (back_a0, back_a1), mixed, grad_middle, push_a.came))
     push_a.keep(kept, True)
     line.mark(kept)
 
     heads = push_a.second(True) + push_a.second(False)
-    grad_down = push_down.result(core)
     back_b1 = back(1, 1, line.at(grad_heads))
-    line.mark(back_b1, heads, up)
+    line.mark(back_b1, heads, up, down)
 
     heads = push_a.first()
-    up = push_up.own_half()
+    up = push_up.outer_rest()
     (sent,) = heads_chunks(grid, at, False, *line.at(normed1_t, (back_b0, back_b1)))
-    line.mark(sent, up)
+    line.mark(sent)
 
     push_b = Push(grid, line, line.at(sent))
     kept = push_b.keep(heads_chunks(grid, at, True, *line.at(normed1_t, (back_b0, back_b1))), False)
-    line.mark(kept, push_b.came, heads)
+    line.mark(kept, push_b.came)
 
     last = push_b.second(True) + push_b.second(False)
-    heads = push_a.outer()
     grads = line.at((back_a0, back_a1, back_b0, back_b1))
     grad_x, grad_x_theirs, sums1 = norm_back(
         grid, at, grads, x, eff1, grad_middle, (heads_a.weight(), heads_b.weight(0, group_width)), group_width, 2
     )
-    line.mark(sums1, last, heads)
-
-    def sums_step(v, far):
-        return jnp.concatenate([v[:4] + far[:4], v[4:], far[4:]])
+    line.mark(sums1, last, heads, up)
 
     vector, two = whole((1, width)), whole((2, width))
     every = call(
         sums_kernel, "sums", (1,), [two, two] + [vector] * 4 + [whole((1, 1))], [whole((8, width))], [((8, width), F32)],
         [], 0, 64 * width,
     )(line.at(sums1), sums2, gain1, gain2, scale1, scale2, my_time.astype(F32)[None])[0]
-    bits = [grid.chunks << i for i in reversed(range((grid.n0 - 1).bit_length()))] + inner_bits
+    bits = [grid.chunks << i for i in reversed(range((grid.n0 - 1).bit_length()))]
     far = doubled(grid, every, bits[0])
     last = push_b.first()
-    heads = push_a.outer_rest()
+    heads = push_a.outer()
+    up = push_up.own_half()
     grad_x_theirs = grid.swap(line.at(grad_x_theirs))
     out_theirs = down_product(grid, at, 1, *line.at(active, middle), down_w.weight())
-    line.mark(out_theirs, last, heads, far, grad_x_theirs)
-
-    every = sums_step(*line.at(every, far))
-    far = doubled(grid, every, bits[1])
+    line.mark(out_theirs, last, heads, up, far, grad_x_theirs)
+
+    every = jnp.concatenate(line.at(every, far), axis=1)
+    far = [doubled(grid, every, bit) for bit in bits[1:]]
     last = push_b.outer()
-    heads = push_a.own_half()
+    heads = push_a.outer_rest()
     out_theirs = grid.swap(line.at(out_theirs))
-    grad_up = push_up.result(core)
+    grad_up, grad_down = push_up.result(core), push_down.result(core)
     out_mine = down_product(grid, at, 0, *line.at(active, middle), down_w.weight())
     line.mark(out_mine, last, heads, far, out_theirs)
 
-    def to_blocks(mine, theirs):
-        return jnp.where(core == 0, jnp.stack([mine, theirs]), jnp.stack([theirs, mine]))
-
-    every = sums_step(*line.at(every, far))
-    far = doubled(grid, every, bits[2])
+    every = jnp.concatenate([line.at(every)] + list(line.at(far)), axis=1)
+    far = [doubled(grid, every, bit) for bit in range(1, grid.chunks)]
     last = push_b.outer_rest()
-    grad_tokens = to_blocks(*line.at(grad_x, grad_x_theirs))
+    push_a.own_half()
+    grad_tokens = to_blocks(at, *line.at(grad_x, grad_x_theirs))
     line.mark(far, last, grad_tokens)
+
     push_b.own_half()
-    for bit in bits[3:]:
-        every = sums_step(*line.at(every, far))
-        far = doubled(grid, every, bit)
-        line.mark(far)
-    layer_out = to_blocks(*line.at(out_mine, out_theirs))
-    grad_out = push_a.result(core, group_width, width // 2)
-    every = sums_step(*line.at(every, far))
-    sums, rest = every[:4], [every[4:]]
+    every = jnp.concatenate([line.at(every)] + list(line.at(far)), axis=1)
+    parts = [every]
     for k in range(1, grid.blocks):
         pairs = [
             (d * grid.blocks + b, d * grid.blocks + (b - k) % grid.blocks)
             for d in range(grid.groups) for b in range(grid.blocks)
         ]
-        far = lax.ppermute(every, AXES, pairs)
-        sums, rest = sums + far[:4], rest + [far[4:]]
-    both = jnp.stack([p.result(core, 0, group_width).reshape(-1, 2, 3, width // 4) for p in (push_a, push_b)], axis=1)
-    grad_qkv = both.transpose(0, 3, 1, 2, 4).reshape(-1, 3 * width)
-    rest = jnp.concatenate(rest).reshape(-1, 4, width)
-    my_features = time_features(rest[:, 2, 0], group * t_rows + jnp.arange(t_rows, dtype=jnp.int32))
-    grad_scales = rest[:, :2].reshape(-1, 2 * width)
-    grad_time = lax.dot_general(
-        my_features, grad_scales, (((0,), (0,)), ((), ())), precision=lax.Precision.HIGHEST
-    )
+        parts.append(lax.ppermute(every, AXES, pairs))
+    layer_out = to_blocks(at, *line.at(out_mine, out_theirs))
+    grad_qkv, grad_out = heads_grads(at, (push_a.own, push_a.other), (push_b.own, push_b.other), width)
+    index = group * t_rows + jnp.arange(t_rows, dtype=jnp.int32)
+    sums, grad_time = last_sums(parts, index, width)
     sums = lax.dynamic_slice_in_dim(sums, group * per, per, 1)
     return (
         layer_out, grad_tokens, grad_qkv, grad_out, grad_up, grad_down, grad_time,

time: 466 us -> 437 us (0.938)
  waiting for transfers between devices: 70.6 us -> 45.4 us
  local copies, waits for them, and re-layouts: 29.7 us -> 23 us
  Pallas kernels: 247 us -> 252 us
    ppermute x48, waiting for transfers between devices: 40.7 us -> 20.9 us  [shift(): return lax.ppermute(v, AXES, pairs)]
    select_n x2 -> x0, other arithmetic: 4.97 us -> none  [to_blocks(): jnp.where(core == 0, jnp.stack([mine, theirs]), jnp.stack([theirs, mine]))]
    pallas_call x30 -> x34, Pallas kernels: 222 us -> 227 us  [run(): kernel_call(kernel, name, grid, ins, outs, shapes, scratch, flops, moved,...]
    ppermute x8 -> x9, waiting for transfers between devices: 19.4 us -> 14.8 us  [doubled(): return lax.ppermute(v, AXES, pairs)]
    unnamed x249 -> x272, local copies, waits for them, and re-layouts: 15 us -> 12.1 us
    ppermute x8 -> x9, starting transfers between devices: 8.22 us -> 9.38 us  [doubled(): return lax.ppermute(v, AXES, pairs)]
  transfers between devices with their start and end apart: 85 -> 86, of which waited for: 29 -> 23; matrix products, arithmetic and copies ran while one was open for 7% -> 8% of each run, Pallas kernels for 47% -> 49%
where the time goes in v5:
time: 437 us; the launch traced here: 430 us
  Pallas kernels  252 us (58%)
  starting transfers between devices  82.1 us (19%)
  waiting for transfers between devices  45.4 us (10%)
  other arithmetic  24.2 us (6%)
  local copies, waits for them, and re-layouts  23 us (5%)
    pallas_call x34, Pallas kernels, run(): kernel_call(kernel, name, grid, ins, outs, shapes, scratch, flops, moved,...  227 us
    ppermute x48, starting transfers between devices, shift(): return lax.ppermute(v, AXES, pairs)  46.7 us
    ppermute x28, starting transfers between devices, swap(): return lax.ppermute(v, AXES, pairs)  25.7 us
    pallas_call x2, Pallas kernels, up_product(): pl.pallas_call(kernel, grid=(per,), in_specs=[SCALARS, whole(normed.shape...  24.6 us
    ppermute x48, waiting for transfers between devices, shift(): return lax.ppermute(v, AXES, pairs)  20.9 us
    ppermute x9, waiting for transfers between devices, doubled(): return lax.ppermute(v, AXES, pairs)  14.8 us
    unnamed x272, local copies, waits for them, and re-layouts  12.1 us
    ppermute x28, waiting for transfers between devices, swap(): return lax.ppermute(v, AXES, pairs)  9.66 us
  transfers between devices with their start and end apart: 86, of which 23 were waited for; matrix products, arithmetic and copies ran while one was open for 8% of the time, Pallas kernels for 49%

profile of v5, /device:TPU:1, one launch (start us, length us, event | category | flops | bytes accessed | tf_op | source)
XLA Modules:
  0.0 430.0 jit_solution(12648667065519536752)
XLA Ops:
  1.8 4.2 collective-permute-start.1
  7.5 1.5 collective-permute-start
  9.1 2.3 collective-permute-start.4
  12.8 3.1 collective-permute-done.4
  18.0 2.8 pad_maximum_fusion.refs_0_.x.x_far
  21.9 1.5 collective-permute-done.6.refs_6_.refs_1_
  23.4 3.9 collective-permute-start.12
  34.5 6.6 %collective-permute-done.8 = bf16[4,8,2176]{2,1,0:T(8,128)(2,1)S(1)} collective-permute-done((bf16[4,8,2176]{2,1,0:T(8,128)(2,1)S(1)}, bf16[4,8,2176]{2,1,0:T(8,128)(2,1)S(1)}, u32[]{:S(2)}, u32[]{:S(2)}) %collective-permute-start.8) | collective-permute-done | bytes 139296 | tf_op jit(solution)/shard_map/ppermute | solution.py:906
  45.3 4.0 collective-permute-done.13
  53.6 1.9 collective-permute-start.19
  55.5 9.1 %qkv_first.1 = (bf16[1024,1024]{1,0:T(8,128)(2,1)}, bf16[1024,1024]{1,0:T(8,128)(2,1)}, bf16[1024,1536]{1,0:T(8,128)(2,1)}) custom-call(s32[24]{0:T(128)} %fusion.24.place, bf16[1024,1024]{1,0:T(8,128)(2,1)} %pad_maximum_fusion.refs_0_.x.x_far, f32[1,1024]{1,0:T(1,128)} %get-tuple-element.294.refs_1_.gain, f32[1,1024]{1,0:T(1,128)} %squeeze.128.refs_2_, ...), custom_call_target="tpu_custom_call" | custom-call | flops 3221225472 | bytes 12582912 | tf_op jit(solution)/shard_map/qkv_first/pallas_call | solution.py:106
  64.6 3.0 collective-permute-start.22
  69.5 1.9 copy-done.67
  71.4 5.7 %attend.4 = (bf16[1024,256]{1,0:T(8,128)(2,1)S(1)}, f32[1024,128]{1,0:T(8,128)S(1)}) custom-call(bf16[1024,1536]{1,0:T(8,128)(2,1)S(1)} %copy-done.67, bf16[1024,1536]{1,0:T(8,128)(2,1)S(1)} %copy-done.67, bf16[1024,1]{1,0:T(8,128)(2,1)S(1)} %copy.38.mask), custom_call_target="tpu_custom_call" | custom-call | flops 4294967296 | bytes 2097152 | tf_op jit(solution)/shard_map/attend/pallas_call | solution.py:106
  78.6 5.7 %attend.5 = (bf16[1024,256]{1,0:T(8,128)(2,1)S(1)}, f32[1024,128]{1,0:T(8,128)S(1)}) custom-call(bf16[1024,1536]{1,0:T(8,128)(2,1)S(1)} %copy-done.67, bf16[1024,1536]{1,0:T(8,128)(2,1)S(1)} %copy-done.67, bf16[1024,1]{1,0:T(8,128)(2,1)S(1)} %copy.38.mask), custom_call_target="tpu_custom_call" | custom-call | flops 4294967296 | bytes 2097152 | tf_op jit(solution)/shard_map/attend/pallas_call | solution.py:106
  85.4 2.0 collective-permute-start.26
  90.3 1.9 collective-permute-start.29
  92.2 5.2 %qkv.1.q.kv = bf16[1024,1536]{1,0:T(8,128)(2,1)S(1)} custom-call(s32[24]{0:T(128)S(1)} %copy-done.53, bf16[1024,1024]{1,0:T(8,128)(2,1)S(1)} %copy-done.66, f32[1024,128]{1,0:T(8,128)S(1)} %copy-done.43, f32[1024,128]{1,0:T(8,128)S(1)} %copy-done.46, bf16[4,64,1280]{2,1,0:T(8,128)(2,1)S(1)} %rolled.5.refs_3_.refs_0_.refs_8_, ...), custom_call_target="tpu_custom_call" | custom-call | flops 3221225472 | bytes 12582912 | tf_op jit(solution)/shard_map/qkv/pallas_call | solution.py:106
  97.5 2.9 collective-permute-start.31
  100.4 5.8 %attend.6 = (bf16[1024,256]{1,0:T(8,128)(2,1)S(1)}, f32[1024,128]{1,0:T(8,128)S(1)}) custom-call(bf16[1024,1536]{1,0:T(8,128)(2,1)S(1)} %qkv.1.q.kv, bf16[1024,1536]{1,0:T(8,128)(2,1)S(1)} %qkv.1.q.kv, bf16[1024,1]{1,0:T(8,128)(2,1)S(1)} %copy.38.mask), custom_call_target="tpu_custom_call" | custom-call | flops 4294967296 | bytes 2097152 | tf_op jit(solution)/shard_map/attend/pallas_call | solution.py:106
  106.3 1.5 pad_maximum_fusion.1.refs_4_.grad.base_far
  107.9 2.8 collective-permute-start.32
  112.5 5.8 %attend.7 = (bf16[1024,256]{1,0:T(8,128)(2,1)S(1)}, f32[1024,128]{1,0:T(8,128)S(1)}) custom-call(bf16[1024,1536]{1,0:T(8,128)(2,1)S(1)} %qkv.1.q.kv, bf16[1024,1536]{1,0:T(8,128)(2,1)S(1)} %qkv.1.q.kv, bf16[1024,1]{1,0:T(8,128)(2,1)S(1)} %copy.38.mask), custom_call_target="tpu_custom_call" | custom-call | flops 4294967296 | bytes 2097152 | tf_op jit(solution)/shard_map/attend/pallas_call | solution.py:106
  119.1 8.4 %out.1 = (bf16[1024,1024]{1,0:T(8,128)(2,1)S(1)}, bf16[1024,1024]{1,0:T(8,128)(2,1)S(1)}, bf16[1024,1024]{1,0:T(8,128)(2,1)}) custom-call(s32[24]{0:T(128)S(1)} %copy-done.53, bf16[1024,1024]{1,0:T(8,128)(2,1)} %pad_maximum_fusion.refs_0_.x.x_far, f32[1,1024]{1,0:T(1,128)S(1)} %get-tuple-element.554.gain, f32[1,1024]{1,0:T(1,128)S(1)} %squeeze.126.bias, ...), custom_call_target="tpu_custom_call" | custom-call | flops 2147483648 | bytes 10485760 | tf_op jit(solution)/shard_map/out/pallas_call | solution.py:106
  128.9 7.0 %collective-permute-done.36.refs_3_ = bf16[4,64,2048]{2,1,0:T(8,128)(2,1)S(1)} collective-permute-done((bf16[4,64,2048]{2,1,0:T(8,128)(2,1)S(1)}, bf16[4,64,2048]{2,1,0:T(8,128)(2,1)S(1)}, u32[]{:S(2)}, u32[]{:S(2)}) %collective-permute-start.36) | collective-permute-done | bytes 1048608 | tf_op jit(solution)/shard_map/ppermute | solution.py:48
  137.3 2.2 collective-permute-done.37.refs_6_
  139.5 1.5 collective-permute-done.38.refs_7_
  142.2 12.3 %up.2 = (bf16[1024,4096]{1,0:T(8,128)(2,1)}, bf16[1024,4096]{1,0:T(8,128)(2,1)}) custom-call(s32[24]{0:T(128)} %fusion.24.place, bf16[1024,1024]{1,0:T(8,128)(2,1)} %copy-done.37, bf16[4,64,2048]{2,1,0:T(8,128)(2,1)} %copy-done.20, bf16[4,64,2048]{2,1,0:T(8,128)(2,1)} %copy-done.87, bf16[4,64,2048]{2,1,0:T(8,128)(2,1)} %copy-done.90, ...), custom_call_target="tpu_custom_call" | custom-call | flops 4294967296 | bytes 12582912 | tf_op jit(solution)/shard_map/up/pallas_call | solution.py:449
  157.6 12.3 %up.3 = (bf16[1024,4096]{1,0:T(8,128)(2,1)}, bf16[1024,4096]{1,0:T(8,128)(2,1)}) custom-call(s32[24]{0:T(128)} %fusion.24.place, bf16[1024,1024]{1,0:T(8,128)(2,1)} %copy-done.37, bf16[4,64,2048]{2,1,0:T(8,128)(2,1)} %copy-done.20, bf16[4,64,2048]{2,1,0:T(8,128)(2,1)} %copy-done.87, ...), custom_call_target="tpu_custom_call", output_to_operand_aliasing={{0}: (10, {}), {1}: (11, {})} | custom-call | flops 4294967296 | bytes 12582912 | tf_op jit(solution)/shard_map/up/pallas_call | solution.py:449
  170.0 9.8 %wide_chunks.2 = bf16[4,4,256,512]{3,2,1,0:T(8,128)(2,1)} custom-call(s32[24]{0:T(128)} %fusion.24.place, bf16[1024,4096]{1,0:T(8,128)(2,1)} %get-tuple-element.479.refs_0_.refs_1_.refs_2_.refs_3_.active, bf16[1024,4096]{1,0:T(8,128)(2,1)} %get-tuple-element.479.refs_0_.refs_1_.refs_2_.refs_3_.active, ...), custom_call_target="tpu_custom_call" | custom-call | flops 4294967296 | bytes 14680064 | tf_op jit(solution)/shard_map/wide_chunks/pallas_call | solution.py:106
  179.8 1.7 collective-permute-done.43.refs_3_
  182.8 3.7 collective-permute-done.44.refs_6_
  187.8 14.9 %hidden_back.1.b.refs_8_ = bf16[1024,4096]{1,0:T(8,128)(2,1)} custom-call(s32[24]{0:T(128)} %fusion.24.place, bf16[1024,1024]{1,0:T(8,128)(2,1)} %pad_maximum_fusion.1.refs_4_.grad.base_far, bf16[1024,4096]{1,0:T(8,128)(2,1)} %get-tuple-element.367.slope, bf16[4,256,512]{2,1,0:T(8,128)(2,1)} %copy-done.5, bf16[4,256,512]{2,1,0:T(8,128)(2,1)} %copy-done.77, ...), custom_call_target="tpu_custom_call" | custom-call | flops 8589934592 | bytes 25165824 | tf_op jit(solution)/shard_map/hidden_back/pallas_call | solution.py:106
  202.8 11.5 %wide_chunks.3 = (bf16[4,256,512]{2,1,0:T(8,128)(2,1)}, bf16[4,256,512]{2,1,0:T(8,128)(2,1)}, bf16[4,256,512]{2,1,0:T(8,128)(2,1)}, bf16[4,256,512]{2,1,0:T(8,128)(2,1)}) custom-call(s32[24]{0:T(128)} %fusion.24.place, bf16[1024,4096]{1,0:T(8,128)(2,1)} %get-tuple-element.479.refs_0_.refs_1_.refs_2_.refs_3_.active, ...), custom_call_target="tpu_custom_call" | custom-call | flops 4294967296 | bytes 14680064 | tf_op jit(solution)/shard_map/wide_chunks/pallas_call | solution.py:106
  214.2 9.5 %row_chunks.2 = bf16[4,4,64,2048]{3,2,1,0:T(8,128)(2,1)} custom-call(s32[24]{0:T(128)} %fusion.24.place, bf16[1024,1024]{1,0:T(8,128)(2,1)} %get-tuple-element.383.a, bf16[1024,4096]{1,0:T(8,128)(2,1)} %hidden_back.1.b.refs_8_), custom_call_target="tpu_custom_call" | custom-call | flops 4294967296 | bytes 10485760 | tf_op jit(solution)/shard_map/row_chunks/pallas_call | solution.py:106
  225.6 16.4 %norm_back.2 = (bf16[1024,1024]{1,0:T(8,128)(2,1)}, f32[2,1024]{1,0:T(2,128)}) custom-call(s32[24]{0:T(128)} %fusion.24.place, f32[1,1024]{1,0:T(1,128)} %copy-done.60, bf16[1024,1024]{1,0:T(8,128)(2,1)} %copy-done.6, bf16[1024,1024]{1,0:T(8,128)(2,1)} %pad_maximum_fusion.1.refs_4_.grad.base_far, bf16[4,64,2048]{2,1,0:T(8,128)(2,1)} %copy-done.20, ...), custom_call_target="tpu_custom_call" | custom-call | flops 8589934592 | bytes 23068672 | tf_op jit(solution)/shard_map/norm_back/pallas_call | solution.py:106
  244.6 10.6 %row_chunks.3 = (bf16[4,64,2048]{2,1,0:T(8,128)(2,1)}, bf16[4,64,2048]{2,1,0:T(8,128)(2,1)}, bf16[4,64,2048]{2,1,0:T(8,128)(2,1)}, bf16[4,64,2048]{2,1,0:T(8,128)(2,1)}) custom-call(s32[24]{0:T(128)} %fusion.24.place, bf16[1024,1024]{1,0:T(8,128)(2,1)} %get-tuple-element.383.a, bf16[1024,4096]{1,0:T(8,128)(2,1)} %hidden_back.1.b.refs_8_, ...), custom_call_target="tpu_custom_call" | custom-call | flops 4294967296 | bytes 10485760 | tf_op jit(solution)/shard_map/row_chunks/pallas_call | solution.py:106
  257.4 4.3 %heads_back.1.grad = bf16[1024,1024]{1,0:T(8,128)(2,1)S(1)} custom-call(s32[24]{0:T(128)S(1)} %copy-done.54, bf16[1024,1024]{1,0:T(8,128)(2,1)S(1)} %copy-done.2, bf16[4,64,1280]{2,1,0:T(8,128)(2,1)S(1)} %copy-done.10, bf16[4,64,1280]{2,1,0:T(8,128)(2,1)S(1)} %copy-done.22, bf16[4,64,1280]{2,1,0:T(8,128)(2,1)S(1)} %copy-done.28, ...), custom_call_target="tpu_custom_call" | custom-call | flops 2147483648 | bytes 6291456 | tf_op jit(solution)/shard_map/heads_back/pallas_call | solution.py:106
  262.9 2.1 add_convert_fusion.2
  266.7 11.1 %attend_back.4.refs_0_.refs_16_ = bf16[1024,768]{1,0:T(8,128)(2,1)S(1)} custom-call(bf16[1024,1536]{1,0:T(8,128)(2,1)S(1)} %copy-done.68, bf16[1024,1536]{1,0:T(8,128)(2,1)S(1)} %copy-done.68, bf16[1024,256]{1,0:T(8,128)(2,1)S(1)} %copy-done.12, bf16[1024,1024]{1,0:T(8,128)(2,1)S(1)} %heads_back.1.grad, f32[1024,128]{1,0:T(8,128)S(1)} %copy-done.72, ...), custom_call_target="tpu_custom_call" | custom-call | flops 10737418240 | bytes 4194304 | tf_op jit(solution)/shard_map/attend_back/pallas_call | solution.py:106
  277.8 2.5 collective-permute-done.51
  281.1 11.2 %attend_back.5.refs_1_.refs_17_ = bf16[1024,768]{1,0:T(8,128)(2,1)S(1)} custom-call(bf16[1024,1536]{1,0:T(8,128)(2,1)S(1)} %copy-done.68, bf16[1024,1536]{1,0:T(8,128)(2,1)S(1)} %copy-done.68, bf16[1024,256]{1,0:T(8,128)(2,1)S(1)} %copy-done.14, bf16[1024,1024]{1,0:T(8,128)(2,1)S(1)} %heads_back.1.grad, f32[1024,128]{1,0:T(8,128)S(1)} %copy-done.70, ...), custom_call_target="tpu_custom_call" | custom-call | flops 10737418240 | bytes 4194304 | tf_op jit(solution)/shard_map/attend_back/pallas_call | solution.py:106
  292.4 2.3 collective-permute-done.53
  294.8 6.2 %heads_chunks.4 = bf16[4,4,64,1280]{3,2,1,0:T(8,128)(2,1)} custom-call(s32[24]{0:T(128)S(1)} %copy-done.54, bf16[1024,1024]{1,0:T(8,128)(2,1)S(1)} %copy-done.3, bf16[1024,768]{1,0:T(8,128)(2,1)S(1)} %attend_back.4.refs_0_.refs_16_, bf16[1024,768]{1,0:T(8,128)(2,1)S(1)} %attend_back.5.refs_1_.refs_17_, bf16[1024,256]{1,0:T(8,128)(2,1)S(1)} %copy-done.12, ...), custom_call_target="tpu_custom_call" | custom-call | flops 2684354560 | bytes 7340032 | tf_op jit(solution)/shard_map/heads_chunks/pallas_call | solution.py:106
  303.0 1.5 collective-permute-start.57
  304.5 11.1 %attend_back.6.refs_0_.refs_18_ = bf16[1024,768]{1,0:T(8,128)(2,1)S(1)} custom-call(bf16[1024,1536]{1,0:T(8,128)(2,1)S(1)} %copy-done.64, bf16[1024,1536]{1,0:T(8,128)(2,1)S(1)} %copy-done.64, bf16[1024,256]{1,0:T(8,128)(2,1)S(1)} %copy-done.18, bf16[1024,1024]{1,0:T(8,128)(2,1)S(1)} %heads_back.1.grad, f32[1024,128]{1,0:T(8,128)S(1)} %copy-done.76, ...), custom_call_target="tpu_custom_call" | custom-call | flops 10737418240 | bytes 4194304 | tf_op jit(solution)/shard_map/attend_back/pallas_call | solution.py:106
  317.8 1.5 copy-done.83
  319.3 8.6 %heads_chunks.5 = (bf16[4,64,1280]{2,1,0:T(8,128)(2,1)S(1)}, bf16[4,64,1280]{2,1,0:T(8,128)(2,1)S(1)}, bf16[4,64,1280]{2,1,0:T(8,128)(2,1)S(1)}, bf16[4,64,1280]{2,1,0:T(8,128)(2,1)S(1)}) custom-call(s32[24]{0:T(128)S(1)} %copy-done.54, bf16[1024,1024]{1,0:T(8,128)(2,1)} %get-tuple-element.442.a, bf16[1024,768]{1,0:T(8,128)(2,1)} %copy-done.7, ...), custom_call_target="tpu_custom_call" | custom-call | flops 2684354560 | bytes 7340032 | tf_op jit(solution)/shard_map/heads_chunks/pallas_call | solution.py:106
  332.8 2.0 collective-permute-start.61
  334.9 11.3 %attend_back.7.refs_1_.refs_19_ = bf16[1024,768]{1,0:T(8,128)(2,1)S(1)} custom-call(bf16[1024,1536]{1,0:T(8,128)(2,1)S(1)} %copy-done.65, bf16[1024,1536]{1,0:T(8,128)(2,1)S(1)} %copy-done.65, bf16[1024,256]{1,0:T(8,128)(2,1)S(1)} %copy-done.16, bf16[1024,1024]{1,0:T(8,128)(2,1)S(1)} %copy-done.36, f32[1024,128]{1,0:T(8,128)S(1)} %copy-done.74, ...), custom_call_target="tpu_custom_call" | custom-call | flops 10737418240 | bytes 4194304 | tf_op jit(solution)/shard_map/attend_back/pallas_call | solution.py:106
  346.2 3.7 heads_chunks.6
  351.2 2.5 maximum_select_fusion.1
  357.6 2.5 heads_chunks.7
  360.1 1.5 slice_bitcast_fusion
  363.4 12.9 %norm_back.3 = (bf16[512,1024]{1,0:T(8,128)(2,1)}, bf16[512,1024]{1,0:T(8,128)(2,1)}, f32[2,1024]{1,0:T(2,128)}) custom-call(s32[24]{0:T(128)} %fusion.24.place, f32[1,1024]{1,0:T(1,128)} %get-tuple-element.294.refs_1_.gain, bf16[1024,1024]{1,0:T(8,128)(2,1)} %pad_maximum_fusion.refs_0_.x.x_far, ...), custom_call_target="tpu_custom_call" | custom-call | flops 6442450944 | bytes 18874368 | tf_op jit(solution)/shard_map/norm_back/pallas_call | solution.py:106
  377.8 1.8 collective-permute-start.72
  382.5 1.9 fusion.27
  385.8 9.6 %down.2 = bf16[512,1024]{1,0:T(8,128)(2,1)} custom-call(s32[24]{0:T(128)} %fusion.24.place, bf16[1024,4096]{1,0:T(8,128)(2,1)} %get-tuple-element.479.refs_0_.refs_1_.refs_2_.refs_3_.active, bf16[1024,1024]{1,0:T(8,128)(2,1)} %copy-done.6, bf16[4,256,512]{2,1,0:T(8,128)(2,1)} %copy-done.5, bf16[4,256,512]{2,1,0:T(8,128)(2,1)} %copy-done.77, ...), custom_call_target="tpu_custom_call" | custom-call | flops 4294967296 | bytes 12582912 | tf_op jit(solution)/shard_map/down/pallas_call | solution.py:106
  401.2 9.4 %down.3.mine = bf16[512,1024]{1,0:T(8,128)(2,1)} custom-call(s32[24]{0:T(128)} %fusion.24.place, bf16[1024,4096]{1,0:T(8,128)(2,1)} %get-tuple-element.479.refs_0_.refs_1_.refs_2_.refs_3_.active, bf16[1024,1024]{1,0:T(8,128)(2,1)} %copy-done.6, bf16[4,256,512]{2,1,0:T(8,128)(2,1)} %copy-done.5, bf16[4,256,512]{2,1,0:T(8,128)(2,1)} %copy-done.77, ...), custom_call_target="tpu_custom_call" | custom-call | flops 4294967296 | bytes 12582912 | tf_op jit(solution)/shard_map/down/pallas_call | solution.py:106
  414.8 2.1 collective-permute-start.82
  417.0 2.0 to_blocks.2
  419.9 2.9 collective-permute-start.83
  424.6 2.0 to_blocks.3
  426.6 1.6 heads_grads.1
  (492 shorter events, 88.0 us)
Async XLA Ops:
  1.8 14.1 %collective-permute-start.1 = (bf16[1,64,768]{2,1,0:T(8,128)(2,1)S(1)}, bf16[1,64,768]{2,1,0:T(8,128)(2,1)S(1)}, u32[]{:S(2)}, u32[]{:S(2)}) collective-permute-start(bf16[1,64,768]{2,1,0:T(8,128)(2,1)S(1)} %maximum_bitcast_fusion.1.refs_0_), channel_id=1, source_target_pairs={{0,24},{1,25},{2,26},{3,27},{4,28},{5,29},{6,30},{7,31},{8,0},{9,1... | collective-permute-start | bytes 294920 | tf_op jit(solution)/shard_map/ppermute | solution.py:48
  6.0 10.0 %collective-permute-start.2 = (bf16[1,64,768]{2,1,0:T(8,128)(2,1)S(1)}, bf16[1,64,768]{2,1,0:T(8,128)(2,1)S(1)}, u32[]{:S(2)}, u32[]{:S(2)}) collective-permute-start(bf16[1,64,768]{2,1,0:T(8,128)(2,1)S(1)} %maximum_bitcast_fusion.1.refs_0_), channel_id=1, source_target_pairs={{0,16},{1,17},{2,18},{3,19},{4,20},{5,21},{6,22},{7,23},{8,24},{9,... | collective-permute-start | bytes 294920 | tf_op jit(solution)/shard_map/ppermute | solution.py:48
  6.0 10.0 %collective-permute-start.3 = (bf16[1,64,768]{2,1,0:T(8,128)(2,1)S(1)}, bf16[1,64,768]{2,1,0:T(8,128)(2,1)S(1)}, u32[]{:S(2)}, u32[]{:S(2)}) collective-permute-start(bf16[1,64,768]{2,1,0:T(8,128)(2,1)S(1)} %maximum_bitcast_fusion.1.refs_0_), channel_id=1, source_target_pairs={{0,8},{1,9},{2,10},{3,11},{4,12},{5,13},{6,14},{7,15},{8,16},{9,17... | collective-permute-start | bytes 294920 | tf_op jit(solution)/shard_map/ppermute | solution.py:48
  7.5 8.5 %collective-permute-start = (bf16[512,1024]{1,0:T(8,128)(2,1)}, bf16[512,1024]{1,0:T(8,128)(2,1)}, u32[]{:S(2)}, u32[]{:S(2)}) collective-permute-start(bf16[512,1024]{1,0:T(8,128)(2,1)} %dynamic-slice_bitcast_fusion.3), channel_id=1, source_target_pairs={{0,1},{1,0},{2,3},{3,2},{4,5},{5,4},{6,7},{7,6},{8,9},{9,8},{10,11... | collective-permute-start | bytes 3145736 | tf_op jit(solution)/shard_map/ppermute | solution.py:55
  23.4 17.7 %collective-permute-start.12 = (bf16[1,64,1280]{2,1,0:T(8,128)(2,1)S(1)}, bf16[1,64,1280]{2,1,0:T(8,128)(2,1)S(1)}, u32[]{:S(2)}, u32[]{:S(2)}) collective-permute-start(bf16[1,64,1280]{2,1,0:T(8,128)(2,1)S(1)} %collective-permute-done.7.refs_1_), channel_id=1, source_target_pairs={{0,24},{1,25},{2,26},{3,27},{4,28},{5,29},{6,30},{7,31},{8,0},{9,1... | collective-permute-start | bytes 491528 | tf_op jit(solution)/shard_map/ppermute | solution.py:48
  27.3 13.9 %collective-permute-start.9 = (bf16[4,64,768]{2,1,0:T(8,128)(2,1)S(1)}, bf16[4,64,768]{2,1,0:T(8,128)(2,1)}, u32[]{:S(2)}, u32[]{:S(2)}) collective-permute-start(bf16[4,64,768]{2,1,0:T(8,128)(2,1)S(1)} %rolled.4.refs_5_.refs_0_), channel_id=1, source_target_pairs={{0,4},{1,3},{2,6},{3,1},{4,0},{5,7},{6,2},{7,5},{8,12},{9,11},{10,... | collective-permute-start | bytes 1179656 | tf_op jit(solution)/shard_map/ppermute | solution.py:48
  28.5 12.7 %collective-permute-start.10 = (bf16[4,64,768]{2,1,0:T(8,128)(2,1)}, bf16[4,64,768]{2,1,0:T(8,128)(2,1)}, u32[]{:S(2)}, u32[]{:S(2)}) collective-permute-start(bf16[4,64,768]{2,1,0:T(8,128)(2,1)} %collective-permute-done.6.refs_6_.refs_1_), channel_id=1, source_target_pairs={{0,4},{1,3},{2,6},{3,1},{4,0},{5,7},{6,2},{7,5},{8,12},{9,11},{10,... | collective-permute-start | bytes 1179656 | tf_op jit(solution)/shard_map/ppermute | solution.py:48
  28.8 12.4 %collective-permute-start.11 = (bf16[4,64,768]{2,1,0:T(8,128)(2,1)S(1)}, bf16[4,64,768]{2,1,0:T(8,128)(2,1)}, u32[]{:S(2)}, u32[]{:S(2)}) collective-permute-start(bf16[4,64,768]{2,1,0:T(8,128)(2,1)S(1)} %rolled.4.refs_5_.refs_0_), channel_id=1, source_target_pairs={{0,1},{1,0},{2,3},{3,2},{4,5},{5,4},{6,7},{7,6},{8,9},{9,8},{10,11... | collective-permute-start | bytes 1179656 | tf_op jit(solution)/shard_map/ppermute | solution.py:55
  30.1 11.0 %collective-permute-start.8 = (bf16[4,8,2176]{2,1,0:T(8,128)(2,1)S(1)}, bf16[4,8,2176]{2,1,0:T(8,128)(2,1)S(1)}, u32[]{:S(2)}, u32[]{:S(2)}) collective-permute-start(bf16[4,8,2176]{2,1,0:T(8,128)(2,1)S(1)} %pad_maximum_fusion.6), channel_id=1, source_target_pairs={{0,2},{1,3},{2,0},{3,1},{4,6},{5,7},{6,4},{7,5},{8,10},{9,11},{10,... | collective-permute-start | bytes 417800 | tf_op jit(solution)/shard_map/ppermute | solution.py:906
  41.2 8.1 %collective-permute-start.13 = (bf16[8,8,2176]{2,1,0:T(8,128)(2,1)S(1)}, bf16[8,8,2176]{2,1,0:T(8,128)(2,1)S(1)}, u32[]{:S(2)}, u32[]{:S(2)}) collective-permute-start(bf16[8,8,2176]{2,1,0:T(8,128)(2,1)S(1)} %pad_maximum_fusion.5), channel_id=1, source_target_pairs={{0,4},{1,5},{2,6},{3,7},{4,0},{5,1},{6,2},{7,3},{8,12},{9,13},{10,... | collective-permute-start | bytes 835592 | tf_op jit(solution)/shard_map/ppermute | solution.py:906
  51.6 13.0 %collective-permute-start.18 = (bf16[4,64,1280]{2,1,0:T(8,128)(2,1)S(1)}, bf16[4,64,1280]{2,1,0:T(8,128)(2,1)S(1)}, u32[]{:S(2)}, u32[]{:S(2)}) collective-permute-start(bf16[4,64,1280]{2,1,0:T(8,128)(2,1)S(1)} %rolled.5.refs_3_.refs_0_.refs_8_), channel_id=1, source_target_pairs={{0,2},{1,5},{2,0},{3,7},{4,6},{5,1},{6,4},{7,3},{8,10},{9,13},{10,... | collective-permute-start | bytes 1966088 | tf_op jit(solution)/shard_map/ppermute | solution.py:48
  53.6 11.0 %collective-permute-start.19 = (bf16[1,64,2048]{2,1,0:T(8,128)(2,1)S(1)}, bf16[1,64,2048]{2,1,0:T(8,128)(2,1)S(1)}, u32[]{:S(2)}, u32[]{:S(2)}) collective-permute-start(bf16[1,64,2048]{2,1,0:T(8,128)(2,1)S(1)} %dynamic-slice_bitcast_fusion.13.refs_0_), channel_id=1, source_target_pairs={{0,24},{1,25},{2,26},{3,27},{4,28},{5,29},{6,30},{7,31},{8,0},{9,1... | collective-permute-start | bytes 786440 | tf_op jit(solution)/shard_map/ppermute | solution.py:48
  64.6 13.3 %collective-permute-start.22 = (bf16[4,64,1280]{2,1,0:T(8,128)(2,1)S(1)}, bf16[4,64,1280]{2,1,0:T(8,128)(2,1)S(1)}, u32[]{:S(2)}, u32[]{:S(2)}) collective-permute-start(bf16[4,64,1280]{2,1,0:T(8,128)(2,1)S(1)} %rolled.5.refs_3_.refs_0_.refs_8_), channel_id=1, source_target_pairs={{0,1},{1,0},{2,3},{3,2},{4,5},{5,4},{6,7},{7,6},{8,9},{9,8},{10,11... | collective-permute-start | bytes 1966088 | tf_op jit(solution)/shard_map/ppermute | solution.py:55
  67.6 10.4 %collective-permute-start.23 = (bf16[4,64,1280]{2,1,0:T(8,128)(2,1)S(1)}, bf16[4,64,1280]{2,1,0:T(8,128)(2,1)S(1)}, u32[]{:S(2)}, u32[]{:S(2)}) collective-permute-start(bf16[4,64,1280]{2,1,0:T(8,128)(2,1)S(1)} %collective-permute-done.18.refs_4_.refs_1_.refs_9_), channel_id=1, source_target_pairs={{0,1},{1,0},{2,3},{3,2},{4,5},{5,4},{6,7},{7,6},{8,9},{9,8},{10,11... | collective-permute-start | bytes 1966088 | tf_op jit(solution)/shard_map/ppermute | solution.py:55
  67.7 17.5 %collective-permute-start.20 = (bf16[4,64,1280]{2,1,0:T(8,128)(2,1)S(1)}, bf16[4,64,1280]{2,1,0:T(8,128)(2,1)S(1)}, u32[]{:S(2)}, u32[]{:S(2)}) collective-permute-start(bf16[4,64,1280]{2,1,0:T(8,128)(2,1)S(1)} %rolled.5.refs_3_.refs_0_.refs_8_), channel_id=1, source_target_pairs={{0,4},{1,3},{2,6},{3,1},{4,0},{5,7},{6,2},{7,5},{8,12},{9,11},{10,... | collective-permute-start | bytes 1966088 | tf_op jit(solution)/shard_map/ppermute | solution.py:48
  67.9 10.0 %collective-permute-start.24 = (bf16[1,64,2048]{2,1,0:T(8,128)(2,1)S(1)}, bf16[1,64,2048]{2,1,0:T(8,128)(2,1)S(1)}, u32[]{:S(2)}, u32[]{:S(2)}) collective-permute-start(bf16[1,64,2048]{2,1,0:T(8,128)(2,1)S(1)} %collective-permute-done.19.refs_1_), channel_id=1, source_target_pairs={{0,24},{1,25},{2,26},{3,27},{4,28},{5,29},{6,30},{7,31},{8,0},{9,1... | collective-permute-start | bytes 786440 | tf_op jit(solution)/shard_map/ppermute | solution.py:48
  68.2 16.9 %collective-permute-start.21 = (bf16[4,64,1280]{2,1,0:T(8,128)(2,1)S(1)}, bf16[4,64,1280]{2,1,0:T(8,128)(2,1)S(1)}, u32[]{:S(2)}, u32[]{:S(2)}) collective-permute-start(bf16[4,64,1280]{2,1,0:T(8,128)(2,1)S(1)} %collective-permute-done.18.refs_4_.refs_1_.refs_9_), channel_id=1, source_target_pairs={{0,4},{1,3},{2,6},{3,1},{4,0},{5,7},{6,2},{7,5},{8,12},{9,11},{10,... | collective-permute-start | bytes 1966088 | tf_op jit(solution)/shard_map/ppermute | solution.py:48
  87.5 10.0 %collective-permute-start.28 = (bf16[512,1024]{1,0:T(8,128)(2,1)S(1)}, bf16[512,1024]{1,0:T(8,128)(2,1)S(1)}, u32[]{:S(2)}, u32[]{:S(2)}) collective-permute-start(bf16[512,1024]{1,0:T(8,128)(2,1)S(1)} %dynamic-slice_bitcast_fusion.1), channel_id=1, source_target_pairs={{0,1},{1,0},{2,3},{3,2},{4,5},{5,4},{6,7},{7,6},{8,9},{9,8},{10,11... | collective-permute-start | bytes 3145736 | tf_op jit(solution)/shard_map/ppermute | solution.py:55
  90.0 17.8 %collective-permute-start.30 = (bf16[4,64,2048]{2,1,0:T(8,128)(2,1)S(1)}, bf16[4,64,2048]{2,1,0:T(8,128)(2,1)S(1)}, u32[]{:S(2)}, u32[]{:S(2)}) collective-permute-start(bf16[4,64,2048]{2,1,0:T(8,128)(2,1)S(1)} %rolled.6.refs_0_), channel_id=1, source_target_pairs={{0,2},{1,5},{2,0},{3,7},{4,6},{5,1},{6,4},{7,3},{8,10},{9,13},{10,... | collective-permute-start | bytes 3145736 | tf_op jit(solution)/shard_map/ppermute | solution.py:48
  97.5 10.3 %collective-permute-start.31 = (bf16[1,256,512]{2,1,0:T(8,128)(2,1)S(1)}, bf16[1,256,512]{2,1,0:T(8,128)(2,1)S(1)}, u32[]{:S(2)}, u32[]{:S(2)}) collective-permute-start(bf16[1,256,512]{2,1,0:T(8,128)(2,1)S(1)} %collective-permute-done.29.refs_1_), channel_id=1, source_target_pairs={{0,24},{1,25},{2,26},{3,27},{4,28},{5,29},{6,30},{7,31},{8,0},{9,1... | collective-permute-start | bytes 786440 | tf_op jit(solution)/shard_map/ppermute | solution.py:48
  107.9 11.1 %collective-permute-start.32 = (bf16[4,64,2048]{2,1,0:T(8,128)(2,1)S(1)}, bf16[4,64,2048]{2,1,0:T(8,128)(2,1)S(1)}, u32[]{:S(2)}, u32[]{:S(2)}) collective-permute-start(bf16[4,64,2048]{2,1,0:T(8,128)(2,1)S(1)} %rolled.6.refs_0_), channel_id=1, source_target_pairs={{0,1},{1,0},{2,3},{3,2},{4,5},{5,4},{6,7},{7,6},{8,9},{9,8},{10,11... | collective-permute-start | bytes 3145736 | tf_op jit(solution)/shard_map/ppermute | solution.py:55
  110.6 8.4 %collective-permute-start.33 = (bf16[4,64,2048]{2,1,0:T(8,128)(2,1)S(1)}, bf16[4,64,2048]{2,1,0:T(8,128)(2,1)S(1)}, u32[]{:S(2)}, u32[]{:S(2)}) collective-permute-start(bf16[4,64,2048]{2,1,0:T(8,128)(2,1)S(1)} %collective-permute-done.30.refs_1_), channel_id=1, source_target_pairs={{0,1},{1,0},{2,3},{3,2},{4,5},{5,4},{6,7},{7,6},{8,9},{9,8},{10,11... | collective-permute-start | bytes 3145736 | tf_op jit(solution)/shard_map/ppermute | solution.py:55
  110.7 18.2 %collective-permute-start.35 = (bf16[4,64,2048]{2,1,0:T(8,128)(2,1)S(1)}, bf16[4,64,2048]{2,1,0:T(8,128)(2,1)S(1)}, u32[]{:S(2)}, u32[]{:S(2)}) collective-permute-start(bf16[4,64,2048]{2,1,0:T(8,128)(2,1)S(1)} %rolled.6.refs_0_), channel_id=1, source_target_pairs={{0,4},{1,3},{2,6},{3,1},{4,0},{5,7},{6,2},{7,5},{8,12},{9,11},{10,... | collective-permute-start | bytes 3145736 | tf_op jit(solution)/shard_map/ppermute | solution.py:48
  111.5 24.3 %collective-permute-start.36 = (bf16[4,64,2048]{2,1,0:T(8,128)(2,1)S(1)}, bf16[4,64,2048]{2,1,0:T(8,128)(2,1)S(1)}, u32[]{:S(2)}, u32[]{:S(2)}) collective-permute-start(bf16[4,64,2048]{2,1,0:T(8,128)(2,1)S(1)} %collective-permute-done.30.refs_1_), channel_id=1, source_target_pairs={{0,4},{1,3},{2,6},{3,1},{4,0},{5,7},{6,2},{7,5},{8,12},{9,11},{10,... | collective-permute-start | bytes 3145736 | tf_op jit(solution)/shard_map/ppermute | solution.py:48
  141.0 13.9 %collective-permute-start.39 = (bf16[4,256,512]{2,1,0:T(8,128)(2,1)S(1)}, bf16[4,256,512]{2,1,0:T(8,128)(2,1)S(1)}, u32[]{:S(2)}, u32[]{:S(2)}) collective-permute-start(bf16[4,256,512]{2,1,0:T(8,128)(2,1)S(1)} %rolled.7.refs_0_), channel_id=1, source_target_pairs={{0,2},{1,5},{2,0},{3,7},{4,6},{5,1},{6,4},{7,3},{8,10},{9,13},{10,... | collective-permute-start | bytes 3145736 | tf_op jit(solution)/shard_map/ppermute | solution.py:48
  154.9 15.0 %collective-permute-start.41 = (bf16[4,256,512]{2,1,0:T(8,128)(2,1)S(1)}, bf16[4,256,512]{2,1,0:T(8,128)(2,1)S(1)}, u32[]{:S(2)}, u32[]{:S(2)}) collective-permute-start(bf16[4,256,512]{2,1,0:T(8,128)(2,1)S(1)} %rolled.7.refs_0_), channel_id=1, source_target_pairs={{0,1},{1,0},{2,3},{3,2},{4,5},{5,4},{6,7},{7,6},{8,9},{9,8},{10,11... | collective-permute-start | bytes 3145736 | tf_op jit(solution)/shard_map/ppermute | solution.py:55
  156.1 13.8 %collective-permute-start.42 = (bf16[4,256,512]{2,1,0:T(8,128)(2,1)S(1)}, bf16[4,256,512]{2,1,0:T(8,128)(2,1)S(1)}, u32[]{:S(2)}, u32[]{:S(2)}) collective-permute-start(bf16[4,256,512]{2,1,0:T(8,128)(2,1)S(1)} %collective-permute-done.39.refs_1_), channel_id=1, source_target_pairs={{0,1},{1,0},{2,3},{3,2},{4,5},{5,4},{6,7},{7,6},{8,9},{9,8},{10,11... | collective-permute-start | bytes 3145736 | tf_op jit(solution)/shard_map/ppermute | solution.py:55
  156.2 23.6 %collective-permute-start.40 = (bf16[4,256,512]{2,1,0:T(8,128)(2,1)S(1)}, bf16[4,256,512]{2,1,0:T(8,128)(2,1)S(1)}, u32[]{:S(2)}, u32[]{:S(2)}) collective-permute-start(bf16[4,256,512]{2,1,0:T(8,128)(2,1)S(1)} %rolled.7.refs_0_), channel_id=1, source_target_pairs={{0,4},{1,3},{2,6},{3,1},{4,0},{5,7},{6,2},{7,5},{8,12},{9,11},{10,... | collective-permute-start | bytes 3145736 | tf_op jit(solution)/shard_map/ppermute | solution.py:48
  157.0 24.4 %collective-permute-start.43 = (bf16[4,256,512]{2,1,0:T(8,128)(2,1)S(1)}, bf16[4,256,512]{2,1,0:T(8,128)(2,1)}, u32[]{:S(2)}, u32[]{:S(2)}) collective-permute-start(bf16[4,256,512]{2,1,0:T(8,128)(2,1)S(1)} %collective-permute-done.39.refs_1_), channel_id=1, source_target_pairs={{0,4},{1,3},{2,6},{3,1},{4,0},{5,7},{6,2},{7,5},{8,12},{9,11},{10,... | collective-permute-start | bytes 3145736 | tf_op jit(solution)/shard_map/ppermute | solution.py:48
  186.8 16.0 %collective-permute-start.46 = (bf16[4,4,256,512]{3,2,1,0:T(8,128)(2,1)}, bf16[4,4,256,512]{3,2,1,0:T(8,128)(2,1)}, u32[]{:S(2)}, u32[]{:S(2)}) collective-permute-start(bf16[4,4,256,512]{3,2,1,0:T(8,128)(2,1)} %wide_chunks.2), channel_id=1, source_target_pairs={{0,1},{1,0},{2,3},{3,2},{4,5},{5,4},{6,7},{7,6},{8,9},{9,8},{10,11... | collective-permute-start | bytes 12582920 | tf_op jit(solution)/shard_map/ppermute | solution.py:55
  223.7 18.2 %collective-permute-start.47 = (bf16[4,4,64,2048]{3,2,1,0:T(8,128)(2,1)}, bf16[4,4,64,2048]{3,2,1,0:T(8,128)(2,1)}, u32[]{:S(2)}, u32[]{:S(2)}) collective-permute-start(bf16[4,4,64,2048]{3,2,1,0:T(8,128)(2,1)} %row_chunks.2), channel_id=1, source_target_pairs={{0,1},{1,0},{2,3},{3,2},{4,5},{5,4},{6,7},{7,6},{8,9},{9,8},{10,11... | collective-permute-start | bytes 12582920 | tf_op jit(solution)/shard_map/ppermute | solution.py:55
  224.1 17.9 %collective-permute-start.48 = (bf16[4,256,512]{2,1,0:T(8,128)(2,1)S(1)}, bf16[4,256,512]{2,1,0:T(8,128)(2,1)S(1)}, u32[]{:S(2)}, u32[]{:S(2)}) collective-permute-start(bf16[4,256,512]{2,1,0:T(8,128)(2,1)S(1)} %copy-done.126), channel_id=1, source_target_pairs={{0,4},{1,3},{2,6},{3,1},{4,0},{5,7},{6,2},{7,5},{8,12},{9,11},{10,... | collective-permute-start | bytes 3145736 | tf_op jit(solution)/shard_map/ppermute | solution.py:48
  225.0 36.8 %collective-permute-start.50 = (bf16[4,256,512]{2,1,0:T(8,128)(2,1)}, bf16[4,256,512]{2,1,0:T(8,128)(2,1)}, u32[]{:S(2)}, u32[]{:S(2)}) collective-permute-start(bf16[4,256,512]{2,1,0:T(8,128)(2,1)} %get-tuple-element.393), channel_id=1, source_target_pairs={{0,4},{1,3},{2,6},{3,1},{4,0},{5,7},{6,2},{7,5},{8,12},{9,11},{10,... | collective-permute-start | bytes 3145736 | tf_op jit(solution)/shard_map/ppermute | solution.py:48
  243.3 18.5 %collective-permute-start.49 = (bf16[4,256,512]{2,1,0:T(8,128)(2,1)}, bf16[4,256,512]{2,1,0:T(8,128)(2,1)}, u32[]{:S(2)}, u32[]{:S(2)}) collective-permute-start(bf16[4,256,512]{2,1,0:T(8,128)(2,1)} %add_convert_fusion.3), channel_id=1, source_target_pairs={{0,2},{1,5},{2,0},{3,7},{4,6},{5,1},{6,4},{7,3},{8,10},{9,13},{10,... | collective-permute-start | bytes 3145736 | tf_op jit(solution)/shard_map/ppermute | solution.py:48
  261.8 18.5 %collective-permute-start.52 = (bf16[4,64,2048]{2,1,0:T(8,128)(2,1)S(1)}, bf16[4,64,2048]{2,1,0:T(8,128)(2,1)S(1)}, u32[]{:S(2)}, u32[]{:S(2)}) collective-permute-start(bf16[4,64,2048]{2,1,0:T(8,128)(2,1)S(1)} %copy-done.125), channel_id=1, source_target_pairs={{0,4},{1,3},{2,6},{3,1},{4,0},{5,7},{6,2},{7,5},{8,12},{9,11},{10,... | collective-permute-start | bytes 3145736 | tf_op jit(solution)/shard_map/ppermute | solution.py:48
  265.8 14.4 %collective-permute-start.51 = (bf16[256,512]{1,0:T(8,128)(2,1)S(1)}, bf16[256,512]{1,0:T(8,128)(2,1)S(1)}, u32[]{:S(2)}, u32[]{:S(2)}) collective-permute-start(bf16[256,512]{1,0:T(8,128)(2,1)S(1)} %get-tuple-element.530), channel_id=1, source_target_pairs={{0,16},{1,17},{2,18},{3,19},{4,20},{5,21},{6,22},{7,23},{8,24},{9,... | collective-permute-start | bytes 786440 | tf_op jit(solution)/shard_map/ppermute | solution.py:48
  280.7 14.0 %collective-permute-start.53 = (bf16[4,64,2048]{2,1,0:T(8,128)(2,1)S(1)}, bf16[4,64,2048]{2,1,0:T(8,128)(2,1)S(1)}, u32[]{:S(2)}, u32[]{:S(2)}) collective-permute-start(bf16[4,64,2048]{2,1,0:T(8,128)(2,1)S(1)} %add_convert_fusion.1), channel_id=1, source_target_pairs={{0,2},{1,5},{2,0},{3,7},{4,6},{5,1},{6,4},{7,3},{8,10},{9,13},{10,... | collective-permute-start | bytes 3145736 | tf_op jit(solution)/shard_map/ppermute | solution.py:48
  301.0 16.8 %collective-permute-start.54 = (bf16[4,4,64,1280]{3,2,1,0:T(8,128)(2,1)}, bf16[4,4,64,1280]{3,2,1,0:T(8,128)(2,1)S(1)}, u32[]{:S(2)}, u32[]{:S(2)}) collective-permute-start(bf16[4,4,64,1280]{3,2,1,0:T(8,128)(2,1)} %heads_chunks.4), channel_id=1, source_target_pairs={{0,1},{1,0},{2,3},{3,2},{4,5},{5,4},{6,7},{7,6},{8,9},{9,8},{10,11... | collective-permute-start | bytes 7864328 | tf_op jit(solution)/shard_map/ppermute | solution.py:55
  302.3 14.7 %collective-permute-start.56 = (bf16[256,512]{1,0:T(8,128)(2,1)S(1)}, bf16[256,512]{1,0:T(8,128)(2,1)S(1)}, u32[]{:S(2)}, u32[]{:S(2)}) collective-permute-start(bf16[256,512]{1,0:T(8,128)(2,1)S(1)} %get-tuple-element.414), channel_id=1, source_target_pairs={{0,16},{1,17},{2,18},{3,19},{4,20},{5,21},{6,22},{7,23},{8,24},{9,... | collective-permute-start | bytes 786440 | tf_op jit(solution)/shard_map/ppermute | solution.py:48
  302.5 14.5 %collective-permute-start.55 = (bf16[4,64,2048]{2,1,0:T(8,128)(2,1)S(1)}, bf16[4,64,2048]{2,1,0:T(8,128)(2,1)S(1)}, u32[]{:S(2)}, u32[]{:S(2)}) collective-permute-start(bf16[4,64,2048]{2,1,0:T(8,128)(2,1)S(1)} %copy-done.124), channel_id=1, source_target_pairs={{0,4},{1,3},{2,6},{3,1},{4,0},{5,7},{6,2},{7,5},{8,12},{9,11},{10,... | collective-permute-start | bytes 3145736 | tf_op jit(solution)/shard_map/ppermute | solution.py:48
  303.0 14.0 %collective-permute-start.57 = (bf16[256,512]{1,0:T(8,128)(2,1)S(1)}, bf16[256,512]{1,0:T(8,128)(2,1)S(1)}, u32[]{:S(2)}, u32[]{:S(2)}) collective-permute-start(bf16[256,512]{1,0:T(8,128)(2,1)S(1)} %add_convert_fusion.13), channel_id=1, source_target_pairs={{0,8},{1,9},{2,10},{3,11},{4,12},{5,13},{6,14},{7,15},{8,0},{9,1},... | collective-permute-start | bytes 786440 | tf_op jit(solution)/shard_map/ppermute | solution.py:48
  327.9 18.3 %collective-permute-start.58 = (bf16[4,64,1280]{2,1,0:T(8,128)(2,1)S(1)}, bf16[4,64,1280]{2,1,0:T(8,128)(2,1)S(1)}, u32[]{:S(2)}, u32[]{:S(2)}) collective-permute-start(bf16[4,64,1280]{2,1,0:T(8,128)(2,1)S(1)} %get-tuple-element.431), channel_id=1, source_target_pairs={{0,4},{1,3},{2,6},{3,1},{4,0},{5,7},{6,2},{7,5},{8,12},{9,11},{10,... | collective-permute-start | bytes 1966088 | tf_op jit(solution)/shard_map/ppermute | solution.py:48
  328.6 17.6 %collective-permute-start.59 = (bf16[4,64,1280]{2,1,0:T(8,128)(2,1)S(1)}, bf16[4,64,1280]{2,1,0:T(8,128)(2,1)S(1)}, u32[]{:S(2)}, u32[]{:S(2)}) collective-permute-start(bf16[4,64,1280]{2,1,0:T(8,128)(2,1)S(1)} %get-tuple-element.432), channel_id=1, source_target_pairs={{0,4},{1,3},{2,6},{3,1},{4,0},{5,7},{6,2},{7,5},{8,12},{9,11},{10,... | collective-permute-start | bytes 1966088 | tf_op jit(solution)/shard_map/ppermute | solution.py:48
  331.0 15.1 %collective-permute-start.60 = (bf16[64,2048]{1,0:T(8,128)(2,1)S(1)}, bf16[64,2048]{1,0:T(8,128)(2,1)S(1)}, u32[]{:S(2)}, u32[]{:S(2)}) collective-permute-start(bf16[64,2048]{1,0:T(8,128)(2,1)S(1)} %get-tuple-element.526), channel_id=1, source_target_pairs={{0,16},{1,17},{2,18},{3,19},{4,20},{5,21},{6,22},{7,23},{8,24},{9,... | collective-permute-start | bytes 786440 | tf_op jit(solution)/shard_map/ppermute | solution.py:48
  332.8 13.4 %collective-permute-start.61 = (bf16[256,512]{1,0:T(8,128)(2,1)S(1)}, bf16[256,512]{1,0:T(8,128)(2,1)S(1)}, u32[]{:S(2)}, u32[]{:S(2)}) collective-permute-start(bf16[256,512]{1,0:T(8,128)(2,1)S(1)} %get-tuple-element.516), channel_id=1, source_target_pairs={{0,1},{1,0},{2,3},{3,2},{4,5},{5,4},{6,7},{7,6},{8,9},{9,8},{10,11... | collective-permute-start | bytes 786440 | tf_op jit(solution)/shard_map/ppermute | solution.py:55
  349.9 10.2 %collective-permute-start.62 = (bf16[4,4,64,768]{3,2,1,0:T(8,128)(2,1)}, bf16[4,4,64,768]{3,2,1,0:T(8,128)(2,1)}, u32[]{:S(2)}, u32[]{:S(2)}) collective-permute-start(bf16[4,4,64,768]{3,2,1,0:T(8,128)(2,1)} %heads_chunks.6), channel_id=1, source_target_pairs={{0,1},{1,0},{2,3},{3,2},{4,5},{5,4},{6,7},{7,6},{8,9},{9,8},{10,11... | collective-permute-start | bytes 4718600 | tf_op jit(solution)/shard_map/ppermute | solution.py:55
  354.7 21.6 %collective-permute-start.65 = (bf16[4,64,1280]{2,1,0:T(8,128)(2,1)}, bf16[4,64,1280]{2,1,0:T(8,128)(2,1)}, u32[]{:S(2)}, u32[]{:S(2)}) collective-permute-start(bf16[4,64,1280]{2,1,0:T(8,128)(2,1)} %add_convert_fusion.5), channel_id=1, source_target_pairs={{0,2},{1,5},{2,0},{3,7},{4,6},{5,1},{6,4},{7,3},{8,10},{9,13},{10,... | collective-permute-start | bytes 1966088 | tf_op jit(solution)/shard_map/ppermute | solution.py:48
  355.1 21.2 %collective-permute-start.66 = (bf16[64,2048]{1,0:T(8,128)(2,1)S(1)}, bf16[64,2048]{1,0:T(8,128)(2,1)}, u32[]{:S(2)}, u32[]{:S(2)}) collective-permute-start(bf16[64,2048]{1,0:T(8,128)(2,1)S(1)} %copy-done.109), channel_id=1, source_target_pairs={{0,16},{1,17},{2,18},{3,19},{4,20},{5,21},{6,22},{7,23},{8,24},{9,... | collective-permute-start | bytes 786440 | tf_op jit(solution)/shard_map/ppermute | solution.py:48
  357.2 19.1 %collective-permute-start.67 = (bf16[64,2048]{1,0:T(8,128)(2,1)}, bf16[64,2048]{1,0:T(8,128)(2,1)}, u32[]{:S(2)}, u32[]{:S(2)}) collective-permute-start(bf16[64,2048]{1,0:T(8,128)(2,1)} %add_convert_fusion.11), channel_id=1, source_target_pairs={{0,8},{1,9},{2,10},{3,11},{4,12},{5,13},{6,14},{7,15},{8,0},{9,1},... | collective-permute-start | bytes 786440 | tf_op jit(solution)/shard_map/ppermute | solution.py:48
  361.7 14.6 %collective-permute-start.63 = (bf16[4,64,768]{2,1,0:T(8,128)(2,1)S(1)}, bf16[4,64,768]{2,1,0:T(8,128)(2,1)S(1)}, u32[]{:S(2)}, u32[]{:S(2)}) collective-permute-start(bf16[4,64,768]{2,1,0:T(8,128)(2,1)S(1)} %add_convert_fusion.9), channel_id=1, source_target_pairs={{0,4},{1,3},{2,6},{3,1},{4,0},{5,7},{6,2},{7,5},{8,12},{9,11},{10,... | collective-permute-start | bytes 1179656 | tf_op jit(solution)/shard_map/ppermute | solution.py:48
  362.9 13.4 %collective-permute-start.64 = (bf16[4,64,768]{2,1,0:T(8,128)(2,1)S(1)}, bf16[4,64,768]{2,1,0:T(8,128)(2,1)S(1)}, u32[]{:S(2)}, u32[]{:S(2)}) collective-permute-start(bf16[4,64,768]{2,1,0:T(8,128)(2,1)S(1)} %add_convert_fusion.8), channel_id=1, source_target_pairs={{0,4},{1,3},{2,6},{3,1},{4,0},{5,7},{6,2},{7,5},{8,12},{9,11},{10,... | collective-permute-start | bytes 1179656 | tf_op jit(solution)/shard_map/ppermute | solution.py:48
  376.5 19.7 %collective-permute-start.68 = (bf16[4,64,768]{2,1,0:T(8,128)(2,1)S(1)}, bf16[4,64,768]{2,1,0:T(8,128)(2,1)S(1)}, u32[]{:S(2)}, u32[]{:S(2)}) collective-permute-start(bf16[4,64,768]{2,1,0:T(8,128)(2,1)S(1)} %add_convert_fusion.7), channel_id=1, source_target_pairs={{0,2},{1,5},{2,0},{3,7},{4,6},{5,1},{6,4},{7,3},{8,10},{9,13},{10,... | collective-permute-start | bytes 1179656 | tf_op jit(solution)/shard_map/ppermute | solution.py:48
  377.8 18.4 %collective-permute-start.72 = (bf16[512,1024]{1,0:T(8,128)(2,1)}, bf16[512,1024]{1,0:T(8,128)(2,1)S(1)}, u32[]{:S(2)}, u32[]{:S(2)}) collective-permute-start(bf16[512,1024]{1,0:T(8,128)(2,1)} %get-tuple-element.478), channel_id=1, source_target_pairs={{0,1},{1,0},{2,3},{3,2},{4,5},{5,4},{6,7},{7,6},{8,9},{9,8},{10,11... | collective-permute-start | bytes 3145736 | tf_op jit(solution)/shard_map/ppermute | solution.py:55
  381.0 15.2 %collective-permute-start.69 = (bf16[64,1280]{1,0:T(8,128)(2,1)S(1)}, bf16[64,1280]{1,0:T(8,128)(2,1)S(1)}, u32[]{:S(2)}, u32[]{:S(2)}) collective-permute-start(bf16[64,1280]{1,0:T(8,128)(2,1)S(1)} %get-tuple-element.534), channel_id=1, source_target_pairs={{0,16},{1,17},{2,18},{3,19},{4,20},{5,21},{6,22},{7,23},{8,24},{9,... | collective-permute-start | bytes 491528 | tf_op jit(solution)/shard_map/ppermute | solution.py:48
  384.4 11.0 %collective-permute-start.70 = (bf16[64,2048]{1,0:T(8,128)(2,1)S(1)}, bf16[64,2048]{1,0:T(8,128)(2,1)S(1)}, u32[]{:S(2)}, u32[]{:S(2)}) collective-permute-start(bf16[64,2048]{1,0:T(8,128)(2,1)S(1)} %get-tuple-element.518), channel_id=1, source_target_pairs={{0,1},{1,0},{2,3},{3,2},{4,5},{5,4},{6,7},{7,6},{8,9},{9,8},{10,11... | collective-permute-start | bytes 786440 | tf_op jit(solution)/shard_map/ppermute | solution.py:55
  384.8 11.5 %collective-permute-start.71 = (f32[8,1024]{1,0:T(8,128)S(1)}, f32[8,1024]{1,0:T(8,128)S(1)}, u32[]{:S(2)}, u32[]{:S(2)}) collective-permute-start(f32[8,1024]{1,0:T(8,128)S(1)} %sums.1), channel_id=1, source_target_pairs={{0,16},{1,17},{2,18},{3,19},{4,20},{5,21},{6,22},{7,23},{8,24},{9,... | collective-permute-start | bytes 98312 | tf_op jit(solution)/shard_map/ppermute | solution.py:906
  396.3 15.4 %collective-permute-start.73 = (bf16[512,1024]{1,0:T(8,128)(2,1)}, bf16[512,1024]{1,0:T(8,128)(2,1)S(1)}, u32[]{:S(2)}, u32[]{:S(2)}) collective-permute-start(bf16[512,1024]{1,0:T(8,128)(2,1)} %down.2), channel_id=1, source_target_pairs={{0,1},{1,0},{2,3},{3,2},{4,5},{5,4},{6,7},{7,6},{8,9},{9,8},{10,11... | collective-permute-start | bytes 3145736 | tf_op jit(solution)/shard_map/ppermute | solution.py:55
  397.1 13.6 %collective-permute-start.74 = (bf16[64,768]{1,0:T(8,128)(2,1)S(1)}, bf16[64,768]{1,0:T(8,128)(2,1)S(1)}, u32[]{:S(2)}, u32[]{:S(2)}) collective-permute-start(bf16[64,768]{1,0:T(8,128)(2,1)S(1)} %get-tuple-element.542), channel_id=1, source_target_pairs={{0,16},{1,17},{2,18},{3,19},{4,20},{5,21},{6,22},{7,23},{8,24},{9,... | collective-permute-start | bytes 294920 | tf_op jit(solution)/shard_map/ppermute | solution.py:48
  398.5 13.1 %collective-permute-start.75 = (bf16[64,1280]{1,0:T(8,128)(2,1)S(1)}, bf16[64,1280]{1,0:T(8,128)(2,1)S(1)}, u32[]{:S(2)}, u32[]{:S(2)}) collective-permute-start(bf16[64,1280]{1,0:T(8,128)(2,1)S(1)} %get-tuple-element.488), channel_id=1, source_target_pairs={{0,16},{1,17},{2,18},{3,19},{4,20},{5,21},{6,22},{7,23},{8,24},{9,... | collective-permute-start | bytes 491528 | tf_op jit(solution)/shard_map/ppermute | solution.py:48
  399.5 12.1 %collective-permute-start.76 = (bf16[64,1280]{1,0:T(8,128)(2,1)S(1)}, bf16[64,1280]{1,0:T(8,128)(2,1)S(1)}, u32[]{:S(2)}, u32[]{:S(2)}) collective-permute-start(bf16[64,1280]{1,0:T(8,128)(2,1)S(1)} %add_convert_fusion.15), channel_id=1, source_target_pairs={{0,8},{1,9},{2,10},{3,11},{4,12},{5,13},{6,14},{7,15},{8,0},{9,1},... | collective-permute-start | bytes 491528 | tf_op jit(solution)/shard_map/ppermute | solution.py:48
  400.5 10.1 %collective-permute-start.77 = (f32[8,2048]{1,0:T(8,128)S(1)}, f32[8,2048]{1,0:T(8,128)S(1)}, u32[]{:S(2)}, u32[]{:S(2)}) collective-permute-start(f32[8,2048]{1,0:T(8,128)S(1)} %constant_dynamic-update-slice_fusion), channel_id=1, source_target_pairs={{0,8},{1,9},{2,10},{3,11},{4,12},{5,13},{6,14},{7,15},{8,0},{9,1},... | collective-permute-start | bytes 196616 | tf_op jit(solution)/shard_map/ppermute | solution.py:906
  411.7 11.1 %collective-permute-start.78 = (f32[8,4096]{1,0:T(8,128)S(1)}, f32[8,4096]{1,0:T(8,128)S(1)}, u32[]{:S(2)}, u32[]{:S(2)}) collective-permute-start(f32[8,4096]{1,0:T(8,128)S(1)} %constant_dynamic-update-slice_fusion.2), channel_id=1, source_target_pairs={{0,2},{1,3},{2,0},{3,1},{4,6},{5,7},{6,4},{7,5},{8,10},{9,11},{10,... | collective-permute-start | bytes 393224 | tf_op jit(solution)/shard_map/ppermute | solution.py:906
  412.7 10.0 %collective-permute-start.79 = (f32[8,4096]{1,0:T(8,128)S(1)}, f32[8,4096]{1,0:T(8,128)S(1)}, u32[]{:S(2)}, u32[]{:S(2)}) collective-permute-start(f32[8,4096]{1,0:T(8,128)S(1)} %constant_dynamic-update-slice_fusion.2), channel_id=1, source_target_pairs={{0,4},{1,5},{2,6},{3,7},{4,0},{5,1},{6,2},{7,3},{8,12},{9,13},{10,... | collective-permute-start | bytes 393224 | tf_op jit(solution)/shard_map/ppermute | solution.py:906
  413.0 9.7 %collective-permute-start.80 = (f32[8,4096]{1,0:T(8,128)S(1)}, f32[8,4096]{1,0:T(8,128)S(1)}, u32[]{:S(2)}, u32[]{:S(2)}) collective-permute-start(f32[8,4096]{1,0:T(8,128)S(1)} %constant_dynamic-update-slice_fusion.2), channel_id=1, source_target_pairs={{0,6},{1,7},{2,4},{3,5},{4,2},{5,3},{6,0},{7,1},{8,14},{9,15},{10,... | collective-permute-start | bytes 393224 | tf_op jit(solution)/shard_map/ppermute | solution.py:906
  (155 other events, 1630.1 us)

commit v6 on v5

--- a/solution.py
+++ b/solution.py
@@ -22,7 +22,7 @@
 VMEM_LIMIT = 58 << 20
 ROOM = 14 << 20
 ANY = pl.BlockSpec(memory_space=pltpu.HBM)
-TIGHT = ("qkv", "attend", "attend_back", "heads_chunks", "heads_back", "rolled", "out", "to_blocks", "heads_grads", "sums", "last_sums")
+TIGHT = ("qkv", "attend", "attend_back", "heads_chunks", "heads_back", "rolled", "out", "to_blocks", "heads_grads", "sums", "last_sums", "halves_joined")
 
 
 class Grid:
@@ -632,16 +632,17 @@
 def spread(place, result, outs, came, kept, lead=0):
     size = result.shape[-1]
     to = slice(lead, lead + size)
-    chunks = len(outs) if kept else outs[0].shape[0]
+    joined = len(outs) == 1
+    chunks = outs[0].shape[0] if joined else len(outs)
     for i in range(chunks):
         at = 3 * (i if kept else chunks + i)
         part = result[:, place[at], place[at + 1]]
         if came is not None:
             part = part + came[i, :, :, to].astype(F32)
-        if kept:
+        if joined:
+            outs[0][i, :, :, to] = part.astype(BF16)
+        else:
             outs[i][:, :, to] = part.astype(BF16)
-        else:
-            outs[0][i, :, :, to] = part.astype(BF16)
 
 
 def chunk_outputs(grid, kept, part, full, block, index):
@@ -701,12 +702,12 @@
         spread(place, last, refs, came, kept, result.shape[-1])
 
 
-def heads_chunks(grid, places, kept, a, halves, mixed=(), grad=None, came=None):
+def heads_chunks(grid, places, kept, a, halves, mixed=(), grad=None, came=None, joined=False):
     width, rows = a.shape
     block, more = halves[0].shape[1], len(mixed)
     part = width // grid.groups
     full = block + (width // 2 if more else 0)
-    outs, shapes = chunk_outputs(grid, kept, part, full, full, lambda j, place: 0)
+    outs, shapes = chunk_outputs(grid, kept and not joined, part, full, full, lambda j, place: 0)
     level = (grid.n0, grid.n, grid.n, part)
     scratch = [pltpu.VMEM(level + (block,), F32)]
     extra = [] if came is None else [came]
@@ -831,7 +832,7 @@
 class Push:
     def __init__(self, grid, line, sent):
         self.grid, self.line = grid, line
-        self.came, self.second_in, self.first_in = grid.swap(sent), {}, []
+        self.came, self.second_in, self.first_in, self.kept = grid.swap(sent), {}, [], None
 
     def keep(self, chunks, fused):
         self.terms = [[v] if fused else [v, self.came[i]] for i, v in enumerate(chunks)]
@@ -854,9 +855,28 @@
             self.first_in.append(self.grid.shift(plus(*terms).astype(BF16), 1, -k))
         return self.first_in
 
+    def second_joined(self):
+        n = self.grid.n
+        kept, came = self.line.at(self.kept, self.came)
+        values = [plus(v[0], v[1]) for v in ((kept[k * n : (k + 1) * n], came[k * n : (k + 1) * n]) for k in range(1, n))]
+        self.seconds = [self.grid.shift(v.astype(BF16), 2, -k - 1) for k, v in enumerate(values)]
+        return self.seconds
+
+    def first_joined(self):
+        kept, came, seconds = self.line.at(self.kept, self.came, self.seconds)
+        for k in range(1, self.grid.n):
+            value = plus(kept[k], came[k], *[v[k] for v in seconds]).astype(BF16)
+            self.first_in.append(self.grid.shift(value, 1, -k))
+        return self.first_in
+
     def outer(self):
-        seconds = [self.second_in[k, 0] for k in range(1, self.grid.n)]
-        total = plus(*self.line.at(self.terms[0] + seconds + self.first_in)).astype(BF16)
+        if self.kept is None:
+            seconds = [self.second_in[k, 0] for k in range(1, self.grid.n)]
+            terms = self.line.at(self.terms[0] + seconds + self.first_in)
+        else:
+            kept, came, seconds, firsts = self.line.at(self.kept, self.came, self.seconds, self.first_in)
+            terms = [kept[0], came[0]] + [v[0] for v in seconds] + list(firsts)
+        total = plus(*terms).astype(BF16)
         z = self.grid.coords(lax.axis_index("dp"))[0]
         size = self.grid.n0 // 2
         total = total.reshape((2, size) + total.shape[1:])
@@ -884,10 +904,6 @@
         self.other = self.grid.swap(self.own)
         return self.other
 
-    def result(self, core, lead=0, width=None):
-        own, other = [v.astype(F32)[:, lead : None if width is None else lead + width] for v in (self.own, self.other)]
-        return jnp.where(core == 0, jnp.concatenate([own, other], axis=1), jnp.concatenate([other, own], axis=1))
-
 
 def rank_groups(grid):
     return [[b for b in range(grid.blocks) if b % 2 == c] for c in range(2)]
@@ -940,6 +956,28 @@
         [spec((1,) + mine.shape, lambda j, place: (jnp.where(j == 0, place[2], 1 - place[2]), 0, 0))],
         [(shape, mine.dtype)], [], 0, 4 * math.prod(shape), prefetch=1,
     )(places, mine, theirs)[0]
+
+
+def halves_joined_kernel(place, own, other, out):
+    width = own.shape[1]
+    for half in range(2):
+        to = slice(half * width, (half + 1) * width)
+
+        @pl.when(place[2] == half)
+        def _():
+            out[:, to] = own[...].astype(F32)
+
+        @pl.when(place[2] != half)
+        def _():
+            out[:, to] = other[...].astype(F32)
+
+
+def halves_joined(places, own, other):
+    shape = (own.shape[0], 2 * own.shape[1])
+    return call(
+        halves_joined_kernel, "halves_joined", (1,), [SCALARS, whole(own.shape), whole(own.shape)],
+        [whole(shape)], [(shape, F32)], [], 0, 6 * math.prod(shape),
+    )(places, own, other)[0]
 
 
 def heads_grads_kernel(place, *refs):
@@ -1268,10 +1306,10 @@
     line.mark(sent)
 
     push_b = Push(grid, line, line.at(sent))
-    kept = push_b.keep(heads_chunks(grid, at, True, *line.at(normed1_t, (back_b0, back_b1))), False)
-    line.mark(kept, push_b.came)
-
-    last = push_b.second(True) + push_b.second(False)
+    (push_b.kept,) = heads_chunks(grid, at, True, *line.at(normed1_t, (back_b0, back_b1)), joined=True)
+    line.mark(push_b.kept, push_b.came)
+
+    last = push_b.second_joined()
     grads = line.at((back_a0, back_a1, back_b0, back_b1))
     grad_x, grad_x_theirs, sums1 = norm_back(
         grid, at, grads, x, eff1, grad_middle, (heads_a.weight(), heads_b.weight(0, group_width)), group_width, 2
@@ -1285,7 +1323,7 @@
     )(line.at(sums1), sums2, gain1, gain2, scale1, scale2, my_time.astype(F32)[None])[0]
     bits = [grid.chunks << i for i in reversed(range((grid.n0 - 1).bit_length()))]
     far = doubled(grid, every, bits[0])
-    last = push_b.first()
+    last = push_b.first_joined()
     heads = push_a.outer()
     up = push_up.own_half()
     grad_x_theirs = grid.swap(line.at(grad_x_theirs))
@@ -1297,7 +1335,7 @@
     last = push_b.outer()
     heads = push_a.outer_rest()
     out_theirs = grid.swap(line.at(out_theirs))
-    grad_up, grad_down = push_up.result(core), push_down.result(core)
+    grad_up, grad_down = [halves_joined(at, *line.at(p.own, p.other)) for p in (push_up, push_down)]
     out_mine = down_product(grid, at, 0, *line.at(active, middle), down_w.weight())
     line.mark(out_mine, last, heads, far, out_theirs)
 

time: 437 us -> 443 us (1.014)
  local copies, waits for them, and re-layouts: 23 us -> 28.2 us
    unnamed x272 -> x254, local copies, waits for them, and re-layouts: 12.1 us -> 18.1 us
    pallas_call x34 -> x36, Pallas kernels: 227 us -> 230 us  [run(): kernel_call(kernel, name, grid, ins, outs, shapes, scratch, flops, moved,...]
    ppermute x48 -> x47, waiting for transfers between devices: 20.9 us -> 22.2 us  [shift(): return lax.ppermute(v, AXES, pairs)]
    convert_element_type x10 -> x6, other arithmetic: 9.18 us -> 10.1 us  [the longest x4 6.87 us: outer(): total = plus(*terms).astype(BF16)]
    ppermute x48 -> x47, starting transfers between devices: 46.7 us -> 47.1 us  [shift(): return lax.ppermute(v, AXES, pairs)]
  transfers between devices with their start and end apart: 86 -> 85, of which waited for: 23 -> 25; matrix products, arithmetic and copies ran while one was open for 8% -> 7% of each run, Pallas kernels for 49% -> 49%
where the time goes in v6:
time: 443 us; the launch traced here: 436 us
  Pallas kernels  254 us (57%)
  starting transfers between devices  81.3 us (18%)
  waiting for transfers between devices  45.6 us (10%)
  local copies, waits for them, and re-layouts  28.2 us (6%)
  other arithmetic  23.1 us (5%)
    pallas_call x36, Pallas kernels, run(): kernel_call(kernel, name, grid, ins, outs, shapes, scratch, flops, moved,...  230 us
    ppermute x47, starting transfers between devices, shift(): return lax.ppermute(v, AXES, pairs)  47.1 us
    pallas_call x2, Pallas kernels, up_product(): pl.pallas_call(kernel, grid=(per,), in_specs=[SCALARS, whole(normed.shape...  24.6 us
    ppermute x47, waiting for transfers between devices, shift(): return lax.ppermute(v, AXES, pairs)  22.2 us
    ppermute x28, starting transfers between devices, swap(): return lax.ppermute(v, AXES, pairs)  21.5 us
    unnamed x254, local copies, waits for them, and re-layouts  18.1 us
    ppermute x9, waiting for transfers between devices, doubled(): return lax.ppermute(v, AXES, pairs)  13.8 us
    ppermute x28, waiting for transfers between devices, swap(): return lax.ppermute(v, AXES, pairs)  9.65 us
  transfers between devices with their start and end apart: 85, of which 25 were waited for; matrix products, arithmetic and copies ran while one was open for 7% of the time, Pallas kernels for 49%

profile of v6, /device:TPU:1, one launch (start us, length us, event | category | flops | bytes accessed | tf_op | source)
XLA Modules:
  0.0 436.3 jit_solution(16347690727715031845)
XLA Ops:
  1.8 4.2 collective-permute-start.1
  9.1 2.3 collective-permute-start.4
  12.8 3.1 collective-permute-done.4
  18.0 2.8 pad_maximum_fusion.refs_0_.x.x_far
  23.4 3.9 collective-permute-start.12
  34.5 6.6 %collective-permute-done.8 = bf16[4,8,2176]{2,1,0:T(8,128)(2,1)S(1)} collective-permute-done((bf16[4,8,2176]{2,1,0:T(8,128)(2,1)S(1)}, bf16[4,8,2176]{2,1,0:T(8,128)(2,1)S(1)}, u32[]{:S(2)}, u32[]{:S(2)}) %collective-permute-start.8) | collective-permute-done | bytes 139296 | tf_op jit(solution)/shard_map/ppermute | solution.py:922
  46.0 3.0 collective-permute-done.13
  49.1 2.1 collective-permute-done.17.refs_3_
  54.3 1.9 collective-permute-start.19
  56.2 9.1 %qkv_first.1 = (bf16[1024,1024]{1,0:T(8,128)(2,1)}, bf16[1024,1024]{1,0:T(8,128)(2,1)}, bf16[1024,1536]{1,0:T(8,128)(2,1)}) custom-call(s32[24]{0:T(128)} %fusion.26.place, bf16[1024,1024]{1,0:T(8,128)(2,1)} %pad_maximum_fusion.refs_0_.x.x_far, f32[1,1024]{1,0:T(1,128)} %get-tuple-element.292.refs_1_.gain, f32[1,1024]{1,0:T(1,128)} %squeeze.122.refs_2_, ...), custom_call_target="tpu_custom_call" | custom-call | flops 3221225472 | bytes 12582912 | tf_op jit(solution)/shard_map/qkv_first/pallas_call | solution.py:106
  65.3 3.0 collective-permute-start.22
  70.2 1.9 copy-done.67
  72.1 5.7 %attend.4 = (bf16[1024,256]{1,0:T(8,128)(2,1)S(1)}, f32[1024,128]{1,0:T(8,128)S(1)}) custom-call(bf16[1024,1536]{1,0:T(8,128)(2,1)S(1)} %copy-done.67, bf16[1024,1536]{1,0:T(8,128)(2,1)S(1)} %copy-done.67, bf16[1024,1]{1,0:T(8,128)(2,1)S(1)} %copy.38.mask), custom_call_target="tpu_custom_call" | custom-call | flops 4294967296 | bytes 2097152 | tf_op jit(solution)/shard_map/attend/pallas_call | solution.py:106
  79.2 5.7 %attend.5 = (bf16[1024,256]{1,0:T(8,128)(2,1)S(1)}, f32[1024,128]{1,0:T(8,128)S(1)}) custom-call(bf16[1024,1536]{1,0:T(8,128)(2,1)S(1)} %copy-done.67, bf16[1024,1536]{1,0:T(8,128)(2,1)S(1)} %copy-done.67, bf16[1024,1]{1,0:T(8,128)(2,1)S(1)} %copy.38.mask), custom_call_target="tpu_custom_call" | custom-call | flops 4294967296 | bytes 2097152 | tf_op jit(solution)/shard_map/attend/pallas_call | solution.py:106
  86.1 2.0 collective-permute-start.26
  91.0 1.9 collective-permute-start.29
  92.8 5.2 %qkv.1.q.kv = bf16[1024,1536]{1,0:T(8,128)(2,1)S(1)} custom-call(s32[24]{0:T(128)S(1)} %copy-done.53, bf16[1024,1024]{1,0:T(8,128)(2,1)S(1)} %copy-done.66, f32[1024,128]{1,0:T(8,128)S(1)} %copy-done.44, f32[1024,128]{1,0:T(8,128)S(1)} %copy-done.46, bf16[4,64,1280]{2,1,0:T(8,128)(2,1)S(1)} %rolled.5.refs_3_.refs_0_.refs_8_, ...), custom_call_target="tpu_custom_call" | custom-call | flops 3221225472 | bytes 12582912 | tf_op jit(solution)/shard_map/qkv/pallas_call | solution.py:106
  98.2 2.9 collective-permute-start.31
  101.1 5.8 %attend.6 = (bf16[1024,256]{1,0:T(8,128)(2,1)S(1)}, f32[1024,128]{1,0:T(8,128)S(1)}) custom-call(bf16[1024,1536]{1,0:T(8,128)(2,1)S(1)} %qkv.1.q.kv, bf16[1024,1536]{1,0:T(8,128)(2,1)S(1)} %qkv.1.q.kv, bf16[1024,1]{1,0:T(8,128)(2,1)S(1)} %copy.38.mask), custom_call_target="tpu_custom_call" | custom-call | flops 4294967296 | bytes 2097152 | tf_op jit(solution)/shard_map/attend/pallas_call | solution.py:106
  108.5 2.8 collective-permute-start.32
  113.2 5.8 %attend.7 = (bf16[1024,256]{1,0:T(8,128)(2,1)S(1)}, f32[1024,128]{1,0:T(8,128)S(1)}) custom-call(bf16[1024,1536]{1,0:T(8,128)(2,1)S(1)} %qkv.1.q.kv, bf16[1024,1536]{1,0:T(8,128)(2,1)S(1)} %qkv.1.q.kv, bf16[1024,1]{1,0:T(8,128)(2,1)S(1)} %copy.38.mask), custom_call_target="tpu_custom_call" | custom-call | flops 4294967296 | bytes 2097152 | tf_op jit(solution)/shard_map/attend/pallas_call | solution.py:106
  121.0 8.2 %out.1 = (bf16[1024,1024]{1,0:T(8,128)(2,1)S(1)}, bf16[1024,1024]{1,0:T(8,128)(2,1)S(1)}, bf16[1024,1024]{1,0:T(8,128)(2,1)}) custom-call(s32[24]{0:T(128)S(1)} %copy-done.53, bf16[1024,1024]{1,0:T(8,128)(2,1)} %pad_maximum_fusion.refs_0_.x.x_far, f32[1,1024]{1,0:T(1,128)S(1)} %get-tuple-element.542.gain, f32[1,1024]{1,0:T(1,128)S(1)} %squeeze.120.bias, ...), custom_call_target="tpu_custom_call" | custom-call | flops 2147483648 | bytes 10485760 | tf_op jit(solution)/shard_map/out/pallas_call | solution.py:106
  130.6 5.9 %collective-permute-done.36.refs_3_ = bf16[4,64,2048]{2,1,0:T(8,128)(2,1)S(1)} collective-permute-done((bf16[4,64,2048]{2,1,0:T(8,128)(2,1)S(1)}, bf16[4,64,2048]{2,1,0:T(8,128)(2,1)S(1)}, u32[]{:S(2)}, u32[]{:S(2)}) %collective-permute-start.36) | collective-permute-done | bytes 1048608 | tf_op jit(solution)/shard_map/ppermute | solution.py:48
  137.9 2.2 collective-permute-done.37.refs_6_
  143.9 12.3 %up.2 = (bf16[1024,4096]{1,0:T(8,128)(2,1)}, bf16[1024,4096]{1,0:T(8,128)(2,1)}) custom-call(s32[24]{0:T(128)} %fusion.26.place, bf16[1024,1024]{1,0:T(8,128)(2,1)} %copy-done.41, bf16[4,64,2048]{2,1,0:T(8,128)(2,1)} %copy-done.25, bf16[4,64,2048]{2,1,0:T(8,128)(2,1)} %copy-done.82, bf16[4,64,2048]{2,1,0:T(8,128)(2,1)} %copy-done.85, ...), custom_call_target="tpu_custom_call" | custom-call | flops 4294967296 | bytes 12582912 | tf_op jit(solution)/shard_map/up/pallas_call | solution.py:449
  159.3 12.3 %up.3 = (bf16[1024,4096]{1,0:T(8,128)(2,1)}, bf16[1024,4096]{1,0:T(8,128)(2,1)}) custom-call(s32[24]{0:T(128)} %fusion.26.place, bf16[1024,1024]{1,0:T(8,128)(2,1)} %copy-done.41, bf16[4,64,2048]{2,1,0:T(8,128)(2,1)} %copy-done.25, bf16[4,64,2048]{2,1,0:T(8,128)(2,1)} %copy-done.82, ...), custom_call_target="tpu_custom_call", output_to_operand_aliasing={{0}: (10, {}), {1}: (11, {})} | custom-call | flops 4294967296 | bytes 12582912 | tf_op jit(solution)/shard_map/up/pallas_call | solution.py:449
  171.6 9.7 %wide_chunks.2 = bf16[4,4,256,512]{3,2,1,0:T(8,128)(2,1)} custom-call(s32[24]{0:T(128)} %fusion.26.place, bf16[1024,4096]{1,0:T(8,128)(2,1)} %get-tuple-element.471.refs_0_.refs_1_.refs_2_.refs_3_.active, bf16[1024,4096]{1,0:T(8,128)(2,1)} %get-tuple-element.471.refs_0_.refs_1_.refs_2_.refs_3_.active, ...), custom_call_target="tpu_custom_call" | custom-call | flops 4294967296 | bytes 14680064 | tf_op jit(solution)/shard_map/wide_chunks/pallas_call | solution.py:106
  181.3 1.8 collective-permute-done.43.refs_3_
  184.5 2.5 collective-permute-done.44.refs_6_
  189.4 14.9 %hidden_back.1.b.refs_8_ = bf16[1024,4096]{1,0:T(8,128)(2,1)} custom-call(s32[24]{0:T(128)} %fusion.26.place, bf16[1024,1024]{1,0:T(8,128)(2,1)} %pad_maximum_fusion.1.refs_4_.grad.base_far, bf16[1024,4096]{1,0:T(8,128)(2,1)} %get-tuple-element.365.slope, bf16[4,256,512]{2,1,0:T(8,128)(2,1)} %copy-done.5, bf16[4,256,512]{2,1,0:T(8,128)(2,1)} %copy-done.77, ...), custom_call_target="tpu_custom_call" | custom-call | flops 8589934592 | bytes 25165824 | tf_op jit(solution)/shard_map/hidden_back/pallas_call | solution.py:106
  204.4 11.4 %wide_chunks.3 = (bf16[4,256,512]{2,1,0:T(8,128)(2,1)}, bf16[4,256,512]{2,1,0:T(8,128)(2,1)}, bf16[4,256,512]{2,1,0:T(8,128)(2,1)}, bf16[4,256,512]{2,1,0:T(8,128)(2,1)}) custom-call(s32[24]{0:T(128)} %fusion.26.place, bf16[1024,4096]{1,0:T(8,128)(2,1)} %get-tuple-element.471.refs_0_.refs_1_.refs_2_.refs_3_.active, ...), custom_call_target="tpu_custom_call" | custom-call | flops 4294967296 | bytes 14680064 | tf_op jit(solution)/shard_map/wide_chunks/pallas_call | solution.py:106
  215.8 9.5 %row_chunks.2 = bf16[4,4,64,2048]{3,2,1,0:T(8,128)(2,1)} custom-call(s32[24]{0:T(128)} %fusion.26.place, bf16[1024,1024]{1,0:T(8,128)(2,1)} %get-tuple-element.381.a, bf16[1024,4096]{1,0:T(8,128)(2,1)} %hidden_back.1.b.refs_8_), custom_call_target="tpu_custom_call" | custom-call | flops 4294967296 | bytes 10485760 | tf_op jit(solution)/shard_map/row_chunks/pallas_call | solution.py:106
  227.2 16.4 %norm_back.2 = (bf16[1024,1024]{1,0:T(8,128)(2,1)}, f32[2,1024]{1,0:T(2,128)}) custom-call(s32[24]{0:T(128)} %fusion.26.place, f32[1,1024]{1,0:T(1,128)} %copy-done.60, bf16[1024,1024]{1,0:T(8,128)(2,1)} %copy-done.6, bf16[1024,1024]{1,0:T(8,128)(2,1)} %pad_maximum_fusion.1.refs_4_.grad.base_far, bf16[4,64,2048]{2,1,0:T(8,128)(2,1)} %copy-done.25, ...), custom_call_target="tpu_custom_call" | custom-call | flops 8589934592 | bytes 23068672 | tf_op jit(solution)/shard_map/norm_back/pallas_call | solution.py:106
  246.1 10.3 %row_chunks.3 = (bf16[4,64,2048]{2,1,0:T(8,128)(2,1)}, bf16[4,64,2048]{2,1,0:T(8,128)(2,1)}, bf16[4,64,2048]{2,1,0:T(8,128)(2,1)}, bf16[4,64,2048]{2,1,0:T(8,128)(2,1)}) custom-call(s32[24]{0:T(128)} %fusion.26.place, bf16[1024,1024]{1,0:T(8,128)(2,1)} %get-tuple-element.381.a, bf16[1024,4096]{1,0:T(8,128)(2,1)} %hidden_back.1.b.refs_8_, ...), custom_call_target="tpu_custom_call" | custom-call | flops 4294967296 | bytes 10485760 | tf_op jit(solution)/shard_map/row_chunks/pallas_call | solution.py:106
  260.8 4.3 heads_back.1.grad
  266.3 2.1 add_convert_fusion.2
  270.1 11.0 %attend_back.4.refs_0_.refs_16_ = bf16[1024,768]{1,0:T(8,128)(2,1)S(1)} custom-call(bf16[1024,1536]{1,0:T(8,128)(2,1)S(1)} %copy-done.68, bf16[1024,1536]{1,0:T(8,128)(2,1)S(1)} %copy-done.68, bf16[1024,256]{1,0:T(8,128)(2,1)S(1)} %get-tuple-element.419.refs_8_.mixed.refs_2_.refs_3_, bf16[1024,1024]{1,0:T(8,128)(2,1)S(1)} %heads_back.1.grad, ...), custom_call_target="tpu_custom_call" | custom-call | flops 10737418240 | bytes 4194304 | tf_op jit(solution)/shard_map/attend_back/pallas_call | solution.py:106
  281.1 2.6 collective-permute-done.51
  284.3 11.2 %attend_back.5.refs_1_.refs_17_ = bf16[1024,768]{1,0:T(8,128)(2,1)S(1)} custom-call(bf16[1024,1536]{1,0:T(8,128)(2,1)S(1)} %copy-done.68, bf16[1024,1536]{1,0:T(8,128)(2,1)S(1)} %copy-done.68, bf16[1024,256]{1,0:T(8,128)(2,1)S(1)} %copy-done.19, bf16[1024,1024]{1,0:T(8,128)(2,1)S(1)} %heads_back.1.grad, f32[1024,128]{1,0:T(8,128)S(1)} %copy-done.70, ...), custom_call_target="tpu_custom_call" | custom-call | flops 10737418240 | bytes 4194304 | tf_op jit(solution)/shard_map/attend_back/pallas_call | solution.py:106
  295.5 2.7 collective-permute-done.53
  299.2 6.2 %heads_chunks.4 = bf16[4,4,64,1280]{3,2,1,0:T(8,128)(2,1)} custom-call(s32[24]{0:T(128)S(1)} %copy-done.54, bf16[1024,1024]{1,0:T(8,128)(2,1)S(1)} %copy-done.2, bf16[1024,768]{1,0:T(8,128)(2,1)S(1)} %attend_back.4.refs_0_.refs_16_, bf16[1024,768]{1,0:T(8,128)(2,1)S(1)} %attend_back.5.refs_1_.refs_17_, bf16[1024,256]{1,0:T(8,128)(2,1)S(1)} %copy-done.17, ...), custom_call_target="tpu_custom_call" | custom-call | flops 2684354560 | bytes 7340032 | tf_op jit(solution)/shard_map/heads_chunks/pallas_call | solution.py:106
  308.9 11.1 %attend_back.6.refs_0_.refs_18_ = bf16[1024,768]{1,0:T(8,128)(2,1)S(1)} custom-call(bf16[1024,1536]{1,0:T(8,128)(2,1)S(1)} %copy-done.64, bf16[1024,1536]{1,0:T(8,128)(2,1)S(1)} %copy-done.64, bf16[1024,256]{1,0:T(8,128)(2,1)S(1)} %copy-done.23, bf16[1024,1024]{1,0:T(8,128)(2,1)S(1)} %heads_back.1.grad, f32[1024,128]{1,0:T(8,128)S(1)} %copy-done.76, ...), custom_call_target="tpu_custom_call" | custom-call | flops 10737418240 | bytes 4194304 | tf_op jit(solution)/shard_map/attend_back/pallas_call | solution.py:106
  321.4 8.6 %heads_chunks.5 = (bf16[4,64,1280]{2,1,0:T(8,128)(2,1)S(1)}, bf16[4,64,1280]{2,1,0:T(8,128)(2,1)S(1)}, bf16[4,64,1280]{2,1,0:T(8,128)(2,1)S(1)}, bf16[4,64,1280]{2,1,0:T(8,128)(2,1)S(1)}) custom-call(s32[24]{0:T(128)S(1)} %copy-done.54, bf16[1024,1024]{1,0:T(8,128)(2,1)} %get-tuple-element.440.a, bf16[1024,768]{1,0:T(8,128)(2,1)} %copy-done.7, ...), custom_call_target="tpu_custom_call" | custom-call | flops 2684354560 | bytes 7340032 | tf_op jit(solution)/shard_map/heads_chunks/pallas_call | solution.py:106
  331.6 1.9 add_convert_fusion
  334.5 1.7 collective-permute-start.60
  336.2 2.0 collective-permute-start.61
  338.3 11.4 %attend_back.7.refs_1_.refs_19_ = bf16[1024,768]{1,0:T(8,128)(2,1)S(1)} custom-call(bf16[1024,1536]{1,0:T(8,128)(2,1)S(1)} %copy-done.65, bf16[1024,1536]{1,0:T(8,128)(2,1)S(1)} %copy-done.65, bf16[1024,256]{1,0:T(8,128)(2,1)S(1)} %copy-done.21, bf16[1024,1024]{1,0:T(8,128)(2,1)S(1)} %copy-done.40, f32[1024,128]{1,0:T(8,128)S(1)} %copy-done.74, ...), custom_call_target="tpu_custom_call" | custom-call | flops 10737418240 | bytes 4194304 | tf_op jit(solution)/shard_map/attend_back/pallas_call | solution.py:106
  349.8 3.7 heads_chunks.6
  353.7 2.4 add_convert_fusion.6
  358.4 2.5 heads_chunks.7
  364.1 1.7 collective-permute-start.66
  365.8 12.9 %norm_back.3 = (bf16[512,1024]{1,0:T(8,128)(2,1)}, bf16[512,1024]{1,0:T(8,128)(2,1)}, f32[2,1024]{1,0:T(2,128)}) custom-call(s32[24]{0:T(128)} %fusion.26.place, f32[1,1024]{1,0:T(1,128)} %get-tuple-element.292.refs_1_.gain, bf16[1024,1024]{1,0:T(8,128)(2,1)} %pad_maximum_fusion.refs_0_.x.x_far, ...), custom_call_target="tpu_custom_call" | custom-call | flops 6442450944 | bytes 18874368 | tf_op jit(solution)/shard_map/norm_back/pallas_call | solution.py:106
  378.8 1.9 fusion.4
  384.7 1.8 collective-permute-start.68
  388.8 9.6 %down.2 = bf16[512,1024]{1,0:T(8,128)(2,1)} custom-call(s32[24]{0:T(128)} %fusion.26.place, bf16[1024,4096]{1,0:T(8,128)(2,1)} %get-tuple-element.471.refs_0_.refs_1_.refs_2_.refs_3_.active, bf16[1024,1024]{1,0:T(8,128)(2,1)} %copy-done.6, bf16[4,256,512]{2,1,0:T(8,128)(2,1)} %copy-done.5, bf16[4,256,512]{2,1,0:T(8,128)(2,1)} %copy-done.77, ...), custom_call_target="tpu_custom_call" | custom-call | flops 4294967296 | bytes 12582912 | tf_op jit(solution)/shard_map/down/pallas_call | solution.py:106
  400.8 1.8 collective-permute-start.73
  404.9 9.4 %down.3.mine = bf16[512,1024]{1,0:T(8,128)(2,1)} custom-call(s32[24]{0:T(128)} %fusion.26.place, bf16[1024,4096]{1,0:T(8,128)(2,1)} %get-tuple-element.471.refs_0_.refs_1_.refs_2_.refs_3_.active, bf16[1024,1024]{1,0:T(8,128)(2,1)} %copy-done.6, bf16[4,256,512]{2,1,0:T(8,128)(2,1)} %copy-done.5, bf16[4,256,512]{2,1,0:T(8,128)(2,1)} %copy-done.77, ...), custom_call_target="tpu_custom_call" | custom-call | flops 4294967296 | bytes 12582912 | tf_op jit(solution)/shard_map/down/pallas_call | solution.py:106
  418.9 1.7 collective-permute-start.81
  420.6 2.0 to_blocks.2
  423.9 3.1 collective-permute-start.84
  427.7 1.6 halves_joined.2
  429.4 1.6 halves_joined.3
  431.0 2.0 to_blocks.3
  432.9 1.6 heads_grads.1
  (468 shorter events, 95.8 us)
Async XLA Ops:
  1.8 14.1 %collective-permute-start.1 = (bf16[1,64,768]{2,1,0:T(8,128)(2,1)S(1)}, bf16[1,64,768]{2,1,0:T(8,128)(2,1)S(1)}, u32[]{:S(2)}, u32[]{:S(2)}) collective-permute-start(bf16[1,64,768]{2,1,0:T(8,128)(2,1)S(1)} %maximum_bitcast_fusion.1.refs_0_), channel_id=1, source_target_pairs={{0,24},{1,25},{2,26},{3,27},{4,28},{5,29},{6,30},{7,31},{8,0},{9,1... | collective-permute-start | bytes 294920 | tf_op jit(solution)/shard_map/ppermute | solution.py:48
  6.0 10.0 %collective-permute-start.2 = (bf16[1,64,768]{2,1,0:T(8,128)(2,1)S(1)}, bf16[1,64,768]{2,1,0:T(8,128)(2,1)S(1)}, u32[]{:S(2)}, u32[]{:S(2)}) collective-permute-start(bf16[1,64,768]{2,1,0:T(8,128)(2,1)S(1)} %maximum_bitcast_fusion.1.refs_0_), channel_id=1, source_target_pairs={{0,16},{1,17},{2,18},{3,19},{4,20},{5,21},{6,22},{7,23},{8,24},{9,... | collective-permute-start | bytes 294920 | tf_op jit(solution)/shard_map/ppermute | solution.py:48
  6.0 10.0 %collective-permute-start.3 = (bf16[1,64,768]{2,1,0:T(8,128)(2,1)S(1)}, bf16[1,64,768]{2,1,0:T(8,128)(2,1)S(1)}, u32[]{:S(2)}, u32[]{:S(2)}) collective-permute-start(bf16[1,64,768]{2,1,0:T(8,128)(2,1)S(1)} %maximum_bitcast_fusion.1.refs_0_), channel_id=1, source_target_pairs={{0,8},{1,9},{2,10},{3,11},{4,12},{5,13},{6,14},{7,15},{8,16},{9,17... | collective-permute-start | bytes 294920 | tf_op jit(solution)/shard_map/ppermute | solution.py:48
  7.5 8.5 %collective-permute-start = (bf16[512,1024]{1,0:T(8,128)(2,1)}, bf16[512,1024]{1,0:T(8,128)(2,1)}, u32[]{:S(2)}, u32[]{:S(2)}) collective-permute-start(bf16[512,1024]{1,0:T(8,128)(2,1)} %dynamic-slice_bitcast_fusion.3), channel_id=1, source_target_pairs={{0,1},{1,0},{2,3},{3,2},{4,5},{5,4},{6,7},{7,6},{8,9},{9,8},{10,11... | collective-permute-start | bytes 3145736 | tf_op jit(solution)/shard_map/ppermute | solution.py:55
  23.4 17.7 %collective-permute-start.12 = (bf16[1,64,1280]{2,1,0:T(8,128)(2,1)S(1)}, bf16[1,64,1280]{2,1,0:T(8,128)(2,1)S(1)}, u32[]{:S(2)}, u32[]{:S(2)}) collective-permute-start(bf16[1,64,1280]{2,1,0:T(8,128)(2,1)S(1)} %collective-permute-done.7.refs_1_), channel_id=1, source_target_pairs={{0,24},{1,25},{2,26},{3,27},{4,28},{5,29},{6,30},{7,31},{8,0},{9,1... | collective-permute-start | bytes 491528 | tf_op jit(solution)/shard_map/ppermute | solution.py:48
  27.3 13.9 %collective-permute-start.9 = (bf16[4,64,768]{2,1,0:T(8,128)(2,1)S(1)}, bf16[4,64,768]{2,1,0:T(8,128)(2,1)S(1)}, u32[]{:S(2)}, u32[]{:S(2)}) collective-permute-start(bf16[4,64,768]{2,1,0:T(8,128)(2,1)S(1)} %rolled.4.refs_5_.refs_0_), channel_id=1, source_target_pairs={{0,4},{1,3},{2,6},{3,1},{4,0},{5,7},{6,2},{7,5},{8,12},{9,11},{10,... | collective-permute-start | bytes 1179656 | tf_op jit(solution)/shard_map/ppermute | solution.py:48
  28.5 12.7 %collective-permute-start.10 = (bf16[4,64,768]{2,1,0:T(8,128)(2,1)}, bf16[4,64,768]{2,1,0:T(8,128)(2,1)}, u32[]{:S(2)}, u32[]{:S(2)}) collective-permute-start(bf16[4,64,768]{2,1,0:T(8,128)(2,1)} %collective-permute-done.6.refs_6_.refs_1_), channel_id=1, source_target_pairs={{0,4},{1,3},{2,6},{3,1},{4,0},{5,7},{6,2},{7,5},{8,12},{9,11},{10,... | collective-permute-start | bytes 1179656 | tf_op jit(solution)/shard_map/ppermute | solution.py:48
  28.8 13.2 %collective-permute-start.11 = (bf16[4,64,768]{2,1,0:T(8,128)(2,1)S(1)}, bf16[4,64,768]{2,1,0:T(8,128)(2,1)}, u32[]{:S(2)}, u32[]{:S(2)}) collective-permute-start(bf16[4,64,768]{2,1,0:T(8,128)(2,1)S(1)} %rolled.4.refs_5_.refs_0_), channel_id=1, source_target_pairs={{0,1},{1,0},{2,3},{3,2},{4,5},{5,4},{6,7},{7,6},{8,9},{9,8},{10,11... | collective-permute-start | bytes 1179656 | tf_op jit(solution)/shard_map/ppermute | solution.py:55
  30.1 11.0 %collective-permute-start.8 = (bf16[4,8,2176]{2,1,0:T(8,128)(2,1)S(1)}, bf16[4,8,2176]{2,1,0:T(8,128)(2,1)S(1)}, u32[]{:S(2)}, u32[]{:S(2)}) collective-permute-start(bf16[4,8,2176]{2,1,0:T(8,128)(2,1)S(1)} %pad_maximum_fusion.6), channel_id=1, source_target_pairs={{0,2},{1,3},{2,0},{3,1},{4,6},{5,7},{6,4},{7,5},{8,10},{9,11},{10,... | collective-permute-start | bytes 417800 | tf_op jit(solution)/shard_map/ppermute | solution.py:922
  52.3 13.0 %collective-permute-start.18 = (bf16[4,64,1280]{2,1,0:T(8,128)(2,1)S(1)}, bf16[4,64,1280]{2,1,0:T(8,128)(2,1)S(1)}, u32[]{:S(2)}, u32[]{:S(2)}) collective-permute-start(bf16[4,64,1280]{2,1,0:T(8,128)(2,1)S(1)} %rolled.5.refs_3_.refs_0_.refs_8_), channel_id=1, source_target_pairs={{0,2},{1,5},{2,0},{3,7},{4,6},{5,1},{6,4},{7,3},{8,10},{9,13},{10,... | collective-permute-start | bytes 1966088 | tf_op jit(solution)/shard_map/ppermute | solution.py:48
  54.3 11.0 %collective-permute-start.19 = (bf16[1,64,2048]{2,1,0:T(8,128)(2,1)S(1)}, bf16[1,64,2048]{2,1,0:T(8,128)(2,1)S(1)}, u32[]{:S(2)}, u32[]{:S(2)}) collective-permute-start(bf16[1,64,2048]{2,1,0:T(8,128)(2,1)S(1)} %dynamic-slice_bitcast_fusion.13.refs_0_), channel_id=1, source_target_pairs={{0,24},{1,25},{2,26},{3,27},{4,28},{5,29},{6,30},{7,31},{8,0},{9,1... | collective-permute-start | bytes 786440 | tf_op jit(solution)/shard_map/ppermute | solution.py:48
  65.3 13.3 %collective-permute-start.22 = (bf16[4,64,1280]{2,1,0:T(8,128)(2,1)S(1)}, bf16[4,64,1280]{2,1,0:T(8,128)(2,1)S(1)}, u32[]{:S(2)}, u32[]{:S(2)}) collective-permute-start(bf16[4,64,1280]{2,1,0:T(8,128)(2,1)S(1)} %rolled.5.refs_3_.refs_0_.refs_8_), channel_id=1, source_target_pairs={{0,1},{1,0},{2,3},{3,2},{4,5},{5,4},{6,7},{7,6},{8,9},{9,8},{10,11... | collective-permute-start | bytes 1966088 | tf_op jit(solution)/shard_map/ppermute | solution.py:55
  68.3 10.3 %collective-permute-start.23 = (bf16[4,64,1280]{2,1,0:T(8,128)(2,1)S(1)}, bf16[4,64,1280]{2,1,0:T(8,128)(2,1)S(1)}, u32[]{:S(2)}, u32[]{:S(2)}) collective-permute-start(bf16[4,64,1280]{2,1,0:T(8,128)(2,1)S(1)} %collective-permute-done.18.refs_4_.refs_1_.refs_9_), channel_id=1, source_target_pairs={{0,1},{1,0},{2,3},{3,2},{4,5},{5,4},{6,7},{7,6},{8,9},{9,8},{10,11... | collective-permute-start | bytes 1966088 | tf_op jit(solution)/shard_map/ppermute | solution.py:55
  68.4 16.6 %collective-permute-start.20 = (bf16[4,64,1280]{2,1,0:T(8,128)(2,1)S(1)}, bf16[4,64,1280]{2,1,0:T(8,128)(2,1)S(1)}, u32[]{:S(2)}, u32[]{:S(2)}) collective-permute-start(bf16[4,64,1280]{2,1,0:T(8,128)(2,1)S(1)} %rolled.5.refs_3_.refs_0_.refs_8_), channel_id=1, source_target_pairs={{0,4},{1,3},{2,6},{3,1},{4,0},{5,7},{6,2},{7,5},{8,12},{9,11},{10,... | collective-permute-start | bytes 1966088 | tf_op jit(solution)/shard_map/ppermute | solution.py:48
  68.6 10.0 %collective-permute-start.24 = (bf16[1,64,2048]{2,1,0:T(8,128)(2,1)S(1)}, bf16[1,64,2048]{2,1,0:T(8,128)(2,1)S(1)}, u32[]{:S(2)}, u32[]{:S(2)}) collective-permute-start(bf16[1,64,2048]{2,1,0:T(8,128)(2,1)S(1)} %collective-permute-done.19.refs_1_), channel_id=1, source_target_pairs={{0,24},{1,25},{2,26},{3,27},{4,28},{5,29},{6,30},{7,31},{8,0},{9,1... | collective-permute-start | bytes 786440 | tf_op jit(solution)/shard_map/ppermute | solution.py:48
  68.9 16.2 %collective-permute-start.21 = (bf16[4,64,1280]{2,1,0:T(8,128)(2,1)S(1)}, bf16[4,64,1280]{2,1,0:T(8,128)(2,1)S(1)}, u32[]{:S(2)}, u32[]{:S(2)}) collective-permute-start(bf16[4,64,1280]{2,1,0:T(8,128)(2,1)S(1)} %collective-permute-done.18.refs_4_.refs_1_.refs_9_), channel_id=1, source_target_pairs={{0,4},{1,3},{2,6},{3,1},{4,0},{5,7},{6,2},{7,5},{8,12},{9,11},{10,... | collective-permute-start | bytes 1966088 | tf_op jit(solution)/shard_map/ppermute | solution.py:48
  78.7 7.4 %collective-permute-start.25 = (bf16[1,64,2048]{2,1,0:T(8,128)(2,1)S(1)}, bf16[1,64,2048]{2,1,0:T(8,128)(2,1)S(1)}, u32[]{:S(2)}, u32[]{:S(2)}) collective-permute-start(bf16[1,64,2048]{2,1,0:T(8,128)(2,1)S(1)} %collective-permute-done.24.refs_2_), channel_id=1, source_target_pairs={{0,24},{1,25},{2,26},{3,27},{4,28},{5,29},{6,30},{7,31},{8,0},{9,1... | collective-permute-start | bytes 786440 | tf_op jit(solution)/shard_map/ppermute | solution.py:48
  88.2 10.0 %collective-permute-start.28 = (bf16[512,1024]{1,0:T(8,128)(2,1)S(1)}, bf16[512,1024]{1,0:T(8,128)(2,1)S(1)}, u32[]{:S(2)}, u32[]{:S(2)}) collective-permute-start(bf16[512,1024]{1,0:T(8,128)(2,1)S(1)} %dynamic-slice_bitcast_fusion.1), channel_id=1, source_target_pairs={{0,1},{1,0},{2,3},{3,2},{4,5},{5,4},{6,7},{7,6},{8,9},{9,8},{10,11... | collective-permute-start | bytes 3145736 | tf_op jit(solution)/shard_map/ppermute | solution.py:55
  90.7 17.8 %collective-permute-start.30 = (bf16[4,64,2048]{2,1,0:T(8,128)(2,1)S(1)}, bf16[4,64,2048]{2,1,0:T(8,128)(2,1)S(1)}, u32[]{:S(2)}, u32[]{:S(2)}) collective-permute-start(bf16[4,64,2048]{2,1,0:T(8,128)(2,1)S(1)} %rolled.6.refs_0_), channel_id=1, source_target_pairs={{0,2},{1,5},{2,0},{3,7},{4,6},{5,1},{6,4},{7,3},{8,10},{9,13},{10,... | collective-permute-start | bytes 3145736 | tf_op jit(solution)/shard_map/ppermute | solution.py:48
  91.0 7.2 %collective-permute-start.29 = (bf16[1,256,512]{2,1,0:T(8,128)(2,1)S(1)}, bf16[1,256,512]{2,1,0:T(8,128)(2,1)S(1)}, u32[]{:S(2)}, u32[]{:S(2)}) collective-permute-start(bf16[1,256,512]{2,1,0:T(8,128)(2,1)S(1)} %dynamic-slice_bitcast_fusion.12.refs_0_), channel_id=1, source_target_pairs={{0,24},{1,25},{2,26},{3,27},{4,28},{5,29},{6,30},{7,31},{8,0},{9,1... | collective-permute-start | bytes 786440 | tf_op jit(solution)/shard_map/ppermute | solution.py:48
  98.2 10.3 %collective-permute-start.31 = (bf16[1,256,512]{2,1,0:T(8,128)(2,1)S(1)}, bf16[1,256,512]{2,1,0:T(8,128)(2,1)S(1)}, u32[]{:S(2)}, u32[]{:S(2)}) collective-permute-start(bf16[1,256,512]{2,1,0:T(8,128)(2,1)S(1)} %collective-permute-done.29.refs_1_), channel_id=1, source_target_pairs={{0,24},{1,25},{2,26},{3,27},{4,28},{5,29},{6,30},{7,31},{8,0},{9,1... | collective-permute-start | bytes 786440 | tf_op jit(solution)/shard_map/ppermute | solution.py:48
  108.5 11.1 %collective-permute-start.32 = (bf16[4,64,2048]{2,1,0:T(8,128)(2,1)S(1)}, bf16[4,64,2048]{2,1,0:T(8,128)(2,1)S(1)}, u32[]{:S(2)}, u32[]{:S(2)}) collective-permute-start(bf16[4,64,2048]{2,1,0:T(8,128)(2,1)S(1)} %rolled.6.refs_0_), channel_id=1, source_target_pairs={{0,1},{1,0},{2,3},{3,2},{4,5},{5,4},{6,7},{7,6},{8,9},{9,8},{10,11... | collective-permute-start | bytes 3145736 | tf_op jit(solution)/shard_map/ppermute | solution.py:55
  111.3 8.4 %collective-permute-start.33 = (bf16[4,64,2048]{2,1,0:T(8,128)(2,1)S(1)}, bf16[4,64,2048]{2,1,0:T(8,128)(2,1)S(1)}, u32[]{:S(2)}, u32[]{:S(2)}) collective-permute-start(bf16[4,64,2048]{2,1,0:T(8,128)(2,1)S(1)} %collective-permute-done.30.refs_1_), channel_id=1, source_target_pairs={{0,1},{1,0},{2,3},{3,2},{4,5},{5,4},{6,7},{7,6},{8,9},{9,8},{10,11... | collective-permute-start | bytes 3145736 | tf_op jit(solution)/shard_map/ppermute | solution.py:55
  111.4 19.2 %collective-permute-start.35 = (bf16[4,64,2048]{2,1,0:T(8,128)(2,1)S(1)}, bf16[4,64,2048]{2,1,0:T(8,128)(2,1)S(1)}, u32[]{:S(2)}, u32[]{:S(2)}) collective-permute-start(bf16[4,64,2048]{2,1,0:T(8,128)(2,1)S(1)} %rolled.6.refs_0_), channel_id=1, source_target_pairs={{0,4},{1,3},{2,6},{3,1},{4,0},{5,7},{6,2},{7,5},{8,12},{9,11},{10,... | collective-permute-start | bytes 3145736 | tf_op jit(solution)/shard_map/ppermute | solution.py:48
  112.2 24.3 %collective-permute-start.36 = (bf16[4,64,2048]{2,1,0:T(8,128)(2,1)S(1)}, bf16[4,64,2048]{2,1,0:T(8,128)(2,1)S(1)}, u32[]{:S(2)}, u32[]{:S(2)}) collective-permute-start(bf16[4,64,2048]{2,1,0:T(8,128)(2,1)S(1)} %collective-permute-done.30.refs_1_), channel_id=1, source_target_pairs={{0,4},{1,3},{2,6},{3,1},{4,0},{5,7},{6,2},{7,5},{8,12},{9,11},{10,... | collective-permute-start | bytes 3145736 | tf_op jit(solution)/shard_map/ppermute | solution.py:48
  142.6 13.9 %collective-permute-start.39 = (bf16[4,256,512]{2,1,0:T(8,128)(2,1)S(1)}, bf16[4,256,512]{2,1,0:T(8,128)(2,1)S(1)}, u32[]{:S(2)}, u32[]{:S(2)}) collective-permute-start(bf16[4,256,512]{2,1,0:T(8,128)(2,1)S(1)} %rolled.7.refs_0_), channel_id=1, source_target_pairs={{0,2},{1,5},{2,0},{3,7},{4,6},{5,1},{6,4},{7,3},{8,10},{9,13},{10,... | collective-permute-start | bytes 3145736 | tf_op jit(solution)/shard_map/ppermute | solution.py:48
  156.6 15.0 %collective-permute-start.41 = (bf16[4,256,512]{2,1,0:T(8,128)(2,1)S(1)}, bf16[4,256,512]{2,1,0:T(8,128)(2,1)S(1)}, u32[]{:S(2)}, u32[]{:S(2)}) collective-permute-start(bf16[4,256,512]{2,1,0:T(8,128)(2,1)S(1)} %rolled.7.refs_0_), channel_id=1, source_target_pairs={{0,1},{1,0},{2,3},{3,2},{4,5},{5,4},{6,7},{7,6},{8,9},{9,8},{10,11... | collective-permute-start | bytes 3145736 | tf_op jit(solution)/shard_map/ppermute | solution.py:55
  157.8 13.8 %collective-permute-start.42 = (bf16[4,256,512]{2,1,0:T(8,128)(2,1)S(1)}, bf16[4,256,512]{2,1,0:T(8,128)(2,1)}, u32[]{:S(2)}, u32[]{:S(2)}) collective-permute-start(bf16[4,256,512]{2,1,0:T(8,128)(2,1)S(1)} %collective-permute-done.39.refs_1_), channel_id=1, source_target_pairs={{0,1},{1,0},{2,3},{3,2},{4,5},{5,4},{6,7},{7,6},{8,9},{9,8},{10,11... | collective-permute-start | bytes 3145736 | tf_op jit(solution)/shard_map/ppermute | solution.py:55
  157.8 23.5 %collective-permute-start.40 = (bf16[4,256,512]{2,1,0:T(8,128)(2,1)S(1)}, bf16[4,256,512]{2,1,0:T(8,128)(2,1)}, u32[]{:S(2)}, u32[]{:S(2)}) collective-permute-start(bf16[4,256,512]{2,1,0:T(8,128)(2,1)S(1)} %rolled.7.refs_0_), channel_id=1, source_target_pairs={{0,4},{1,3},{2,6},{3,1},{4,0},{5,7},{6,2},{7,5},{8,12},{9,11},{10,... | collective-permute-start | bytes 3145736 | tf_op jit(solution)/shard_map/ppermute | solution.py:48
  158.7 24.4 %collective-permute-start.43 = (bf16[4,256,512]{2,1,0:T(8,128)(2,1)S(1)}, bf16[4,256,512]{2,1,0:T(8,128)(2,1)}, u32[]{:S(2)}, u32[]{:S(2)}) collective-permute-start(bf16[4,256,512]{2,1,0:T(8,128)(2,1)S(1)} %collective-permute-done.39.refs_1_), channel_id=1, source_target_pairs={{0,4},{1,3},{2,6},{3,1},{4,0},{5,7},{6,2},{7,5},{8,12},{9,11},{10,... | collective-permute-start | bytes 3145736 | tf_op jit(solution)/shard_map/ppermute | solution.py:48
  188.5 15.9 %collective-permute-start.46 = (bf16[4,4,256,512]{3,2,1,0:T(8,128)(2,1)}, bf16[4,4,256,512]{3,2,1,0:T(8,128)(2,1)}, u32[]{:S(2)}, u32[]{:S(2)}) collective-permute-start(bf16[4,4,256,512]{3,2,1,0:T(8,128)(2,1)} %wide_chunks.2), channel_id=1, source_target_pairs={{0,1},{1,0},{2,3},{3,2},{4,5},{5,4},{6,7},{7,6},{8,9},{9,8},{10,11... | collective-permute-start | bytes 12582920 | tf_op jit(solution)/shard_map/ppermute | solution.py:55
  225.3 18.2 %collective-permute-start.47 = (bf16[4,4,64,2048]{3,2,1,0:T(8,128)(2,1)}, bf16[4,4,64,2048]{3,2,1,0:T(8,128)(2,1)}, u32[]{:S(2)}, u32[]{:S(2)}) collective-permute-start(bf16[4,4,64,2048]{3,2,1,0:T(8,128)(2,1)} %row_chunks.2), channel_id=1, source_target_pairs={{0,1},{1,0},{2,3},{3,2},{4,5},{5,4},{6,7},{7,6},{8,9},{9,8},{10,11... | collective-permute-start | bytes 12582920 | tf_op jit(solution)/shard_map/ppermute | solution.py:55
  225.7 17.8 %collective-permute-start.48 = (bf16[4,256,512]{2,1,0:T(8,128)(2,1)S(1)}, bf16[4,256,512]{2,1,0:T(8,128)(2,1)S(1)}, u32[]{:S(2)}, u32[]{:S(2)}) collective-permute-start(bf16[4,256,512]{2,1,0:T(8,128)(2,1)S(1)} %copy-done.116), channel_id=1, source_target_pairs={{0,4},{1,3},{2,6},{3,1},{4,0},{5,7},{6,2},{7,5},{8,12},{9,11},{10,... | collective-permute-start | bytes 3145736 | tf_op jit(solution)/shard_map/ppermute | solution.py:48
  226.6 38.6 %collective-permute-start.50 = (bf16[4,256,512]{2,1,0:T(8,128)(2,1)}, bf16[4,256,512]{2,1,0:T(8,128)(2,1)}, u32[]{:S(2)}, u32[]{:S(2)}) collective-permute-start(bf16[4,256,512]{2,1,0:T(8,128)(2,1)} %get-tuple-element.391), channel_id=1, source_target_pairs={{0,4},{1,3},{2,6},{3,1},{4,0},{5,7},{6,2},{7,5},{8,12},{9,11},{10,... | collective-permute-start | bytes 3145736 | tf_op jit(solution)/shard_map/ppermute | solution.py:48
  244.8 20.4 %collective-permute-start.49 = (bf16[4,256,512]{2,1,0:T(8,128)(2,1)}, bf16[4,256,512]{2,1,0:T(8,128)(2,1)}, u32[]{:S(2)}, u32[]{:S(2)}) collective-permute-start(bf16[4,256,512]{2,1,0:T(8,128)(2,1)} %add_convert_fusion.3), channel_id=1, source_target_pairs={{0,2},{1,5},{2,0},{3,7},{4,6},{5,1},{6,4},{7,3},{8,10},{9,13},{10,... | collective-permute-start | bytes 3145736 | tf_op jit(solution)/shard_map/ppermute | solution.py:48
  265.2 18.6 %collective-permute-start.52 = (bf16[4,64,2048]{2,1,0:T(8,128)(2,1)S(1)}, bf16[4,64,2048]{2,1,0:T(8,128)(2,1)S(1)}, u32[]{:S(2)}, u32[]{:S(2)}) collective-permute-start(bf16[4,64,2048]{2,1,0:T(8,128)(2,1)S(1)} %copy-done.115), channel_id=1, source_target_pairs={{0,4},{1,3},{2,6},{3,1},{4,0},{5,7},{6,2},{7,5},{8,12},{9,11},{10,... | collective-permute-start | bytes 3145736 | tf_op jit(solution)/shard_map/ppermute | solution.py:48
  269.3 14.5 %collective-permute-start.51 = (bf16[256,512]{1,0:T(8,128)(2,1)S(1)}, bf16[256,512]{1,0:T(8,128)(2,1)S(1)}, u32[]{:S(2)}, u32[]{:S(2)}) collective-permute-start(bf16[256,512]{1,0:T(8,128)(2,1)S(1)} %get-tuple-element.518), channel_id=1, source_target_pairs={{0,16},{1,17},{2,18},{3,19},{4,20},{5,21},{6,22},{7,23},{8,24},{9,... | collective-permute-start | bytes 786440 | tf_op jit(solution)/shard_map/ppermute | solution.py:48
  284.2 14.0 %collective-permute-start.53 = (bf16[4,64,2048]{2,1,0:T(8,128)(2,1)S(1)}, bf16[4,64,2048]{2,1,0:T(8,128)(2,1)S(1)}, u32[]{:S(2)}, u32[]{:S(2)}) collective-permute-start(bf16[4,64,2048]{2,1,0:T(8,128)(2,1)S(1)} %add_convert_fusion.1), channel_id=1, source_target_pairs={{0,2},{1,5},{2,0},{3,7},{4,6},{5,1},{6,4},{7,3},{8,10},{9,13},{10,... | collective-permute-start | bytes 3145736 | tf_op jit(solution)/shard_map/ppermute | solution.py:48
  305.4 16.0 %collective-permute-start.54 = (bf16[4,4,64,1280]{3,2,1,0:T(8,128)(2,1)}, bf16[4,4,64,1280]{3,2,1,0:T(8,128)(2,1)}, u32[]{:S(2)}, u32[]{:S(2)}) collective-permute-start(bf16[4,4,64,1280]{3,2,1,0:T(8,128)(2,1)} %heads_chunks.4), channel_id=1, source_target_pairs={{0,1},{1,0},{2,3},{3,2},{4,5},{5,4},{6,7},{7,6},{8,9},{9,8},{10,11... | collective-permute-start | bytes 7864328 | tf_op jit(solution)/shard_map/ppermute | solution.py:55
  306.8 14.6 %collective-permute-start.56 = (bf16[256,512]{1,0:T(8,128)(2,1)S(1)}, bf16[256,512]{1,0:T(8,128)(2,1)S(1)}, u32[]{:S(2)}, u32[]{:S(2)}) collective-permute-start(bf16[256,512]{1,0:T(8,128)(2,1)S(1)} %get-tuple-element.412), channel_id=1, source_target_pairs={{0,16},{1,17},{2,18},{3,19},{4,20},{5,21},{6,22},{7,23},{8,24},{9,... | collective-permute-start | bytes 786440 | tf_op jit(solution)/shard_map/ppermute | solution.py:48
  306.9 14.5 %collective-permute-start.55 = (bf16[4,64,2048]{2,1,0:T(8,128)(2,1)S(1)}, bf16[4,64,2048]{2,1,0:T(8,128)(2,1)S(1)}, u32[]{:S(2)}, u32[]{:S(2)}) collective-permute-start(bf16[4,64,2048]{2,1,0:T(8,128)(2,1)S(1)} %copy-done.114), channel_id=1, source_target_pairs={{0,4},{1,3},{2,6},{3,1},{4,0},{5,7},{6,2},{7,5},{8,12},{9,11},{10,... | collective-permute-start | bytes 3145736 | tf_op jit(solution)/shard_map/ppermute | solution.py:48
  307.4 14.0 %collective-permute-start.57 = (bf16[256,512]{1,0:T(8,128)(2,1)S(1)}, bf16[256,512]{1,0:T(8,128)(2,1)S(1)}, u32[]{:S(2)}, u32[]{:S(2)}) collective-permute-start(bf16[256,512]{1,0:T(8,128)(2,1)S(1)} %add_convert_fusion.11), channel_id=1, source_target_pairs={{0,8},{1,9},{2,10},{3,11},{4,12},{5,13},{6,14},{7,15},{8,0},{9,1},... | collective-permute-start | bytes 786440 | tf_op jit(solution)/shard_map/ppermute | solution.py:48
  330.0 19.8 %collective-permute-start.58 = (bf16[4,64,1280]{2,1,0:T(8,128)(2,1)S(1)}, bf16[4,64,1280]{2,1,0:T(8,128)(2,1)S(1)}, u32[]{:S(2)}, u32[]{:S(2)}) collective-permute-start(bf16[4,64,1280]{2,1,0:T(8,128)(2,1)S(1)} %get-tuple-element.429), channel_id=1, source_target_pairs={{0,4},{1,3},{2,6},{3,1},{4,0},{5,7},{6,2},{7,5},{8,12},{9,11},{10,... | collective-permute-start | bytes 1966088 | tf_op jit(solution)/shard_map/ppermute | solution.py:48
  330.9 18.9 %collective-permute-start.59 = (bf16[4,64,1280]{2,1,0:T(8,128)(2,1)S(1)}, bf16[4,64,1280]{2,1,0:T(8,128)(2,1)S(1)}, u32[]{:S(2)}, u32[]{:S(2)}) collective-permute-start(bf16[4,64,1280]{2,1,0:T(8,128)(2,1)S(1)} %get-tuple-element.430), channel_id=1, source_target_pairs={{0,4},{1,3},{2,6},{3,1},{4,0},{5,7},{6,2},{7,5},{8,12},{9,11},{10,... | collective-permute-start | bytes 1966088 | tf_op jit(solution)/shard_map/ppermute | solution.py:48
  334.5 15.3 %collective-permute-start.60 = (bf16[64,2048]{1,0:T(8,128)(2,1)S(1)}, bf16[64,2048]{1,0:T(8,128)(2,1)S(1)}, u32[]{:S(2)}, u32[]{:S(2)}) collective-permute-start(bf16[64,2048]{1,0:T(8,128)(2,1)S(1)} %get-tuple-element.514), channel_id=1, source_target_pairs={{0,16},{1,17},{2,18},{3,19},{4,20},{5,21},{6,22},{7,23},{8,24},{9,... | collective-permute-start | bytes 786440 | tf_op jit(solution)/shard_map/ppermute | solution.py:48
  336.2 13.5 %collective-permute-start.61 = (bf16[256,512]{1,0:T(8,128)(2,1)S(1)}, bf16[256,512]{1,0:T(8,128)(2,1)S(1)}, u32[]{:S(2)}, u32[]{:S(2)}) collective-permute-start(bf16[256,512]{1,0:T(8,128)(2,1)S(1)} %add_convert_fusion.10.own), channel_id=1, source_target_pairs={{0,1},{1,0},{2,3},{3,2},{4,5},{5,4},{6,7},{7,6},{8,9},{9,8},{10,11... | collective-permute-start | bytes 786440 | tf_op jit(solution)/shard_map/ppermute | solution.py:55
  353.6 7.4 %collective-permute-start.62 = (bf16[4,4,64,768]{3,2,1,0:T(8,128)(2,1)}, bf16[4,4,64,768]{3,2,1,0:T(8,128)(2,1)}, u32[]{:S(2)}, u32[]{:S(2)}) collective-permute-start(bf16[4,4,64,768]{3,2,1,0:T(8,128)(2,1)} %heads_chunks.6), channel_id=1, source_target_pairs={{0,1},{1,0},{2,3},{3,2},{4,5},{5,4},{6,7},{7,6},{8,9},{9,8},{10,11... | collective-permute-start | bytes 4718600 | tf_op jit(solution)/shard_map/ppermute | solution.py:55
  356.1 22.7 %collective-permute-start.64 = (bf16[4,64,1280]{2,1,0:T(8,128)(2,1)}, bf16[4,64,1280]{2,1,0:T(8,128)(2,1)}, u32[]{:S(2)}, u32[]{:S(2)}) collective-permute-start(bf16[4,64,1280]{2,1,0:T(8,128)(2,1)} %add_convert_fusion.6), channel_id=1, source_target_pairs={{0,2},{1,5},{2,0},{3,7},{4,6},{5,1},{6,4},{7,3},{8,10},{9,13},{10,... | collective-permute-start | bytes 1966088 | tf_op jit(solution)/shard_map/ppermute | solution.py:48
  356.1 22.6 %collective-permute-start.65 = (bf16[64,2048]{1,0:T(8,128)(2,1)}, bf16[64,2048]{1,0:T(8,128)(2,1)}, u32[]{:S(2)}, u32[]{:S(2)}) collective-permute-start(bf16[64,2048]{1,0:T(8,128)(2,1)} %get-tuple-element.453), channel_id=1, source_target_pairs={{0,16},{1,17},{2,18},{3,19},{4,20},{5,21},{6,22},{7,23},{8,24},{9,... | collective-permute-start | bytes 786440 | tf_op jit(solution)/shard_map/ppermute | solution.py:48
  363.4 15.3 %collective-permute-start.63 = (bf16[2,4,64,768]{3,2,1,0:T(8,128)(2,1)S(1)}, bf16[2,4,64,768]{3,2,1,0:T(8,128)(2,1)S(1)}, u32[]{:S(2)}, u32[]{:S(2)}) collective-permute-start(bf16[2,4,64,768]{3,2,1,0:T(8,128)(2,1)S(1)} %add_convert_fusion.4), channel_id=1, source_target_pairs={{0,4},{1,3},{2,6},{3,1},{4,0},{5,7},{6,2},{7,5},{8,12},{9,11},{10,... | collective-permute-start | bytes 2359304 | tf_op jit(solution)/shard_map/ppermute | solution.py:48
  364.1 14.7 %collective-permute-start.66 = (bf16[64,2048]{1,0:T(8,128)(2,1)S(1)}, bf16[64,2048]{1,0:T(8,128)(2,1)S(1)}, u32[]{:S(2)}, u32[]{:S(2)}) collective-permute-start(bf16[64,2048]{1,0:T(8,128)(2,1)S(1)} %add_convert_fusion.9), channel_id=1, source_target_pairs={{0,8},{1,9},{2,10},{3,11},{4,12},{5,13},{6,14},{7,15},{8,0},{9,1},... | collective-permute-start | bytes 786440 | tf_op jit(solution)/shard_map/ppermute | solution.py:48
  380.7 17.8 %collective-permute-start.67 = (bf16[4,64,768]{2,1,0:T(8,128)(2,1)}, bf16[4,64,768]{2,1,0:T(8,128)(2,1)}, u32[]{:S(2)}, u32[]{:S(2)}) collective-permute-start(bf16[4,64,768]{2,1,0:T(8,128)(2,1)} %fusion.4), channel_id=1, source_target_pairs={{0,2},{1,5},{2,0},{3,7},{4,6},{5,1},{6,4},{7,3},{8,10},{9,13},{10,... | collective-permute-start | bytes 1179656 | tf_op jit(solution)/shard_map/ppermute | solution.py:48
  382.1 16.4 %collective-permute-start.71 = (bf16[512,1024]{1,0:T(8,128)(2,1)}, bf16[512,1024]{1,0:T(8,128)(2,1)S(1)}, u32[]{:S(2)}, u32[]{:S(2)}) collective-permute-start(bf16[512,1024]{1,0:T(8,128)(2,1)} %get-tuple-element.470), channel_id=1, source_target_pairs={{0,1},{1,0},{2,3},{3,2},{4,5},{5,4},{6,7},{7,6},{8,9},{9,8},{10,11... | collective-permute-start | bytes 3145736 | tf_op jit(solution)/shard_map/ppermute | solution.py:55
  384.7 13.8 %collective-permute-start.68 = (bf16[64,1280]{1,0:T(8,128)(2,1)S(1)}, bf16[64,1280]{1,0:T(8,128)(2,1)S(1)}, u32[]{:S(2)}, u32[]{:S(2)}) collective-permute-start(bf16[64,1280]{1,0:T(8,128)(2,1)S(1)} %get-tuple-element.522), channel_id=1, source_target_pairs={{0,16},{1,17},{2,18},{3,19},{4,20},{5,21},{6,22},{7,23},{8,24},{9,... | collective-permute-start | bytes 491528 | tf_op jit(solution)/shard_map/ppermute | solution.py:48
  387.5 10.9 %collective-permute-start.69 = (bf16[64,2048]{1,0:T(8,128)(2,1)S(1)}, bf16[64,2048]{1,0:T(8,128)(2,1)S(1)}, u32[]{:S(2)}, u32[]{:S(2)}) collective-permute-start(bf16[64,2048]{1,0:T(8,128)(2,1)S(1)} %add_convert_fusion.8.own), channel_id=1, source_target_pairs={{0,1},{1,0},{2,3},{3,2},{4,5},{5,4},{6,7},{7,6},{8,9},{9,8},{10,11... | collective-permute-start | bytes 786440 | tf_op jit(solution)/shard_map/ppermute | solution.py:55
  388.0 10.4 %collective-permute-start.70 = (f32[8,1024]{1,0:T(8,128)S(1)}, f32[8,1024]{1,0:T(8,128)S(1)}, u32[]{:S(2)}, u32[]{:S(2)}) collective-permute-start(f32[8,1024]{1,0:T(8,128)S(1)} %sums.1), channel_id=1, source_target_pairs={{0,16},{1,17},{2,18},{3,19},{4,20},{5,21},{6,22},{7,23},{8,24},{9,... | collective-permute-start | bytes 98312 | tf_op jit(solution)/shard_map/ppermute | solution.py:922
  399.1 16.1 %collective-permute-start.72 = (bf16[512,1024]{1,0:T(8,128)(2,1)}, bf16[512,1024]{1,0:T(8,128)(2,1)S(1)}, u32[]{:S(2)}, u32[]{:S(2)}) collective-permute-start(bf16[512,1024]{1,0:T(8,128)(2,1)} %down.2), channel_id=1, source_target_pairs={{0,1},{1,0},{2,3},{3,2},{4,5},{5,4},{6,7},{7,6},{8,9},{9,8},{10,11... | collective-permute-start | bytes 3145736 | tf_op jit(solution)/shard_map/ppermute | solution.py:55
  400.8 13.6 %collective-permute-start.73 = (bf16[64,768]{1,0:T(8,128)(2,1)S(1)}, bf16[64,768]{1,0:T(8,128)(2,1)S(1)}, u32[]{:S(2)}, u32[]{:S(2)}) collective-permute-start(bf16[64,768]{1,0:T(8,128)(2,1)S(1)} %get-tuple-element.530), channel_id=1, source_target_pairs={{0,16},{1,17},{2,18},{3,19},{4,20},{5,21},{6,22},{7,23},{8,24},{9,... | collective-permute-start | bytes 294920 | tf_op jit(solution)/shard_map/ppermute | solution.py:48
  402.6 12.6 %collective-permute-start.74 = (bf16[64,1280]{1,0:T(8,128)(2,1)}, bf16[64,1280]{1,0:T(8,128)(2,1)S(1)}, u32[]{:S(2)}, u32[]{:S(2)}) collective-permute-start(bf16[64,1280]{1,0:T(8,128)(2,1)} %get-tuple-element.480), channel_id=1, source_target_pairs={{0,16},{1,17},{2,18},{3,19},{4,20},{5,21},{6,22},{7,23},{8,24},{9,... | collective-permute-start | bytes 491528 | tf_op jit(solution)/shard_map/ppermute | solution.py:48
  403.3 11.9 %collective-permute-start.75 = (bf16[64,1280]{1,0:T(8,128)(2,1)S(1)}, bf16[64,1280]{1,0:T(8,128)(2,1)S(1)}, u32[]{:S(2)}, u32[]{:S(2)}) collective-permute-start(bf16[64,1280]{1,0:T(8,128)(2,1)S(1)} %add_convert_fusion.13), channel_id=1, source_target_pairs={{0,8},{1,9},{2,10},{3,11},{4,12},{5,13},{6,14},{7,15},{8,0},{9,1},... | collective-permute-start | bytes 491528 | tf_op jit(solution)/shard_map/ppermute | solution.py:48
  404.2 10.2 %collective-permute-start.76 = (f32[8,2048]{1,0:T(8,128)S(1)}, f32[8,2048]{1,0:T(8,128)S(1)}, u32[]{:S(2)}, u32[]{:S(2)}) collective-permute-start(f32[8,2048]{1,0:T(8,128)S(1)} %constant_dynamic-update-slice_fusion), channel_id=1, source_target_pairs={{0,8},{1,9},{2,10},{3,11},{4,12},{5,13},{6,14},{7,15},{8,0},{9,1},... | collective-permute-start | bytes 196616 | tf_op jit(solution)/shard_map/ppermute | solution.py:922
  415.2 8.5 %collective-permute-start.77 = (f32[8,4096]{1,0:T(8,128)S(1)}, f32[8,4096]{1,0:T(8,128)S(1)}, u32[]{:S(2)}, u32[]{:S(2)}) collective-permute-start(f32[8,4096]{1,0:T(8,128)S(1)} %constant_dynamic-update-slice_fusion.2), channel_id=1, source_target_pairs={{0,2},{1,3},{2,0},{3,1},{4,6},{5,7},{6,4},{7,5},{8,10},{9,11},{10,... | collective-permute-start | bytes 393224 | tf_op jit(solution)/shard_map/ppermute | solution.py:922
  416.4 7.3 %collective-permute-start.78 = (f32[8,4096]{1,0:T(8,128)S(1)}, f32[8,4096]{1,0:T(8,128)S(1)}, u32[]{:S(2)}, u32[]{:S(2)}) collective-permute-start(f32[8,4096]{1,0:T(8,128)S(1)} %constant_dynamic-update-slice_fusion.2), channel_id=1, source_target_pairs={{0,4},{1,5},{2,6},{3,7},{4,0},{5,1},{6,2},{7,3},{8,12},{9,13},{10,... | collective-permute-start | bytes 393224 | tf_op jit(solution)/shard_map/ppermute | solution.py:922
  423.9 10.7 %collective-permute-start.84 = (f32[8,16384]{1,0:T(8,128)S(1)}, f32[8,16384]{1,0:T(8,128)S(1)}, u32[]{:S(2)}, u32[]{:S(2)}) collective-permute-start(f32[8,16384]{1,0:T(8,128)S(1)} %constant_dynamic-update-slice_fusion.4.refs_0_), channel_id=1, source_target_pairs={{0,1},{1,0},{2,3},{3,2},{4,5},{5,4},{6,7},{7,6},{8,9},{9,8},{10,11... | collective-permute-start | bytes 1572872 | tf_op jit(solution)/shard_map/ppermute | solution.py:1357
  (145 other events, 1977.7 us)
